TPU v7x, 32 devices: a whole 2x2x4 slice. The times are simulated.
32 devices in a mesh: tile: 8 (over y, x, core), sub: 4 (over z).
Axes of the slice: x: 2, y: 2, z: 4, core: 2. Of those that a mesh axis runs over, the one named last changes fastest.
Arguments:
- right_side: float32 [8, 131072], P(None, ('tile', 'sub')), may hold values from -6 to 6
- point_order: int32 [32, 4096], P(('tile', 'sub')), may hold values from 0 to 4095, each once within a row
- noise_var: float32 [131072], P(('tile', 'sub')), may hold values from 0.1 to 1
- block_pairs: int32 [3072, 2], P(('tile', 'sub')), may hold values from -1 to 511, as said below
- pair_blocks: bfloat16 [3072, 256, 256], P(('tile', 'sub')), as said below
- diag_blocks: bfloat16 [512, 256, 256], P(('tile', 'sub')), as said below
Outputs:
- solution: float32 [8, 131072], P(None, ('tile', 'sub'))
- residual: float32 [8, 131072], P(None, ('tile', 'sub'))
Inputs may be any that keep to these rules, and one draw needn't show every extreme that they name: `block_pairs`: the blocks form a grid of rows of 16 blocks in row-major order; device d (tile slowest, then sub) owns blocks 16 d to 16 d + 15, one grid row. A slot holds (r, c) with c the right, lower-left, lower or lower-right grid neighbour of r, or (-1, -1) when empty; every such neighbouring pair is held exactly once, by a device of the tile that owns r. On each device the live slots come first, and in every tile some device has all 96 slots live. pair_blocks[p] has the rows of block r and the columns of block c of block_pairs[p], and is zero for an empty slot; with diag_blocks these are the bfloat16 values of all nonzero blocks of a kernel matrix that is positive semi-definite before rounding. Each diag_blocks[q] is symmetric.
All inputs are finite; a program needn't handle non-finite values.
Results may differ from a plain program's by a relative error of at most 0.0075.
Values may be sent and summed in bfloat16 or wider, within the bound.
No kernel may reach another device: no remote copies, remote signals or barrier semaphores. Data moves between devices by JAX's collectives and lax.ppermute only.
A program may use at most 64 MiB of HBM per device.

v0:
```python
import jax
import jax.numpy as jnp
from jax import lax
from jax.sharding import PartitionSpec as P

ITERS = 3


def from_behind(block, axis, distance):
    devices = range(lax.axis_size(axis))
    route = [(i - distance, i) for i in devices if i - distance in devices]
    return lax.ppermute(block, axis, route)


def on_device(right_side, point_order, noise_var, block_pairs, pair_blocks, diag_blocks):
    sub_count = lax.axis_size("sub")
    sub_index = lax.axis_index("sub")
    tile_index = lax.axis_index("tile")
    rhs_count = right_side.shape[0]
    points_dev = right_side.shape[1]
    blocks_dev = diag_blocks.shape[0]
    block_len = diag_blocks.shape[1]
    tile_blocks = blocks_dev * sub_count
    tile_points = tile_blocks * block_len
    extended = tile_blocks + blocks_dev
    first_block = tile_index * tile_blocks
    live_slot = block_pairs[:, 0] >= 0
    row_local = jnp.where(live_slot, block_pairs[:, 0] - first_block, 0)
    col_local = jnp.where(live_slot, block_pairs[:, 1] - first_block, 0)
    slot_ids = lax.broadcasted_iota(jnp.int32, (1, extended), 1)
    weight = live_slot.astype(jnp.float32)[:, None]
    row_hot = (row_local[:, None] == slot_ids).astype(jnp.float32) * weight
    col_hot = (col_local[:, None] == slot_ids).astype(jnp.float32) * weight
    curve_rhs = jnp.take(right_side, point_order[0], axis=1)
    own_start = sub_index * points_dev
    start_vec = lax.all_gather(curve_rhs.astype(jnp.bfloat16), "sub", axis=1, tiled=True).astype(
        curve_rhs.dtype
    )

    def reduce_all(values):
        return lax.psum(values, "tile")

    solution = jnp.zeros_like(start_vec)
    residual = start_vec
    direction = start_vec
    norm_now = reduce_all(jnp.sum(residual * residual, axis=1))
    for iteration in range(ITERS):
        rounded = direction.astype(jnp.bfloat16)
        image_own_direction = lax.dynamic_slice_in_dim(direction, own_start, points_dev, 1)
        image_own_rounded = lax.dynamic_slice_in_dim(rounded, own_start, points_dev, 1)
        ahead_row = from_behind(rounded[:, :points_dev], "tile", -1)
        joined = jnp.concatenate([rounded, ahead_row], axis=1).reshape(
            rhs_count, extended, block_len
        )
        from_cols = jnp.take(joined, col_local, axis=1)
        from_rows = jnp.take(joined, row_local, axis=1)
        to_rows = jnp.einsum(
            "pij,rpj->rpi", pair_blocks, from_cols, preferred_element_type=jnp.float32
        )
        to_cols = jnp.einsum(
            "pij,rpi->rpj", pair_blocks, from_rows, preferred_element_type=jnp.float32
        )
        spread = jnp.einsum("rpi,pq->rqi", to_rows, row_hot, precision=lax.Precision.HIGHEST)
        spread = spread + jnp.einsum(
            "rpj,pq->rqj", to_cols, col_hot, precision=lax.Precision.HIGHEST
        )
        spread = spread.reshape(rhs_count, extended * block_len)
        arrived = from_behind(spread[:, tile_points:].astype(jnp.bfloat16), "tile", 1).astype(
            jnp.float32
        )
        pair_sums = jnp.concatenate(
            [spread[:, :points_dev] + arrived, spread[:, points_dev:tile_points]], axis=1
        )
        diag_part = jnp.einsum(
            "bij,rbj->rbi",
            diag_blocks,
            image_own_rounded.reshape(rhs_count, blocks_dev, block_len),
            preferred_element_type=jnp.float32,
        )
        placed = lax.dynamic_slice_in_dim(pair_sums, own_start, points_dev, 1) + (
            diag_part.reshape(rhs_count, points_dev) + noise_var[None, :] * image_own_direction
        )
        pair_sums = lax.dynamic_update_slice_in_dim(pair_sums, placed, own_start, 1)
        image_vec = lax.psum(pair_sums, "sub")
        curvature = reduce_all(jnp.sum(direction * image_vec, axis=1))
        step_size = norm_now / curvature
        solution = solution + step_size[:, None] * direction
        new_residual = residual - step_size[:, None] * image_vec
        if iteration + 1 < ITERS:
            norm_next = reduce_all(jnp.sum(new_residual * new_residual, axis=1))
            direction = new_residual + (norm_next / norm_now)[:, None] * direction
            norm_now = norm_next
        residual = new_residual
    own_solution = lax.dynamic_slice_in_dim(solution, own_start, points_dev, 1)
    own_residual = lax.dynamic_slice_in_dim(residual, own_start, points_dev, 1)
    return (own_solution, own_residual)


def solution(mesh):
    placed = (
        P(None, ("tile", "sub")),
        P(("tile", "sub"), None),
        P(("tile", "sub")),
        P(("tile", "sub"), None),
        P(("tile", "sub"), None, None),
        P(("tile", "sub"), None, None),
    )
    return jax.shard_map(
        on_device,
        mesh=mesh,
        in_specs=placed,
        out_specs=(P(None, ("tile", "sub")), P(None, ("tile", "sub"))),
        check_vma=False,
    )
```

profile of v0, /device:TPU:0, one launch (start us, length us, event | category | flops | bytes accessed | tf_op | source)
XLA Modules:
  0.0 326.3 jit_solution(12015650363193205063)
XLA Ops:
  9.5 14.9 %gather_fusion = bf16[4096,8]{1,0:T(8,128)(2,1)} fusion(bf16[8,4096]{0,1:T(8,128)(2,1)S(1)} %copy.71, s32[4096]{0:T(1024)S(1)} %broadcast_clamp_fusion), kind=kCustom, calls=%fused_computation.6 | custom fusion | bytes 147456 | tf_op jit(solution)/shard_map/jit(_take)/gather | solution.py:34
  26.7 15.6 %all_gather.3 = bf16[8,16384]{1,0:T(8,128)(2,1)S(1)} all-gather(bf16[8,4096]{1,0:T(8,128)(2,1)S(1)} %fusion.45), channel_id=1, replica_groups=mesh['tile'=8,'sub'=4] {'sub'}, dimensions={1}, use_global_device_ids=true | all-gather | bytes 327680 | tf_op jit(solution)/shard_map/all_gather | solution.py:36
  48.8 8.2 %convolution_bitcast_fusion.5 = f32[8,96,256]{2,0,1:T(8,128)S(1)} fusion(bf16[96,256,256]{2,1,0:T(8,128)(2,1)} %param.12, bf16[96,8,256]{2,1,0:T(8,128)(2,1)} %gather_fusion.1, pred[96]{0:T(512)(128)(4,1)} %get-tuple-element.29), kind=kOutput, calls=%fused_computation.12 | convolution fusion | flops 100859904 | bytes 13762656 | tf_op jit(solution)/shard_map/pij,rpj->rpi/dot_general | solution.py:57
  58.0 1.8 convolution_bitcast_fusion.4
  61.1 3.5 %collective-permute-start.1 = (bf16[8,4096]{1,0:T(8,128)(2,1)S(1)}, bf16[8,4096]{1,0:T(8,128)(2,1)S(1)}, u32[]{:S(2)}, u32[]{:S(2)}) collective-permute-start(bf16[8,4096]{1,0:T(8,128)(2,1)S(1)} %slice.103), channel_id=1, source_target_pairs={{0,4},{4,8},{8,12},{12,16},{16,20},{20,24},{24,28},{1,5},{5,9},{9,... | collective-permute-start | bytes 196616 | tf_op jit(solution)/shard_map/ppermute | solution.py:12
  67.2 41.2 %all-reduce.5.cloned.1.call-done = f32[8,16384]{1,0:T(8,128)} async-done(((f32[8,16384]{1,0:T(8,128)}), f32[8,16384]{1,0:T(8,128)}) %all-reduce.5.cloned.1.call-update) | async-done | bytes 524304 | tf_op jit(solution)/shard_map/psum | solution.py:84
  109.7 12.9 %all-reduce = (f32[8]{0:T(128)S(1)}, f32[8]{0:T(128)S(1)}) all-reduce(f32[8]{0:T(128)S(1)} %get-tuple-element.10, f32[8]{0:T(128)S(1)} %get-tuple-element.9), channel_id=1, replica_groups=mesh['tile'=8,'sub'=4] {'tile'}, use_global_device_ids=true, to_apply=%region_1.2 | all-reduce | flops 16 | bytes 128 | tf_op jit(solution)/shard_map/psum | solution.py:41
  124.0 11.8 %psum.66 = f32[8]{0:T(128)S(1)} all-reduce(f32[8]{0:T(128)S(1)} %multiply_reduce_fusion.3), channel_id=1, replica_groups=mesh['tile'=8,'sub'=4] {'tile'}, use_global_device_ids=true, to_apply=%region_6.8 | all-reduce | flops 8 | bytes 64 | tf_op jit(solution)/shard_map/psum | solution.py:41
  138.5 1.7 collective-permute-done.2
  143.2 8.1 %convolution_bitcast_fusion.3 = f32[8,96,256]{2,0,1:T(8,128)S(1)} fusion(bf16[96,256,256]{2,1,0:T(8,128)(2,1)} %param.12, bf16[96,8,256]{2,1,0:T(8,128)(2,1)} %gather_fusion.3, pred[96]{0:T(512)(128)(4,1)S(1)} %copy-done.10), kind=kOutput, calls=%fused_computation.10 | convolution fusion | flops 100859904 | bytes 13762656 | tf_op jit(solution)/shard_map/pij,rpj->rpi/dot_general | solution.py:57
  152.3 6.4 %convolution_bitcast_fusion.2 = f32[8,96,256]{2,0,1:T(8,128)S(1)} fusion(bf16[96,256,256]{2,1,0:T(8,128)(2,1)} %param.12, bf16[96,8,256]{2,1,0:T(8,128)(2,1)S(1)} %copy-done.5, pred[96]{0:T(512)(128)(4,1)S(1)} %get-tuple-element.19), kind=kOutput, calls=%fused_computation.9 | convolution fusion | flops 100859904 | bytes 13762656 | tf_op jit(solution)/shard_map/pij,rpi->rpj/dot_general | solution.py:60
  160.0 4.2 %collective-permute-start.3 = (bf16[8,4096]{1,0:T(8,128)(2,1)S(1)}, bf16[8,4096]{1,0:T(8,128)(2,1)S(1)}, u32[]{:S(2)}, u32[]{:S(2)}) collective-permute-start(bf16[8,4096]{1,0:T(8,128)(2,1)S(1)} %slice.102), channel_id=1, source_target_pairs={{0,4},{4,8},{8,12},{12,16},{16,20},{20,24},{24,28},{1,5},{5,9},{9,... | collective-permute-start | bytes 196616 | tf_op jit(solution)/shard_map/ppermute | solution.py:12
  166.8 38.5 %all-reduce.7.cloned.1.call-done = f32[8,16384]{1,0:T(8,128)} async-done(((f32[8,16384]{1,0:T(8,128)}), f32[8,16384]{1,0:T(8,128)}) %all-reduce.7.cloned.1.call-update) | async-done | bytes 524304 | tf_op jit(solution)/shard_map/psum | solution.py:84
  206.6 12.9 %psum.68 = f32[8]{0:T(128)S(1)} all-reduce(f32[8]{0:T(128)S(1)} %multiply_reduce_fusion.2), channel_id=1, replica_groups=mesh['tile'=8,'sub'=4] {'tile'}, use_global_device_ids=true, to_apply=%region_9.11 | all-reduce | flops 8 | bytes 64 | tf_op jit(solution)/shard_map/psum | solution.py:41
  219.5 2.1 multiply_reduce_fusion.1
  221.6 11.8 %psum.69 = f32[8]{0:T(128)S(1)} all-reduce(f32[8]{0:T(128)S(1)} %get-tuple-element.15), channel_id=1, replica_groups=mesh['tile'=8,'sub'=4] {'tile'}, use_global_device_ids=true, to_apply=%region_11.13 | all-reduce | flops 8 | bytes 64 | tf_op jit(solution)/shard_map/psum | solution.py:41
  233.4 2.0 fusion.88
  237.0 1.6 collective-permute-done.4
  241.6 8.1 %convolution_bitcast_fusion.1 = f32[8,96,256]{2,0,1:T(8,128)S(1)} fusion(bf16[96,256,256]{2,1,0:T(8,128)(2,1)} %param.12, bf16[96,8,256]{2,1,0:T(8,128)(2,1)} %gather_fusion.5, pred[96]{0:T(512)(128)(4,1)S(1)} %copy-done.10), kind=kOutput, calls=%fused_computation.8 | convolution fusion | flops 100859904 | bytes 13762656 | tf_op jit(solution)/shard_map/pij,rpj->rpi/dot_general | solution.py:57
  250.7 6.4 %convolution_bitcast_fusion = f32[8,96,256]{2,0,1:T(8,128)S(1)} fusion(bf16[96,256,256]{2,1,0:T(8,128)(2,1)} %param.12, bf16[96,8,256]{2,1,0:T(8,128)(2,1)S(1)} %copy-done.4, pred[96]{0:T(512)(128)(4,1)S(1)} %get-tuple-element.19), kind=kOutput, calls=%fused_computation.7 | convolution fusion | flops 100859904 | bytes 13762656 | tf_op jit(solution)/shard_map/pij,rpi->rpj/dot_general | solution.py:60
  258.4 4.2 %collective-permute-start.5 = (bf16[8,4096]{1,0:T(8,128)(2,1)S(1)}, bf16[8,4096]{1,0:T(8,128)(2,1)S(1)}, u32[]{:S(2)}, u32[]{:S(2)}) collective-permute-start(bf16[8,4096]{1,0:T(8,128)(2,1)S(1)} %slice.101), channel_id=1, source_target_pairs={{0,4},{4,8},{8,12},{12,16},{16,20},{20,24},{24,28},{1,5},{5,9},{9,... | collective-permute-start | bytes 196616 | tf_op jit(solution)/shard_map/ppermute | solution.py:12
  265.1 38.6 %all-reduce.9.cloned.1.call-done = f32[8,16384]{1,0:T(8,128)} async-done(((f32[8,16384]{1,0:T(8,128)}), f32[8,16384]{1,0:T(8,128)}) %all-reduce.9.cloned.1.call-update) | async-done | bytes 524304 | tf_op jit(solution)/shard_map/psum | solution.py:84
  305.0 12.9 %psum.71 = f32[8]{0:T(128)S(1)} all-reduce(f32[8]{0:T(128)S(1)} %multiply_reduce_fusion), channel_id=1, replica_groups=mesh['tile'=8,'sub'=4] {'tile'}, use_global_device_ids=true, to_apply=%region_14.16 | all-reduce | flops 8 | bytes 64 | tf_op jit(solution)/shard_map/psum | solution.py:41
  317.9 1.8 dynamic-slice_subtract_fusion
  (100 shorter events, 40.8 us)
Async XLA Ops:
  7.2 57.5 %copy-start = (bf16[16,256,256]{2,1,0:T(8,128)(2,1)S(1)}, bf16[16,256,256]{2,1,0:T(8,128)(2,1)}, u32[]{:S(2)}) copy-start(bf16[16,256,256]{2,1,0:T(8,128)(2,1)} %param.13) | copy-start | bytes 6291460
  7.2 101.2 %all-reduce.5.cloned.1.call-start = ((), (), s32[]{:S(2)}) async-start(), calls=%async_computation | async-start | bytes 1048576 | tf_op jit(solution)/shard_map/psum | solution.py:84
  43.0 3.3 %collective-permute-start = (bf16[8,4096]{1,0:T(8,128)(2,1)S(1)}, bf16[8,4096]{1,0:T(8,128)(2,1)S(1)}, u32[]{:S(2)}, u32[]{:S(2)}) collective-permute-start(bf16[8,4096]{1,0:T(8,128)(2,1)S(1)} %get-tuple-element.28), channel_id=1, source_target_pairs={{4,0},{8,4},{12,8},{16,12},{20,16},{24,20},{28,24},{5,1},{9,5},{13... | collective-permute-start | bytes 196616 | tf_op jit(solution)/shard_map/ppermute | solution.py:12
  46.2 0.6 copy-start.11
  46.3 2.6 copy-start.12
  48.8 9.1 %copy-start.1 = (bf16[96,256,256]{2,1,0:T(8,128)(2,1)S(1)}, bf16[96,256,256]{2,1,0:T(8,128)(2,1)}, u32[]{:S(2)}) copy-start(bf16[96,256,256]{2,1,0:T(8,128)(2,1)} %param.12) | copy-start | bytes 37748740
  58.0 6.7 %copy-start.8 = (bf16[8,4096]{1,0:T(8,128)(2,1)S(1)}, bf16[8,4096]{1,0:T(8,128)(2,1)}, u32[]{:S(2)}) copy-start(bf16[8,4096]{1,0:T(8,128)(2,1)} %get-tuple-element.27) | copy-start | bytes 196612
  58.0 8.2 %copy-start.9 = (f32[4096]{0:T(1024)S(1)}, f32[4096]{0:T(1024)}, u32[]{:S(2)}) copy-start(f32[4096]{0:T(1024)} %param.10) | copy-start | bytes 49156
  59.8 83.4 %copy-start.10 = (pred[96]{0:T(512)(128)(4,1)S(1)}, pred[96]{0:T(512)(128)(4,1)}, u32[]{:S(2)}) copy-start(pred[96]{0:T(512)(128)(4,1)} %get-tuple-element.29) | copy-start | bytes 292
  61.1 4.4 %collective-permute-start.1 = (bf16[8,4096]{1,0:T(8,128)(2,1)S(1)}, bf16[8,4096]{1,0:T(8,128)(2,1)S(1)}, u32[]{:S(2)}, u32[]{:S(2)}) collective-permute-start(bf16[8,4096]{1,0:T(8,128)(2,1)S(1)} %slice.103), channel_id=1, source_target_pairs={{0,4},{4,8},{8,12},{12,16},{16,20},{20,24},{24,28},{1,5},{5,9},{9,... | collective-permute-start | bytes 196616 | tf_op jit(solution)/shard_map/ppermute | solution.py:12
  65.4 0.8 copy-start.7
  66.3 0.8 copy-start.6
  67.1 138.2 %all-reduce.7.cloned.1.call-start = ((), (), s32[]{:S(2)}) async-start(), calls=%async_computation.1 | async-start | bytes 1048576 | tf_op jit(solution)/shard_map/psum | solution.py:84
  137.0 3.1 collective-permute-start.2
  143.2 9.0 %copy-start.5 = (bf16[96,8,256]{2,1,0:T(8,128)(2,1)S(1)}, bf16[96,8,256]{2,1,0:T(8,128)(2,1)}, u32[]{:S(2)}) copy-start(bf16[96,8,256]{2,1,0:T(8,128)(2,1)} %gather_fusion.4) | copy-start | bytes 1179652
  152.2 67.2 %copy-start.2 = (f32[8,16384]{1,0:T(8,128)S(1)}, f32[8,16384]{1,0:T(8,128)}, u32[]{:S(2)}) copy-start(f32[8,16384]{1,0:T(8,128)} %all-reduce.5.cloned.1.call-done) | copy-start | bytes 1572868
  160.0 5.1 %collective-permute-start.3 = (bf16[8,4096]{1,0:T(8,128)(2,1)S(1)}, bf16[8,4096]{1,0:T(8,128)(2,1)S(1)}, u32[]{:S(2)}, u32[]{:S(2)}) collective-permute-start(bf16[8,4096]{1,0:T(8,128)(2,1)S(1)} %slice.102), channel_id=1, source_target_pairs={{0,4},{4,8},{8,12},{12,16},{16,20},{20,24},{24,28},{1,5},{5,9},{9,... | collective-permute-start | bytes 196616 | tf_op jit(solution)/shard_map/ppermute | solution.py:12
  166.7 137.0 %all-reduce.9.cloned.1.call-start = ((), (), s32[]{:S(2)}) async-start(), calls=%async_computation.2 | async-start | bytes 1048576 | tf_op jit(solution)/shard_map/psum | solution.py:84
  235.4 3.1 collective-permute-start.4
  241.6 9.0 %copy-start.4 = (bf16[96,8,256]{2,1,0:T(8,128)(2,1)S(1)}, bf16[96,8,256]{2,1,0:T(8,128)(2,1)}, u32[]{:S(2)}) copy-start(bf16[96,8,256]{2,1,0:T(8,128)(2,1)} %gather_fusion.6) | copy-start | bytes 1179652
  250.7 13.7 %copy-start.3 = (f32[8,16384]{1,0:T(8,128)S(1)}, f32[8,16384]{1,0:T(8,128)}, u32[]{:S(2)}) copy-start(f32[8,16384]{1,0:T(8,128)} %get-tuple-element.14) | copy-start | bytes 1572868
  258.4 5.1 %collective-permute-start.5 = (bf16[8,4096]{1,0:T(8,128)(2,1)S(1)}, bf16[8,4096]{1,0:T(8,128)(2,1)S(1)}, u32[]{:S(2)}, u32[]{:S(2)}) collective-permute-start(bf16[8,4096]{1,0:T(8,128)(2,1)S(1)} %slice.101), channel_id=1, source_target_pairs={{0,4},{4,8},{8,12},{12,16},{16,20},{20,24},{24,28},{1,5},{5,9},{9,... | collective-permute-start | bytes 196616 | tf_op jit(solution)/shard_map/ppermute | solution.py:12
Sparse Core Ops, SparseCore 0:
  67.2 41.0 all-reduce.4
  166.9 38.3 all-reduce.6
  265.3 38.4 all-reduce.8
where the time goes:
time: 327 us; the launch traced here: 326 us
  waiting for transfers between devices  122 us (37%)
  blocking collectives  77.9 us (24%)
  matrix products  46.5 us (14%)
  local copies, waits for them, and re-layouts  29.8 us (9%)
  other arithmetic  19.4 us (6%)
  starting transfers between devices  16.3 us (5%)
  between operations  14.2 us (4%)
    psum x3, waiting for transfers between devices, on_device(): image_vec = lax.psum(pair_sums, 'sub')  118 us
    psum x5, blocking collectives, reduce_all(): return lax.psum(values, 'tile')  62.3 us
    dot_general x3, matrix products, on_device(): jnp.einsum('pij,rpj->rpi', pair_blocks, from_cols, preferred_element_type...  24.4 us
    gather x2, local copies, waits for them, and re-layouts, on_device(): curve_rhs = jnp.take(right_side, point_order[0], axis=1)  16.4 us
    ppermute x6, starting transfers between devices, from_behind(): return lax.ppermute(block, axis, route)  16.2 us
    all_gather x1, blocking collectives, on_device(): lax.all_gather(curve_rhs.astype(jnp.bfloat16), 'sub', axis=1, tiled=True)  15.6 us
    dot_general x3, matrix products, on_device(): jnp.einsum('pij,rpi->rpj', pair_blocks, from_rows, preferred_element_type...  14.6 us
  transfers between devices with their start and end apart: 9, of which 8 were waited for; matrix products, arithmetic and copies ran while one was open for 1% of the time, Pallas kernels for 0%

commit v1 on v0

v1 whole, which is shorter than its diff:
```python
import functools

import jax
import jax.numpy as jnp
from jax import lax
from jax.experimental import pallas as pl
from jax.experimental.pallas import tpu as pltpu
from jax.sharding import PartitionSpec as P

ITERS = 3
LANES = 128
GROUP = 16
F32 = jnp.float32
BF16 = jnp.bfloat16
VMEM = pl.BlockSpec(memory_space=pltpu.VMEM)
SMEM = pl.BlockSpec(memory_space=pltpu.SMEM)
PARAMS = pltpu.CompilerParams(vmem_limit_bytes=16 * 1024 * 1024)


def times(field, block):
    return lax.dot_general(field, block, (((1,), (0,)), ((), ())), preferred_element_type=F32)


def times_transposed(field, block):
    return lax.dot_general(field, block, (((1,), (1,)), ((), ())), preferred_element_type=F32)


def order_kernel(right_ref, order_ref, curve_ref, rounded_ref):
    rhs_count, points = right_ref.shape
    for start in range(0, points, LANES):
        at = jnp.broadcast_to(order_ref[:, start : start + LANES], (rhs_count, LANES))
        chunk = at // LANES
        lane = at % LANES
        result = jnp.zeros((rhs_count, LANES), F32)
        for source in range(points // LANES):
            values = right_ref[:, source * LANES : (source + 1) * LANES]
            picked = jnp.take_along_axis(values, lane, axis=1)
            result = jnp.where(chunk == source, picked, result)
        curve_ref[:, start : start + LANES] = result
        rounded_ref[:, start : start + LANES] = result.astype(BF16)


def ahead_kernel(sub_count, where_ref, pairs_ref, blocks_ref, *refs):
    row_refs = refs[:sub_count]
    even_ref, odd_ref, field_ref, total = refs[sub_count:]
    sub_index, parity, live = where_ref[0], where_ref[1], where_ref[2]
    rhs_count, points_dev = even_ref.shape
    block_len = blocks_ref.shape[1]
    blocks_dev = points_dev // block_len
    tile_blocks = sub_count * blocks_dev
    for step, row_ref in enumerate(row_refs):
        first = (sub_index ^ step) * blocks_dev
        for block in range(blocks_dev):
            piece = row_ref[:, block * block_len : (block + 1) * block_len]
            field_ref[first + block] = piece.astype(F32)
    for block in range(blocks_dev):
        total[block] = jnp.zeros((rhs_count, block_len), F32)

    def one_slot(slot, carry):
        row, col = pairs_ref[2 * slot], pairs_ref[2 * slot + 1]

        @pl.when(col >= tile_blocks)
        def _():
            at = col - tile_blocks
            total[at] += times(field_ref[row].astype(BF16), blocks_ref[slot])

        return carry

    lax.fori_loop(0, live, one_slot, 0)
    is_odd = parity == 1
    for block in range(blocks_dev):
        span = slice(block * block_len, (block + 1) * block_len)
        products = total[block].astype(BF16)
        first_row = field_ref[block].astype(BF16)
        even_ref[:, span] = jnp.where(is_odd, first_row, products)
        odd_ref[:, span] = jnp.where(is_odd, products, first_row)


def product_kernel(
    sub_count, where_ref, pairs_ref, blocks_ref, diag_ref, noise_ref, own_ref, field_ref, even_ref,
    odd_ref, *refs
):
    part_refs = refs[:sub_count]
    total, ahead = refs[sub_count:]
    sub_index, parity, live = where_ref[0], where_ref[1], where_ref[2]
    rhs_count, points_dev = own_ref.shape
    block_len = blocks_ref.shape[1]
    blocks_dev = points_dev // block_len
    tile_blocks = sub_count * blocks_dev
    is_odd = parity == 1
    for block in range(tile_blocks):
        ahead[block] = field_ref[block].astype(BF16).astype(F32)
        if block >= blocks_dev:
            total[block] = jnp.zeros((rhs_count, block_len), F32)
    for block in range(blocks_dev):
        span = slice(block * block_len, (block + 1) * block_len)
        even = even_ref[:, span].astype(F32)
        odd = odd_ref[:, span].astype(F32)
        ahead[tile_blocks + block] = jnp.where(is_odd, odd, even)
        total[block] = jnp.where(is_odd, even, odd)
        total[tile_blocks + block] = jnp.zeros((rhs_count, block_len), F32)

    def one_group(group, carry):
        results = []
        for step in range(GROUP):
            slot = group * GROUP + step
            row, col = pairs_ref[2 * slot], pairs_ref[2 * slot + 1]
            block = blocks_ref[slot]
            results.append((row, times_transposed(ahead[col].astype(BF16), block)))
            results.append((col, times(ahead[row].astype(BF16), block)))
        for at, value in results:
            total[at] += value
        return carry

    lax.fori_loop(0, (live + GROUP - 1) // GROUP, one_group, 0)
    own_first = sub_index * blocks_dev
    for block in range(blocks_dev):
        span = slice(block * block_len, (block + 1) * block_len)
        value = total[own_first + block] + noise_ref[:, span] * own_ref[:, span]
        value += times(ahead[own_first + block].astype(BF16), diag_ref[block])
        part_refs[0][:, span] = value
        for step in range(1, sub_count):
            first = (sub_index ^ step) * blocks_dev
            part_refs[step][:, span] = total[first + block].astype(part_refs[step].dtype)


def join_kernel(index, own_ref, old_ref, moments_in_ref, *refs):
    part_refs = refs[:-3]
    next_ref, rounded_ref, moments_ref = refs[-3:]
    value = own_ref[...]
    for part_ref in part_refs:
        value += part_ref[...].astype(F32)
    next_ref[...] = value
    rounded_ref[...] = value.astype(BF16)
    old = old_ref[...]
    lane = lax.broadcasted_iota(jnp.int32, moments_ref.shape, 1)
    moments = moments_in_ref[...]
    found = {2 * index + 1: old * value}
    if index == 0:
        found[0] = old * old
    if index + 1 < ITERS:
        found[2 * index + 2] = value * value
    for order, product in found.items():
        moments = jnp.where(lane == order, jnp.sum(product, axis=1, keepdims=True), moments)
    moments_ref[...] = moments


def finish_kernel(moments_ref, *refs):
    basis_refs = refs[: ITERS + 1]
    solution_ref, residual_ref = refs[ITERS + 1 :]
    moments = [moments_ref[:, order : order + 1] for order in range(2 * ITERS)]

    def inner(first, second, shift):
        value = 0.0
        for i, a in enumerate(first):
            for j, b in enumerate(second):
                value = value + a * b * moments[i + j + shift]
        return value

    one = jnp.ones_like(moments[0])
    zero = jnp.zeros_like(one)
    direction, residual = [one], [one]
    answer = [zero] * ITERS
    norm_now = moments[0]
    for iteration in range(ITERS):
        step_size = norm_now / inner(direction, direction, 1)
        for power, weight in enumerate(direction):
            answer[power] = answer[power] + step_size * weight
        residual = residual + [zero]
        for power, weight in enumerate(direction):
            residual[power + 1] = residual[power + 1] - step_size * weight
        if iteration + 1 < ITERS:
            norm_next = inner(residual, residual, 0)
            direction = [
                value + (norm_next / norm_now) * old
                for value, old in zip(residual, direction + [zero])
            ]
            norm_now = norm_next
    fields = [basis_ref[...] for basis_ref in basis_refs]
    solution_ref[...] = sum(weight * field for weight, field in zip(answer, fields))
    residual_ref[...] = sum(weight * field for weight, field in zip(residual, fields))


def shape(rows, columns, kind):
    return jax.ShapeDtypeStruct((rows, columns), kind)


def exchange(block, axis, step):
    count = lax.axis_size(axis)
    return lax.ppermute(block, axis, [(i, i ^ step) for i in range(count)])


def swap(block, axis, first):
    count = lax.axis_size(axis)
    route = []
    for i in range(first, count - 1, 2):
        route += [(i, i + 1), (i + 1, i)]
    return lax.ppermute(block, axis, route)


def on_device(right_side, point_order, noise_var, block_pairs, pair_blocks, diag_blocks):
    sub_count = lax.axis_size("sub")
    tile_count = lax.axis_size("tile")
    sub_index = lax.axis_index("sub")
    tile_index = lax.axis_index("tile")
    rhs_count, points_dev = right_side.shape
    blocks_dev, block_len = diag_blocks.shape[:2]
    extended = (sub_count + 1) * blocks_dev
    live = jnp.sum((block_pairs[:, 0] >= 0).astype(jnp.int32))
    first_block = tile_index * (blocks_dev * sub_count)
    pairs = jnp.where(block_pairs >= 0, block_pairs - first_block, 0).reshape(-1)
    where = jnp.stack([sub_index, tile_index % 2, live]).astype(jnp.int32)
    blocks = pltpu.with_memory_space_constraint(pair_blocks, pltpu.VMEM)
    noise = noise_var[None, :]
    full = shape(rhs_count, points_dev, F32)
    half = shape(rhs_count, points_dev, BF16)
    field, rounded = pl.pallas_call(
        order_kernel,
        out_shape=(full, half),
        in_specs=[VMEM, VMEM],
        out_specs=(VMEM, VMEM),
        compiler_params=PARAMS,
        name="curve_order",
    )(right_side, point_order)
    basis = [field]
    moments = jnp.zeros((rhs_count, LANES), F32)
    for index in range(ITERS):
        rows = [rounded] + [exchange(rounded, "sub", step) for step in range(1, sub_count)]
        by_block = (extended, rhs_count, block_len)
        even, odd, tile_field = pl.pallas_call(
            functools.partial(ahead_kernel, sub_count),
            out_shape=(half, half, jax.ShapeDtypeStruct(by_block, F32)),
            in_specs=[SMEM, SMEM, VMEM] + [VMEM] * sub_count,
            out_specs=(VMEM, VMEM, VMEM),
            scratch_shapes=[pltpu.VMEM((blocks_dev, rhs_count, block_len), F32)],
            compiler_params=PARAMS,
            name="ahead",
        )(where, pairs, blocks, *rows)
        even = swap(even, "tile", 0)
        odd = swap(odd, "tile", 1)
        sent = F32 if index + 1 == ITERS else BF16
        part = shape(rhs_count, points_dev, sent)
        parts = pl.pallas_call(
            functools.partial(product_kernel, sub_count),
            out_shape=(full,) + (part,) * (sub_count - 1),
            in_specs=[SMEM, SMEM] + [VMEM] * 7,
            out_specs=(VMEM,) * sub_count,
            scratch_shapes=[pltpu.VMEM(by_block, F32), pltpu.VMEM(by_block, F32)],
            compiler_params=PARAMS,
            name="products",
        )(where, pairs, blocks, diag_blocks, noise, field, tile_field, even, odd)
        arrived = [exchange(parts[step], "sub", step) for step in range(1, sub_count)]
        field, rounded, moments = pl.pallas_call(
            functools.partial(join_kernel, index),
            out_shape=(full, half, shape(rhs_count, LANES, F32)),
            in_specs=[VMEM] * (3 + len(arrived)),
            out_specs=(VMEM, VMEM, VMEM),
            compiler_params=PARAMS,
            name="join",
        )(parts[0], field, moments, *arrived)
        basis.append(field)
    for axis, count in (("sub", sub_count), ("tile", tile_count)):
        step = 1
        while step < count:
            moments = moments + exchange(moments, axis, step)
            step *= 2
    return pl.pallas_call(
        finish_kernel,
        out_shape=(full, full),
        in_specs=[VMEM] * (ITERS + 2),
        out_specs=(VMEM, VMEM),
        compiler_params=PARAMS,
        name="finish",
    )(moments, *basis)


def solution(mesh):
    placed = (
        P(None, ("tile", "sub")),
        P(("tile", "sub"), None),
        P(("tile", "sub")),
        P(("tile", "sub"), None),
        P(("tile", "sub"), None, None),
        P(("tile", "sub"), None, None),
    )
    return jax.shard_map(
        on_device,
        mesh=mesh,
        in_specs=placed,
        out_specs=(P(None, ("tile", "sub")), P(None, ("tile", "sub"))),
        check_vma=False,
    )
```

time: 327 us -> 134 us (0.41)
  waiting for transfers between devices: 122 us -> 35.7 us
  blocking collectives: 77.9 us -> 0 us
  matrix products: 46.5 us -> 0 us
  starting transfers between devices: 16.3 us -> 60.2 us
  Pallas kernels: 0 us -> 27.5 us
  local copies, waits for them, and re-layouts: 29.8 us -> 8.06 us
  other arithmetic: 19.4 us -> 2.74 us
  between operations: 14.2 us -> 0.76 us
    psum x3 -> x0, waiting for transfers between devices: 118 us -> none  [on_device(): image_vec = lax.psum(pair_sums, 'sub')]
    psum x5 -> x0, blocking collectives: 62.3 us -> none  [reduce_all(): return lax.psum(values, 'tile')]
    dot_general x15 -> x0, matrix products: 46.5 us -> none  [the longest x3 24.4 us: on_device(): jnp.einsum('pij,rpj->rpi', pair_blocks, from_cols, preferred_element_type...]
    ppermute x6 -> x29, starting transfers between devices: 16.2 us -> 60.2 us  [the longest x23 50.1 us: exchange(): return lax.ppermute(block, axis, [(i, i ^ step) for i in range(count)])]
    ppermute x6 -> x29, waiting for transfers between devices: 3.81 us -> 35.7 us  [the longest x23 34.7 us: exchange(): return lax.ppermute(block, axis, [(i, i ^ step) for i in range(count)])]
    pallas_call x0 -> x11, Pallas kernels: none -> 27.5 us  [the longest x3 14.7 us: on_device(): pl.pallas_call(functools.partial(product_kernel, sub_count), out_shape=(f...]
    gather x8 -> x0, local copies, waits for them, and re-layouts: 24.4 us -> none  [the longest x2 16.4 us: on_device(): curve_rhs = jnp.take(right_side, point_order[0], axis=1)]
    all_gather x1 -> x0, blocking collectives: 15.6 us -> none  [on_device(): lax.all_gather(curve_rhs.astype(jnp.bfloat16), 'sub', axis=1, tiled=True)]
  transfers between devices with their start and end apart: 9 -> 29, of which waited for: 8 -> 19; matrix products, arithmetic and copies ran while one was open for 1% -> 2% of each run, Pallas kernels for 0% -> 0%
where the time goes in v1:
time: 134 us; the launch traced here: 135 us
  starting transfers between devices  60.2 us (45%)
  waiting for transfers between devices  35.7 us (27%)
  Pallas kernels  27.5 us (21%)
  local copies, waits for them, and re-layouts  8.06 us (6%)
  other arithmetic  2.74 us (2%)
    ppermute x23, starting transfers between devices, exchange(): return lax.ppermute(block, axis, [(i, i ^ step) for i in range(count)])  50.1 us
    ppermute x23, waiting for transfers between devices, exchange(): return lax.ppermute(block, axis, [(i, i ^ step) for i in range(count)])  34.7 us
    pallas_call x3, Pallas kernels, on_device(): pl.pallas_call(functools.partial(product_kernel, sub_count), out_shape=(f...  14.7 us
    ppermute x6, starting transfers between devices, swap(): return lax.ppermute(block, axis, route)  10.1 us
    pallas_call x3, Pallas kernels, on_device(): pl.pallas_call(functools.partial(ahead_kernel, sub_count), out_shape=(hal...  9.64 us
    unnamed x14, local copies, waits for them, and re-layouts  7.82 us
  transfers between devices with their start and end apart: 29, of which 19 were waited for; matrix products, arithmetic and copies ran while one was open for 2% of the time, Pallas kernels for 0%

profile of v1, /device:TPU:0, one launch (start us, length us, event | category | flops | bytes accessed | tf_op | source)
XLA Modules:
  0.0 135.0 jit_solution(9490515205366870306)
XLA Ops:
  3.5 5.1 %collective-permute-start.2 = (bf16[8,4096]{1,0:T(8,128)(2,1)S(1)}, bf16[8,4096]{1,0:T(8,128)(2,1)S(1)}, u32[]{:S(2)}, u32[]{:S(2)}) collective-permute-start(bf16[8,4096]{1,0:T(8,128)(2,1)S(1)} %get-tuple-element.34.refs_0_), channel_id=1, source_target_pairs={{0,3},{1,2},{2,1},{3,0},{4,7},{5,6},{6,5},{7,4},{8,11},{9,10},{10,... | collective-permute-start | bytes 196616 | tf_op jit(solution)/shard_map/ppermute | solution.py:190
  14.2 4.6 %copy-done = bf16[96,256,256]{2,1,0:T(8,128)(2,1)S(1)} copy-done((bf16[96,256,256]{2,1,0:T(8,128)(2,1)S(1)}, bf16[96,256,256]{2,1,0:T(8,128)(2,1)}, u32[]{:S(2)}) %copy-start) | copy-done | bytes 12582936
  18.8 3.2 %ahead.3 = (bf16[8,4096]{1,0:T(8,128)(2,1)S(1)}, bf16[8,4096]{1,0:T(8,128)(2,1)S(1)}, f32[80,8,256]{2,1,0:T(8,128)S(1)}) custom-call(s32[3]{0:T(128)S(1)} %pad_add_fusion.where_ref, s32[192]{0:T(256)S(1)} %reshape.10.pairs_ref, bf16[96,256,256]{2,1,0:T(8,128)(2,1)S(1)} %copy-done, bf16[8,4096]{1,0:T(8,128)(2,1)S(1)} %get-tuple-element.34.refs_0_, ...), custom_call_target="tpu_custom_call" | custom-call | tf_op jit(solution)/shard_map/ahead/pallas_call | solution.py:230
  25.0 4.9 %products.3 = (f32[8,4096]{1,0:T(8,128)S(1)}, bf16[8,4096]{1,0:T(8,128)(2,1)S(1)}, bf16[8,4096]{1,0:T(8,128)(2,1)S(1)}, bf16[8,4096]{1,0:T(8,128)(2,1)S(1)}) custom-call(s32[3]{0:T(128)S(1)} %pad_add_fusion.where_ref, s32[192]{0:T(256)S(1)} %reshape.10.pairs_ref, bf16[96,256,256]{2,1,0:T(8,128)(2,1)S(1)} %copy-done.1, bf16[16,256,256]{2,1,0:T(8,128)(2,1)S(1)} %copy-done.2, ...), custom_call_target="tpu_custom_call" | custom-call | tf_op jit(solution)/shard_map/products/pallas_call | solution.py:243
  29.9 3.8 %collective-permute-start.6 = (bf16[8,4096]{1,0:T(8,128)(2,1)S(1)}, bf16[8,4096]{1,0:T(8,128)(2,1)S(1)}, u32[]{:S(2)}, u32[]{:S(2)}) collective-permute-start(bf16[8,4096]{1,0:T(8,128)(2,1)S(1)} %get-tuple-element.40), channel_id=1, source_target_pairs={{0,2},{1,3},{2,0},{3,1},{4,6},{5,7},{6,4},{7,5},{8,10},{9,11},{10,... | collective-permute-start | bytes 196616 | tf_op jit(solution)/shard_map/ppermute | solution.py:190
  35.9 4.1 %collective-permute-done.7.refs_2_ = bf16[8,4096]{1,0:T(8,128)(2,1)S(1)} collective-permute-done((bf16[8,4096]{1,0:T(8,128)(2,1)S(1)}, bf16[8,4096]{1,0:T(8,128)(2,1)S(1)}, u32[]{:S(2)}, u32[]{:S(2)}) %collective-permute-start.7) | collective-permute-done | bytes 65568 | tf_op jit(solution)/shard_map/ppermute | solution.py:190
  42.2 2.3 %collective-permute-start.8 = (bf16[8,4096]{1,0:T(8,128)(2,1)S(1)}, bf16[8,4096]{1,0:T(8,128)(2,1)S(1)}, u32[]{:S(2)}, u32[]{:S(2)}) collective-permute-start(bf16[8,4096]{1,0:T(8,128)(2,1)S(1)} %get-tuple-element.43.refs_0_), channel_id=1, source_target_pairs={{0,1},{1,0},{2,3},{3,2},{4,5},{5,4},{6,7},{7,6},{8,9},{9,8},{10,11... | collective-permute-start | bytes 196616 | tf_op jit(solution)/shard_map/ppermute | solution.py:190
  46.2 3.5 %collective-permute-done.9.refs_2_ = bf16[8,4096]{1,0:T(8,128)(2,1)S(1)} collective-permute-done((bf16[8,4096]{1,0:T(8,128)(2,1)S(1)}, bf16[8,4096]{1,0:T(8,128)(2,1)S(1)}, u32[]{:S(2)}, u32[]{:S(2)}) %collective-permute-start.9) | collective-permute-done | bytes 65568 | tf_op jit(solution)/shard_map/ppermute | solution.py:190
  49.7 3.2 %ahead.4 = (bf16[8,4096]{1,0:T(8,128)(2,1)S(1)}, bf16[8,4096]{1,0:T(8,128)(2,1)S(1)}, f32[80,8,256]{2,1,0:T(8,128)S(1)}) custom-call(s32[3]{0:T(128)S(1)} %pad_add_fusion.where_ref, s32[192]{0:T(256)S(1)} %reshape.10.pairs_ref, bf16[96,256,256]{2,1,0:T(8,128)(2,1)S(1)} %copy-done.1, bf16[8,4096]{1,0:T(8,128)(2,1)S(1)} %get-tuple-element.43.refs_0_, ...), custom_call_target="tpu_custom_call" | custom-call | tf_op jit(solution)/shard_map/ahead/pallas_call | solution.py:230
  54.8 4.9 %products.4 = (f32[8,4096]{1,0:T(8,128)S(1)}, bf16[8,4096]{1,0:T(8,128)(2,1)S(1)}, bf16[8,4096]{1,0:T(8,128)(2,1)S(1)}, bf16[8,4096]{1,0:T(8,128)(2,1)S(1)}) custom-call(s32[3]{0:T(128)S(1)} %pad_add_fusion.where_ref, s32[192]{0:T(256)S(1)} %reshape.10.pairs_ref, bf16[96,256,256]{2,1,0:T(8,128)(2,1)S(1)} %copy-done.1, bf16[16,256,256]{2,1,0:T(8,128)(2,1)S(1)} %copy-done.3, ...), custom_call_target="tpu_custom_call" | custom-call | tf_op jit(solution)/shard_map/products/pallas_call | solution.py:243
  61.5 2.6 %collective-permute-start.15 = (bf16[8,4096]{1,0:T(8,128)(2,1)S(1)}, bf16[8,4096]{1,0:T(8,128)(2,1)S(1)}, u32[]{:S(2)}, u32[]{:S(2)}) collective-permute-start(bf16[8,4096]{1,0:T(8,128)(2,1)S(1)} %get-tuple-element.51), channel_id=1, source_target_pairs={{0,3},{1,2},{2,1},{3,0},{4,7},{5,6},{6,5},{7,4},{8,11},{9,10},{10,... | collective-permute-start | bytes 196616 | tf_op jit(solution)/shard_map/ppermute | solution.py:190
  65.0 2.7 %collective-permute-done.15.refs_2_ = bf16[8,4096]{1,0:T(8,128)(2,1)S(1)} collective-permute-done((bf16[8,4096]{1,0:T(8,128)(2,1)S(1)}, bf16[8,4096]{1,0:T(8,128)(2,1)S(1)}, u32[]{:S(2)}, u32[]{:S(2)}) %collective-permute-start.15) | collective-permute-done | bytes 65568 | tf_op jit(solution)/shard_map/ppermute | solution.py:190
  67.8 2.5 %collective-permute-start.18 = (bf16[8,4096]{1,0:T(8,128)(2,1)S(1)}, bf16[8,4096]{1,0:T(8,128)(2,1)S(1)}, u32[]{:S(2)}, u32[]{:S(2)}) collective-permute-start(bf16[8,4096]{1,0:T(8,128)(2,1)S(1)} %get-tuple-element.53.refs_0_), channel_id=1, source_target_pairs={{0,3},{1,2},{2,1},{3,0},{4,7},{5,6},{6,5},{7,4},{8,11},{9,10},{10,... | collective-permute-start | bytes 196616 | tf_op jit(solution)/shard_map/ppermute | solution.py:190
  73.9 3.6 %collective-permute-done.17.refs_2_ = bf16[8,4096]{1,0:T(8,128)(2,1)S(1)} collective-permute-done((bf16[8,4096]{1,0:T(8,128)(2,1)S(1)}, bf16[8,4096]{1,0:T(8,128)(2,1)S(1)}, u32[]{:S(2)}, u32[]{:S(2)}) %collective-permute-start.17) | collective-permute-done | bytes 65568 | tf_op jit(solution)/shard_map/ppermute | solution.py:190
  77.6 3.2 %ahead.5 = (bf16[8,4096]{1,0:T(8,128)(2,1)S(1)}, bf16[8,4096]{1,0:T(8,128)(2,1)S(1)}, f32[80,8,256]{2,1,0:T(8,128)S(1)}) custom-call(s32[3]{0:T(128)S(1)} %pad_add_fusion.where_ref, s32[192]{0:T(256)S(1)} %reshape.10.pairs_ref, bf16[96,256,256]{2,1,0:T(8,128)(2,1)S(1)} %copy-done.1, bf16[8,4096]{1,0:T(8,128)(2,1)S(1)} %get-tuple-element.53.refs_0_, ...), custom_call_target="tpu_custom_call" | custom-call | tf_op jit(solution)/shard_map/ahead/pallas_call | solution.py:230
  80.8 7.0 %collective-permute-start.19 = (bf16[8,4096]{1,0:T(8,128)(2,1)S(1)}, bf16[8,4096]{1,0:T(8,128)(2,1)S(1)}, u32[]{:S(2)}, u32[]{:S(2)}) collective-permute-start(bf16[8,4096]{1,0:T(8,128)(2,1)S(1)} %get-tuple-element.55), channel_id=1, source_target_pairs={{0,4},{4,0},{8,12},{12,8},{16,20},{20,16},{24,28},{28,24},{1,5},{5... | collective-permute-start | bytes 196616 | tf_op jit(solution)/shard_map/ppermute | solution.py:198
  88.7 4.9 %products.5 = (f32[8,4096]{1,0:T(8,128)S(1)}, f32[8,4096]{1,0:T(8,128)S(1)}, f32[8,4096]{1,0:T(8,128)S(1)}, f32[8,4096]{1,0:T(8,128)S(1)}) custom-call(s32[3]{0:T(128)S(1)} %pad_add_fusion.where_ref, s32[192]{0:T(256)S(1)} %reshape.10.pairs_ref, bf16[96,256,256]{2,1,0:T(8,128)(2,1)S(1)} %copy-done.1, bf16[16,256,256]{2,1,0:T(8,128)(2,1)S(1)} %copy-done.3, ...), custom_call_target="tpu_custom_call" | custom-call | tf_op jit(solution)/shard_map/products/pallas_call | solution.py:243
  95.4 2.6 %collective-permute-start.23 = (f32[8,4096]{1,0:T(8,128)S(1)}, f32[8,4096]{1,0:T(8,128)S(1)}, u32[]{:S(2)}, u32[]{:S(2)}) collective-permute-start(f32[8,4096]{1,0:T(8,128)S(1)} %get-tuple-element.61), channel_id=1, source_target_pairs={{0,3},{1,2},{2,1},{3,0},{4,7},{5,6},{6,5},{7,4},{8,11},{9,10},{10,... | collective-permute-start | bytes 393224 | tf_op jit(solution)/shard_map/ppermute | solution.py:190
  100.0 2.7 %collective-permute-done.23.refs_2_ = f32[8,4096]{1,0:T(8,128)S(1)} collective-permute-done((f32[8,4096]{1,0:T(8,128)S(1)}, f32[8,4096]{1,0:T(8,128)S(1)}, u32[]{:S(2)}, u32[]{:S(2)}) %collective-permute-start.23) | collective-permute-done | bytes 131104 | tf_op jit(solution)/shard_map/ppermute | solution.py:190
  105.2 2.6 %collective-permute-done.24 = f32[8,128]{1,0:T(8,128)S(1)} collective-permute-done((f32[8,128]{1,0:T(8,128)S(1)}, f32[8,128]{1,0:T(8,128)S(1)}, u32[]{:S(2)}, u32[]{:S(2)}) %collective-permute-start.24) | collective-permute-done | bytes 4128 | tf_op jit(solution)/shard_map/ppermute | solution.py:190
  109.9 2.4 %collective-permute-done.25 = f32[8,128]{1,0:T(8,128)S(1)} collective-permute-done((f32[8,128]{1,0:T(8,128)S(1)}, f32[8,128]{1,0:T(8,128)S(1)}, u32[]{:S(2)}, u32[]{:S(2)}) %collective-permute-start.25) | collective-permute-done | bytes 4128 | tf_op jit(solution)/shard_map/ppermute | solution.py:190
  112.3 4.9 %collective-permute-start.26 = (f32[8,128]{1,0:T(8,128)S(1)}, f32[8,128]{1,0:T(8,128)S(1)}, u32[]{:S(2)}, u32[]{:S(2)}) collective-permute-start(f32[8,128]{1,0:T(8,128)S(1)} %add.21), channel_id=1, source_target_pairs={{0,4},{4,0},{8,12},{12,8},{16,20},{20,16},{24,28},{28,24},{1,5},{5... | collective-permute-start | bytes 12296 | tf_op jit(solution)/shard_map/ppermute | solution.py:190
  118.0 9.6 %collective-permute-start.27 = (f32[8,128]{1,0:T(8,128)S(1)}, f32[8,128]{1,0:T(8,128)S(1)}, u32[]{:S(2)}, u32[]{:S(2)}) collective-permute-start(f32[8,128]{1,0:T(8,128)S(1)} %add.22), channel_id=1, source_target_pairs={{0,8},{4,12},{8,0},{12,4},{16,24},{20,28},{24,16},{28,20},{1,9},{5... | collective-permute-start | bytes 12296 | tf_op jit(solution)/shard_map/ppermute | solution.py:190
  129.2 3.2 %collective-permute-start.28 = (f32[8,128]{1,0:T(8,128)S(1)}, f32[8,128]{1,0:T(8,128)S(1)}, u32[]{:S(2)}, u32[]{:S(2)}) collective-permute-start(f32[8,128]{1,0:T(8,128)S(1)} %add.23), channel_id=1, source_target_pairs={{0,16},{4,20},{8,24},{12,28},{16,0},{20,4},{24,8},{28,12},{1,17},{... | collective-permute-start | bytes 12296 | tf_op jit(solution)/shard_map/ppermute | solution.py:190
  (70 shorter events, 40.1 us)
Async XLA Ops:
  3.5 8.7 %collective-permute-start.2 = (bf16[8,4096]{1,0:T(8,128)(2,1)S(1)}, bf16[8,4096]{1,0:T(8,128)(2,1)S(1)}, u32[]{:S(2)}, u32[]{:S(2)}) collective-permute-start(bf16[8,4096]{1,0:T(8,128)(2,1)S(1)} %get-tuple-element.34.refs_0_), channel_id=1, source_target_pairs={{0,3},{1,2},{2,1},{3,0},{4,7},{5,6},{6,5},{7,4},{8,11},{9,10},{10,... | collective-permute-start | bytes 196616 | tf_op jit(solution)/shard_map/ppermute | solution.py:190
  8.6 5.6 %collective-permute-start.1 = (bf16[8,4096]{1,0:T(8,128)(2,1)S(1)}, bf16[8,4096]{1,0:T(8,128)(2,1)S(1)}, u32[]{:S(2)}, u32[]{:S(2)}) collective-permute-start(bf16[8,4096]{1,0:T(8,128)(2,1)S(1)} %get-tuple-element.34.refs_0_), channel_id=1, source_target_pairs={{0,2},{1,3},{2,0},{3,1},{4,6},{5,7},{6,4},{7,5},{8,10},{9,11},{10,... | collective-permute-start | bytes 196616 | tf_op jit(solution)/shard_map/ppermute | solution.py:190
  8.6 5.6 %collective-permute-start = (bf16[8,4096]{1,0:T(8,128)(2,1)S(1)}, bf16[8,4096]{1,0:T(8,128)(2,1)S(1)}, u32[]{:S(2)}, u32[]{:S(2)}) collective-permute-start(bf16[8,4096]{1,0:T(8,128)(2,1)S(1)} %get-tuple-element.34.refs_0_), channel_id=1, source_target_pairs={{0,1},{1,0},{2,3},{3,2},{4,5},{5,4},{6,7},{7,6},{8,9},{9,8},{10,11... | collective-permute-start | bytes 196616 | tf_op jit(solution)/shard_map/ppermute | solution.py:190
  29.9 5.2 %collective-permute-start.5 = (bf16[8,4096]{1,0:T(8,128)(2,1)S(1)}, bf16[8,4096]{1,0:T(8,128)(2,1)S(1)}, u32[]{:S(2)}, u32[]{:S(2)}) collective-permute-start(bf16[8,4096]{1,0:T(8,128)(2,1)S(1)} %get-tuple-element.39), channel_id=1, source_target_pairs={{0,1},{1,0},{2,3},{3,2},{4,5},{5,4},{6,7},{7,6},{8,9},{9,8},{10,11... | collective-permute-start | bytes 196616 | tf_op jit(solution)/shard_map/ppermute | solution.py:190
  29.9 6.0 %collective-permute-start.6 = (bf16[8,4096]{1,0:T(8,128)(2,1)S(1)}, bf16[8,4096]{1,0:T(8,128)(2,1)S(1)}, u32[]{:S(2)}, u32[]{:S(2)}) collective-permute-start(bf16[8,4096]{1,0:T(8,128)(2,1)S(1)} %get-tuple-element.40), channel_id=1, source_target_pairs={{0,2},{1,3},{2,0},{3,1},{4,6},{5,7},{6,4},{7,5},{8,10},{9,11},{10,... | collective-permute-start | bytes 196616 | tf_op jit(solution)/shard_map/ppermute | solution.py:190
  33.7 6.3 %collective-permute-start.7 = (bf16[8,4096]{1,0:T(8,128)(2,1)S(1)}, bf16[8,4096]{1,0:T(8,128)(2,1)S(1)}, u32[]{:S(2)}, u32[]{:S(2)}) collective-permute-start(bf16[8,4096]{1,0:T(8,128)(2,1)S(1)} %get-tuple-element.41), channel_id=1, source_target_pairs={{0,3},{1,2},{2,1},{3,0},{4,7},{5,6},{6,5},{7,4},{8,11},{9,10},{10,... | collective-permute-start | bytes 196616 | tf_op jit(solution)/shard_map/ppermute | solution.py:190
  40.1 6.1 %collective-permute-start.10 = (bf16[8,4096]{1,0:T(8,128)(2,1)S(1)}, bf16[8,4096]{1,0:T(8,128)(2,1)S(1)}, u32[]{:S(2)}, u32[]{:S(2)}) collective-permute-start(bf16[8,4096]{1,0:T(8,128)(2,1)S(1)} %get-tuple-element.43.refs_0_), channel_id=1, source_target_pairs={{0,3},{1,2},{2,1},{3,0},{4,7},{5,6},{6,5},{7,4},{8,11},{9,10},{10,... | collective-permute-start | bytes 196616 | tf_op jit(solution)/shard_map/ppermute | solution.py:190
  41.4 8.3 %collective-permute-start.9 = (bf16[8,4096]{1,0:T(8,128)(2,1)S(1)}, bf16[8,4096]{1,0:T(8,128)(2,1)S(1)}, u32[]{:S(2)}, u32[]{:S(2)}) collective-permute-start(bf16[8,4096]{1,0:T(8,128)(2,1)S(1)} %get-tuple-element.43.refs_0_), channel_id=1, source_target_pairs={{0,2},{1,3},{2,0},{3,1},{4,6},{5,7},{6,4},{7,5},{8,10},{9,11},{10,... | collective-permute-start | bytes 196616 | tf_op jit(solution)/shard_map/ppermute | solution.py:190
  42.2 7.5 %collective-permute-start.8 = (bf16[8,4096]{1,0:T(8,128)(2,1)S(1)}, bf16[8,4096]{1,0:T(8,128)(2,1)S(1)}, u32[]{:S(2)}, u32[]{:S(2)}) collective-permute-start(bf16[8,4096]{1,0:T(8,128)(2,1)S(1)} %get-tuple-element.43.refs_0_), channel_id=1, source_target_pairs={{0,1},{1,0},{2,3},{3,2},{4,5},{5,4},{6,7},{7,6},{8,9},{9,8},{10,11... | collective-permute-start | bytes 196616 | tf_op jit(solution)/shard_map/ppermute | solution.py:190
  59.7 4.4 %collective-permute-start.13 = (bf16[8,4096]{1,0:T(8,128)(2,1)S(1)}, bf16[8,4096]{1,0:T(8,128)(2,1)S(1)}, u32[]{:S(2)}, u32[]{:S(2)}) collective-permute-start(bf16[8,4096]{1,0:T(8,128)(2,1)S(1)} %get-tuple-element.49), channel_id=1, source_target_pairs={{0,1},{1,0},{2,3},{3,2},{4,5},{5,4},{6,7},{7,6},{8,9},{9,8},{10,11... | collective-permute-start | bytes 196616 | tf_op jit(solution)/shard_map/ppermute | solution.py:190
  59.7 5.2 %collective-permute-start.14 = (bf16[8,4096]{1,0:T(8,128)(2,1)S(1)}, bf16[8,4096]{1,0:T(8,128)(2,1)S(1)}, u32[]{:S(2)}, u32[]{:S(2)}) collective-permute-start(bf16[8,4096]{1,0:T(8,128)(2,1)S(1)} %get-tuple-element.50), channel_id=1, source_target_pairs={{0,2},{1,3},{2,0},{3,1},{4,6},{5,7},{6,4},{7,5},{8,10},{9,11},{10,... | collective-permute-start | bytes 196616 | tf_op jit(solution)/shard_map/ppermute | solution.py:190
  61.5 6.2 %collective-permute-start.15 = (bf16[8,4096]{1,0:T(8,128)(2,1)S(1)}, bf16[8,4096]{1,0:T(8,128)(2,1)S(1)}, u32[]{:S(2)}, u32[]{:S(2)}) collective-permute-start(bf16[8,4096]{1,0:T(8,128)(2,1)S(1)} %get-tuple-element.51), channel_id=1, source_target_pairs={{0,3},{1,2},{2,1},{3,0},{4,7},{5,6},{6,5},{7,4},{8,11},{9,10},{10,... | collective-permute-start | bytes 196616 | tf_op jit(solution)/shard_map/ppermute | solution.py:190
  67.8 6.1 %collective-permute-start.18 = (bf16[8,4096]{1,0:T(8,128)(2,1)S(1)}, bf16[8,4096]{1,0:T(8,128)(2,1)S(1)}, u32[]{:S(2)}, u32[]{:S(2)}) collective-permute-start(bf16[8,4096]{1,0:T(8,128)(2,1)S(1)} %get-tuple-element.53.refs_0_), channel_id=1, source_target_pairs={{0,3},{1,2},{2,1},{3,0},{4,7},{5,6},{6,5},{7,4},{8,11},{9,10},{10,... | collective-permute-start | bytes 196616 | tf_op jit(solution)/shard_map/ppermute | solution.py:190
  70.3 7.3 %collective-permute-start.17 = (bf16[8,4096]{1,0:T(8,128)(2,1)S(1)}, bf16[8,4096]{1,0:T(8,128)(2,1)S(1)}, u32[]{:S(2)}, u32[]{:S(2)}) collective-permute-start(bf16[8,4096]{1,0:T(8,128)(2,1)S(1)} %get-tuple-element.53.refs_0_), channel_id=1, source_target_pairs={{0,2},{1,3},{2,0},{3,1},{4,6},{5,7},{6,4},{7,5},{8,10},{9,11},{10,... | collective-permute-start | bytes 196616 | tf_op jit(solution)/shard_map/ppermute | solution.py:190
  70.3 7.3 %collective-permute-start.16 = (bf16[8,4096]{1,0:T(8,128)(2,1)S(1)}, bf16[8,4096]{1,0:T(8,128)(2,1)S(1)}, u32[]{:S(2)}, u32[]{:S(2)}) collective-permute-start(bf16[8,4096]{1,0:T(8,128)(2,1)S(1)} %get-tuple-element.53.refs_0_), channel_id=1, source_target_pairs={{0,1},{1,0},{2,3},{3,2},{4,5},{5,4},{6,7},{7,6},{8,9},{9,8},{10,11... | collective-permute-start | bytes 196616 | tf_op jit(solution)/shard_map/ppermute | solution.py:190
  80.8 7.9 %collective-permute-start.19 = (bf16[8,4096]{1,0:T(8,128)(2,1)S(1)}, bf16[8,4096]{1,0:T(8,128)(2,1)S(1)}, u32[]{:S(2)}, u32[]{:S(2)}) collective-permute-start(bf16[8,4096]{1,0:T(8,128)(2,1)S(1)} %get-tuple-element.55), channel_id=1, source_target_pairs={{0,4},{4,0},{8,12},{12,8},{16,20},{20,16},{24,28},{28,24},{1,5},{5... | collective-permute-start | bytes 196616 | tf_op jit(solution)/shard_map/ppermute | solution.py:198
  93.6 6.4 %collective-permute-start.21 = (f32[8,4096]{1,0:T(8,128)S(1)}, f32[8,4096]{1,0:T(8,128)S(1)}, u32[]{:S(2)}, u32[]{:S(2)}) collective-permute-start(f32[8,4096]{1,0:T(8,128)S(1)} %get-tuple-element.59), channel_id=1, source_target_pairs={{0,1},{1,0},{2,3},{3,2},{4,5},{5,4},{6,7},{7,6},{8,9},{9,8},{10,11... | collective-permute-start | bytes 393224 | tf_op jit(solution)/shard_map/ppermute | solution.py:190
  93.6 6.4 %collective-permute-start.22 = (f32[8,4096]{1,0:T(8,128)S(1)}, f32[8,4096]{1,0:T(8,128)S(1)}, u32[]{:S(2)}, u32[]{:S(2)}) collective-permute-start(f32[8,4096]{1,0:T(8,128)S(1)} %get-tuple-element.60), channel_id=1, source_target_pairs={{0,2},{1,3},{2,0},{3,1},{4,6},{5,7},{6,4},{7,5},{8,10},{9,11},{10,... | collective-permute-start | bytes 393224 | tf_op jit(solution)/shard_map/ppermute | solution.py:190
  95.4 7.2 %collective-permute-start.23 = (f32[8,4096]{1,0:T(8,128)S(1)}, f32[8,4096]{1,0:T(8,128)S(1)}, u32[]{:S(2)}, u32[]{:S(2)}) collective-permute-start(f32[8,4096]{1,0:T(8,128)S(1)} %get-tuple-element.61), channel_id=1, source_target_pairs={{0,3},{1,2},{2,1},{3,0},{4,7},{5,6},{6,5},{7,4},{8,11},{9,10},{10,... | collective-permute-start | bytes 393224 | tf_op jit(solution)/shard_map/ppermute | solution.py:190
  103.3 4.5 %collective-permute-start.24 = (f32[8,128]{1,0:T(8,128)S(1)}, f32[8,128]{1,0:T(8,128)S(1)}, u32[]{:S(2)}, u32[]{:S(2)}) collective-permute-start(f32[8,128]{1,0:T(8,128)S(1)} %get-tuple-element.62), channel_id=1, source_target_pairs={{0,1},{1,0},{2,3},{3,2},{4,5},{5,4},{6,7},{7,6},{8,9},{9,8},{10,11... | collective-permute-start | bytes 12296 | tf_op jit(solution)/shard_map/ppermute | solution.py:190
  107.8 4.5 %collective-permute-start.25 = (f32[8,128]{1,0:T(8,128)S(1)}, f32[8,128]{1,0:T(8,128)S(1)}, u32[]{:S(2)}, u32[]{:S(2)}) collective-permute-start(f32[8,128]{1,0:T(8,128)S(1)} %add.20), channel_id=1, source_target_pairs={{0,2},{1,3},{2,0},{3,1},{4,6},{5,7},{6,4},{7,5},{8,10},{9,11},{10,... | collective-permute-start | bytes 12296 | tf_op jit(solution)/shard_map/ppermute | solution.py:190
  112.3 5.7 %collective-permute-start.26 = (f32[8,128]{1,0:T(8,128)S(1)}, f32[8,128]{1,0:T(8,128)S(1)}, u32[]{:S(2)}, u32[]{:S(2)}) collective-permute-start(f32[8,128]{1,0:T(8,128)S(1)} %add.21), channel_id=1, source_target_pairs={{0,4},{4,0},{8,12},{12,8},{16,20},{20,16},{24,28},{28,24},{1,5},{5... | collective-permute-start | bytes 12296 | tf_op jit(solution)/shard_map/ppermute | solution.py:190
  118.0 11.2 %collective-permute-start.27 = (f32[8,128]{1,0:T(8,128)S(1)}, f32[8,128]{1,0:T(8,128)S(1)}, u32[]{:S(2)}, u32[]{:S(2)}) collective-permute-start(f32[8,128]{1,0:T(8,128)S(1)} %add.22), channel_id=1, source_target_pairs={{0,8},{4,12},{8,0},{12,4},{16,24},{20,28},{24,16},{28,20},{1,9},{5... | collective-permute-start | bytes 12296 | tf_op jit(solution)/shard_map/ppermute | solution.py:190
  129.2 4.8 %collective-permute-start.28 = (f32[8,128]{1,0:T(8,128)S(1)}, f32[8,128]{1,0:T(8,128)S(1)}, u32[]{:S(2)}, u32[]{:S(2)}) collective-permute-start(f32[8,128]{1,0:T(8,128)S(1)} %add.23), channel_id=1, source_target_pairs={{0,16},{4,20},{8,24},{12,28},{16,0},{20,4},{24,8},{28,12},{1,17},{... | collective-permute-start | bytes 12296 | tf_op jit(solution)/shard_map/ppermute | solution.py:190
  (12 other events, 69.5 us)

commit v2 on v1

v2 whole, which is shorter than its diff:
```python
import functools

import jax
import jax.numpy as jnp
from jax import lax
from jax.experimental import pallas as pl
from jax.experimental.pallas import tpu as pltpu
from jax.sharding import PartitionSpec as P

ITERS = 3
LANES = 128
GROUP = 8
CHUNKS = 8
F32 = jnp.float32
BF16 = jnp.bfloat16
VMEM = pl.BlockSpec(memory_space=pltpu.VMEM)
SMEM = pl.BlockSpec(memory_space=pltpu.SMEM)
SLOTS = 128
EARLY_ROWS, EARLY_COLS, AHEAD_COLS, LATE_ROWS, LATE_COLS, FROM_AHEAD = range(6)
PARAMS = pltpu.CompilerParams(vmem_limit_bytes=16 * 1024 * 1024)


def times(field, block):
    return lax.dot_general(field, block, (((1,), (0,)), ((), ())), preferred_element_type=F32)


def times_transposed(field, block):
    return lax.dot_general(field, block, (((1,), (1,)), ((), ())), preferred_element_type=F32)


def order_kernel(right_ref, order_ref, curve_ref, rounded_ref):
    rhs_count, points = right_ref.shape
    for start in range(0, points, LANES):
        at = jnp.broadcast_to(order_ref[:, start : start + LANES], (rhs_count, LANES))
        chunk = at // LANES
        lane = at % LANES
        result = jnp.zeros((rhs_count, LANES), F32)
        for source in range(points // LANES):
            values = right_ref[:, source * LANES : (source + 1) * LANES]
            picked = jnp.take_along_axis(values, lane, axis=1)
            result = jnp.where(chunk == source, picked, result)
        curve_ref[:, start : start + LANES] = result
        rounded_ref[:, start : start + LANES] = result.astype(BF16)


def device_place(block_len, field_ref, sub_count):
    blocks_dev = field_ref.shape[1] // block_len
    sub_index = lax.axis_index("sub")
    return sub_index, blocks_dev, sub_index * blocks_dev, blocks_dev * sub_count


def load_kernel(sub_count, blocks_dev, pairs_ref, blocks_in, diag_in, blocks_ref, diag_ref, lists_ref, sems):
    slot_count = pairs_ref.shape[1]
    size = slot_count // CHUNKS
    copies = [
        pltpu.make_async_copy(
            blocks_in.at[pl.ds(part * size, size)], blocks_ref.at[pl.ds(part * size, size)], sems.at[part]
        )
        for part in range(CHUNKS)
    ]
    copies.append(pltpu.make_async_copy(diag_in, diag_ref, sems.at[CHUNKS]))
    for copy in copies:
        copy.start()
    sub_index = lax.axis_index("sub")
    tile_blocks = blocks_dev * sub_count
    own_first = sub_index * blocks_dev
    first_block = lax.axis_index("tile") * tile_blocks
    idle = (tile_blocks + blocks_dev) * 65536
    idle_source = {
        EARLY_ROWS: own_first,
        EARLY_COLS: own_first,
        AHEAD_COLS: tile_blocks - blocks_dev,
        LATE_ROWS: 0,
        LATE_COLS: 0,
        FROM_AHEAD: tile_blocks,
    }
    for index, source in idle_source.items():
        entry = idle + 256 * source

        def clear(at, carry, index=index, entry=entry):
            lists_ref[index * SLOTS + at] = entry
            return carry

        lax.fori_loop(0, SLOTS, clear, 0, unroll=8)

    def one_slot(slot, counts):
        row, col = pairs_ref[0, slot], pairs_ref[1, slot]
        live = row >= 0
        row, col = row - first_block, col - first_block

        def append(counts, source, target, kinds):
            early = (source // blocks_dev) // 2 == sub_index // 2
            entry = slot + 256 * source + 65536 * target
            for index, chosen in kinds(early):
                chosen = chosen & live
                count = counts[index]

                @pl.when(chosen)
                def _():
                    lists_ref[index * SLOTS + count] = entry

                counts[index] = count + chosen.astype(jnp.int32)

        counts = list(counts)
        outside = col >= tile_blocks
        append(
            counts, col, row,
            lambda early: (
                (EARLY_ROWS, early & ~outside), (LATE_ROWS, ~early & ~outside), (FROM_AHEAD, outside)
            ),
        )
        append(
            counts, row, col,
            lambda early: (
                (EARLY_COLS, early), (LATE_COLS, ~early & ~outside), (AHEAD_COLS, ~early & outside)
            ),
        )
        return tuple(counts)

    counts = lax.fori_loop(0, slot_count, one_slot, (jnp.int32(0),) * 6)
    for index, count in enumerate(counts):
        lists_ref[6 * SLOTS + index] = count
    for copy in copies:
        copy.wait()


def add_products(lists_ref, blocks_ref, field, total, row_list, col_list, source_from=0, target_from=0):
    kinds = [(index, kind) for index, kind in ((row_list, times_transposed), (col_list, times)) if index is not None]
    longest = functools.reduce(jnp.maximum, [lists_ref[6 * SLOTS + index] for index, _ in kinds])

    def one_group(group, carry):
        results = []
        for step in range(GROUP):
            for index, kind in kinds:
                entry = lists_ref[index * SLOTS + group * GROUP + step]
                slot, source, target = entry & 255, (entry >> 8) & 255, entry >> 16
                value = kind(field[source - source_from].astype(BF16), blocks_ref[slot])
                results.append((target - target_from, value))
        for at, value in results:
            total[at] += value
        return carry

    lax.fori_loop(0, (longest + GROUP - 1) // GROUP, one_group, 0)


def lay_out(row_ref, field, first, block_len):
    for block in range(row_ref.shape[1] // block_len):
        piece = row_ref[:, block * block_len : (block + 1) * block_len]
        field[first + block] = piece.astype(F32)


def early_kernel(sub_count, lists_ref, blocks_ref, diag_ref, noise_ref, own_ref, *refs):
    row_refs, (total, field) = refs[:-2], refs[-2:]
    block_len = blocks_ref.shape[1]
    sub_index, blocks_dev, own_first, _ = device_place(block_len, own_ref, sub_count)
    for step, row_ref in enumerate(row_refs):
        lay_out(row_ref, field, (sub_index ^ step) * blocks_dev, block_len)
    for block in range(total.shape[0]):
        total[block] = jnp.zeros(total.shape[1:], F32)
    for block in range(blocks_dev):
        span = slice(block * block_len, (block + 1) * block_len)
        value = noise_ref[:, span] * own_ref[:, span]
        total[own_first + block] = value + times(field[own_first + block].astype(BF16), diag_ref[block])
    add_products(lists_ref, blocks_ref, field, total, EARLY_ROWS, EARLY_COLS)


def ahead_kernel(sub_count, lists_ref, blocks_ref, begun_ref, *refs):
    row_refs = refs[:sub_count]
    even_ref, odd_ref, field_ref, total = refs[sub_count:]
    block_len = blocks_ref.shape[1]
    sub_index, blocks_dev, _, tile_blocks = device_place(block_len, even_ref, sub_count)
    for step, row_ref in enumerate(row_refs):
        lay_out(row_ref, field_ref, (sub_index ^ step) * blocks_dev, block_len)
    for block in range(blocks_dev):
        total[block] = begun_ref[tile_blocks + block]
    total[blocks_dev] = jnp.zeros(total.shape[1:], F32)
    add_products(lists_ref, blocks_ref, field_ref, total, None, AHEAD_COLS, 0, tile_blocks)
    is_odd = lax.axis_index("tile") % 2 == 1
    for block in range(blocks_dev):
        span = slice(block * block_len, (block + 1) * block_len)
        products = total[block]
        first_row = field_ref[block]
        even_ref[:, span] = jnp.where(is_odd, first_row, products).astype(BF16)
        odd_ref[:, span] = jnp.where(is_odd, products, first_row).astype(BF16)


def late_kernel(lists_ref, blocks_ref, begun_ref, field_ref, total):
    total[...] = begun_ref[...]
    add_products(lists_ref, blocks_ref, field_ref, total, LATE_ROWS, LATE_COLS)


def part_kernel(sub_count, is_last, lists_ref, blocks_ref, begun_ref, field_ref, even_ref, odd_ref, moments_in_ref, *refs):
    part_refs = refs[:sub_count]
    moments_ref, total, ahead = refs[sub_count:]
    block_len = blocks_ref.shape[1]
    sub_index, blocks_dev, own_first, tile_blocks = device_place(block_len, even_ref, sub_count)
    is_odd = lax.axis_index("tile") % 2 == 1
    for block in range(blocks_dev):
        span = slice(block * block_len, (block + 1) * block_len)
        even = even_ref[:, span].astype(F32)
        odd = odd_ref[:, span].astype(F32)
        ahead[block] = jnp.where(is_odd, odd, even)
        total[block] = begun_ref[block] + jnp.where(is_odd, even, odd)
    for block in range(blocks_dev, tile_blocks):
        total[block] = begun_ref[block]
    total[begun_ref.shape[0] - 1] = jnp.zeros(total.shape[1:], F32)
    add_products(lists_ref, blocks_ref, ahead, total, FROM_AHEAD, None, tile_blocks, 0)
    for step in range(sub_count):
        first = (sub_index ^ step) * blocks_dev
        for block in range(blocks_dev):
            span = slice(block * block_len, (block + 1) * block_len)
            part_refs[step][:, span] = total[first + block].astype(part_refs[step].dtype)
    moments = moments_in_ref[...]
    if is_last:
        product = jnp.zeros(total.shape[1:], F32)
        for block in range(tile_blocks):
            product += field_ref[block] * total[block]
        lane = lax.broadcasted_iota(jnp.int32, moments.shape, 1)
        moments = jnp.where(lane == 2 * ITERS - 1, jnp.sum(product, axis=1, keepdims=True), moments)
    moments_ref[...] = moments


def join_kernel(index, own_ref, old_ref, moments_in_ref, *refs):
    part_refs = refs[:-3]
    next_ref, rounded_ref, moments_ref = refs[-3:]
    value = own_ref[...]
    for part_ref in part_refs:
        value += part_ref[...].astype(F32)
    next_ref[...] = value
    rounded_ref[...] = value.astype(BF16)
    old = old_ref[...]
    lane = lax.broadcasted_iota(jnp.int32, moments_ref.shape, 1)
    moments = moments_in_ref[...] if index else jnp.zeros(moments_ref.shape, F32)
    found = {2 * index + 1: old * value, 2 * index + 2: value * value}
    if index == 0:
        found[0] = old * old
    for order, product in found.items():
        moments = jnp.where(lane == order, jnp.sum(product, axis=1, keepdims=True), moments)
    moments_ref[...] = moments


def finish_kernel(sub_count, moments_ref, *refs):
    part_refs, basis_refs = refs[:sub_count], refs[sub_count:-2]
    solution_ref, residual_ref = refs[-2:]
    moments = [moments_ref[:, order : order + 1] for order in range(2 * ITERS)]

    def inner(first, second, shift):
        value = 0.0
        for i, a in enumerate(first):
            for j, b in enumerate(second):
                value = value + a * b * moments[i + j + shift]
        return value

    one = jnp.ones_like(moments[0])
    zero = jnp.zeros_like(one)
    direction, residual = [one], [one]
    answer = [zero] * ITERS
    norm_now = moments[0]
    for iteration in range(ITERS):
        step_size = norm_now / inner(direction, direction, 1)
        for power, weight in enumerate(direction):
            answer[power] = answer[power] + step_size * weight
        residual = residual + [zero]
        for power, weight in enumerate(direction):
            residual[power + 1] = residual[power + 1] - step_size * weight
        if iteration + 1 < ITERS:
            norm_next = inner(residual, residual, 0)
            direction = [
                value + (norm_next / norm_now) * old
                for value, old in zip(residual, direction + [zero])
            ]
            norm_now = norm_next
    fields = [basis_ref[...] for basis_ref in basis_refs]
    fields.append(sum(part_ref[...].astype(F32) for part_ref in part_refs))
    solution_ref[...] = sum(weight * field for weight, field in zip(answer, fields))
    residual_ref[...] = sum(weight * field for weight, field in zip(residual, fields))


def shape(rows, columns, kind):
    return jax.ShapeDtypeStruct((rows, columns), kind)


def exchange(block, axis, step):
    count = lax.axis_size(axis)
    return lax.ppermute(block, axis, [(i, i ^ step) for i in range(count)])


def swap(block, axis, first):
    count = lax.axis_size(axis)
    route = []
    for i in range(first, count - 1, 2):
        route += [(i, i + 1), (i + 1, i)]
    return lax.ppermute(block, axis, route)


def call(kernel, outs, ins, name, cost=0, **options):
    single = not isinstance(outs, tuple)
    specs = [SMEM if getattr(value, "dtype", None) == jnp.int32 and value.ndim == 1 else VMEM for value in ins]
    options.setdefault("in_specs", specs)
    options.setdefault("out_specs", VMEM if single else (VMEM,) * len(outs))
    return pl.pallas_call(
        kernel,
        out_shape=outs,
        compiler_params=PARAMS,
        name=name,
        cost_estimate=pl.CostEstimate(flops=int(cost * 1e9), bytes_accessed=0, transcendentals=0),
        **options,
    )(*ins)


def on_device(right_side, point_order, noise_var, block_pairs, pair_blocks, diag_blocks):
    sub_count = lax.axis_size("sub")
    tile_count = lax.axis_size("tile")
    rhs_count, points_dev = right_side.shape
    blocks_dev, block_len = diag_blocks.shape[:2]
    extended = (sub_count + 1) * blocks_dev
    noise = noise_var[None, :]
    full = shape(rhs_count, points_dev, F32)
    half = shape(rhs_count, points_dev, BF16)
    scalars = shape(rhs_count, LANES, F32)
    sums = jax.ShapeDtypeStruct((extended + 1, rhs_count, block_len), F32)

    def scratch(blocks):
        return pltpu.VMEM((blocks, rhs_count, block_len), F32)

    any_space = pl.BlockSpec(memory_space=pl.ANY)
    blocks, diag, lists = call(
        functools.partial(load_kernel, sub_count, blocks_dev),
        (
            pltpu.VMEM(pair_blocks.shape, BF16),
            pltpu.VMEM(diag_blocks.shape, BF16),
            jax.ShapeDtypeStruct((8 * SLOTS,), jnp.int32),
        ),
        (block_pairs.T, pair_blocks, diag_blocks),
        "load",
        4,
        in_specs=[SMEM, any_space, any_space],
        out_specs=(VMEM, VMEM, SMEM),
        scratch_shapes=[pltpu.SemaphoreType.DMA((CHUNKS + 1,))],
    )
    field, rounded = call(order_kernel, (full, half), (right_side, point_order), "curve_order", 1, in_specs=[VMEM, VMEM])
    basis = [field]
    moments = jnp.zeros(scalars.shape, F32)
    for index in range(ITERS):
        is_last = index + 1 == ITERS
        rows = [rounded] + [exchange(rounded, "sub", step) for step in range(1, sub_count)]
        begun = call(
            functools.partial(early_kernel, sub_count),
            sums,
            (lists, blocks, diag, noise, field, *rows[:2]),
            "early",
            3,
            scratch_shapes=[scratch(extended)],
        )
        even, odd, tile_field = call(
            functools.partial(ahead_kernel, sub_count),
            (half, half, jax.ShapeDtypeStruct((sub_count * blocks_dev, rhs_count, block_len), F32)),
            (lists, blocks, begun, *rows),
            "ahead",
            1,
            scratch_shapes=[scratch(blocks_dev + 1)],
        )
        even = swap(even, "tile", 0)
        odd = swap(odd, "tile", 1)
        begun = call(late_kernel, sums, (lists, blocks, begun, tile_field), "late", 3)
        part = shape(rhs_count, points_dev, F32 if is_last else BF16)
        *parts, moments = call(
            functools.partial(part_kernel, sub_count, is_last),
            (full,) + (part,) * (sub_count - 1) + (scalars,),
            (lists, blocks, begun, tile_field, even, odd, moments),
            "parts",
            1,
            scratch_shapes=[scratch(extended + 1), scratch(blocks_dev)],
        )
        arrived = [exchange(parts[step], "sub", step) for step in range(1, sub_count)]
        if not is_last:
            field, rounded, moments = call(
                functools.partial(join_kernel, index),
                (full, half, scalars),
                (parts[0], field, moments, *arrived),
                "join",
            )
            basis.append(field)
    for axis, count in (("sub", sub_count), ("tile", tile_count)):
        step = 1
        while step < count:
            moments = moments + exchange(moments, axis, step)
            step *= 2
    return call(
        functools.partial(finish_kernel, sub_count),
        (full, full),
        (moments, parts[0], *arrived, *basis),
        "finish",
    )


def solution(mesh):
    placed = (
        P(None, ("tile", "sub")),
        P(("tile", "sub"), None),
        P(("tile", "sub")),
        P(("tile", "sub"), None),
        P(("tile", "sub"), None, None),
        P(("tile", "sub"), None, None),
    )
    return jax.shard_map(
        on_device,
        mesh=mesh,
        in_specs=placed,
        out_specs=(P(None, ("tile", "sub")), P(None, ("tile", "sub"))),
        check_vma=False,
    )
```

time: 134 us -> 120 us (0.90)
  starting transfers between devices: 60.2 us -> 44.7 us
  Pallas kernels: 27.5 us -> 37.6 us
  waiting for transfers between devices: 35.7 us -> 28.8 us
  other arithmetic: 2.74 us -> 0.02 us
    pallas_call x11 -> x17, Pallas kernels: 27.5 us -> 37.6 us  [call(): pl.pallas_call(kernel, out_shape=outs, compiler_params=PARAMS, name=name,...]
    ppermute x23, starting transfers between devices: 50.1 us -> 41.1 us  [exchange(): return lax.ppermute(block, axis, [(i, i ^ step) for i in range(count)])]
    ppermute x6, starting transfers between devices: 10.1 us -> 3.6 us  [swap(): return lax.ppermute(block, axis, route)]
    ppermute x23, waiting for transfers between devices: 34.7 us -> 28.7 us  [exchange(): return lax.ppermute(block, axis, [(i, i ^ step) for i in range(count)])]
    unnamed x14 -> x12, local copies, waits for them, and re-layouts: 7.82 us -> 8.46 us
  transfers between devices with their start and end apart: 29 -> 29, of which waited for: 19 -> 14; matrix products, arithmetic and copies ran while one was open for 2% -> 0% of each run, Pallas kernels for 0% -> 22%
where the time goes in v2:
time: 120 us
  starting transfers between devices  44.7 us (37%)
  Pallas kernels  37.6 us (31%)
  waiting for transfers between devices  28.8 us (24%)
  local copies, waits for them, and re-layouts  8.46 us (7%)
    ppermute x23, starting transfers between devices, exchange(): return lax.ppermute(block, axis, [(i, i ^ step) for i in range(count)])  41.1 us
    pallas_call x17, Pallas kernels, call(): pl.pallas_call(kernel, out_shape=outs, compiler_params=PARAMS, name=name,...  37.6 us
    ppermute x23, waiting for transfers between devices, exchange(): return lax.ppermute(block, axis, [(i, i ^ step) for i in range(count)])  28.7 us
    unnamed x12, local copies, waits for them, and re-layouts  8.46 us
    ppermute x6, starting transfers between devices, swap(): return lax.ppermute(block, axis, route)  3.6 us
  transfers between devices with their start and end apart: 29, of which 14 were waited for; matrix products, arithmetic and copies ran while one was open for 0% of the time, Pallas kernels for 22%

profile of v2, /device:TPU:0, one launch (start us, length us, event | category | flops | bytes accessed | tf_op | source)
XLA Modules:
  0.0 120.4 jit_solution(4219946486444509202)
XLA Ops:
  3.5 5.1 %collective-permute-start.2 = (bf16[8,4096]{1,0:T(8,128)(2,1)S(1)}, bf16[8,4096]{1,0:T(8,128)(2,1)S(1)}, u32[]{:S(2)}, u32[]{:S(2)}) collective-permute-start(bf16[8,4096]{1,0:T(8,128)(2,1)S(1)} %get-tuple-element.41.refs_0_), channel_id=1, source_target_pairs={{0,3},{1,2},{2,1},{3,0},{4,7},{5,6},{6,5},{7,4},{8,11},{9,10},{10,... | collective-permute-start | bytes 196616 | tf_op jit(solution)/shard_map/ppermute | solution.py:285
  9.3 4.6 %copy-done.1 = bf16[96,256,256]{2,1,0:T(8,128)(2,1)S(1)} copy-done((bf16[96,256,256]{2,1,0:T(8,128)(2,1)S(1)}, bf16[96,256,256]{2,1,0:T(8,128)(2,1)}, u32[]{:S(2)}) %copy-start.1) | copy-done | bytes 12582936
  16.1 7.7 %load.1 = (bf16[96,256,256]{2,1,0:T(8,128)(2,1)S(1)}, bf16[16,256,256]{2,1,0:T(8,128)(2,1)S(1)}, s32[1024]{0:T(1024)S(1)}) custom-call(s32[2,96]{1,0:T(2,128)S(1)} %bitcast.5, bf16[96,256,256]{2,1,0:T(8,128)(2,1)S(1)} %copy-done.1, bf16[16,256,256]{2,1,0:T(8,128)(2,1)S(1)} %copy-done.2), custom_call_target="tpu_custom_call" | custom-call | flops 4000000000 | tf_op jit(solution)/shard_map/load/pallas_call | solution.py:301
  23.8 3.1 %early.3.begun_ref = f32[81,8,256]{2,1,0:T(8,128)S(1)} custom-call(s32[1024]{0:T(1024)S(1)} %get-tuple-element.37.lists_ref, bf16[96,256,256]{2,1,0:T(8,128)(2,1)S(1)} %get-tuple-element.38.blocks_ref, bf16[16,256,256]{2,1,0:T(8,128)(2,1)S(1)} %get-tuple-element.39.diag_ref, f32[1,4096]{1,0:T(1,128)S(1)} %bitcast.2, ...), custom_call_target="tpu_custom_call" | custom-call | flops 3000000000 | tf_op jit(solution)/shard_map/early/pallas_call | solution.py:301
  29.5 3.3 %late.3.begun_ref = f32[81,8,256]{2,1,0:T(8,128)S(1)} custom-call(s32[1024]{0:T(1024)S(1)} %get-tuple-element.37.lists_ref, bf16[96,256,256]{2,1,0:T(8,128)(2,1)S(1)} %get-tuple-element.38.blocks_ref, f32[81,8,256]{2,1,0:T(8,128)S(1)} %early.3.begun_ref, f32[64,8,256]{2,1,0:T(8,128)S(1)} %get-tuple-element.42.field_ref), custom_call_target="tpu_custom_call" | custom-call | flops 3000000000 | tf_op jit(solution)/shard_map/late/pallas_call | solution.py:301
  34.7 5.5 %collective-permute-start.6 = (bf16[8,4096]{1,0:T(8,128)(2,1)S(1)}, bf16[8,4096]{1,0:T(8,128)(2,1)S(1)}, u32[]{:S(2)}, u32[]{:S(2)}) collective-permute-start(bf16[8,4096]{1,0:T(8,128)(2,1)S(1)} %get-tuple-element.48), channel_id=1, source_target_pairs={{0,2},{1,3},{2,0},{3,1},{4,6},{5,7},{6,4},{7,5},{8,10},{9,11},{10,... | collective-permute-start | bytes 196616 | tf_op jit(solution)/shard_map/ppermute | solution.py:285
  40.2 4.2 %collective-permute-done.6.refs_1_ = bf16[8,4096]{1,0:T(8,128)(2,1)S(1)} collective-permute-done((bf16[8,4096]{1,0:T(8,128)(2,1)S(1)}, bf16[8,4096]{1,0:T(8,128)(2,1)S(1)}, u32[]{:S(2)}, u32[]{:S(2)}) %collective-permute-start.6) | collective-permute-done | bytes 65568 | tf_op jit(solution)/shard_map/ppermute | solution.py:285
  47.9 2.3 %collective-permute-start.10 = (bf16[8,4096]{1,0:T(8,128)(2,1)S(1)}, bf16[8,4096]{1,0:T(8,128)(2,1)S(1)}, u32[]{:S(2)}, u32[]{:S(2)}) collective-permute-start(bf16[8,4096]{1,0:T(8,128)(2,1)S(1)} %get-tuple-element.51.refs_0_), channel_id=1, source_target_pairs={{0,3},{1,2},{2,1},{3,0},{4,7},{5,6},{6,5},{7,4},{8,11},{9,10},{10,... | collective-permute-start | bytes 196616 | tf_op jit(solution)/shard_map/ppermute | solution.py:285
  50.7 3.1 %early.4.begun_ref = f32[81,8,256]{2,1,0:T(8,128)S(1)} custom-call(s32[1024]{0:T(1024)S(1)} %get-tuple-element.37.lists_ref, bf16[96,256,256]{2,1,0:T(8,128)(2,1)S(1)} %get-tuple-element.38.blocks_ref, bf16[16,256,256]{2,1,0:T(8,128)(2,1)S(1)} %get-tuple-element.39.diag_ref, f32[1,4096]{1,0:T(1,128)S(1)} %bitcast.3, ...), custom_call_target="tpu_custom_call" | custom-call | flops 3000000000 | tf_op jit(solution)/shard_map/early/pallas_call | solution.py:301
  54.5 2.1 %collective-permute-done.9.refs_2_ = bf16[8,4096]{1,0:T(8,128)(2,1)S(1)} collective-permute-done((bf16[8,4096]{1,0:T(8,128)(2,1)S(1)}, bf16[8,4096]{1,0:T(8,128)(2,1)S(1)}, u32[]{:S(2)}, u32[]{:S(2)}) %collective-permute-start.9) | collective-permute-done | bytes 65568 | tf_op jit(solution)/shard_map/ppermute | solution.py:285
  58.9 3.3 %late.4.begun_ref = f32[81,8,256]{2,1,0:T(8,128)S(1)} custom-call(s32[1024]{0:T(1024)S(1)} %get-tuple-element.37.lists_ref, bf16[96,256,256]{2,1,0:T(8,128)(2,1)S(1)} %get-tuple-element.38.blocks_ref, f32[81,8,256]{2,1,0:T(8,128)S(1)} %early.4.begun_ref, f32[64,8,256]{2,1,0:T(8,128)S(1)} %get-tuple-element.52.field_ref), custom_call_target="tpu_custom_call" | custom-call | flops 3000000000 | tf_op jit(solution)/shard_map/late/pallas_call | solution.py:301
  63.8 3.1 %collective-permute-start.14 = (bf16[8,4096]{1,0:T(8,128)(2,1)S(1)}, bf16[8,4096]{1,0:T(8,128)(2,1)S(1)}, u32[]{:S(2)}, u32[]{:S(2)}) collective-permute-start(bf16[8,4096]{1,0:T(8,128)(2,1)S(1)} %get-tuple-element.59), channel_id=1, source_target_pairs={{0,2},{1,3},{2,0},{3,1},{4,6},{5,7},{6,4},{7,5},{8,10},{9,11},{10,... | collective-permute-start | bytes 196616 | tf_op jit(solution)/shard_map/ppermute | solution.py:285
  69.1 3.9 %collective-permute-done.15.refs_2_ = bf16[8,4096]{1,0:T(8,128)(2,1)S(1)} collective-permute-done((bf16[8,4096]{1,0:T(8,128)(2,1)S(1)}, bf16[8,4096]{1,0:T(8,128)(2,1)S(1)}, u32[]{:S(2)}, u32[]{:S(2)}) %collective-permute-start.15) | collective-permute-done | bytes 65568 | tf_op jit(solution)/shard_map/ppermute | solution.py:285
  73.1 2.1 %collective-permute-start.18 = (bf16[8,4096]{1,0:T(8,128)(2,1)S(1)}, bf16[8,4096]{1,0:T(8,128)(2,1)S(1)}, u32[]{:S(2)}, u32[]{:S(2)}) collective-permute-start(bf16[8,4096]{1,0:T(8,128)(2,1)S(1)} %get-tuple-element.62.refs_0_), channel_id=1, source_target_pairs={{0,3},{1,2},{2,1},{3,0},{4,7},{5,6},{6,5},{7,4},{8,11},{9,10},{10,... | collective-permute-start | bytes 196616 | tf_op jit(solution)/shard_map/ppermute | solution.py:285
  77.4 3.1 %early.5.begun_ref = f32[81,8,256]{2,1,0:T(8,128)S(1)} custom-call(s32[1024]{0:T(1024)S(1)} %get-tuple-element.37.lists_ref, bf16[96,256,256]{2,1,0:T(8,128)(2,1)S(1)} %get-tuple-element.38.blocks_ref, bf16[16,256,256]{2,1,0:T(8,128)(2,1)S(1)} %get-tuple-element.39.diag_ref, f32[1,4096]{1,0:T(1,128)S(1)} %bitcast.4, ...), custom_call_target="tpu_custom_call" | custom-call | flops 3000000000 | tf_op jit(solution)/shard_map/early/pallas_call | solution.py:301
  80.5 2.8 %collective-permute-done.17.refs_2_ = bf16[8,4096]{1,0:T(8,128)(2,1)S(1)} collective-permute-done((bf16[8,4096]{1,0:T(8,128)(2,1)S(1)}, bf16[8,4096]{1,0:T(8,128)(2,1)S(1)}, u32[]{:S(2)}, u32[]{:S(2)}) %collective-permute-start.17) | collective-permute-done | bytes 65568 | tf_op jit(solution)/shard_map/ppermute | solution.py:285
  85.8 3.3 %late.5.begun_ref = f32[81,8,256]{2,1,0:T(8,128)S(1)} custom-call(s32[1024]{0:T(1024)S(1)} %get-tuple-element.37.lists_ref, bf16[96,256,256]{2,1,0:T(8,128)(2,1)S(1)} %get-tuple-element.38.blocks_ref, f32[81,8,256]{2,1,0:T(8,128)S(1)} %early.5.begun_ref, f32[64,8,256]{2,1,0:T(8,128)S(1)} %get-tuple-element.63.field_ref), custom_call_target="tpu_custom_call" | custom-call | flops 3000000000 | tf_op jit(solution)/shard_map/late/pallas_call | solution.py:301
  90.8 3.4 %collective-permute-start.27 = (f32[8,4096]{1,0:T(8,128)S(1)}, f32[8,4096]{1,0:T(8,128)S(1)}, u32[]{:S(2)}, u32[]{:S(2)}) collective-permute-start(f32[8,4096]{1,0:T(8,128)S(1)} %get-tuple-element.70), channel_id=1, source_target_pairs={{0,2},{1,3},{2,0},{3,1},{4,6},{5,7},{6,4},{7,5},{8,10},{9,11},{10,... | collective-permute-start | bytes 393224 | tf_op jit(solution)/shard_map/ppermute | solution.py:285
  95.1 3.9 %collective-permute-done.21 = f32[8,128]{1,0:T(8,128)S(1)} collective-permute-done((f32[8,128]{1,0:T(8,128)S(1)}, f32[8,128]{1,0:T(8,128)S(1)}, u32[]{:S(2)}, u32[]{:S(2)}) %collective-permute-start.21) | collective-permute-done | bytes 4128 | tf_op jit(solution)/shard_map/ppermute | solution.py:285
  99.0 2.5 %collective-permute-start.22 = (f32[8,128]{1,0:T(8,128)S(1)}, f32[8,128]{1,0:T(8,128)S(1)}, u32[]{:S(2)}, u32[]{:S(2)}) collective-permute-start(f32[8,128]{1,0:T(8,128)S(1)} %add.15), channel_id=1, source_target_pairs={{0,2},{1,3},{2,0},{3,1},{4,6},{5,7},{6,4},{7,5},{8,10},{9,11},{10,... | collective-permute-start | bytes 12296 | tf_op jit(solution)/shard_map/ppermute | solution.py:285
  101.5 3.0 %collective-permute-done.22 = f32[8,128]{1,0:T(8,128)S(1)} collective-permute-done((f32[8,128]{1,0:T(8,128)S(1)}, f32[8,128]{1,0:T(8,128)S(1)}, u32[]{:S(2)}, u32[]{:S(2)}) %collective-permute-start.22) | collective-permute-done | bytes 4128 | tf_op jit(solution)/shard_map/ppermute | solution.py:285
  104.5 2.4 %collective-permute-start.23 = (f32[8,128]{1,0:T(8,128)S(1)}, f32[8,128]{1,0:T(8,128)S(1)}, u32[]{:S(2)}, u32[]{:S(2)}) collective-permute-start(f32[8,128]{1,0:T(8,128)S(1)} %add.16), channel_id=1, source_target_pairs={{0,4},{4,0},{8,12},{12,8},{16,20},{20,16},{24,28},{28,24},{1,5},{5... | collective-permute-start | bytes 12296 | tf_op jit(solution)/shard_map/ppermute | solution.py:285
  107.7 5.1 %collective-permute-start.24 = (f32[8,128]{1,0:T(8,128)S(1)}, f32[8,128]{1,0:T(8,128)S(1)}, u32[]{:S(2)}, u32[]{:S(2)}) collective-permute-start(f32[8,128]{1,0:T(8,128)S(1)} %add.17), channel_id=1, source_target_pairs={{0,8},{4,12},{8,0},{12,4},{16,24},{20,28},{24,16},{28,20},{1,9},{5... | collective-permute-start | bytes 12296 | tf_op jit(solution)/shard_map/ppermute | solution.py:285
  114.4 3.4 %collective-permute-start.25 = (f32[8,128]{1,0:T(8,128)S(1)}, f32[8,128]{1,0:T(8,128)S(1)}, u32[]{:S(2)}, u32[]{:S(2)}) collective-permute-start(f32[8,128]{1,0:T(8,128)S(1)} %add.18), channel_id=1, source_target_pairs={{0,16},{4,20},{8,24},{12,28},{16,0},{20,4},{24,8},{28,12},{1,17},{... | collective-permute-start | bytes 12296 | tf_op jit(solution)/shard_map/ppermute | solution.py:285
  (69 shorter events, 33.3 us)
Async XLA Ops:
  3.5 23.4 %collective-permute-start.2 = (bf16[8,4096]{1,0:T(8,128)(2,1)S(1)}, bf16[8,4096]{1,0:T(8,128)(2,1)S(1)}, u32[]{:S(2)}, u32[]{:S(2)}) collective-permute-start(bf16[8,4096]{1,0:T(8,128)(2,1)S(1)} %get-tuple-element.41.refs_0_), channel_id=1, source_target_pairs={{0,3},{1,2},{2,1},{3,0},{4,7},{5,6},{6,5},{7,4},{8,11},{9,10},{10,... | collective-permute-start | bytes 196616 | tf_op jit(solution)/shard_map/ppermute | solution.py:285
  8.6 18.3 %collective-permute-start.1 = (bf16[8,4096]{1,0:T(8,128)(2,1)S(1)}, bf16[8,4096]{1,0:T(8,128)(2,1)S(1)}, u32[]{:S(2)}, u32[]{:S(2)}) collective-permute-start(bf16[8,4096]{1,0:T(8,128)(2,1)S(1)} %get-tuple-element.41.refs_0_), channel_id=1, source_target_pairs={{0,2},{1,3},{2,0},{3,1},{4,6},{5,7},{6,4},{7,5},{8,10},{9,11},{10,... | collective-permute-start | bytes 196616 | tf_op jit(solution)/shard_map/ppermute | solution.py:285
  8.6 15.2 %collective-permute-start = (bf16[8,4096]{1,0:T(8,128)(2,1)S(1)}, bf16[8,4096]{1,0:T(8,128)(2,1)S(1)}, u32[]{:S(2)}, u32[]{:S(2)}) collective-permute-start(bf16[8,4096]{1,0:T(8,128)(2,1)S(1)} %get-tuple-element.41.refs_0_), channel_id=1, source_target_pairs={{0,1},{1,0},{2,3},{3,2},{4,5},{5,4},{6,7},{7,6},{8,9},{9,8},{10,11... | collective-permute-start | bytes 196616 | tf_op jit(solution)/shard_map/ppermute | solution.py:285
  28.2 4.7 %collective-permute-start.3 = (bf16[8,4096]{1,0:T(8,128)(2,1)S(1)}, bf16[8,4096]{1,0:T(8,128)(2,1)S(1)}, u32[]{:S(2)}, u32[]{:S(2)}) collective-permute-start(bf16[8,4096]{1,0:T(8,128)(2,1)S(1)} %get-tuple-element.43), channel_id=1, source_target_pairs={{0,4},{4,0},{8,12},{12,8},{16,20},{20,16},{24,28},{28,24},{1,5},{5... | collective-permute-start | bytes 196616 | tf_op jit(solution)/shard_map/ppermute | solution.py:293
  34.4 5.8 %collective-permute-start.5 = (bf16[8,4096]{1,0:T(8,128)(2,1)S(1)}, bf16[8,4096]{1,0:T(8,128)(2,1)S(1)}, u32[]{:S(2)}, u32[]{:S(2)}) collective-permute-start(bf16[8,4096]{1,0:T(8,128)(2,1)S(1)} %get-tuple-element.47), channel_id=1, source_target_pairs={{0,1},{1,0},{2,3},{3,2},{4,5},{5,4},{6,7},{7,6},{8,9},{9,8},{10,11... | collective-permute-start | bytes 196616 | tf_op jit(solution)/shard_map/ppermute | solution.py:285
  34.7 9.7 %collective-permute-start.6 = (bf16[8,4096]{1,0:T(8,128)(2,1)S(1)}, bf16[8,4096]{1,0:T(8,128)(2,1)S(1)}, u32[]{:S(2)}, u32[]{:S(2)}) collective-permute-start(bf16[8,4096]{1,0:T(8,128)(2,1)S(1)} %get-tuple-element.48), channel_id=1, source_target_pairs={{0,2},{1,3},{2,0},{3,1},{4,6},{5,7},{6,4},{7,5},{8,10},{9,11},{10,... | collective-permute-start | bytes 196616 | tf_op jit(solution)/shard_map/ppermute | solution.py:285
  40.2 6.1 %collective-permute-start.7 = (bf16[8,4096]{1,0:T(8,128)(2,1)S(1)}, bf16[8,4096]{1,0:T(8,128)(2,1)S(1)}, u32[]{:S(2)}, u32[]{:S(2)}) collective-permute-start(bf16[8,4096]{1,0:T(8,128)(2,1)S(1)} %get-tuple-element.49), channel_id=1, source_target_pairs={{0,3},{1,2},{2,1},{3,0},{4,7},{5,6},{6,5},{7,4},{8,11},{9,10},{10,... | collective-permute-start | bytes 196616 | tf_op jit(solution)/shard_map/ppermute | solution.py:285
  46.4 4.3 %collective-permute-start.8 = (bf16[8,4096]{1,0:T(8,128)(2,1)S(1)}, bf16[8,4096]{1,0:T(8,128)(2,1)S(1)}, u32[]{:S(2)}, u32[]{:S(2)}) collective-permute-start(bf16[8,4096]{1,0:T(8,128)(2,1)S(1)} %get-tuple-element.51.refs_0_), channel_id=1, source_target_pairs={{0,1},{1,0},{2,3},{3,2},{4,5},{5,4},{6,7},{7,6},{8,9},{9,8},{10,11... | collective-permute-start | bytes 196616 | tf_op jit(solution)/shard_map/ppermute | solution.py:285
  47.9 6.7 %collective-permute-start.10 = (bf16[8,4096]{1,0:T(8,128)(2,1)S(1)}, bf16[8,4096]{1,0:T(8,128)(2,1)S(1)}, u32[]{:S(2)}, u32[]{:S(2)}) collective-permute-start(bf16[8,4096]{1,0:T(8,128)(2,1)S(1)} %get-tuple-element.51.refs_0_), channel_id=1, source_target_pairs={{0,3},{1,2},{2,1},{3,0},{4,7},{5,6},{6,5},{7,4},{8,11},{9,10},{10,... | collective-permute-start | bytes 196616 | tf_op jit(solution)/shard_map/ppermute | solution.py:285
  50.2 6.5 %collective-permute-start.9 = (bf16[8,4096]{1,0:T(8,128)(2,1)S(1)}, bf16[8,4096]{1,0:T(8,128)(2,1)S(1)}, u32[]{:S(2)}, u32[]{:S(2)}) collective-permute-start(bf16[8,4096]{1,0:T(8,128)(2,1)S(1)} %get-tuple-element.51.refs_0_), channel_id=1, source_target_pairs={{0,2},{1,3},{2,0},{3,1},{4,6},{5,7},{6,4},{7,5},{8,10},{9,11},{10,... | collective-permute-start | bytes 196616 | tf_op jit(solution)/shard_map/ppermute | solution.py:285
  57.8 4.4 %collective-permute-start.11 = (bf16[8,4096]{1,0:T(8,128)(2,1)S(1)}, bf16[8,4096]{1,0:T(8,128)(2,1)S(1)}, u32[]{:S(2)}, u32[]{:S(2)}) collective-permute-start(bf16[8,4096]{1,0:T(8,128)(2,1)S(1)} %get-tuple-element.53), channel_id=1, source_target_pairs={{0,4},{4,0},{8,12},{12,8},{16,20},{20,16},{24,28},{28,24},{1,5},{5... | collective-permute-start | bytes 196616 | tf_op jit(solution)/shard_map/ppermute | solution.py:293
  63.7 4.5 %collective-permute-start.13 = (bf16[8,4096]{1,0:T(8,128)(2,1)S(1)}, bf16[8,4096]{1,0:T(8,128)(2,1)S(1)}, u32[]{:S(2)}, u32[]{:S(2)}) collective-permute-start(bf16[8,4096]{1,0:T(8,128)(2,1)S(1)} %get-tuple-element.58), channel_id=1, source_target_pairs={{0,1},{1,0},{2,3},{3,2},{4,5},{5,4},{6,7},{7,6},{8,9},{9,8},{10,11... | collective-permute-start | bytes 196616 | tf_op jit(solution)/shard_map/ppermute | solution.py:285
  63.8 5.3 %collective-permute-start.14 = (bf16[8,4096]{1,0:T(8,128)(2,1)S(1)}, bf16[8,4096]{1,0:T(8,128)(2,1)S(1)}, u32[]{:S(2)}, u32[]{:S(2)}) collective-permute-start(bf16[8,4096]{1,0:T(8,128)(2,1)S(1)} %get-tuple-element.59), channel_id=1, source_target_pairs={{0,2},{1,3},{2,0},{3,1},{4,6},{5,7},{6,4},{7,5},{8,10},{9,11},{10,... | collective-permute-start | bytes 196616 | tf_op jit(solution)/shard_map/ppermute | solution.py:285
  66.9 6.1 %collective-permute-start.15 = (bf16[8,4096]{1,0:T(8,128)(2,1)S(1)}, bf16[8,4096]{1,0:T(8,128)(2,1)S(1)}, u32[]{:S(2)}, u32[]{:S(2)}) collective-permute-start(bf16[8,4096]{1,0:T(8,128)(2,1)S(1)} %get-tuple-element.60), channel_id=1, source_target_pairs={{0,3},{1,2},{2,1},{3,0},{4,7},{5,6},{6,5},{7,4},{8,11},{9,10},{10,... | collective-permute-start | bytes 196616 | tf_op jit(solution)/shard_map/ppermute | solution.py:285
  73.1 4.3 %collective-permute-start.16 = (bf16[8,4096]{1,0:T(8,128)(2,1)S(1)}, bf16[8,4096]{1,0:T(8,128)(2,1)S(1)}, u32[]{:S(2)}, u32[]{:S(2)}) collective-permute-start(bf16[8,4096]{1,0:T(8,128)(2,1)S(1)} %get-tuple-element.62.refs_0_), channel_id=1, source_target_pairs={{0,1},{1,0},{2,3},{3,2},{4,5},{5,4},{6,7},{7,6},{8,9},{9,8},{10,11... | collective-permute-start | bytes 196616 | tf_op jit(solution)/shard_map/ppermute | solution.py:285
  73.1 7.4 %collective-permute-start.18 = (bf16[8,4096]{1,0:T(8,128)(2,1)S(1)}, bf16[8,4096]{1,0:T(8,128)(2,1)S(1)}, u32[]{:S(2)}, u32[]{:S(2)}) collective-permute-start(bf16[8,4096]{1,0:T(8,128)(2,1)S(1)} %get-tuple-element.62.refs_0_), channel_id=1, source_target_pairs={{0,3},{1,2},{2,1},{3,0},{4,7},{5,6},{6,5},{7,4},{8,11},{9,10},{10,... | collective-permute-start | bytes 196616 | tf_op jit(solution)/shard_map/ppermute | solution.py:285
  75.2 8.1 %collective-permute-start.17 = (bf16[8,4096]{1,0:T(8,128)(2,1)S(1)}, bf16[8,4096]{1,0:T(8,128)(2,1)S(1)}, u32[]{:S(2)}, u32[]{:S(2)}) collective-permute-start(bf16[8,4096]{1,0:T(8,128)(2,1)S(1)} %get-tuple-element.62.refs_0_), channel_id=1, source_target_pairs={{0,2},{1,3},{2,0},{3,1},{4,6},{5,7},{6,4},{7,5},{8,10},{9,11},{10,... | collective-permute-start | bytes 196616 | tf_op jit(solution)/shard_map/ppermute | solution.py:285
  84.5 4.6 %collective-permute-start.19 = (bf16[8,4096]{1,0:T(8,128)(2,1)S(1)}, bf16[8,4096]{1,0:T(8,128)(2,1)S(1)}, u32[]{:S(2)}, u32[]{:S(2)}) collective-permute-start(bf16[8,4096]{1,0:T(8,128)(2,1)S(1)} %get-tuple-element.64), channel_id=1, source_target_pairs={{0,4},{4,0},{8,12},{12,8},{16,20},{20,16},{24,28},{28,24},{1,5},{5... | collective-permute-start | bytes 196616 | tf_op jit(solution)/shard_map/ppermute | solution.py:293
  90.8 28.7 %collective-permute-start.26 = (f32[8,4096]{1,0:T(8,128)S(1)}, f32[8,4096]{1,0:T(8,128)S(1)}, u32[]{:S(2)}, u32[]{:S(2)}) collective-permute-start(f32[8,4096]{1,0:T(8,128)S(1)} %get-tuple-element.69), channel_id=1, source_target_pairs={{0,1},{1,0},{2,3},{3,2},{4,5},{5,4},{6,7},{7,6},{8,9},{9,8},{10,11... | collective-permute-start | bytes 393224 | tf_op jit(solution)/shard_map/ppermute | solution.py:285
  90.8 28.7 %collective-permute-start.27 = (f32[8,4096]{1,0:T(8,128)S(1)}, f32[8,4096]{1,0:T(8,128)S(1)}, u32[]{:S(2)}, u32[]{:S(2)}) collective-permute-start(f32[8,4096]{1,0:T(8,128)S(1)} %get-tuple-element.70), channel_id=1, source_target_pairs={{0,2},{1,3},{2,0},{3,1},{4,6},{5,7},{6,4},{7,5},{8,10},{9,11},{10,... | collective-permute-start | bytes 393224 | tf_op jit(solution)/shard_map/ppermute | solution.py:285
  94.2 25.3 %collective-permute-start.28 = (f32[8,4096]{1,0:T(8,128)S(1)}, f32[8,4096]{1,0:T(8,128)S(1)}, u32[]{:S(2)}, u32[]{:S(2)}) collective-permute-start(f32[8,4096]{1,0:T(8,128)S(1)} %get-tuple-element.71), channel_id=1, source_target_pairs={{0,3},{1,2},{2,1},{3,0},{4,7},{5,6},{6,5},{7,4},{8,11},{9,10},{10,... | collective-permute-start | bytes 393224 | tf_op jit(solution)/shard_map/ppermute | solution.py:285
  99.0 5.5 %collective-permute-start.22 = (f32[8,128]{1,0:T(8,128)S(1)}, f32[8,128]{1,0:T(8,128)S(1)}, u32[]{:S(2)}, u32[]{:S(2)}) collective-permute-start(f32[8,128]{1,0:T(8,128)S(1)} %add.15), channel_id=1, source_target_pairs={{0,2},{1,3},{2,0},{3,1},{4,6},{5,7},{6,4},{7,5},{8,10},{9,11},{10,... | collective-permute-start | bytes 12296 | tf_op jit(solution)/shard_map/ppermute | solution.py:285
  107.7 6.7 %collective-permute-start.24 = (f32[8,128]{1,0:T(8,128)S(1)}, f32[8,128]{1,0:T(8,128)S(1)}, u32[]{:S(2)}, u32[]{:S(2)}) collective-permute-start(f32[8,128]{1,0:T(8,128)S(1)} %add.17), channel_id=1, source_target_pairs={{0,8},{4,12},{8,0},{12,4},{16,24},{20,28},{24,16},{28,20},{1,9},{5... | collective-permute-start | bytes 12296 | tf_op jit(solution)/shard_map/ppermute | solution.py:285
  114.4 5.0 %collective-permute-start.25 = (f32[8,128]{1,0:T(8,128)S(1)}, f32[8,128]{1,0:T(8,128)S(1)}, u32[]{:S(2)}, u32[]{:S(2)}) collective-permute-start(f32[8,128]{1,0:T(8,128)S(1)} %add.18), channel_id=1, source_target_pairs={{0,16},{4,20},{8,24},{12,28},{16,0},{20,4},{24,8},{28,12},{1,17},{... | collective-permute-start | bytes 12296 | tf_op jit(solution)/shard_map/ppermute | solution.py:285
  (11 other events, 49.2 us)

commit v3 on v2

--- a/solution.py
+++ b/solution.py
@@ -9,23 +9,19 @@
 
 ITERS = 3
 LANES = 128
-GROUP = 8
-CHUNKS = 8
+LONG_GROUP = 16
+SHORT_GROUP = 8
+TURN_GROUP = 4
 F32 = jnp.float32
 BF16 = jnp.bfloat16
 VMEM = pl.BlockSpec(memory_space=pltpu.VMEM)
 SMEM = pl.BlockSpec(memory_space=pltpu.SMEM)
-SLOTS = 128
-EARLY_ROWS, EARLY_COLS, AHEAD_COLS, LATE_ROWS, LATE_COLS, FROM_AHEAD = range(6)
-PARAMS = pltpu.CompilerParams(vmem_limit_bytes=16 * 1024 * 1024)
+EARLY, AHEAD, LATE, FROM_AHEAD = KINDS = range(4)
+PARAMS = pltpu.CompilerParams(vmem_limit_bytes=4 * 1024 * 1024)
 
 
 def times(field, block):
     return lax.dot_general(field, block, (((1,), (0,)), ((), ())), preferred_element_type=F32)
-
-
-def times_transposed(field, block):
-    return lax.dot_general(field, block, (((1,), (1,)), ((), ())), preferred_element_type=F32)
 
 
 def order_kernel(right_ref, order_ref, curve_ref, rounded_ref):
@@ -49,98 +45,102 @@
     return sub_index, blocks_dev, sub_index * blocks_dev, blocks_dev * sub_count
 
 
-def load_kernel(sub_count, blocks_dev, pairs_ref, blocks_in, diag_in, blocks_ref, diag_ref, lists_ref, sems):
-    slot_count = pairs_ref.shape[1]
-    size = slot_count // CHUNKS
-    copies = [
-        pltpu.make_async_copy(
-            blocks_in.at[pl.ds(part * size, size)], blocks_ref.at[pl.ds(part * size, size)], sems.at[part]
-        )
-        for part in range(CHUNKS)
-    ]
-    copies.append(pltpu.make_async_copy(diag_in, diag_ref, sems.at[CHUNKS]))
-    for copy in copies:
-        copy.start()
+def list_stride(slot_count):
+    return -(-(2 * slot_count + LONG_GROUP) // LANES) * LANES
+
+
+def lists_kernel(sub_count, blocks_dev, slot_count, pairs_ref, lists_ref, padded):
+    width = padded.shape[1]
+    stride = list_stride(slot_count)
     sub_index = lax.axis_index("sub")
     tile_blocks = blocks_dev * sub_count
-    own_first = sub_index * blocks_dev
     first_block = lax.axis_index("tile") * tile_blocks
+    padded[...] = jnp.full(padded.shape, -1.0, F32)
+    padded[0:2, 0:slot_count] = pairs_ref[...].astype(F32)
+    by_lane = padded[...]
+    by_row = jnp.transpose(by_lane)
+
+    def sides(row, col, axis):
+        live = jnp.concatenate([row, row], axis) >= 0.0
+        row = row.astype(jnp.int32) - first_block
+        col = col.astype(jnp.int32) - first_block
+        source = jnp.concatenate([row, col], axis)
+        target = jnp.concatenate([col, row], axis)
+        return live, source, target
+
+    live, source, target = sides(by_row[:, 0:1], by_row[:, 1:2], 0)
+    kind = jnp.where(target >= tile_blocks, AHEAD, LATE)
+    first_row = (sub_index // 2) * (2 * blocks_dev)
+    is_early = (source >= first_row) & (source < first_row + 2 * blocks_dev) & (source < tile_blocks)
+    kind = jnp.where(is_early, EARLY, kind)
+    kind = jnp.where(source >= tile_blocks, FROM_AHEAD, kind)
+    kind = jnp.where(live, kind, -1)
+    hot = (kind == lax.broadcasted_iota(jnp.int32, (2 * width, LANES), 1)).astype(F32)
+    below = lax.broadcasted_iota(jnp.int32, (2 * width, 2 * width), 0) > lax.broadcasted_iota(
+        jnp.int32, (2 * width, 2 * width), 1
+    )
+    ranks = times(below.astype(F32).astype(BF16), hot.astype(BF16))
+    rank = jnp.sum(ranks * hot, axis=1, keepdims=True).astype(jnp.int32)
+    counts = jnp.sum(hot, axis=0, keepdims=True)
+    at = jnp.where(live, kind * stride + rank, -1)
+    spread = at == lax.broadcasted_iota(jnp.int32, (2 * width, len(KINDS) * stride), 1)
+    live, source, target = sides(by_lane[0:1, :], by_lane[1:2, :], 1)
+    lane = lax.broadcasted_iota(jnp.int32, (1, 2 * width), 1)
+    block = jnp.where(lane < width, lane, lane - width + slot_count)
+    fields = jnp.concatenate(
+        [jnp.where(live, value, 0).astype(F32) for value in (block, source, target)]
+        + [jnp.zeros((5, 2 * width), F32)],
+        0,
+    )
+    found = times(fields.astype(BF16), spread.astype(F32).astype(BF16))
+    entries = found[0:1] + 256.0 * found[1:2] + 65536.0 * found[2:3]
+    entries = entries.astype(jnp.int32)
     idle = (tile_blocks + blocks_dev) * 65536
     idle_source = {
-        EARLY_ROWS: own_first,
-        EARLY_COLS: own_first,
-        AHEAD_COLS: tile_blocks - blocks_dev,
-        LATE_ROWS: 0,
-        LATE_COLS: 0,
+        EARLY: sub_index * blocks_dev,
+        AHEAD: tile_blocks - blocks_dev,
+        LATE: 0,
         FROM_AHEAD: tile_blocks,
     }
-    for index, source in idle_source.items():
-        entry = idle + 256 * source
-
-        def clear(at, carry, index=index, entry=entry):
-            lists_ref[index * SLOTS + at] = entry
-            return carry
-
-        lax.fori_loop(0, SLOTS, clear, 0, unroll=8)
-
-    def one_slot(slot, counts):
-        row, col = pairs_ref[0, slot], pairs_ref[1, slot]
-        live = row >= 0
-        row, col = row - first_block, col - first_block
-
-        def append(counts, source, target, kinds):
-            early = (source // blocks_dev) // 2 == sub_index // 2
-            entry = slot + 256 * source + 65536 * target
-            for index, chosen in kinds(early):
-                chosen = chosen & live
-                count = counts[index]
-
-                @pl.when(chosen)
-                def _():
-                    lists_ref[index * SLOTS + count] = entry
-
-                counts[index] = count + chosen.astype(jnp.int32)
-
-        counts = list(counts)
-        outside = col >= tile_blocks
-        append(
-            counts, col, row,
-            lambda early: (
-                (EARLY_ROWS, early & ~outside), (LATE_ROWS, ~early & ~outside), (FROM_AHEAD, outside)
-            ),
-        )
-        append(
-            counts, row, col,
-            lambda early: (
-                (EARLY_COLS, early), (LATE_COLS, ~early & ~outside), (AHEAD_COLS, ~early & outside)
-            ),
-        )
-        return tuple(counts)
-
-    counts = lax.fori_loop(0, slot_count, one_slot, (jnp.int32(0),) * 6)
-    for index, count in enumerate(counts):
-        lists_ref[6 * SLOTS + index] = count
-    for copy in copies:
-        copy.wait()
-
-
-def add_products(lists_ref, blocks_ref, field, total, row_list, col_list, source_from=0, target_from=0):
-    kinds = [(index, kind) for index, kind in ((row_list, times_transposed), (col_list, times)) if index is not None]
-    longest = functools.reduce(jnp.maximum, [lists_ref[6 * SLOTS + index] for index, _ in kinds])
+    place = lax.broadcasted_iota(jnp.int32, (1, stride), 1)
+    for index in KINDS:
+        span = slice(index * stride, (index + 1) * stride)
+        count = counts[:, index : index + 1].astype(jnp.int32)
+        lists_ref[:, span] = jnp.where(place < count, entries[:, span], idle + 256 * idle_source[index])
+    lists_ref[:, len(KINDS) * stride :] = counts.astype(jnp.int32)
+
+
+def turn_kernel(pairs_blocks_ref, blocks_ref, sem):
+    slot_count = pairs_blocks_ref.shape[0]
+    copy = pltpu.make_async_copy(pairs_blocks_ref, blocks_ref.at[pl.ds(0, slot_count)], sem)
+    copy.start()
+
+    def one_group(group, carry):
+        for step in range(TURN_GROUP):
+            slot = group * TURN_GROUP + step
+            blocks_ref[slot_count + slot] = jnp.transpose(pairs_blocks_ref[slot])
+        return carry
+
+    lax.fori_loop(0, slot_count // TURN_GROUP, one_group, 0)
+    copy.wait()
+
+
+def add_products(lists_ref, blocks_ref, field, total, index, size, source_from=0, target_from=0):
+    stride = list_stride(blocks_ref.shape[0] // 2)
+    count = lists_ref[0, len(KINDS) * stride + index]
 
     def one_group(group, carry):
         results = []
-        for step in range(GROUP):
-            for index, kind in kinds:
-                entry = lists_ref[index * SLOTS + group * GROUP + step]
-                slot, source, target = entry & 255, (entry >> 8) & 255, entry >> 16
-                value = kind(field[source - source_from].astype(BF16), blocks_ref[slot])
-                results.append((target - target_from, value))
+        for step in range(size):
+            entry = lists_ref[0, index * stride + group * size + step]
+            block, source, target = entry & 255, (entry >> 8) & 255, entry >> 16
+            value = times(field[source - source_from].astype(BF16), blocks_ref[block])
+            results.append((target - target_from, value))
         for at, value in results:
             total[at] += value
         return carry
 
-    lax.fori_loop(0, (longest + GROUP - 1) // GROUP, one_group, 0)
+    lax.fori_loop(0, (count + size - 1) // size, one_group, 0)
 
 
 def lay_out(row_ref, field, first, block_len):
@@ -161,7 +161,7 @@
         span = slice(block * block_len, (block + 1) * block_len)
         value = noise_ref[:, span] * own_ref[:, span]
         total[own_first + block] = value + times(field[own_first + block].astype(BF16), diag_ref[block])
-    add_products(lists_ref, blocks_ref, field, total, EARLY_ROWS, EARLY_COLS)
+    add_products(lists_ref, blocks_ref, field, total, EARLY, LONG_GROUP)
 
 
 def ahead_kernel(sub_count, lists_ref, blocks_ref, begun_ref, *refs):
@@ -174,7 +174,7 @@
     for block in range(blocks_dev):
         total[block] = begun_ref[tile_blocks + block]
     total[blocks_dev] = jnp.zeros(total.shape[1:], F32)
-    add_products(lists_ref, blocks_ref, field_ref, total, None, AHEAD_COLS, 0, tile_blocks)
+    add_products(lists_ref, blocks_ref, field_ref, total, AHEAD, SHORT_GROUP, 0, tile_blocks)
     is_odd = lax.axis_index("tile") % 2 == 1
     for block in range(blocks_dev):
         span = slice(block * block_len, (block + 1) * block_len)
@@ -186,7 +186,7 @@
 
 def late_kernel(lists_ref, blocks_ref, begun_ref, field_ref, total):
     total[...] = begun_ref[...]
-    add_products(lists_ref, blocks_ref, field_ref, total, LATE_ROWS, LATE_COLS)
+    add_products(lists_ref, blocks_ref, field_ref, total, LATE, LONG_GROUP)
 
 
 def part_kernel(sub_count, is_last, lists_ref, blocks_ref, begun_ref, field_ref, even_ref, odd_ref, moments_in_ref, *refs):
@@ -204,7 +204,7 @@
     for block in range(blocks_dev, tile_blocks):
         total[block] = begun_ref[block]
     total[begun_ref.shape[0] - 1] = jnp.zeros(total.shape[1:], F32)
-    add_products(lists_ref, blocks_ref, ahead, total, FROM_AHEAD, None, tile_blocks, 0)
+    add_products(lists_ref, blocks_ref, ahead, total, FROM_AHEAD, SHORT_GROUP, tile_blocks, 0)
     for step in range(sub_count):
         first = (sub_index ^ step) * blocks_dev
         for block in range(blocks_dev):
@@ -295,7 +295,7 @@
 
 def call(kernel, outs, ins, name, cost=0, **options):
     single = not isinstance(outs, tuple)
-    specs = [SMEM if getattr(value, "dtype", None) == jnp.int32 and value.ndim == 1 else VMEM for value in ins]
+    specs = [SMEM if value.dtype == jnp.int32 else VMEM for value in ins]
     options.setdefault("in_specs", specs)
     options.setdefault("out_specs", VMEM if single else (VMEM,) * len(outs))
     return pl.pallas_call(
@@ -323,22 +323,27 @@
     def scratch(blocks):
         return pltpu.VMEM((blocks, rhs_count, block_len), F32)
 
-    any_space = pl.BlockSpec(memory_space=pl.ANY)
-    blocks, diag, lists = call(
-        functools.partial(load_kernel, sub_count, blocks_dev),
-        (
-            pltpu.VMEM(pair_blocks.shape, BF16),
-            pltpu.VMEM(diag_blocks.shape, BF16),
-            jax.ShapeDtypeStruct((8 * SLOTS,), jnp.int32),
-        ),
-        (block_pairs.T, pair_blocks, diag_blocks),
-        "load",
+    slot_count = pair_blocks.shape[0]
+    width = -(-slot_count // LANES) * LANES
+    assert 2 * width <= 256 and extended < 256 and slot_count % TURN_GROUP == 0
+    lists = call(
+        functools.partial(lists_kernel, sub_count, blocks_dev, slot_count),
+        jax.ShapeDtypeStruct((1, len(KINDS) * list_stride(slot_count) + LANES), jnp.int32),
+        (block_pairs.T,),
+        "lists",
+        1,
+        in_specs=[VMEM],
+        scratch_shapes=[pltpu.VMEM((8, width), F32)],
+    )
+    blocks = call(
+        turn_kernel,
+        pltpu.VMEM((2 * slot_count, block_len, block_len), BF16),
+        (pair_blocks,),
+        "turn",
         4,
-        in_specs=[SMEM, any_space, any_space],
-        out_specs=(VMEM, VMEM, SMEM),
-        scratch_shapes=[pltpu.SemaphoreType.DMA((CHUNKS + 1,))],
-    )
-    field, rounded = call(order_kernel, (full, half), (right_side, point_order), "curve_order", 1, in_specs=[VMEM, VMEM])
+        scratch_shapes=[pltpu.SemaphoreType.DMA(())],
+    )
+    field, rounded = call(order_kernel, (full, half), (right_side, point_order), "curve_order", 10, in_specs=[VMEM, VMEM])
     basis = [field]
     moments = jnp.zeros(scalars.shape, F32)
     for index in range(ITERS):
@@ -347,7 +352,7 @@
         begun = call(
             functools.partial(early_kernel, sub_count),
             sums,
-            (lists, blocks, diag, noise, field, *rows[:2]),
+            (lists, blocks, diag_blocks, noise, field, *rows[:2]),
             "early",
             3,
             scratch_shapes=[scratch(extended)],
@@ -372,20 +377,28 @@
             1,
             scratch_shapes=[scratch(extended + 1), scratch(blocks_dev)],
         )
+        if is_last:
+            break
         arrived = [exchange(parts[step], "sub", step) for step in range(1, sub_count)]
-        if not is_last:
-            field, rounded, moments = call(
-                functools.partial(join_kernel, index),
-                (full, half, scalars),
-                (parts[0], field, moments, *arrived),
-                "join",
-            )
-            basis.append(field)
+        field, rounded, moments = call(
+            functools.partial(join_kernel, index),
+            (full, half, scalars),
+            (parts[0], field, moments, *arrived),
+            "join",
+        )
+        basis.append(field)
+    arrived = []
     for axis, count in (("sub", sub_count), ("tile", tile_count)):
         step = 1
         while step < count:
             moments = moments + exchange(moments, axis, step)
+            if len(arrived) < sub_count - 1:
+                far = sub_count - 1 - len(arrived)
+                arrived.append(exchange(parts[far], "sub", far))
+                moments, *parts = lax.optimization_barrier((moments, *parts))
             step *= 2
+    for far in range(sub_count - 1 - len(arrived), 0, -1):
+        arrived.append(exchange(parts[far], "sub", far))
     return call(
         functools.partial(finish_kernel, sub_count),
         (full, full),

time: 120 us -> 102 us (0.85); the launches traced: 120 us -> 101 us
  local copies, waits for them, and re-layouts: 8.46 us -> 1.99 us
  starting transfers between devices: 44.7 us -> 38.7 us
  waiting for transfers between devices: 28.8 us -> 25 us
  Pallas kernels: 37.6 us -> 34.4 us
    unnamed x12, local copies, waits for them, and re-layouts: 8.46 us -> 1.99 us
    ppermute x23, starting transfers between devices: 41.1 us -> 36.5 us  [exchange(): return lax.ppermute(block, axis, [(i, i ^ step) for i in range(count)])]
    ppermute x23, waiting for transfers between devices: 28.7 us -> 25 us  [exchange(): return lax.ppermute(block, axis, [(i, i ^ step) for i in range(count)])]
    pallas_call x17 -> x18, Pallas kernels: 37.6 us -> 34.4 us  [call(): pl.pallas_call(kernel, out_shape=outs, compiler_params=PARAMS, name=name,...]
    ppermute x6, starting transfers between devices: 3.6 us -> 2.21 us  [swap(): return lax.ppermute(block, axis, route)]
  transfers between devices with their start and end apart: 29 -> 29, of which waited for: 14 -> 13; matrix products, arithmetic and copies ran while one was open for 0% -> 0% of each run, Pallas kernels for 22% -> 23%
where the time goes in v3:
time: 102 us; the launch traced here: 101 us
  starting transfers between devices  38.7 us (38%)
  Pallas kernels  34.4 us (34%)
  waiting for transfers between devices  25 us (25%)
  local copies, waits for them, and re-layouts  1.99 us (2%)
    ppermute x23, starting transfers between devices, exchange(): return lax.ppermute(block, axis, [(i, i ^ step) for i in range(count)])  36.5 us
    pallas_call x18, Pallas kernels, call(): pl.pallas_call(kernel, out_shape=outs, compiler_params=PARAMS, name=name,...  34.4 us
    ppermute x23, waiting for transfers between devices, exchange(): return lax.ppermute(block, axis, [(i, i ^ step) for i in range(count)])  25 us
    ppermute x6, starting transfers between devices, swap(): return lax.ppermute(block, axis, route)  2.21 us
  transfers between devices with their start and end apart: 29, of which 13 were waited for; matrix products, arithmetic and copies ran while one was open for 0% of the time, Pallas kernels for 23%

profile of v3, /device:TPU:0, one launch (start us, length us, event | category | flops | bytes accessed | tf_op | source)
XLA Modules:
  0.0 101.1 jit_solution(914452134545892845)
XLA Ops:
  3.9 5.1 %collective-permute-start.2 = (bf16[8,4096]{1,0:T(8,128)(2,1)S(1)}, bf16[8,4096]{1,0:T(8,128)(2,1)S(1)}, u32[]{:S(2)}, u32[]{:S(2)}) collective-permute-start(bf16[8,4096]{1,0:T(8,128)(2,1)S(1)} %get-tuple-element.44.refs_0_), channel_id=1, source_target_pairs={{0,3},{1,2},{2,1},{3,0},{4,7},{5,6},{6,5},{7,4},{8,11},{9,10},{10,... | collective-permute-start | bytes 196616 | tf_op jit(solution)/shard_map/ppermute | solution.py:285
  9.7 5.4 %turn.1.blocks_ref = bf16[192,256,256]{2,1,0:T(8,128)(2,1)S(1)} custom-call(bf16[96,256,256]{2,1,0:T(8,128)(2,1)S(1)} %copy-done.1), custom_call_target="tpu_custom_call" | custom-call | flops 4000000000 | tf_op jit(solution)/shard_map/turn/pallas_call | solution.py:301
  16.0 3.0 %early.3.begun_ref = f32[81,8,256]{2,1,0:T(8,128)S(1)} custom-call(s32[1,1152]{1,0:T(1,128)S(1)} %lists.1.lists_ref, bf16[192,256,256]{2,1,0:T(8,128)(2,1)S(1)} %turn.1.blocks_ref, bf16[16,256,256]{2,1,0:T(8,128)(2,1)S(1)} %copy-done, f32[1,4096]{1,0:T(1,128)S(1)} %bitcast.2, f32[8,4096]{1,0:T(8,128)S(1)} %get-tuple-element.43.own_ref.old_ref.refs_4_, ...), custom_call_target="tpu_custom_call" | custom-call | flops 3000000000 | tf_op jit(solution)/shard_map/early/pallas_call | solution.py:301
  21.2 2.6 %late.3.begun_ref = f32[81,8,256]{2,1,0:T(8,128)S(1)} custom-call(s32[1,1152]{1,0:T(1,128)S(1)} %lists.1.lists_ref, bf16[192,256,256]{2,1,0:T(8,128)(2,1)S(1)} %turn.1.blocks_ref, f32[81,8,256]{2,1,0:T(8,128)S(1)} %early.3.begun_ref, f32[64,8,256]{2,1,0:T(8,128)S(1)} %get-tuple-element.45.field_ref), custom_call_target="tpu_custom_call" | custom-call | flops 3000000000 | tf_op jit(solution)/shard_map/late/pallas_call | solution.py:301
  26.5 3.3 %collective-permute-start.7 = (bf16[8,4096]{1,0:T(8,128)(2,1)S(1)}, bf16[8,4096]{1,0:T(8,128)(2,1)S(1)}, u32[]{:S(2)}, u32[]{:S(2)}) collective-permute-start(bf16[8,4096]{1,0:T(8,128)(2,1)S(1)} %get-tuple-element.52), channel_id=1, source_target_pairs={{0,3},{1,2},{2,1},{3,0},{4,7},{5,6},{6,5},{7,4},{8,11},{9,10},{10,... | collective-permute-start | bytes 196616 | tf_op jit(solution)/shard_map/ppermute | solution.py:285
  30.6 3.0 %collective-permute-done.7.refs_2_ = bf16[8,4096]{1,0:T(8,128)(2,1)S(1)} collective-permute-done((bf16[8,4096]{1,0:T(8,128)(2,1)S(1)}, bf16[8,4096]{1,0:T(8,128)(2,1)S(1)}, u32[]{:S(2)}, u32[]{:S(2)}) %collective-permute-start.7) | collective-permute-done | bytes 65568 | tf_op jit(solution)/shard_map/ppermute | solution.py:285
  33.8 2.6 %collective-permute-start.10 = (bf16[8,4096]{1,0:T(8,128)(2,1)S(1)}, bf16[8,4096]{1,0:T(8,128)(2,1)S(1)}, u32[]{:S(2)}, u32[]{:S(2)}) collective-permute-start(bf16[8,4096]{1,0:T(8,128)(2,1)S(1)} %get-tuple-element.54.refs_0_), channel_id=1, source_target_pairs={{0,3},{1,2},{2,1},{3,0},{4,7},{5,6},{6,5},{7,4},{8,11},{9,10},{10,... | collective-permute-start | bytes 196616 | tf_op jit(solution)/shard_map/ppermute | solution.py:285
  38.5 3.0 %early.4.begun_ref = f32[81,8,256]{2,1,0:T(8,128)S(1)} custom-call(s32[1,1152]{1,0:T(1,128)S(1)} %lists.1.lists_ref, bf16[192,256,256]{2,1,0:T(8,128)(2,1)S(1)} %turn.1.blocks_ref, bf16[16,256,256]{2,1,0:T(8,128)(2,1)S(1)} %copy-done, f32[1,4096]{1,0:T(1,128)S(1)} %bitcast.3, f32[8,4096]{1,0:T(8,128)S(1)} %get-tuple-element.53.own_ref.old_ref.refs_5_, ...), custom_call_target="tpu_custom_call" | custom-call | flops 3000000000 | tf_op jit(solution)/shard_map/early/pallas_call | solution.py:301
  41.5 2.9 %collective-permute-done.9.refs_2_ = bf16[8,4096]{1,0:T(8,128)(2,1)S(1)} collective-permute-done((bf16[8,4096]{1,0:T(8,128)(2,1)S(1)}, bf16[8,4096]{1,0:T(8,128)(2,1)S(1)}, u32[]{:S(2)}, u32[]{:S(2)}) %collective-permute-start.9) | collective-permute-done | bytes 65568 | tf_op jit(solution)/shard_map/ppermute | solution.py:285
  46.6 2.6 %late.4.begun_ref = f32[81,8,256]{2,1,0:T(8,128)S(1)} custom-call(s32[1,1152]{1,0:T(1,128)S(1)} %lists.1.lists_ref, bf16[192,256,256]{2,1,0:T(8,128)(2,1)S(1)} %turn.1.blocks_ref, f32[81,8,256]{2,1,0:T(8,128)S(1)} %early.4.begun_ref, f32[64,8,256]{2,1,0:T(8,128)S(1)} %get-tuple-element.55.field_ref), custom_call_target="tpu_custom_call" | custom-call | flops 3000000000 | tf_op jit(solution)/shard_map/late/pallas_call | solution.py:301
  51.1 4.0 %collective-permute-start.15 = (bf16[8,4096]{1,0:T(8,128)(2,1)S(1)}, bf16[8,4096]{1,0:T(8,128)(2,1)S(1)}, u32[]{:S(2)}, u32[]{:S(2)}) collective-permute-start(bf16[8,4096]{1,0:T(8,128)(2,1)S(1)} %get-tuple-element.63), channel_id=1, source_target_pairs={{0,3},{1,2},{2,1},{3,0},{4,7},{5,6},{6,5},{7,4},{8,11},{9,10},{10,... | collective-permute-start | bytes 196616 | tf_op jit(solution)/shard_map/ppermute | solution.py:285
  56.0 2.5 %collective-permute-done.15.refs_2_ = bf16[8,4096]{1,0:T(8,128)(2,1)S(1)} collective-permute-done((bf16[8,4096]{1,0:T(8,128)(2,1)S(1)}, bf16[8,4096]{1,0:T(8,128)(2,1)S(1)}, u32[]{:S(2)}, u32[]{:S(2)}) %collective-permute-start.15) | collective-permute-done | bytes 65568 | tf_op jit(solution)/shard_map/ppermute | solution.py:285
  58.6 3.2 %collective-permute-start.18 = (bf16[8,4096]{1,0:T(8,128)(2,1)S(1)}, bf16[8,4096]{1,0:T(8,128)(2,1)S(1)}, u32[]{:S(2)}, u32[]{:S(2)}) collective-permute-start(bf16[8,4096]{1,0:T(8,128)(2,1)S(1)} %get-tuple-element.65.refs_0_), channel_id=1, source_target_pairs={{0,3},{1,2},{2,1},{3,0},{4,7},{5,6},{6,5},{7,4},{8,11},{9,10},{10,... | collective-permute-start | bytes 196616 | tf_op jit(solution)/shard_map/ppermute | solution.py:285
  62.8 3.0 %early.5.begun_ref = f32[81,8,256]{2,1,0:T(8,128)S(1)} custom-call(s32[1,1152]{1,0:T(1,128)S(1)} %lists.1.lists_ref, bf16[192,256,256]{2,1,0:T(8,128)(2,1)S(1)} %turn.1.blocks_ref, bf16[16,256,256]{2,1,0:T(8,128)(2,1)S(1)} %copy-done, f32[1,4096]{1,0:T(1,128)S(1)} %bitcast.4, f32[8,4096]{1,0:T(8,128)S(1)} %get-tuple-element.64.own_ref.refs_6_, ...), custom_call_target="tpu_custom_call" | custom-call | flops 3000000000 | tf_op jit(solution)/shard_map/early/pallas_call | solution.py:301
  65.8 3.9 %collective-permute-done.17.refs_2_ = bf16[8,4096]{1,0:T(8,128)(2,1)S(1)} collective-permute-done((bf16[8,4096]{1,0:T(8,128)(2,1)S(1)}, bf16[8,4096]{1,0:T(8,128)(2,1)S(1)}, u32[]{:S(2)}, u32[]{:S(2)}) %collective-permute-start.17) | collective-permute-done | bytes 65568 | tf_op jit(solution)/shard_map/ppermute | solution.py:285
  72.0 2.6 %late.5.begun_ref = f32[81,8,256]{2,1,0:T(8,128)S(1)} custom-call(s32[1,1152]{1,0:T(1,128)S(1)} %lists.1.lists_ref, bf16[192,256,256]{2,1,0:T(8,128)(2,1)S(1)} %turn.1.blocks_ref, f32[81,8,256]{2,1,0:T(8,128)S(1)} %early.5.begun_ref, f32[64,8,256]{2,1,0:T(8,128)S(1)} %get-tuple-element.66.field_ref), custom_call_target="tpu_custom_call" | custom-call | flops 3000000000 | tf_op jit(solution)/shard_map/late/pallas_call | solution.py:301
  74.6 1.6 %parts.5 = (f32[8,4096]{1,0:T(8,128)S(1)}, f32[8,4096]{1,0:T(8,128)S(1)}, f32[8,4096]{1,0:T(8,128)S(1)}, f32[8,4096]{1,0:T(8,128)S(1)}, f32[8,128]{1,0:T(8,128)S(1)}) custom-call(s32[1,1152]{1,0:T(1,128)S(1)} %lists.1.lists_ref, bf16[192,256,256]{2,1,0:T(8,128)(2,1)S(1)} %turn.1.blocks_ref, f32[81,8,256]{2,1,0:T(8,128)S(1)} %late.5.begun_ref, ...), custom_call_target="tpu_custom_call" | custom-call | flops 1000000000 | tf_op jit(solution)/shard_map/parts/pallas_call | solution.py:301
  76.3 3.6 %collective-permute-done.21 = f32[8,128]{1,0:T(8,128)S(1)} collective-permute-done((f32[8,128]{1,0:T(8,128)S(1)}, f32[8,128]{1,0:T(8,128)S(1)}, u32[]{:S(2)}, u32[]{:S(2)}) %collective-permute-start.21) | collective-permute-done | bytes 4128 | tf_op jit(solution)/shard_map/ppermute | solution.py:285
  79.9 2.4 %collective-permute-start.26 = (f32[8,4096]{1,0:T(8,128)S(1)}, f32[8,4096]{1,0:T(8,128)S(1)}, u32[]{:S(2)}, u32[]{:S(2)}) collective-permute-start(f32[8,4096]{1,0:T(8,128)S(1)} %get-tuple-element.74), channel_id=1, source_target_pairs={{0,3},{1,2},{2,1},{3,0},{4,7},{5,6},{6,5},{7,4},{8,11},{9,10},{10,... | collective-permute-start | bytes 393224 | tf_op jit(solution)/shard_map/ppermute | solution.py:285
  84.4 5.8 %collective-permute-start.23 = (f32[8,128]{1,0:T(8,128)S(1)}, f32[8,128]{1,0:T(8,128)S(1)}, u32[]{:S(2)}, u32[]{:S(2)}) collective-permute-start(f32[8,128]{1,0:T(8,128)S(1)} %add.16), channel_id=1, source_target_pairs={{0,4},{4,0},{8,12},{12,8},{16,20},{20,16},{24,28},{28,24},{1,5},{5... | collective-permute-start | bytes 12296 | tf_op jit(solution)/shard_map/ppermute | solution.py:285
  91.0 3.2 %collective-permute-start.24 = (f32[8,128]{1,0:T(8,128)S(1)}, f32[8,128]{1,0:T(8,128)S(1)}, u32[]{:S(2)}, u32[]{:S(2)}) collective-permute-start(f32[8,128]{1,0:T(8,128)S(1)} %add.17), channel_id=1, source_target_pairs={{0,8},{4,12},{8,0},{12,4},{16,24},{20,28},{24,16},{28,20},{1,9},{5... | collective-permute-start | bytes 12296 | tf_op jit(solution)/shard_map/ppermute | solution.py:285
  94.2 1.6 %collective-permute-done.24 = f32[8,128]{1,0:T(8,128)S(1)} collective-permute-done((f32[8,128]{1,0:T(8,128)S(1)}, f32[8,128]{1,0:T(8,128)S(1)}, u32[]{:S(2)}, u32[]{:S(2)}) %collective-permute-start.24) | collective-permute-done | bytes 4128 | tf_op jit(solution)/shard_map/ppermute | solution.py:285
  95.8 2.7 %collective-permute-start.25 = (f32[8,128]{1,0:T(8,128)S(1)}, f32[8,128]{1,0:T(8,128)S(1)}, u32[]{:S(2)}, u32[]{:S(2)}) collective-permute-start(f32[8,128]{1,0:T(8,128)S(1)} %add.18), channel_id=1, source_target_pairs={{0,16},{4,20},{8,24},{12,28},{16,0},{20,4},{24,8},{28,12},{1,17},{... | collective-permute-start | bytes 12296 | tf_op jit(solution)/shard_map/ppermute | solution.py:285
  98.5 1.6 %collective-permute-done.25 = f32[8,128]{1,0:T(8,128)S(1)} collective-permute-done((f32[8,128]{1,0:T(8,128)S(1)}, f32[8,128]{1,0:T(8,128)S(1)}, u32[]{:S(2)}, u32[]{:S(2)}) %collective-permute-start.25) | collective-permute-done | bytes 4128 | tf_op jit(solution)/shard_map/ppermute | solution.py:285
  (70 shorter events, 24.9 us)
Async XLA Ops:
  3.9 15.1 %collective-permute-start.2 = (bf16[8,4096]{1,0:T(8,128)(2,1)S(1)}, bf16[8,4096]{1,0:T(8,128)(2,1)S(1)}, u32[]{:S(2)}, u32[]{:S(2)}) collective-permute-start(bf16[8,4096]{1,0:T(8,128)(2,1)S(1)} %get-tuple-element.44.refs_0_), channel_id=1, source_target_pairs={{0,3},{1,2},{2,1},{3,0},{4,7},{5,6},{6,5},{7,4},{8,11},{9,10},{10,... | collective-permute-start | bytes 196616 | tf_op jit(solution)/shard_map/ppermute | solution.py:285
  9.0 9.9 %collective-permute-start.1 = (bf16[8,4096]{1,0:T(8,128)(2,1)S(1)}, bf16[8,4096]{1,0:T(8,128)(2,1)S(1)}, u32[]{:S(2)}, u32[]{:S(2)}) collective-permute-start(bf16[8,4096]{1,0:T(8,128)(2,1)S(1)} %get-tuple-element.44.refs_0_), channel_id=1, source_target_pairs={{0,2},{1,3},{2,0},{3,1},{4,6},{5,7},{6,4},{7,5},{8,10},{9,11},{10,... | collective-permute-start | bytes 196616 | tf_op jit(solution)/shard_map/ppermute | solution.py:285
  9.0 6.9 %collective-permute-start = (bf16[8,4096]{1,0:T(8,128)(2,1)S(1)}, bf16[8,4096]{1,0:T(8,128)(2,1)S(1)}, u32[]{:S(2)}, u32[]{:S(2)}) collective-permute-start(bf16[8,4096]{1,0:T(8,128)(2,1)S(1)} %get-tuple-element.44.refs_0_), channel_id=1, source_target_pairs={{0,1},{1,0},{2,3},{3,2},{4,5},{5,4},{6,7},{7,6},{8,9},{9,8},{10,11... | collective-permute-start | bytes 196616 | tf_op jit(solution)/shard_map/ppermute | solution.py:285
  25.3 4.5 %collective-permute-start.5 = (bf16[8,4096]{1,0:T(8,128)(2,1)S(1)}, bf16[8,4096]{1,0:T(8,128)(2,1)S(1)}, u32[]{:S(2)}, u32[]{:S(2)}) collective-permute-start(bf16[8,4096]{1,0:T(8,128)(2,1)S(1)} %get-tuple-element.50), channel_id=1, source_target_pairs={{0,1},{1,0},{2,3},{3,2},{4,5},{5,4},{6,7},{7,6},{8,9},{9,8},{10,11... | collective-permute-start | bytes 196616 | tf_op jit(solution)/shard_map/ppermute | solution.py:285
  25.5 5.2 %collective-permute-start.6 = (bf16[8,4096]{1,0:T(8,128)(2,1)S(1)}, bf16[8,4096]{1,0:T(8,128)(2,1)S(1)}, u32[]{:S(2)}, u32[]{:S(2)}) collective-permute-start(bf16[8,4096]{1,0:T(8,128)(2,1)S(1)} %get-tuple-element.51), channel_id=1, source_target_pairs={{0,2},{1,3},{2,0},{3,1},{4,6},{5,7},{6,4},{7,5},{8,10},{9,11},{10,... | collective-permute-start | bytes 196616 | tf_op jit(solution)/shard_map/ppermute | solution.py:285
  26.5 7.2 %collective-permute-start.7 = (bf16[8,4096]{1,0:T(8,128)(2,1)S(1)}, bf16[8,4096]{1,0:T(8,128)(2,1)S(1)}, u32[]{:S(2)}, u32[]{:S(2)}) collective-permute-start(bf16[8,4096]{1,0:T(8,128)(2,1)S(1)} %get-tuple-element.52), channel_id=1, source_target_pairs={{0,3},{1,2},{2,1},{3,0},{4,7},{5,6},{6,5},{7,4},{8,11},{9,10},{10,... | collective-permute-start | bytes 196616 | tf_op jit(solution)/shard_map/ppermute | solution.py:285
  33.8 4.7 %collective-permute-start.8 = (bf16[8,4096]{1,0:T(8,128)(2,1)S(1)}, bf16[8,4096]{1,0:T(8,128)(2,1)S(1)}, u32[]{:S(2)}, u32[]{:S(2)}) collective-permute-start(bf16[8,4096]{1,0:T(8,128)(2,1)S(1)} %get-tuple-element.54.refs_0_), channel_id=1, source_target_pairs={{0,1},{1,0},{2,3},{3,2},{4,5},{5,4},{6,7},{7,6},{8,9},{9,8},{10,11... | collective-permute-start | bytes 196616 | tf_op jit(solution)/shard_map/ppermute | solution.py:285
  33.8 7.6 %collective-permute-start.10 = (bf16[8,4096]{1,0:T(8,128)(2,1)S(1)}, bf16[8,4096]{1,0:T(8,128)(2,1)S(1)}, u32[]{:S(2)}, u32[]{:S(2)}) collective-permute-start(bf16[8,4096]{1,0:T(8,128)(2,1)S(1)} %get-tuple-element.54.refs_0_), channel_id=1, source_target_pairs={{0,3},{1,2},{2,1},{3,0},{4,7},{5,6},{6,5},{7,4},{8,11},{9,10},{10,... | collective-permute-start | bytes 196616 | tf_op jit(solution)/shard_map/ppermute | solution.py:285
  36.5 7.9 %collective-permute-start.9 = (bf16[8,4096]{1,0:T(8,128)(2,1)S(1)}, bf16[8,4096]{1,0:T(8,128)(2,1)S(1)}, u32[]{:S(2)}, u32[]{:S(2)}) collective-permute-start(bf16[8,4096]{1,0:T(8,128)(2,1)S(1)} %get-tuple-element.54.refs_0_), channel_id=1, source_target_pairs={{0,2},{1,3},{2,0},{3,1},{4,6},{5,7},{6,4},{7,5},{8,10},{9,11},{10,... | collective-permute-start | bytes 196616 | tf_op jit(solution)/shard_map/ppermute | solution.py:285
  45.8 3.4 %collective-permute-start.11 = (bf16[8,4096]{1,0:T(8,128)(2,1)S(1)}, bf16[8,4096]{1,0:T(8,128)(2,1)S(1)}, u32[]{:S(2)}, u32[]{:S(2)}) collective-permute-start(bf16[8,4096]{1,0:T(8,128)(2,1)S(1)} %get-tuple-element.56), channel_id=1, source_target_pairs={{0,4},{4,0},{8,12},{12,8},{16,20},{20,16},{24,28},{28,24},{1,5},{5... | collective-permute-start | bytes 196616 | tf_op jit(solution)/shard_map/ppermute | solution.py:293
  50.7 4.5 %collective-permute-start.13 = (bf16[8,4096]{1,0:T(8,128)(2,1)S(1)}, bf16[8,4096]{1,0:T(8,128)(2,1)S(1)}, u32[]{:S(2)}, u32[]{:S(2)}) collective-permute-start(bf16[8,4096]{1,0:T(8,128)(2,1)S(1)} %get-tuple-element.61), channel_id=1, source_target_pairs={{0,1},{1,0},{2,3},{3,2},{4,5},{5,4},{6,7},{7,6},{8,9},{9,8},{10,11... | collective-permute-start | bytes 196616 | tf_op jit(solution)/shard_map/ppermute | solution.py:285
  50.8 5.2 %collective-permute-start.14 = (bf16[8,4096]{1,0:T(8,128)(2,1)S(1)}, bf16[8,4096]{1,0:T(8,128)(2,1)S(1)}, u32[]{:S(2)}, u32[]{:S(2)}) collective-permute-start(bf16[8,4096]{1,0:T(8,128)(2,1)S(1)} %get-tuple-element.62), channel_id=1, source_target_pairs={{0,2},{1,3},{2,0},{3,1},{4,6},{5,7},{6,4},{7,5},{8,10},{9,11},{10,... | collective-permute-start | bytes 196616 | tf_op jit(solution)/shard_map/ppermute | solution.py:285
  51.1 7.4 %collective-permute-start.15 = (bf16[8,4096]{1,0:T(8,128)(2,1)S(1)}, bf16[8,4096]{1,0:T(8,128)(2,1)S(1)}, u32[]{:S(2)}, u32[]{:S(2)}) collective-permute-start(bf16[8,4096]{1,0:T(8,128)(2,1)S(1)} %get-tuple-element.63), channel_id=1, source_target_pairs={{0,3},{1,2},{2,1},{3,0},{4,7},{5,6},{6,5},{7,4},{8,11},{9,10},{10,... | collective-permute-start | bytes 196616 | tf_op jit(solution)/shard_map/ppermute | solution.py:285
  58.6 4.3 %collective-permute-start.16 = (bf16[8,4096]{1,0:T(8,128)(2,1)S(1)}, bf16[8,4096]{1,0:T(8,128)(2,1)S(1)}, u32[]{:S(2)}, u32[]{:S(2)}) collective-permute-start(bf16[8,4096]{1,0:T(8,128)(2,1)S(1)} %get-tuple-element.65.refs_0_), channel_id=1, source_target_pairs={{0,1},{1,0},{2,3},{3,2},{4,5},{5,4},{6,7},{7,6},{8,9},{9,8},{10,11... | collective-permute-start | bytes 196616 | tf_op jit(solution)/shard_map/ppermute | solution.py:285
  58.6 7.2 %collective-permute-start.18 = (bf16[8,4096]{1,0:T(8,128)(2,1)S(1)}, bf16[8,4096]{1,0:T(8,128)(2,1)S(1)}, u32[]{:S(2)}, u32[]{:S(2)}) collective-permute-start(bf16[8,4096]{1,0:T(8,128)(2,1)S(1)} %get-tuple-element.65.refs_0_), channel_id=1, source_target_pairs={{0,3},{1,2},{2,1},{3,0},{4,7},{5,6},{6,5},{7,4},{8,11},{9,10},{10,... | collective-permute-start | bytes 196616 | tf_op jit(solution)/shard_map/ppermute | solution.py:285
  61.8 8.0 %collective-permute-start.17 = (bf16[8,4096]{1,0:T(8,128)(2,1)S(1)}, bf16[8,4096]{1,0:T(8,128)(2,1)S(1)}, u32[]{:S(2)}, u32[]{:S(2)}) collective-permute-start(bf16[8,4096]{1,0:T(8,128)(2,1)S(1)} %get-tuple-element.65.refs_0_), channel_id=1, source_target_pairs={{0,2},{1,3},{2,0},{3,1},{4,6},{5,7},{6,4},{7,5},{8,10},{9,11},{10,... | collective-permute-start | bytes 196616 | tf_op jit(solution)/shard_map/ppermute | solution.py:285
  76.2 3.6 %collective-permute-start.21 = (f32[8,128]{1,0:T(8,128)S(1)}, f32[8,128]{1,0:T(8,128)S(1)}, u32[]{:S(2)}, u32[]{:S(2)}) collective-permute-start(f32[8,128]{1,0:T(8,128)S(1)} %get-tuple-element.70), channel_id=1, source_target_pairs={{0,1},{1,0},{2,3},{3,2},{4,5},{5,4},{6,7},{7,6},{8,9},{9,8},{10,11... | collective-permute-start | bytes 12296 | tf_op jit(solution)/shard_map/ppermute | solution.py:285
  79.9 4.5 %collective-permute-start.22 = (f32[8,128]{1,0:T(8,128)S(1)}, f32[8,128]{1,0:T(8,128)S(1)}, u32[]{:S(2)}, u32[]{:S(2)}) collective-permute-start(f32[8,128]{1,0:T(8,128)S(1)} %add.15), channel_id=1, source_target_pairs={{0,2},{1,3},{2,0},{3,1},{4,6},{5,7},{6,4},{7,5},{8,10},{9,11},{10,... | collective-permute-start | bytes 12296 | tf_op jit(solution)/shard_map/ppermute | solution.py:285
  79.9 20.3 %collective-permute-start.26 = (f32[8,4096]{1,0:T(8,128)S(1)}, f32[8,4096]{1,0:T(8,128)S(1)}, u32[]{:S(2)}, u32[]{:S(2)}) collective-permute-start(f32[8,4096]{1,0:T(8,128)S(1)} %get-tuple-element.74), channel_id=1, source_target_pairs={{0,3},{1,2},{2,1},{3,0},{4,7},{5,6},{6,5},{7,4},{8,11},{9,10},{10,... | collective-permute-start | bytes 393224 | tf_op jit(solution)/shard_map/ppermute | solution.py:285
  82.2 17.9 %collective-permute-start.27 = (f32[8,4096]{1,0:T(8,128)S(1)}, f32[8,4096]{1,0:T(8,128)S(1)}, u32[]{:S(2)}, u32[]{:S(2)}) collective-permute-start(f32[8,4096]{1,0:T(8,128)S(1)} %get-tuple-element.78), channel_id=1, source_target_pairs={{0,2},{1,3},{2,0},{3,1},{4,6},{5,7},{6,4},{7,5},{8,10},{9,11},{10,... | collective-permute-start | bytes 393224 | tf_op jit(solution)/shard_map/ppermute | solution.py:285
  84.4 15.8 %collective-permute-start.28 = (f32[8,4096]{1,0:T(8,128)S(1)}, f32[8,4096]{1,0:T(8,128)S(1)}, u32[]{:S(2)}, u32[]{:S(2)}) collective-permute-start(f32[8,4096]{1,0:T(8,128)S(1)} %get-tuple-element.81), channel_id=1, source_target_pairs={{0,1},{1,0},{2,3},{3,2},{4,5},{5,4},{6,7},{7,6},{8,9},{9,8},{10,11... | collective-permute-start | bytes 393224 | tf_op jit(solution)/shard_map/ppermute | solution.py:285
  84.4 6.6 %collective-permute-start.23 = (f32[8,128]{1,0:T(8,128)S(1)}, f32[8,128]{1,0:T(8,128)S(1)}, u32[]{:S(2)}, u32[]{:S(2)}) collective-permute-start(f32[8,128]{1,0:T(8,128)S(1)} %add.16), channel_id=1, source_target_pairs={{0,4},{4,0},{8,12},{12,8},{16,20},{20,16},{24,28},{28,24},{1,5},{5... | collective-permute-start | bytes 12296 | tf_op jit(solution)/shard_map/ppermute | solution.py:285
  91.0 4.8 %collective-permute-start.24 = (f32[8,128]{1,0:T(8,128)S(1)}, f32[8,128]{1,0:T(8,128)S(1)}, u32[]{:S(2)}, u32[]{:S(2)}) collective-permute-start(f32[8,128]{1,0:T(8,128)S(1)} %add.17), channel_id=1, source_target_pairs={{0,8},{4,12},{8,0},{12,4},{16,24},{20,28},{24,16},{28,20},{1,9},{5... | collective-permute-start | bytes 12296 | tf_op jit(solution)/shard_map/ppermute | solution.py:285
  95.8 4.3 %collective-permute-start.25 = (f32[8,128]{1,0:T(8,128)S(1)}, f32[8,128]{1,0:T(8,128)S(1)}, u32[]{:S(2)}, u32[]{:S(2)}) collective-permute-start(f32[8,128]{1,0:T(8,128)S(1)} %add.18), channel_id=1, source_target_pairs={{0,16},{4,20},{8,24},{12,28},{16,0},{20,4},{24,8},{28,12},{1,17},{... | collective-permute-start | bytes 12296 | tf_op jit(solution)/shard_map/ppermute | solution.py:285
  (11 other events, 63.0 us)

commit v4 on v3

--- a/solution.py
+++ b/solution.py
@@ -22,6 +22,10 @@
 
 def times(field, block):
     return lax.dot_general(field, block, (((1,), (0,)), ((), ())), preferred_element_type=F32)
+
+
+def times_transposed(field, block):
+    return lax.dot_general(field, block, (((1,), (1,)), ((), ())), preferred_element_type=F32)
 
 
 def order_kernel(right_ref, order_ref, curve_ref, rounded_ref):
@@ -49,7 +53,7 @@
     return -(-(2 * slot_count + LONG_GROUP) // LANES) * LANES
 
 
-def lists_kernel(sub_count, blocks_dev, slot_count, pairs_ref, lists_ref, padded):
+def lists_kernel(sub_count, blocks_dev, slot_count, pairs_ref, out_ref, padded, lists_ref, sem):
     width = padded.shape[1]
     stride = list_stride(slot_count)
     sub_index = lax.axis_index("sub")
@@ -107,10 +111,16 @@
         span = slice(index * stride, (index + 1) * stride)
         count = counts[:, index : index + 1].astype(jnp.int32)
         lists_ref[:, span] = jnp.where(place < count, entries[:, span], idle + 256 * idle_source[index])
-    lists_ref[:, len(KINDS) * stride :] = counts.astype(jnp.int32)
-
-
-def turn_kernel(pairs_blocks_ref, blocks_ref, sem):
+    lists_ref[:, len(KINDS) * stride : len(KINDS) * stride + LANES] = counts.astype(jnp.int32)
+    by_column = jnp.sum(hot[:width], axis=0, keepdims=True)
+    lists_ref[:, len(KINDS) * stride + LANES :] = by_column.astype(jnp.int32)
+    copy = pltpu.make_async_copy(lists_ref, out_ref, sem)
+    copy.start()
+    copy.wait()
+
+
+def turn_kernel(pairs_blocks_ref, moments_in_ref, blocks_ref, moments_ref, sem):
+    moments_ref[...] = moments_in_ref[...]
     slot_count = pairs_blocks_ref.shape[0]
     copy = pltpu.make_async_copy(pairs_blocks_ref, blocks_ref.at[pl.ds(0, slot_count)], sem)
     copy.start()
@@ -125,22 +135,36 @@
     copy.wait()
 
 
-def add_products(lists_ref, blocks_ref, field, total, index, size, source_from=0, target_from=0):
-    stride = list_stride(blocks_ref.shape[0] // 2)
+def add_products(lists_ref, blocks_ref, slot_count, field, total, index, size, source_from=0, target_from=0):
+    stride = list_stride(slot_count)
+    idle = lists_ref[0, index * stride + stride - 1] >> 16
     count = lists_ref[0, len(KINDS) * stride + index]
-
-    def one_group(group, carry):
-        results = []
-        for step in range(size):
-            entry = lists_ref[0, index * stride + group * size + step]
-            block, source, target = entry & 255, (entry >> 8) & 255, entry >> 16
-            value = times(field[source - source_from].astype(BF16), blocks_ref[block])
-            results.append((target - target_from, value))
-        for at, value in results:
-            total[at] += value
-        return carry
-
-    lax.fori_loop(0, (count + size - 1) // size, one_group, 0)
+    column_count = lists_ref[0, len(KINDS) * stride + LANES + index]
+
+    def add_part(first, end, kind, plain, cuts):
+        def one_group(group, carry):
+            results = []
+            for step in range(size):
+                place = first + group * size + step
+                entry = lists_ref[0, index * stride + place]
+                block, source, target = entry & 255, (entry >> 8) & 255, entry >> 16
+                if plain:
+                    block = jnp.where(block >= slot_count, block - slot_count, block)
+                if cuts:
+                    target = jnp.where(place < end, target, idle)
+                value = kind(field[source - source_from].astype(BF16), blocks_ref[block])
+                results.append((target - target_from, value))
+            for at, value in results:
+                total[at] += value
+            return carry
+
+        lax.fori_loop(0, (end - first + size - 1) // size, one_group, 0)
+
+    if blocks_ref.shape[0] > slot_count:
+        add_part(0, count, times, False, False)
+    else:
+        add_part(0, column_count, times, True, True)
+        add_part(column_count, count, times_transposed, True, False)
 
 
 def lay_out(row_ref, field, first, block_len):
@@ -149,7 +173,7 @@
         field[first + block] = piece.astype(F32)
 
 
-def early_kernel(sub_count, lists_ref, blocks_ref, diag_ref, noise_ref, own_ref, *refs):
+def early_kernel(sub_count, slot_count, lists_ref, blocks_ref, diag_ref, noise_ref, own_ref, *refs):
     row_refs, (total, field) = refs[:-2], refs[-2:]
     block_len = blocks_ref.shape[1]
     sub_index, blocks_dev, own_first, _ = device_place(block_len, own_ref, sub_count)
@@ -161,10 +185,10 @@
         span = slice(block * block_len, (block + 1) * block_len)
         value = noise_ref[:, span] * own_ref[:, span]
         total[own_first + block] = value + times(field[own_first + block].astype(BF16), diag_ref[block])
-    add_products(lists_ref, blocks_ref, field, total, EARLY, LONG_GROUP)
-
-
-def ahead_kernel(sub_count, lists_ref, blocks_ref, begun_ref, *refs):
+    add_products(lists_ref, blocks_ref, slot_count, field, total, EARLY, LONG_GROUP)
+
+
+def ahead_kernel(sub_count, slot_count, lists_ref, blocks_ref, begun_ref, *refs):
     row_refs = refs[:sub_count]
     even_ref, odd_ref, field_ref, total = refs[sub_count:]
     block_len = blocks_ref.shape[1]
@@ -174,7 +198,7 @@
     for block in range(blocks_dev):
         total[block] = begun_ref[tile_blocks + block]
     total[blocks_dev] = jnp.zeros(total.shape[1:], F32)
-    add_products(lists_ref, blocks_ref, field_ref, total, AHEAD, SHORT_GROUP, 0, tile_blocks)
+    add_products(lists_ref, blocks_ref, slot_count, field_ref, total, AHEAD, SHORT_GROUP, 0, tile_blocks)
     is_odd = lax.axis_index("tile") % 2 == 1
     for block in range(blocks_dev):
         span = slice(block * block_len, (block + 1) * block_len)
@@ -184,12 +208,15 @@
         odd_ref[:, span] = jnp.where(is_odd, products, first_row).astype(BF16)
 
 
-def late_kernel(lists_ref, blocks_ref, begun_ref, field_ref, total):
+def late_kernel(slot_count, lists_ref, blocks_ref, begun_ref, field_ref, total):
     total[...] = begun_ref[...]
-    add_products(lists_ref, blocks_ref, field_ref, total, LATE, LONG_GROUP)
-
-
-def part_kernel(sub_count, is_last, lists_ref, blocks_ref, begun_ref, field_ref, even_ref, odd_ref, moments_in_ref, *refs):
+    add_products(lists_ref, blocks_ref, slot_count, field_ref, total, LATE, LONG_GROUP)
+
+
+def part_kernel(
+    sub_count, slot_count, is_last, lists_ref, blocks_ref, begun_ref, field_ref, even_ref, odd_ref,
+    moments_in_ref, *refs
+):
     part_refs = refs[:sub_count]
     moments_ref, total, ahead = refs[sub_count:]
     block_len = blocks_ref.shape[1]
@@ -204,7 +231,7 @@
     for block in range(blocks_dev, tile_blocks):
         total[block] = begun_ref[block]
     total[begun_ref.shape[0] - 1] = jnp.zeros(total.shape[1:], F32)
-    add_products(lists_ref, blocks_ref, ahead, total, FROM_AHEAD, SHORT_GROUP, tile_blocks, 0)
+    add_products(lists_ref, blocks_ref, slot_count, ahead, total, FROM_AHEAD, SHORT_GROUP, tile_blocks, 0)
     for step in range(sub_count):
         first = (sub_index ^ step) * blocks_dev
         for block in range(blocks_dev):
@@ -326,23 +353,22 @@
     slot_count = pair_blocks.shape[0]
     width = -(-slot_count // LANES) * LANES
     assert 2 * width <= 256 and extended < 256 and slot_count % TURN_GROUP == 0
+    lists_shape = (1, len(KINDS) * list_stride(slot_count) + 2 * LANES)
     lists = call(
         functools.partial(lists_kernel, sub_count, blocks_dev, slot_count),
-        jax.ShapeDtypeStruct((1, len(KINDS) * list_stride(slot_count) + LANES), jnp.int32),
+        pltpu.SMEM(lists_shape, jnp.int32),
         (block_pairs.T,),
         "lists",
         1,
         in_specs=[VMEM],
-        scratch_shapes=[pltpu.VMEM((8, width), F32)],
-    )
-    blocks = call(
-        turn_kernel,
-        pltpu.VMEM((2 * slot_count, block_len, block_len), BF16),
-        (pair_blocks,),
-        "turn",
-        4,
-        scratch_shapes=[pltpu.SemaphoreType.DMA(())],
-    )
+        out_specs=SMEM,
+        scratch_shapes=[
+            pltpu.VMEM((8, width), F32),
+            pltpu.VMEM(lists_shape, jnp.int32),
+            pltpu.SemaphoreType.DMA(()),
+        ],
+    )
+    blocks = pair_blocks
     field, rounded = call(order_kernel, (full, half), (right_side, point_order), "curve_order", 10, in_specs=[VMEM, VMEM])
     basis = [field]
     moments = jnp.zeros(scalars.shape, F32)
@@ -350,7 +376,7 @@
         is_last = index + 1 == ITERS
         rows = [rounded] + [exchange(rounded, "sub", step) for step in range(1, sub_count)]
         begun = call(
-            functools.partial(early_kernel, sub_count),
+            functools.partial(early_kernel, sub_count, slot_count),
             sums,
             (lists, blocks, diag_blocks, noise, field, *rows[:2]),
             "early",
@@ -358,7 +384,7 @@
             scratch_shapes=[scratch(extended)],
         )
         even, odd, tile_field = call(
-            functools.partial(ahead_kernel, sub_count),
+            functools.partial(ahead_kernel, sub_count, slot_count),
             (half, half, jax.ShapeDtypeStruct((sub_count * blocks_dev, rhs_count, block_len), F32)),
             (lists, blocks, begun, *rows),
             "ahead",
@@ -367,10 +393,10 @@
         )
         even = swap(even, "tile", 0)
         odd = swap(odd, "tile", 1)
-        begun = call(late_kernel, sums, (lists, blocks, begun, tile_field), "late", 3)
+        begun = call(functools.partial(late_kernel, slot_count), sums, (lists, blocks, begun, tile_field), "late", 3)
         part = shape(rhs_count, points_dev, F32 if is_last else BF16)
         *parts, moments = call(
-            functools.partial(part_kernel, sub_count, is_last),
+            functools.partial(part_kernel, sub_count, slot_count, is_last),
             (full,) + (part,) * (sub_count - 1) + (scalars,),
             (lists, blocks, begun, tile_field, even, odd, moments),
             "parts",
@@ -379,6 +405,15 @@
         )
         if is_last:
             break
+        if index == 0:
+            blocks, moments = call(
+                turn_kernel,
+                (pltpu.VMEM((2 * slot_count, block_len, block_len), BF16), scalars),
+                (pair_blocks, moments),
+                "turn",
+                4,
+                scratch_shapes=[pltpu.SemaphoreType.DMA(())],
+            )
         arrived = [exchange(parts[step], "sub", step) for step in range(1, sub_count)]
         field, rounded, moments = call(
             functools.partial(join_kernel, index),

time: 102 us -> 118 us (1.16); the launches traced: 101 us -> 119 us
  local copies, waits for them, and re-layouts: 1.99 us -> 24.9 us
  Pallas kernels: 34.4 us -> 26.3 us
  starting transfers between devices: 38.7 us -> 46.7 us
  waiting for transfers between devices: 25 us -> 19.9 us
    unnamed x12 -> x18, local copies, waits for them, and re-layouts: 1.99 us -> 24.9 us
    pallas_call x18, Pallas kernels: 34.4 us -> 26.3 us  [call(): pl.pallas_call(kernel, out_shape=outs, compiler_params=PARAMS, name=name,...]
    ppermute x23, waiting for transfers between devices: 25 us -> 19.9 us  [exchange(): return lax.ppermute(block, axis, [(i, i ^ step) for i in range(count)])]
    ppermute x23, starting transfers between devices: 36.5 us -> 41.5 us  [exchange(): return lax.ppermute(block, axis, [(i, i ^ step) for i in range(count)])]
    ppermute x6, starting transfers between devices: 2.21 us -> 5.2 us  [swap(): return lax.ppermute(block, axis, route)]
  transfers between devices with their start and end apart: 29 -> 29, of which waited for: 13 -> 12; matrix products, arithmetic and copies ran while one was open for 0% -> 0% of each run, Pallas kernels for 23% -> 17%
where the time goes in v4:
time: 118 us; the launch traced here: 119 us
  starting transfers between devices  46.7 us (40%)
  Pallas kernels  26.3 us (22%)
  local copies, waits for them, and re-layouts  24.9 us (21%)
  waiting for transfers between devices  19.9 us (17%)
    ppermute x23, starting transfers between devices, exchange(): return lax.ppermute(block, axis, [(i, i ^ step) for i in range(count)])  41.5 us
    pallas_call x18, Pallas kernels, call(): pl.pallas_call(kernel, out_shape=outs, compiler_params=PARAMS, name=name,...  26.3 us
    unnamed x18, local copies, waits for them, and re-layouts  24.9 us
    ppermute x23, waiting for transfers between devices, exchange(): return lax.ppermute(block, axis, [(i, i ^ step) for i in range(count)])  19.9 us
    ppermute x6, starting transfers between devices, swap(): return lax.ppermute(block, axis, route)  5.2 us
  transfers between devices with their start and end apart: 29, of which 12 were waited for; matrix products, arithmetic and copies ran while one was open for 0% of the time, Pallas kernels for 17%

profile of v4, /device:TPU:0, one launch (start us, length us, event | category | flops | bytes accessed | tf_op | source)
XLA Modules:
  0.0 118.7 jit_solution(15517107933588566442)
XLA Ops:
  4.1 5.1 %collective-permute-start.2 = (bf16[8,4096]{1,0:T(8,128)(2,1)S(1)}, bf16[8,4096]{1,0:T(8,128)(2,1)S(1)}, u32[]{:S(2)}, u32[]{:S(2)}) collective-permute-start(bf16[8,4096]{1,0:T(8,128)(2,1)S(1)} %get-tuple-element.46.refs_0_), channel_id=1, source_target_pairs={{0,3},{1,2},{2,1},{3,0},{4,7},{5,6},{6,5},{7,4},{8,11},{9,10},{10,... | collective-permute-start | bytes 196616 | tf_op jit(solution)/shard_map/ppermute | solution.py:312
  11.4 2.1 %collective-permute-done.refs_1_ = bf16[8,4096]{1,0:T(8,128)(2,1)S(1)} collective-permute-done((bf16[8,4096]{1,0:T(8,128)(2,1)S(1)}, bf16[8,4096]{1,0:T(8,128)(2,1)S(1)}, u32[]{:S(2)}, u32[]{:S(2)}) %collective-permute-start) | collective-permute-done | bytes 65568 | tf_op jit(solution)/shard_map/ppermute | solution.py:312
  13.5 2.9 %early.3.begun_ref = f32[81,8,256]{2,1,0:T(8,128)S(1)} custom-call(s32[1,1280]{1,0:T(1,128)S(4)} %lists.1.lists_ref, bf16[96,256,256]{2,1,0:T(8,128)(2,1)S(1)} %copy-done.3, bf16[16,256,256]{2,1,0:T(8,128)(2,1)S(1)} %copy-done.4, f32[1,4096]{1,0:T(1,128)S(1)} %bitcast.2, f32[8,4096]{1,0:T(8,128)S(1)} %get-tuple-element.45.own_ref.old_ref.refs_4_, ...), custom_call_target="tpu_custom_call" | custom-call | flops 3000000000 | tf_op jit(solution)/shard_map/early/pallas_call | solution.py:328
  17.8 2.8 %late.3.begun_ref = f32[81,8,256]{2,1,0:T(8,128)S(1)} custom-call(s32[1,1280]{1,0:T(1,128)S(4)} %lists.1.lists_ref, bf16[96,256,256]{2,1,0:T(8,128)(2,1)S(1)} %copy-done.3, f32[81,8,256]{2,1,0:T(8,128)S(1)} %early.3.begun_ref, f32[64,8,256]{2,1,0:T(8,128)S(1)} %get-tuple-element.47.field_ref), custom_call_target="tpu_custom_call" | custom-call | flops 3000000000 | tf_op jit(solution)/shard_map/late/pallas_call | solution.py:328
  22.6 3.1 %collective-permute-start.6 = (bf16[8,4096]{1,0:T(8,128)(2,1)S(1)}, bf16[8,4096]{1,0:T(8,128)(2,1)S(1)}, u32[]{:S(2)}, u32[]{:S(2)}) collective-permute-start(bf16[8,4096]{1,0:T(8,128)(2,1)S(1)} %get-tuple-element.55), channel_id=1, source_target_pairs={{0,2},{1,3},{2,0},{3,1},{4,6},{5,7},{6,4},{7,5},{8,10},{9,11},{10,... | collective-permute-start | bytes 196616 | tf_op jit(solution)/shard_map/ppermute | solution.py:312
  26.1 5.4 %turn.1 = (bf16[192,256,256]{2,1,0:T(8,128)(2,1)S(1)}, f32[8,128]{1,0:T(8,128)S(1)}) custom-call(bf16[96,256,256]{2,1,0:T(8,128)(2,1)S(1)} %copy-done.3, f32[8,128]{1,0:T(8,128)S(1)} %get-tuple-element.50.moments_in_ref), custom_call_target="tpu_custom_call" | custom-call | flops 4000000000 | tf_op jit(solution)/shard_map/turn/pallas_call | solution.py:328
  31.5 8.3 %copy-done = bf16[192,256,256]{2,1,0:T(8,128)(2,1)} copy-done((bf16[192,256,256]{2,1,0:T(8,128)(2,1)}, bf16[192,256,256]{2,1,0:T(8,128)(2,1)S(1)}, u32[]{:S(2)}) %copy-start) | copy-done | bytes 25165848
  40.2 3.3 %collective-permute-start.10 = (bf16[8,4096]{1,0:T(8,128)(2,1)S(1)}, bf16[8,4096]{1,0:T(8,128)(2,1)S(1)}, u32[]{:S(2)}, u32[]{:S(2)}) collective-permute-start(bf16[8,4096]{1,0:T(8,128)(2,1)S(1)} %get-tuple-element.58.refs_0_), channel_id=1, source_target_pairs={{0,3},{1,2},{2,1},{3,0},{4,7},{5,6},{6,5},{7,4},{8,11},{9,10},{10,... | collective-permute-start | bytes 196616 | tf_op jit(solution)/shard_map/ppermute | solution.py:312
  44.2 8.2 %copy-done.1 = bf16[192,256,256]{2,1,0:T(8,128)(2,1)S(1)} copy-done((bf16[192,256,256]{2,1,0:T(8,128)(2,1)S(1)}, bf16[192,256,256]{2,1,0:T(8,128)(2,1)}, u32[]{:S(2)}) %copy-start.1) | copy-done | bytes 25165848
  52.3 2.0 %early.4.begun_ref = f32[81,8,256]{2,1,0:T(8,128)S(1)} custom-call(s32[1,1280]{1,0:T(1,128)S(4)} %lists.1.lists_ref, bf16[192,256,256]{2,1,0:T(8,128)(2,1)S(1)} %copy-done.1, bf16[16,256,256]{2,1,0:T(8,128)(2,1)S(1)} %copy-done.4, f32[1,4096]{1,0:T(1,128)S(1)} %bitcast.3, f32[8,4096]{1,0:T(8,128)S(1)} %get-tuple-element.57.own_ref.old_ref.refs_5_, ...), custom_call_target="tpu_custom_call" | custom-call | flops 3000000000 | tf_op jit(solution)/shard_map/early/pallas_call | solution.py:328
  54.3 6.2 %copy-done.2 = bf16[192,256,256]{2,1,0:T(8,128)(2,1)S(1)} copy-done((bf16[192,256,256]{2,1,0:T(8,128)(2,1)S(1)}, bf16[192,256,256]{2,1,0:T(8,128)(2,1)}, u32[]{:S(2)}) %copy-start.2) | copy-done | bytes 25165848
  61.1 2.6 %collective-permute-start.11 = (bf16[8,4096]{1,0:T(8,128)(2,1)S(1)}, bf16[8,4096]{1,0:T(8,128)(2,1)S(1)}, u32[]{:S(2)}, u32[]{:S(2)}) collective-permute-start(bf16[8,4096]{1,0:T(8,128)(2,1)S(1)} %get-tuple-element.60), channel_id=1, source_target_pairs={{0,4},{4,0},{8,12},{12,8},{16,20},{20,16},{24,28},{28,24},{1,5},{5... | collective-permute-start | bytes 196616 | tf_op jit(solution)/shard_map/ppermute | solution.py:320
  64.4 1.6 %late.4.begun_ref = f32[81,8,256]{2,1,0:T(8,128)S(1)} custom-call(s32[1,1280]{1,0:T(1,128)S(4)} %lists.1.lists_ref, bf16[192,256,256]{2,1,0:T(8,128)(2,1)S(1)} %copy-done.2, f32[81,8,256]{2,1,0:T(8,128)S(1)} %early.4.begun_ref, f32[64,8,256]{2,1,0:T(8,128)S(1)} %get-tuple-element.59.field_ref), custom_call_target="tpu_custom_call" | custom-call | flops 3000000000 | tf_op jit(solution)/shard_map/late/pallas_call | solution.py:328
  66.7 2.8 %collective-permute-start.14 = (bf16[8,4096]{1,0:T(8,128)(2,1)S(1)}, bf16[8,4096]{1,0:T(8,128)(2,1)S(1)}, u32[]{:S(2)}, u32[]{:S(2)}) collective-permute-start(bf16[8,4096]{1,0:T(8,128)(2,1)S(1)} %get-tuple-element.66), channel_id=1, source_target_pairs={{0,2},{1,3},{2,0},{3,1},{4,6},{5,7},{6,4},{7,5},{8,10},{9,11},{10,... | collective-permute-start | bytes 196616 | tf_op jit(solution)/shard_map/ppermute | solution.py:312
  71.9 3.8 %collective-permute-done.15.refs_2_ = bf16[8,4096]{1,0:T(8,128)(2,1)S(1)} collective-permute-done((bf16[8,4096]{1,0:T(8,128)(2,1)S(1)}, bf16[8,4096]{1,0:T(8,128)(2,1)S(1)}, u32[]{:S(2)}, u32[]{:S(2)}) %collective-permute-start.15) | collective-permute-done | bytes 65568 | tf_op jit(solution)/shard_map/ppermute | solution.py:312
  77.5 1.9 %collective-permute-start.17 = (bf16[8,4096]{1,0:T(8,128)(2,1)S(1)}, bf16[8,4096]{1,0:T(8,128)(2,1)S(1)}, u32[]{:S(2)}, u32[]{:S(2)}) collective-permute-start(bf16[8,4096]{1,0:T(8,128)(2,1)S(1)} %get-tuple-element.69.refs_0_), channel_id=1, source_target_pairs={{0,2},{1,3},{2,0},{3,1},{4,6},{5,7},{6,4},{7,5},{8,10},{9,11},{10,... | collective-permute-start | bytes 196616 | tf_op jit(solution)/shard_map/ppermute | solution.py:312
  80.2 2.0 %early.5.begun_ref = f32[81,8,256]{2,1,0:T(8,128)S(1)} custom-call(s32[1,1280]{1,0:T(1,128)S(4)} %lists.1.lists_ref, bf16[192,256,256]{2,1,0:T(8,128)(2,1)S(1)} %copy-done.2, bf16[16,256,256]{2,1,0:T(8,128)(2,1)S(1)} %copy-done.4, f32[1,4096]{1,0:T(1,128)S(1)} %bitcast.4, f32[8,4096]{1,0:T(8,128)S(1)} %get-tuple-element.68.own_ref.refs_6_, ...), custom_call_target="tpu_custom_call" | custom-call | flops 3000000000 | tf_op jit(solution)/shard_map/early/pallas_call | solution.py:328
  82.3 3.6 %collective-permute-done.17.refs_2_ = bf16[8,4096]{1,0:T(8,128)(2,1)S(1)} collective-permute-done((bf16[8,4096]{1,0:T(8,128)(2,1)S(1)}, bf16[8,4096]{1,0:T(8,128)(2,1)S(1)}, u32[]{:S(2)}, u32[]{:S(2)}) %collective-permute-start.17) | collective-permute-done | bytes 65568 | tf_op jit(solution)/shard_map/ppermute | solution.py:312
  87.7 1.6 %late.5.begun_ref = f32[81,8,256]{2,1,0:T(8,128)S(1)} custom-call(s32[1,1280]{1,0:T(1,128)S(4)} %lists.1.lists_ref, bf16[192,256,256]{2,1,0:T(8,128)(2,1)S(1)} %copy-done.2, f32[81,8,256]{2,1,0:T(8,128)S(1)} %early.5.begun_ref, f32[64,8,256]{2,1,0:T(8,128)S(1)} %get-tuple-element.70.field_ref), custom_call_target="tpu_custom_call" | custom-call | flops 3000000000 | tf_op jit(solution)/shard_map/late/pallas_call | solution.py:328
  90.1 3.6 %collective-permute-done.21 = f32[8,128]{1,0:T(8,128)S(1)} collective-permute-done((f32[8,128]{1,0:T(8,128)S(1)}, f32[8,128]{1,0:T(8,128)S(1)}, u32[]{:S(2)}, u32[]{:S(2)}) %collective-permute-start.21) | collective-permute-done | bytes 4128 | tf_op jit(solution)/shard_map/ppermute | solution.py:312
  94.0 2.1 %collective-permute-start.26 = (f32[8,4096]{1,0:T(8,128)S(1)}, f32[8,4096]{1,0:T(8,128)S(1)}, u32[]{:S(2)}, u32[]{:S(2)}) collective-permute-start(f32[8,4096]{1,0:T(8,128)S(1)} %get-tuple-element.78), channel_id=1, source_target_pairs={{0,3},{1,2},{2,1},{3,0},{4,7},{5,6},{6,5},{7,4},{8,11},{9,10},{10,... | collective-permute-start | bytes 393224 | tf_op jit(solution)/shard_map/ppermute | solution.py:312
  98.3 6.4 %collective-permute-start.23 = (f32[8,128]{1,0:T(8,128)S(1)}, f32[8,128]{1,0:T(8,128)S(1)}, u32[]{:S(2)}, u32[]{:S(2)}) collective-permute-start(f32[8,128]{1,0:T(8,128)S(1)} %add.16), channel_id=1, source_target_pairs={{0,4},{4,0},{8,12},{12,8},{16,20},{20,16},{24,28},{28,24},{1,5},{5... | collective-permute-start | bytes 12296 | tf_op jit(solution)/shard_map/ppermute | solution.py:312
  105.6 3.4 %collective-permute-start.24 = (f32[8,128]{1,0:T(8,128)S(1)}, f32[8,128]{1,0:T(8,128)S(1)}, u32[]{:S(2)}, u32[]{:S(2)}) collective-permute-start(f32[8,128]{1,0:T(8,128)S(1)} %add.17), channel_id=1, source_target_pairs={{0,8},{4,12},{8,0},{12,4},{16,24},{20,28},{24,16},{28,20},{1,9},{5... | collective-permute-start | bytes 12296 | tf_op jit(solution)/shard_map/ppermute | solution.py:312
  110.6 5.5 %collective-permute-start.25 = (f32[8,128]{1,0:T(8,128)S(1)}, f32[8,128]{1,0:T(8,128)S(1)}, u32[]{:S(2)}, u32[]{:S(2)}) collective-permute-start(f32[8,128]{1,0:T(8,128)S(1)} %add.18), channel_id=1, source_target_pairs={{0,16},{4,20},{8,24},{12,28},{16,0},{20,4},{24,8},{28,12},{1,17},{... | collective-permute-start | bytes 12296 | tf_op jit(solution)/shard_map/ppermute | solution.py:312
  (76 shorter events, 27.4 us)
Async XLA Ops:
  4.1 12.3 %collective-permute-start.2 = (bf16[8,4096]{1,0:T(8,128)(2,1)S(1)}, bf16[8,4096]{1,0:T(8,128)(2,1)S(1)}, u32[]{:S(2)}, u32[]{:S(2)}) collective-permute-start(bf16[8,4096]{1,0:T(8,128)(2,1)S(1)} %get-tuple-element.46.refs_0_), channel_id=1, source_target_pairs={{0,3},{1,2},{2,1},{3,0},{4,7},{5,6},{6,5},{7,4},{8,11},{9,10},{10,... | collective-permute-start | bytes 196616 | tf_op jit(solution)/shard_map/ppermute | solution.py:312
  9.3 7.2 %collective-permute-start.1 = (bf16[8,4096]{1,0:T(8,128)(2,1)S(1)}, bf16[8,4096]{1,0:T(8,128)(2,1)S(1)}, u32[]{:S(2)}, u32[]{:S(2)}) collective-permute-start(bf16[8,4096]{1,0:T(8,128)(2,1)S(1)} %get-tuple-element.46.refs_0_), channel_id=1, source_target_pairs={{0,2},{1,3},{2,0},{3,1},{4,6},{5,7},{6,4},{7,5},{8,10},{9,11},{10,... | collective-permute-start | bytes 196616 | tf_op jit(solution)/shard_map/ppermute | solution.py:312
  9.3 4.3 %collective-permute-start = (bf16[8,4096]{1,0:T(8,128)(2,1)S(1)}, bf16[8,4096]{1,0:T(8,128)(2,1)S(1)}, u32[]{:S(2)}, u32[]{:S(2)}) collective-permute-start(bf16[8,4096]{1,0:T(8,128)(2,1)S(1)} %get-tuple-element.46.refs_0_), channel_id=1, source_target_pairs={{0,1},{1,0},{2,3},{3,2},{4,5},{5,4},{6,7},{7,6},{8,9},{9,8},{10,11... | collective-permute-start | bytes 196616 | tf_op jit(solution)/shard_map/ppermute | solution.py:312
  21.6 18.2 %collective-permute-start.5 = (bf16[8,4096]{1,0:T(8,128)(2,1)S(1)}, bf16[8,4096]{1,0:T(8,128)(2,1)S(1)}, u32[]{:S(2)}, u32[]{:S(2)}) collective-permute-start(bf16[8,4096]{1,0:T(8,128)(2,1)S(1)} %get-tuple-element.54), channel_id=1, source_target_pairs={{0,1},{1,0},{2,3},{3,2},{4,5},{5,4},{6,7},{7,6},{8,9},{9,8},{10,11... | collective-permute-start | bytes 196616 | tf_op jit(solution)/shard_map/ppermute | solution.py:312
  22.6 17.2 %collective-permute-start.6 = (bf16[8,4096]{1,0:T(8,128)(2,1)S(1)}, bf16[8,4096]{1,0:T(8,128)(2,1)S(1)}, u32[]{:S(2)}, u32[]{:S(2)}) collective-permute-start(bf16[8,4096]{1,0:T(8,128)(2,1)S(1)} %get-tuple-element.55), channel_id=1, source_target_pairs={{0,2},{1,3},{2,0},{3,1},{4,6},{5,7},{6,4},{7,5},{8,10},{9,11},{10,... | collective-permute-start | bytes 196616 | tf_op jit(solution)/shard_map/ppermute | solution.py:312
  25.7 14.0 %collective-permute-start.7 = (bf16[8,4096]{1,0:T(8,128)(2,1)S(1)}, bf16[8,4096]{1,0:T(8,128)(2,1)S(1)}, u32[]{:S(2)}, u32[]{:S(2)}) collective-permute-start(bf16[8,4096]{1,0:T(8,128)(2,1)S(1)} %get-tuple-element.56), channel_id=1, source_target_pairs={{0,3},{1,2},{2,1},{3,0},{4,7},{5,6},{6,5},{7,4},{8,11},{9,10},{10,... | collective-permute-start | bytes 196616 | tf_op jit(solution)/shard_map/ppermute | solution.py:312
  39.9 4.3 %collective-permute-start.8 = (bf16[8,4096]{1,0:T(8,128)(2,1)S(1)}, bf16[8,4096]{1,0:T(8,128)(2,1)S(1)}, u32[]{:S(2)}, u32[]{:S(2)}) collective-permute-start(bf16[8,4096]{1,0:T(8,128)(2,1)S(1)} %get-tuple-element.58.refs_0_), channel_id=1, source_target_pairs={{0,1},{1,0},{2,3},{3,2},{4,5},{5,4},{6,7},{7,6},{8,9},{9,8},{10,11... | collective-permute-start | bytes 196616 | tf_op jit(solution)/shard_map/ppermute | solution.py:312
  40.2 14.2 %collective-permute-start.10 = (bf16[8,4096]{1,0:T(8,128)(2,1)S(1)}, bf16[8,4096]{1,0:T(8,128)(2,1)S(1)}, u32[]{:S(2)}, u32[]{:S(2)}) collective-permute-start(bf16[8,4096]{1,0:T(8,128)(2,1)S(1)} %get-tuple-element.58.refs_0_), channel_id=1, source_target_pairs={{0,3},{1,2},{2,1},{3,0},{4,7},{5,6},{6,5},{7,4},{8,11},{9,10},{10,... | collective-permute-start | bytes 196616 | tf_op jit(solution)/shard_map/ppermute | solution.py:312
  43.5 10.8 %collective-permute-start.9 = (bf16[8,4096]{1,0:T(8,128)(2,1)S(1)}, bf16[8,4096]{1,0:T(8,128)(2,1)S(1)}, u32[]{:S(2)}, u32[]{:S(2)}) collective-permute-start(bf16[8,4096]{1,0:T(8,128)(2,1)S(1)} %get-tuple-element.58.refs_0_), channel_id=1, source_target_pairs={{0,2},{1,3},{2,0},{3,1},{4,6},{5,7},{6,4},{7,5},{8,10},{9,11},{10,... | collective-permute-start | bytes 196616 | tf_op jit(solution)/shard_map/ppermute | solution.py:312
  61.1 4.9 %collective-permute-start.11 = (bf16[8,4096]{1,0:T(8,128)(2,1)S(1)}, bf16[8,4096]{1,0:T(8,128)(2,1)S(1)}, u32[]{:S(2)}, u32[]{:S(2)}) collective-permute-start(bf16[8,4096]{1,0:T(8,128)(2,1)S(1)} %get-tuple-element.60), channel_id=1, source_target_pairs={{0,4},{4,0},{8,12},{12,8},{16,20},{20,16},{24,28},{28,24},{1,5},{5... | collective-permute-start | bytes 196616 | tf_op jit(solution)/shard_map/ppermute | solution.py:320
  66.6 4.5 %collective-permute-start.13 = (bf16[8,4096]{1,0:T(8,128)(2,1)S(1)}, bf16[8,4096]{1,0:T(8,128)(2,1)S(1)}, u32[]{:S(2)}, u32[]{:S(2)}) collective-permute-start(bf16[8,4096]{1,0:T(8,128)(2,1)S(1)} %get-tuple-element.65), channel_id=1, source_target_pairs={{0,1},{1,0},{2,3},{3,2},{4,5},{5,4},{6,7},{7,6},{8,9},{9,8},{10,11... | collective-permute-start | bytes 196616 | tf_op jit(solution)/shard_map/ppermute | solution.py:312
  66.7 5.2 %collective-permute-start.14 = (bf16[8,4096]{1,0:T(8,128)(2,1)S(1)}, bf16[8,4096]{1,0:T(8,128)(2,1)S(1)}, u32[]{:S(2)}, u32[]{:S(2)}) collective-permute-start(bf16[8,4096]{1,0:T(8,128)(2,1)S(1)} %get-tuple-element.66), channel_id=1, source_target_pairs={{0,2},{1,3},{2,0},{3,1},{4,6},{5,7},{6,4},{7,5},{8,10},{9,11},{10,... | collective-permute-start | bytes 196616 | tf_op jit(solution)/shard_map/ppermute | solution.py:312
  69.5 6.3 %collective-permute-start.15 = (bf16[8,4096]{1,0:T(8,128)(2,1)S(1)}, bf16[8,4096]{1,0:T(8,128)(2,1)S(1)}, u32[]{:S(2)}, u32[]{:S(2)}) collective-permute-start(bf16[8,4096]{1,0:T(8,128)(2,1)S(1)} %get-tuple-element.67), channel_id=1, source_target_pairs={{0,3},{1,2},{2,1},{3,0},{4,7},{5,6},{6,5},{7,4},{8,11},{9,10},{10,... | collective-permute-start | bytes 196616 | tf_op jit(solution)/shard_map/ppermute | solution.py:312
  75.9 4.3 %collective-permute-start.16 = (bf16[8,4096]{1,0:T(8,128)(2,1)S(1)}, bf16[8,4096]{1,0:T(8,128)(2,1)S(1)}, u32[]{:S(2)}, u32[]{:S(2)}) collective-permute-start(bf16[8,4096]{1,0:T(8,128)(2,1)S(1)} %get-tuple-element.69.refs_0_), channel_id=1, source_target_pairs={{0,1},{1,0},{2,3},{3,2},{4,5},{5,4},{6,7},{7,6},{8,9},{9,8},{10,11... | collective-permute-start | bytes 196616 | tf_op jit(solution)/shard_map/ppermute | solution.py:312
  75.9 6.4 %collective-permute-start.18 = (bf16[8,4096]{1,0:T(8,128)(2,1)S(1)}, bf16[8,4096]{1,0:T(8,128)(2,1)S(1)}, u32[]{:S(2)}, u32[]{:S(2)}) collective-permute-start(bf16[8,4096]{1,0:T(8,128)(2,1)S(1)} %get-tuple-element.69.refs_0_), channel_id=1, source_target_pairs={{0,3},{1,2},{2,1},{3,0},{4,7},{5,6},{6,5},{7,4},{8,11},{9,10},{10,... | collective-permute-start | bytes 196616 | tf_op jit(solution)/shard_map/ppermute | solution.py:312
  77.5 8.4 %collective-permute-start.17 = (bf16[8,4096]{1,0:T(8,128)(2,1)S(1)}, bf16[8,4096]{1,0:T(8,128)(2,1)S(1)}, u32[]{:S(2)}, u32[]{:S(2)}) collective-permute-start(bf16[8,4096]{1,0:T(8,128)(2,1)S(1)} %get-tuple-element.69.refs_0_), channel_id=1, source_target_pairs={{0,2},{1,3},{2,0},{3,1},{4,6},{5,7},{6,4},{7,5},{8,10},{9,11},{10,... | collective-permute-start | bytes 196616 | tf_op jit(solution)/shard_map/ppermute | solution.py:312
  90.1 3.6 %collective-permute-start.21 = (f32[8,128]{1,0:T(8,128)S(1)}, f32[8,128]{1,0:T(8,128)S(1)}, u32[]{:S(2)}, u32[]{:S(2)}) collective-permute-start(f32[8,128]{1,0:T(8,128)S(1)} %get-tuple-element.74), channel_id=1, source_target_pairs={{0,1},{1,0},{2,3},{3,2},{4,5},{5,4},{6,7},{7,6},{8,9},{9,8},{10,11... | collective-permute-start | bytes 12296 | tf_op jit(solution)/shard_map/ppermute | solution.py:312
  93.7 4.5 %collective-permute-start.22 = (f32[8,128]{1,0:T(8,128)S(1)}, f32[8,128]{1,0:T(8,128)S(1)}, u32[]{:S(2)}, u32[]{:S(2)}) collective-permute-start(f32[8,128]{1,0:T(8,128)S(1)} %add.15), channel_id=1, source_target_pairs={{0,2},{1,3},{2,0},{3,1},{4,6},{5,7},{6,4},{7,5},{8,10},{9,11},{10,... | collective-permute-start | bytes 12296 | tf_op jit(solution)/shard_map/ppermute | solution.py:312
  94.0 23.7 %collective-permute-start.26 = (f32[8,4096]{1,0:T(8,128)S(1)}, f32[8,4096]{1,0:T(8,128)S(1)}, u32[]{:S(2)}, u32[]{:S(2)}) collective-permute-start(f32[8,4096]{1,0:T(8,128)S(1)} %get-tuple-element.78), channel_id=1, source_target_pairs={{0,3},{1,2},{2,1},{3,0},{4,7},{5,6},{6,5},{7,4},{8,11},{9,10},{10,... | collective-permute-start | bytes 393224 | tf_op jit(solution)/shard_map/ppermute | solution.py:312
  96.0 21.7 %collective-permute-start.27 = (f32[8,4096]{1,0:T(8,128)S(1)}, f32[8,4096]{1,0:T(8,128)S(1)}, u32[]{:S(2)}, u32[]{:S(2)}) collective-permute-start(f32[8,4096]{1,0:T(8,128)S(1)} %get-tuple-element.82), channel_id=1, source_target_pairs={{0,2},{1,3},{2,0},{3,1},{4,6},{5,7},{6,4},{7,5},{8,10},{9,11},{10,... | collective-permute-start | bytes 393224 | tf_op jit(solution)/shard_map/ppermute | solution.py:312
  98.2 19.5 %collective-permute-start.28 = (f32[8,4096]{1,0:T(8,128)S(1)}, f32[8,4096]{1,0:T(8,128)S(1)}, u32[]{:S(2)}, u32[]{:S(2)}) collective-permute-start(f32[8,4096]{1,0:T(8,128)S(1)} %get-tuple-element.85), channel_id=1, source_target_pairs={{0,1},{1,0},{2,3},{3,2},{4,5},{5,4},{6,7},{7,6},{8,9},{9,8},{10,11... | collective-permute-start | bytes 393224 | tf_op jit(solution)/shard_map/ppermute | solution.py:312
  98.3 7.2 %collective-permute-start.23 = (f32[8,128]{1,0:T(8,128)S(1)}, f32[8,128]{1,0:T(8,128)S(1)}, u32[]{:S(2)}, u32[]{:S(2)}) collective-permute-start(f32[8,128]{1,0:T(8,128)S(1)} %add.16), channel_id=1, source_target_pairs={{0,4},{4,0},{8,12},{12,8},{16,20},{20,16},{24,28},{28,24},{1,5},{5... | collective-permute-start | bytes 12296 | tf_op jit(solution)/shard_map/ppermute | solution.py:312
  105.6 5.0 %collective-permute-start.24 = (f32[8,128]{1,0:T(8,128)S(1)}, f32[8,128]{1,0:T(8,128)S(1)}, u32[]{:S(2)}, u32[]{:S(2)}) collective-permute-start(f32[8,128]{1,0:T(8,128)S(1)} %add.17), channel_id=1, source_target_pairs={{0,8},{4,12},{8,0},{12,4},{16,24},{20,28},{24,16},{28,20},{1,9},{5... | collective-permute-start | bytes 12296 | tf_op jit(solution)/shard_map/ppermute | solution.py:312
  110.6 7.1 %collective-permute-start.25 = (f32[8,128]{1,0:T(8,128)S(1)}, f32[8,128]{1,0:T(8,128)S(1)}, u32[]{:S(2)}, u32[]{:S(2)}) collective-permute-start(f32[8,128]{1,0:T(8,128)S(1)} %add.18), channel_id=1, source_target_pairs={{0,16},{4,20},{8,24},{12,28},{16,0},{20,4},{24,8},{28,12},{1,17},{... | collective-permute-start | bytes 12296 | tf_op jit(solution)/shard_map/ppermute | solution.py:312
  (14 other events, 84.9 us)

commit v5 on v4

--- a/solution.py
+++ b/solution.py
@@ -119,8 +119,7 @@
     copy.wait()
 
 
-def turn_kernel(pairs_blocks_ref, moments_in_ref, blocks_ref, moments_ref, sem):
-    moments_ref[...] = moments_in_ref[...]
+def turn_kernel(pairs_blocks_ref, after_ref, blocks_ref, sem):
     slot_count = pairs_blocks_ref.shape[0]
     copy = pltpu.make_async_copy(pairs_blocks_ref, blocks_ref.at[pl.ds(0, slot_count)], sem)
     copy.start()
@@ -247,7 +246,7 @@
     moments_ref[...] = moments
 
 
-def join_kernel(index, own_ref, old_ref, moments_in_ref, *refs):
+def join_kernel(index, after_ref, own_ref, old_ref, moments_in_ref, *refs):
     part_refs = refs[:-3]
     next_ref, rounded_ref, moments_ref = refs[-3:]
     value = own_ref[...]
@@ -406,9 +405,9 @@
         if is_last:
             break
         if index == 0:
-            blocks, moments = call(
+            blocks = call(
                 turn_kernel,
-                (pltpu.VMEM((2 * slot_count, block_len, block_len), BF16), scalars),
+                pltpu.VMEM((2 * slot_count, block_len, block_len), BF16),
                 (pair_blocks, moments),
                 "turn",
                 4,
@@ -418,7 +417,7 @@
         field, rounded, moments = call(
             functools.partial(join_kernel, index),
             (full, half, scalars),
-            (parts[0], field, moments, *arrived),
+            (blocks, parts[0], field, moments, *arrived),
             "join",
         )
         basis.append(field)

time: 118 us -> 97.6 us (0.83); the launches traced: 119 us -> 96.9 us
  local copies, waits for them, and re-layouts: 24.9 us -> 2.24 us
  Pallas kernels: 26.3 us -> 18.3 us
  starting transfers between devices: 46.7 us -> 54 us
  waiting for transfers between devices: 19.9 us -> 21.4 us
    unnamed x18 -> x12, local copies, waits for them, and re-layouts: 24.9 us -> 2.24 us
    pallas_call x18, Pallas kernels: 26.3 us -> 18.3 us  [call(): pl.pallas_call(kernel, out_shape=outs, compiler_params=PARAMS, name=name,...]
    ppermute x23, starting transfers between devices: 41.5 us -> 47.4 us  [exchange(): return lax.ppermute(block, axis, [(i, i ^ step) for i in range(count)])]
    ppermute x23, waiting for transfers between devices: 19.9 us -> 21.4 us  [exchange(): return lax.ppermute(block, axis, [(i, i ^ step) for i in range(count)])]
    ppermute x6, starting transfers between devices: 5.2 us -> 6.59 us  [swap(): return lax.ppermute(block, axis, route)]
  transfers between devices with their start and end apart: 29 -> 29, of which waited for: 12 -> 13; matrix products, arithmetic and copies ran while one was open for 0% -> 0% of each run, Pallas kernels for 17% -> 14%
where the time goes in v5:
time: 97.6 us; the launch traced here: 96.9 us
  starting transfers between devices  54 us (55%)
  waiting for transfers between devices  21.4 us (22%)
  Pallas kernels  18.3 us (19%)
  local copies, waits for them, and re-layouts  2.24 us (2%)
    ppermute x23, starting transfers between devices, exchange(): return lax.ppermute(block, axis, [(i, i ^ step) for i in range(count)])  47.4 us
    ppermute x23, waiting for transfers between devices, exchange(): return lax.ppermute(block, axis, [(i, i ^ step) for i in range(count)])  21.4 us
    pallas_call x18, Pallas kernels, call(): pl.pallas_call(kernel, out_shape=outs, compiler_params=PARAMS, name=name,...  18.3 us
    ppermute x6, starting transfers between devices, swap(): return lax.ppermute(block, axis, route)  6.59 us
    unnamed x12, local copies, waits for them, and re-layouts  2.24 us
  transfers between devices with their start and end apart: 29, of which 13 were waited for; matrix products, arithmetic and copies ran while one was open for 0% of the time, Pallas kernels for 14%

profile of v5, /device:TPU:0, one launch (start us, length us, event | category | flops | bytes accessed | tf_op | source)
XLA Modules:
  0.0 96.9 jit_solution(5351470343235189924)
XLA Ops:
  4.1 5.1 %collective-permute-start.2 = (bf16[8,4096]{1,0:T(8,128)(2,1)S(1)}, bf16[8,4096]{1,0:T(8,128)(2,1)S(1)}, u32[]{:S(2)}, u32[]{:S(2)}) collective-permute-start(bf16[8,4096]{1,0:T(8,128)(2,1)S(1)} %get-tuple-element.44.refs_0_), channel_id=1, source_target_pairs={{0,3},{1,2},{2,1},{3,0},{4,7},{5,6},{6,5},{7,4},{8,11},{9,10},{10,... | collective-permute-start | bytes 196616 | tf_op jit(solution)/shard_map/ppermute | solution.py:311
  9.9 1.5 %lists.1.lists_ref = s32[1,1280]{1,0:T(1,128)S(4)} custom-call(s32[2,96]{1,0:T(2,128)S(1)} %bitcast.5), custom_call_target="tpu_custom_call" | custom-call | flops 1000000000 | tf_op jit(solution)/shard_map/lists/pallas_call | solution.py:327
  11.4 2.1 %collective-permute-done.refs_1_ = bf16[8,4096]{1,0:T(8,128)(2,1)S(1)} collective-permute-done((bf16[8,4096]{1,0:T(8,128)(2,1)S(1)}, bf16[8,4096]{1,0:T(8,128)(2,1)S(1)}, u32[]{:S(2)}, u32[]{:S(2)}) %collective-permute-start) | collective-permute-done | bytes 65568 | tf_op jit(solution)/shard_map/ppermute | solution.py:311
  13.5 1.5 %early.3.begun_ref = f32[81,8,256]{2,1,0:T(8,128)S(1)} custom-call(s32[1,1280]{1,0:T(1,128)S(4)} %lists.1.lists_ref, bf16[96,256,256]{2,1,0:T(8,128)(2,1)S(1)} %copy-done, bf16[16,256,256]{2,1,0:T(8,128)(2,1)S(1)} %copy-done.1, f32[1,4096]{1,0:T(1,128)S(1)} %bitcast.2, f32[8,4096]{1,0:T(8,128)S(1)} %get-tuple-element.43.own_ref.old_ref.refs_4_, ...), custom_call_target="tpu_custom_call" | custom-call | flops 3000000000 | tf_op jit(solution)/shard_map/early/pallas_call | solution.py:327
  17.8 7.3 %collective-permute-start.5 = (bf16[8,4096]{1,0:T(8,128)(2,1)S(1)}, bf16[8,4096]{1,0:T(8,128)(2,1)S(1)}, u32[]{:S(2)}, u32[]{:S(2)}) collective-permute-start(bf16[8,4096]{1,0:T(8,128)(2,1)S(1)} %get-tuple-element.50), channel_id=1, source_target_pairs={{0,1},{1,0},{2,3},{3,2},{4,5},{5,4},{6,7},{7,6},{8,9},{9,8},{10,11... | collective-permute-start | bytes 196616 | tf_op jit(solution)/shard_map/ppermute | solution.py:311
  25.1 2.4 %collective-permute-start.7 = (bf16[8,4096]{1,0:T(8,128)(2,1)S(1)}, bf16[8,4096]{1,0:T(8,128)(2,1)S(1)}, u32[]{:S(2)}, u32[]{:S(2)}) collective-permute-start(bf16[8,4096]{1,0:T(8,128)(2,1)S(1)} %get-tuple-element.52), channel_id=1, source_target_pairs={{0,3},{1,2},{2,1},{3,0},{4,7},{5,6},{6,5},{7,4},{8,11},{9,10},{10,... | collective-permute-start | bytes 196616 | tf_op jit(solution)/shard_map/ppermute | solution.py:311
  27.5 5.4 %turn.1.after_ref.blocks_ref = bf16[192,256,256]{2,1,0:T(8,128)(2,1)S(1)} custom-call(bf16[96,256,256]{2,1,0:T(8,128)(2,1)S(1)} %copy-done, f32[8,128]{1,0:T(8,128)S(1)} %get-tuple-element.48.after_ref.moments_in_ref), custom_call_target="tpu_custom_call" | custom-call | flops 4000000000 | tf_op jit(solution)/shard_map/turn/pallas_call | solution.py:327
  38.6 2.3 %collective-permute-done.10.refs_3_ = bf16[8,4096]{1,0:T(8,128)(2,1)S(1)} collective-permute-done((bf16[8,4096]{1,0:T(8,128)(2,1)S(1)}, bf16[8,4096]{1,0:T(8,128)(2,1)S(1)}, u32[]{:S(2)}, u32[]{:S(2)}) %collective-permute-start.10) | collective-permute-done | bytes 65568 | tf_op jit(solution)/shard_map/ppermute | solution.py:311
  40.9 2.5 %collective-permute-done.9.refs_2_ = bf16[8,4096]{1,0:T(8,128)(2,1)S(1)} collective-permute-done((bf16[8,4096]{1,0:T(8,128)(2,1)S(1)}, bf16[8,4096]{1,0:T(8,128)(2,1)S(1)}, u32[]{:S(2)}, u32[]{:S(2)}) %collective-permute-start.9) | collective-permute-done | bytes 65568 | tf_op jit(solution)/shard_map/ppermute | solution.py:311
  46.6 1.9 %collective-permute-start.13 = (bf16[8,4096]{1,0:T(8,128)(2,1)S(1)}, bf16[8,4096]{1,0:T(8,128)(2,1)S(1)}, u32[]{:S(2)}, u32[]{:S(2)}) collective-permute-start(bf16[8,4096]{1,0:T(8,128)(2,1)S(1)} %get-tuple-element.61), channel_id=1, source_target_pairs={{0,1},{1,0},{2,3},{3,2},{4,5},{5,4},{6,7},{7,6},{8,9},{9,8},{10,11... | collective-permute-start | bytes 196616 | tf_op jit(solution)/shard_map/ppermute | solution.py:311
  51.1 2.9 %collective-permute-done.14.refs_1_ = bf16[8,4096]{1,0:T(8,128)(2,1)S(1)} collective-permute-done((bf16[8,4096]{1,0:T(8,128)(2,1)S(1)}, bf16[8,4096]{1,0:T(8,128)(2,1)S(1)}, u32[]{:S(2)}, u32[]{:S(2)}) %collective-permute-start.14) | collective-permute-done | bytes 65568 | tf_op jit(solution)/shard_map/ppermute | solution.py:311
  54.0 1.7 %collective-permute-done.15.refs_2_ = bf16[8,4096]{1,0:T(8,128)(2,1)S(1)} collective-permute-done((bf16[8,4096]{1,0:T(8,128)(2,1)S(1)}, bf16[8,4096]{1,0:T(8,128)(2,1)S(1)}, u32[]{:S(2)}, u32[]{:S(2)}) %collective-permute-start.15) | collective-permute-done | bytes 65568 | tf_op jit(solution)/shard_map/ppermute | solution.py:311
  55.8 2.1 %collective-permute-start.18 = (bf16[8,4096]{1,0:T(8,128)(2,1)S(1)}, bf16[8,4096]{1,0:T(8,128)(2,1)S(1)}, u32[]{:S(2)}, u32[]{:S(2)}) collective-permute-start(bf16[8,4096]{1,0:T(8,128)(2,1)S(1)} %get-tuple-element.65.refs_0_), channel_id=1, source_target_pairs={{0,3},{1,2},{2,1},{3,0},{4,7},{5,6},{6,5},{7,4},{8,11},{9,10},{10,... | collective-permute-start | bytes 196616 | tf_op jit(solution)/shard_map/ppermute | solution.py:311
  62.0 1.8 %collective-permute-done.17.refs_2_ = bf16[8,4096]{1,0:T(8,128)(2,1)S(1)} collective-permute-done((bf16[8,4096]{1,0:T(8,128)(2,1)S(1)}, bf16[8,4096]{1,0:T(8,128)(2,1)S(1)}, u32[]{:S(2)}, u32[]{:S(2)}) %collective-permute-start.17) | collective-permute-done | bytes 65568 | tf_op jit(solution)/shard_map/ppermute | solution.py:311
  64.2 3.5 %collective-permute-start.19 = (bf16[8,4096]{1,0:T(8,128)(2,1)S(1)}, bf16[8,4096]{1,0:T(8,128)(2,1)S(1)}, u32[]{:S(2)}, u32[]{:S(2)}) collective-permute-start(bf16[8,4096]{1,0:T(8,128)(2,1)S(1)} %get-tuple-element.67), channel_id=1, source_target_pairs={{0,4},{4,0},{8,12},{12,8},{16,20},{20,16},{24,28},{28,24},{1,5},{5... | collective-permute-start | bytes 196616 | tf_op jit(solution)/shard_map/ppermute | solution.py:319
  69.7 1.9 %collective-permute-start.21 = (f32[8,128]{1,0:T(8,128)S(1)}, f32[8,128]{1,0:T(8,128)S(1)}, u32[]{:S(2)}, u32[]{:S(2)}) collective-permute-start(f32[8,128]{1,0:T(8,128)S(1)} %get-tuple-element.70), channel_id=1, source_target_pairs={{0,1},{1,0},{2,3},{3,2},{4,5},{5,4},{6,7},{7,6},{8,9},{9,8},{10,11... | collective-permute-start | bytes 12296 | tf_op jit(solution)/shard_map/ppermute | solution.py:311
  71.6 1.7 %collective-permute-done.21 = f32[8,128]{1,0:T(8,128)S(1)} collective-permute-done((f32[8,128]{1,0:T(8,128)S(1)}, f32[8,128]{1,0:T(8,128)S(1)}, u32[]{:S(2)}, u32[]{:S(2)}) %collective-permute-start.21) | collective-permute-done | bytes 4128 | tf_op jit(solution)/shard_map/ppermute | solution.py:311
  74.6 3.0 %collective-permute-start.26 = (f32[8,4096]{1,0:T(8,128)S(1)}, f32[8,4096]{1,0:T(8,128)S(1)}, u32[]{:S(2)}, u32[]{:S(2)}) collective-permute-start(f32[8,4096]{1,0:T(8,128)S(1)} %get-tuple-element.74), channel_id=1, source_target_pairs={{0,3},{1,2},{2,1},{3,0},{4,7},{5,6},{6,5},{7,4},{8,11},{9,10},{10,... | collective-permute-start | bytes 393224 | tf_op jit(solution)/shard_map/ppermute | solution.py:311
  78.0 1.6 %collective-permute-start.28 = (f32[8,4096]{1,0:T(8,128)S(1)}, f32[8,4096]{1,0:T(8,128)S(1)}, u32[]{:S(2)}, u32[]{:S(2)}) collective-permute-start(f32[8,4096]{1,0:T(8,128)S(1)} %get-tuple-element.81), channel_id=1, source_target_pairs={{0,1},{1,0},{2,3},{3,2},{4,5},{5,4},{6,7},{7,6},{8,9},{9,8},{10,11... | collective-permute-start | bytes 393224 | tf_op jit(solution)/shard_map/ppermute | solution.py:311
  79.7 6.4 %collective-permute-start.23 = (f32[8,128]{1,0:T(8,128)S(1)}, f32[8,128]{1,0:T(8,128)S(1)}, u32[]{:S(2)}, u32[]{:S(2)}) collective-permute-start(f32[8,128]{1,0:T(8,128)S(1)} %add.16), channel_id=1, source_target_pairs={{0,4},{4,0},{8,12},{12,8},{16,20},{20,16},{24,28},{28,24},{1,5},{5... | collective-permute-start | bytes 12296 | tf_op jit(solution)/shard_map/ppermute | solution.py:311
  86.9 3.0 %collective-permute-start.24 = (f32[8,128]{1,0:T(8,128)S(1)}, f32[8,128]{1,0:T(8,128)S(1)}, u32[]{:S(2)}, u32[]{:S(2)}) collective-permute-start(f32[8,128]{1,0:T(8,128)S(1)} %add.17), channel_id=1, source_target_pairs={{0,8},{4,12},{8,0},{12,4},{16,24},{20,28},{24,16},{28,20},{1,9},{5... | collective-permute-start | bytes 12296 | tf_op jit(solution)/shard_map/ppermute | solution.py:311
  89.9 1.6 %collective-permute-done.24 = f32[8,128]{1,0:T(8,128)S(1)} collective-permute-done((f32[8,128]{1,0:T(8,128)S(1)}, f32[8,128]{1,0:T(8,128)S(1)}, u32[]{:S(2)}, u32[]{:S(2)}) %collective-permute-start.24) | collective-permute-done | bytes 4128 | tf_op jit(solution)/shard_map/ppermute | solution.py:311
  91.5 2.8 %collective-permute-start.25 = (f32[8,128]{1,0:T(8,128)S(1)}, f32[8,128]{1,0:T(8,128)S(1)}, u32[]{:S(2)}, u32[]{:S(2)}) collective-permute-start(f32[8,128]{1,0:T(8,128)S(1)} %add.18), channel_id=1, source_target_pairs={{0,16},{4,20},{8,24},{12,28},{16,0},{20,4},{24,8},{28,12},{1,17},{... | collective-permute-start | bytes 12296 | tf_op jit(solution)/shard_map/ppermute | solution.py:311
  94.3 1.6 %collective-permute-done.25 = f32[8,128]{1,0:T(8,128)S(1)} collective-permute-done((f32[8,128]{1,0:T(8,128)S(1)}, f32[8,128]{1,0:T(8,128)S(1)}, u32[]{:S(2)}, u32[]{:S(2)}) %collective-permute-start.25) | collective-permute-done | bytes 4128 | tf_op jit(solution)/shard_map/ppermute | solution.py:311
  (70 shorter events, 28.3 us)
Async XLA Ops:
  4.1 10.9 %collective-permute-start.2 = (bf16[8,4096]{1,0:T(8,128)(2,1)S(1)}, bf16[8,4096]{1,0:T(8,128)(2,1)S(1)}, u32[]{:S(2)}, u32[]{:S(2)}) collective-permute-start(bf16[8,4096]{1,0:T(8,128)(2,1)S(1)} %get-tuple-element.44.refs_0_), channel_id=1, source_target_pairs={{0,3},{1,2},{2,1},{3,0},{4,7},{5,6},{6,5},{7,4},{8,11},{9,10},{10,... | collective-permute-start | bytes 196616 | tf_op jit(solution)/shard_map/ppermute | solution.py:311
  9.3 5.8 %collective-permute-start.1 = (bf16[8,4096]{1,0:T(8,128)(2,1)S(1)}, bf16[8,4096]{1,0:T(8,128)(2,1)S(1)}, u32[]{:S(2)}, u32[]{:S(2)}) collective-permute-start(bf16[8,4096]{1,0:T(8,128)(2,1)S(1)} %get-tuple-element.44.refs_0_), channel_id=1, source_target_pairs={{0,2},{1,3},{2,0},{3,1},{4,6},{5,7},{6,4},{7,5},{8,10},{9,11},{10,... | collective-permute-start | bytes 196616 | tf_op jit(solution)/shard_map/ppermute | solution.py:311
  9.3 4.3 %collective-permute-start = (bf16[8,4096]{1,0:T(8,128)(2,1)S(1)}, bf16[8,4096]{1,0:T(8,128)(2,1)S(1)}, u32[]{:S(2)}, u32[]{:S(2)}) collective-permute-start(bf16[8,4096]{1,0:T(8,128)(2,1)S(1)} %get-tuple-element.44.refs_0_), channel_id=1, source_target_pairs={{0,1},{1,0},{2,3},{3,2},{4,5},{5,4},{6,7},{7,6},{8,9},{9,8},{10,11... | collective-permute-start | bytes 196616 | tf_op jit(solution)/shard_map/ppermute | solution.py:311
  17.8 15.2 %collective-permute-start.5 = (bf16[8,4096]{1,0:T(8,128)(2,1)S(1)}, bf16[8,4096]{1,0:T(8,128)(2,1)S(1)}, u32[]{:S(2)}, u32[]{:S(2)}) collective-permute-start(bf16[8,4096]{1,0:T(8,128)(2,1)S(1)} %get-tuple-element.50), channel_id=1, source_target_pairs={{0,1},{1,0},{2,3},{3,2},{4,5},{5,4},{6,7},{7,6},{8,9},{9,8},{10,11... | collective-permute-start | bytes 196616 | tf_op jit(solution)/shard_map/ppermute | solution.py:311
  25.1 7.9 %collective-permute-start.6 = (bf16[8,4096]{1,0:T(8,128)(2,1)S(1)}, bf16[8,4096]{1,0:T(8,128)(2,1)S(1)}, u32[]{:S(2)}, u32[]{:S(2)}) collective-permute-start(bf16[8,4096]{1,0:T(8,128)(2,1)S(1)} %get-tuple-element.51), channel_id=1, source_target_pairs={{0,2},{1,3},{2,0},{3,1},{4,6},{5,7},{6,4},{7,5},{8,10},{9,11},{10,... | collective-permute-start | bytes 196616 | tf_op jit(solution)/shard_map/ppermute | solution.py:311
  25.1 7.9 %collective-permute-start.7 = (bf16[8,4096]{1,0:T(8,128)(2,1)S(1)}, bf16[8,4096]{1,0:T(8,128)(2,1)S(1)}, u32[]{:S(2)}, u32[]{:S(2)}) collective-permute-start(bf16[8,4096]{1,0:T(8,128)(2,1)S(1)} %get-tuple-element.52), channel_id=1, source_target_pairs={{0,3},{1,2},{2,1},{3,0},{4,7},{5,6},{6,5},{7,4},{8,11},{9,10},{10,... | collective-permute-start | bytes 196616 | tf_op jit(solution)/shard_map/ppermute | solution.py:311
  33.1 4.3 %collective-permute-start.8 = (bf16[8,4096]{1,0:T(8,128)(2,1)S(1)}, bf16[8,4096]{1,0:T(8,128)(2,1)S(1)}, u32[]{:S(2)}, u32[]{:S(2)}) collective-permute-start(bf16[8,4096]{1,0:T(8,128)(2,1)S(1)} %get-tuple-element.54.refs_0_), channel_id=1, source_target_pairs={{0,1},{1,0},{2,3},{3,2},{4,5},{5,4},{6,7},{7,6},{8,9},{9,8},{10,11... | collective-permute-start | bytes 196616 | tf_op jit(solution)/shard_map/ppermute | solution.py:311
  34.2 6.7 %collective-permute-start.10 = (bf16[8,4096]{1,0:T(8,128)(2,1)S(1)}, bf16[8,4096]{1,0:T(8,128)(2,1)S(1)}, u32[]{:S(2)}, u32[]{:S(2)}) collective-permute-start(bf16[8,4096]{1,0:T(8,128)(2,1)S(1)} %get-tuple-element.54.refs_0_), channel_id=1, source_target_pairs={{0,3},{1,2},{2,1},{3,0},{4,7},{5,6},{6,5},{7,4},{8,11},{9,10},{10,... | collective-permute-start | bytes 196616 | tf_op jit(solution)/shard_map/ppermute | solution.py:311
  35.2 8.2 %collective-permute-start.9 = (bf16[8,4096]{1,0:T(8,128)(2,1)S(1)}, bf16[8,4096]{1,0:T(8,128)(2,1)S(1)}, u32[]{:S(2)}, u32[]{:S(2)}) collective-permute-start(bf16[8,4096]{1,0:T(8,128)(2,1)S(1)} %get-tuple-element.54.refs_0_), channel_id=1, source_target_pairs={{0,2},{1,3},{2,0},{3,1},{4,6},{5,7},{6,4},{7,5},{8,10},{9,11},{10,... | collective-permute-start | bytes 196616 | tf_op jit(solution)/shard_map/ppermute | solution.py:311
  46.6 4.5 %collective-permute-start.13 = (bf16[8,4096]{1,0:T(8,128)(2,1)S(1)}, bf16[8,4096]{1,0:T(8,128)(2,1)S(1)}, u32[]{:S(2)}, u32[]{:S(2)}) collective-permute-start(bf16[8,4096]{1,0:T(8,128)(2,1)S(1)} %get-tuple-element.61), channel_id=1, source_target_pairs={{0,1},{1,0},{2,3},{3,2},{4,5},{5,4},{6,7},{7,6},{8,9},{9,8},{10,11... | collective-permute-start | bytes 196616 | tf_op jit(solution)/shard_map/ppermute | solution.py:311
  48.5 5.5 %collective-permute-start.14 = (bf16[8,4096]{1,0:T(8,128)(2,1)S(1)}, bf16[8,4096]{1,0:T(8,128)(2,1)S(1)}, u32[]{:S(2)}, u32[]{:S(2)}) collective-permute-start(bf16[8,4096]{1,0:T(8,128)(2,1)S(1)} %get-tuple-element.62), channel_id=1, source_target_pairs={{0,2},{1,3},{2,0},{3,1},{4,6},{5,7},{6,4},{7,5},{8,10},{9,11},{10,... | collective-permute-start | bytes 196616 | tf_op jit(solution)/shard_map/ppermute | solution.py:311
  49.6 6.1 %collective-permute-start.15 = (bf16[8,4096]{1,0:T(8,128)(2,1)S(1)}, bf16[8,4096]{1,0:T(8,128)(2,1)S(1)}, u32[]{:S(2)}, u32[]{:S(2)}) collective-permute-start(bf16[8,4096]{1,0:T(8,128)(2,1)S(1)} %get-tuple-element.63), channel_id=1, source_target_pairs={{0,3},{1,2},{2,1},{3,0},{4,7},{5,6},{6,5},{7,4},{8,11},{9,10},{10,... | collective-permute-start | bytes 196616 | tf_op jit(solution)/shard_map/ppermute | solution.py:311
  55.8 4.8 %collective-permute-start.16 = (bf16[8,4096]{1,0:T(8,128)(2,1)S(1)}, bf16[8,4096]{1,0:T(8,128)(2,1)S(1)}, u32[]{:S(2)}, u32[]{:S(2)}) collective-permute-start(bf16[8,4096]{1,0:T(8,128)(2,1)S(1)} %get-tuple-element.65.refs_0_), channel_id=1, source_target_pairs={{0,1},{1,0},{2,3},{3,2},{4,5},{5,4},{6,7},{7,6},{8,9},{9,8},{10,11... | collective-permute-start | bytes 196616 | tf_op jit(solution)/shard_map/ppermute | solution.py:311
  55.8 6.2 %collective-permute-start.18 = (bf16[8,4096]{1,0:T(8,128)(2,1)S(1)}, bf16[8,4096]{1,0:T(8,128)(2,1)S(1)}, u32[]{:S(2)}, u32[]{:S(2)}) collective-permute-start(bf16[8,4096]{1,0:T(8,128)(2,1)S(1)} %get-tuple-element.65.refs_0_), channel_id=1, source_target_pairs={{0,3},{1,2},{2,1},{3,0},{4,7},{5,6},{6,5},{7,4},{8,11},{9,10},{10,... | collective-permute-start | bytes 196616 | tf_op jit(solution)/shard_map/ppermute | solution.py:311
  58.0 5.9 %collective-permute-start.17 = (bf16[8,4096]{1,0:T(8,128)(2,1)S(1)}, bf16[8,4096]{1,0:T(8,128)(2,1)S(1)}, u32[]{:S(2)}, u32[]{:S(2)}) collective-permute-start(bf16[8,4096]{1,0:T(8,128)(2,1)S(1)} %get-tuple-element.65.refs_0_), channel_id=1, source_target_pairs={{0,2},{1,3},{2,0},{3,1},{4,6},{5,7},{6,4},{7,5},{8,10},{9,11},{10,... | collective-permute-start | bytes 196616 | tf_op jit(solution)/shard_map/ppermute | solution.py:311
  64.2 5.0 %collective-permute-start.19 = (bf16[8,4096]{1,0:T(8,128)(2,1)S(1)}, bf16[8,4096]{1,0:T(8,128)(2,1)S(1)}, u32[]{:S(2)}, u32[]{:S(2)}) collective-permute-start(bf16[8,4096]{1,0:T(8,128)(2,1)S(1)} %get-tuple-element.67), channel_id=1, source_target_pairs={{0,4},{4,0},{8,12},{12,8},{16,20},{20,16},{24,28},{28,24},{1,5},{5... | collective-permute-start | bytes 196616 | tf_op jit(solution)/shard_map/ppermute | solution.py:319
  69.7 3.6 %collective-permute-start.21 = (f32[8,128]{1,0:T(8,128)S(1)}, f32[8,128]{1,0:T(8,128)S(1)}, u32[]{:S(2)}, u32[]{:S(2)}) collective-permute-start(f32[8,128]{1,0:T(8,128)S(1)} %get-tuple-element.70), channel_id=1, source_target_pairs={{0,1},{1,0},{2,3},{3,2},{4,5},{5,4},{6,7},{7,6},{8,9},{9,8},{10,11... | collective-permute-start | bytes 12296 | tf_op jit(solution)/shard_map/ppermute | solution.py:311
  73.3 4.7 %collective-permute-start.22 = (f32[8,128]{1,0:T(8,128)S(1)}, f32[8,128]{1,0:T(8,128)S(1)}, u32[]{:S(2)}, u32[]{:S(2)}) collective-permute-start(f32[8,128]{1,0:T(8,128)S(1)} %add.15), channel_id=1, source_target_pairs={{0,2},{1,3},{2,0},{3,1},{4,6},{5,7},{6,4},{7,5},{8,10},{9,11},{10,... | collective-permute-start | bytes 12296 | tf_op jit(solution)/shard_map/ppermute | solution.py:311
  74.6 21.3 %collective-permute-start.26 = (f32[8,4096]{1,0:T(8,128)S(1)}, f32[8,4096]{1,0:T(8,128)S(1)}, u32[]{:S(2)}, u32[]{:S(2)}) collective-permute-start(f32[8,4096]{1,0:T(8,128)S(1)} %get-tuple-element.74), channel_id=1, source_target_pairs={{0,3},{1,2},{2,1},{3,0},{4,7},{5,6},{6,5},{7,4},{8,11},{9,10},{10,... | collective-permute-start | bytes 393224 | tf_op jit(solution)/shard_map/ppermute | solution.py:311
  77.5 18.4 %collective-permute-start.27 = (f32[8,4096]{1,0:T(8,128)S(1)}, f32[8,4096]{1,0:T(8,128)S(1)}, u32[]{:S(2)}, u32[]{:S(2)}) collective-permute-start(f32[8,4096]{1,0:T(8,128)S(1)} %get-tuple-element.78), channel_id=1, source_target_pairs={{0,2},{1,3},{2,0},{3,1},{4,6},{5,7},{6,4},{7,5},{8,10},{9,11},{10,... | collective-permute-start | bytes 393224 | tf_op jit(solution)/shard_map/ppermute | solution.py:311
  78.0 17.9 %collective-permute-start.28 = (f32[8,4096]{1,0:T(8,128)S(1)}, f32[8,4096]{1,0:T(8,128)S(1)}, u32[]{:S(2)}, u32[]{:S(2)}) collective-permute-start(f32[8,4096]{1,0:T(8,128)S(1)} %get-tuple-element.81), channel_id=1, source_target_pairs={{0,1},{1,0},{2,3},{3,2},{4,5},{5,4},{6,7},{7,6},{8,9},{9,8},{10,11... | collective-permute-start | bytes 393224 | tf_op jit(solution)/shard_map/ppermute | solution.py:311
  79.7 7.2 %collective-permute-start.23 = (f32[8,128]{1,0:T(8,128)S(1)}, f32[8,128]{1,0:T(8,128)S(1)}, u32[]{:S(2)}, u32[]{:S(2)}) collective-permute-start(f32[8,128]{1,0:T(8,128)S(1)} %add.16), channel_id=1, source_target_pairs={{0,4},{4,0},{8,12},{12,8},{16,20},{20,16},{24,28},{28,24},{1,5},{5... | collective-permute-start | bytes 12296 | tf_op jit(solution)/shard_map/ppermute | solution.py:311
  86.9 4.6 %collective-permute-start.24 = (f32[8,128]{1,0:T(8,128)S(1)}, f32[8,128]{1,0:T(8,128)S(1)}, u32[]{:S(2)}, u32[]{:S(2)}) collective-permute-start(f32[8,128]{1,0:T(8,128)S(1)} %add.17), channel_id=1, source_target_pairs={{0,8},{4,12},{8,0},{12,4},{16,24},{20,28},{24,16},{28,20},{1,9},{5... | collective-permute-start | bytes 12296 | tf_op jit(solution)/shard_map/ppermute | solution.py:311
  91.5 4.4 %collective-permute-start.25 = (f32[8,128]{1,0:T(8,128)S(1)}, f32[8,128]{1,0:T(8,128)S(1)}, u32[]{:S(2)}, u32[]{:S(2)}) collective-permute-start(f32[8,128]{1,0:T(8,128)S(1)} %add.18), channel_id=1, source_target_pairs={{0,16},{4,20},{8,24},{12,28},{16,0},{20,4},{24,8},{28,12},{1,17},{... | collective-permute-start | bytes 12296 | tf_op jit(solution)/shard_map/ppermute | solution.py:311
  (11 other events, 54.9 us)

commit v6 on v5

--- a/solution.py
+++ b/solution.py
@@ -28,7 +28,15 @@
     return lax.dot_general(field, block, (((1,), (1,)), ((), ())), preferred_element_type=F32)
 
 
-def order_kernel(right_ref, order_ref, curve_ref, rounded_ref):
+def order_kernel(right_in, order_in, curve_ref, rounded_ref, right_ref, order_ref, sems):
+    copies = [
+        pltpu.make_async_copy(right_in, right_ref, sems.at[0]),
+        pltpu.make_async_copy(order_in, order_ref, sems.at[1]),
+    ]
+    for copy in copies:
+        copy.start()
+    for copy in copies:
+        copy.wait()
     rhs_count, points = right_ref.shape
     for start in range(0, points, LANES):
         at = jnp.broadcast_to(order_ref[:, start : start + LANES], (rhs_count, LANES))
@@ -74,8 +82,8 @@
 
     live, source, target = sides(by_row[:, 0:1], by_row[:, 1:2], 0)
     kind = jnp.where(target >= tile_blocks, AHEAD, LATE)
-    first_row = (sub_index // 2) * (2 * blocks_dev)
-    is_early = (source >= first_row) & (source < first_row + 2 * blocks_dev) & (source < tile_blocks)
+    first_own = sub_index * blocks_dev
+    is_early = (source >= first_own) & (source < first_own + blocks_dev)
     kind = jnp.where(is_early, EARLY, kind)
     kind = jnp.where(source >= tile_blocks, FROM_AHEAD, kind)
     kind = jnp.where(live, kind, -1)
@@ -172,12 +180,12 @@
         field[first + block] = piece.astype(F32)
 
 
-def early_kernel(sub_count, slot_count, lists_ref, blocks_ref, diag_ref, noise_ref, own_ref, *refs):
-    row_refs, (total, field) = refs[:-2], refs[-2:]
+def early_kernel(
+    sub_count, slot_count, lists_ref, blocks_ref, diag_ref, noise_ref, own_ref, rounded_ref, total, field
+):
     block_len = blocks_ref.shape[1]
     sub_index, blocks_dev, own_first, _ = device_place(block_len, own_ref, sub_count)
-    for step, row_ref in enumerate(row_refs):
-        lay_out(row_ref, field, (sub_index ^ step) * blocks_dev, block_len)
+    lay_out(rounded_ref, field, own_first, block_len)
     for block in range(total.shape[0]):
         total[block] = jnp.zeros(total.shape[1:], F32)
     for block in range(blocks_dev):
@@ -368,16 +376,28 @@
         ],
     )
     blocks = pair_blocks
-    field, rounded = call(order_kernel, (full, half), (right_side, point_order), "curve_order", 10, in_specs=[VMEM, VMEM])
+    field, rounded = call(
+        order_kernel,
+        (full, half),
+        [pltpu.with_memory_space_constraint(value, pltpu.HBM) for value in (right_side, point_order)],
+        "curve_order",
+        10,
+        in_specs=[pl.BlockSpec(memory_space=pltpu.HBM)] * 2,
+        scratch_shapes=[
+            pltpu.VMEM(right_side.shape, F32),
+            pltpu.VMEM(point_order.shape, jnp.int32),
+            pltpu.SemaphoreType.DMA((2,)),
+        ],
+    )
     basis = [field]
     moments = jnp.zeros(scalars.shape, F32)
     for index in range(ITERS):
         is_last = index + 1 == ITERS
-        rows = [rounded] + [exchange(rounded, "sub", step) for step in range(1, sub_count)]
+        rows = [exchange(rounded, "sub", step) for step in range(1, sub_count)]
         begun = call(
             functools.partial(early_kernel, sub_count, slot_count),
             sums,
-            (lists, blocks, diag_blocks, noise, field, *rows[:2]),
+            (lists, blocks, diag_blocks, noise, field, rounded),
             "early",
             3,
             scratch_shapes=[scratch(extended)],
@@ -385,7 +405,7 @@
         even, odd, tile_field = call(
             functools.partial(ahead_kernel, sub_count, slot_count),
             (half, half, jax.ShapeDtypeStruct((sub_count * blocks_dev, rhs_count, block_len), F32)),
-            (lists, blocks, begun, *rows),
+            (lists, blocks, begun, rounded, *rows),
             "ahead",
             1,
             scratch_shapes=[scratch(blocks_dev + 1)],
@@ -413,7 +433,7 @@
                 4,
                 scratch_shapes=[pltpu.SemaphoreType.DMA(())],
             )
-        arrived = [exchange(parts[step], "sub", step) for step in range(1, sub_count)]
+        arrived = [exchange(parts[step], "sub", step) for step in range(sub_count - 1, 0, -1)]
         field, rounded, moments = call(
             functools.partial(join_kernel, index),
             (full, half, scalars),

time: 97.6 us -> 93.5 us (0.958)
  waiting for transfers between devices: 21.4 us -> 18.6 us
  local copies, waits for them, and re-layouts: 2.24 us -> 0.02 us
  Pallas kernels: 18.3 us -> 19.3 us
    ppermute x23, waiting for transfers between devices: 21.4 us -> 18.6 us  [exchange(): return lax.ppermute(block, axis, [(i, i ^ step) for i in range(count)])]
    ppermute x6, starting transfers between devices: 6.59 us -> 9.16 us  [swap(): return lax.ppermute(block, axis, route)]
    ppermute x23, starting transfers between devices: 47.4 us -> 45.1 us  [exchange(): return lax.ppermute(block, axis, [(i, i ^ step) for i in range(count)])]
    unnamed x12 -> x8, local copies, waits for them, and re-layouts: 2.24 us -> 0.02 us
  transfers between devices with their start and end apart: 29 -> 29, of which waited for: 13 -> 14; matrix products, arithmetic and copies ran while one was open for 0% -> 0% of each run, Pallas kernels for 14% -> 14%
where the time goes in v6:
time: 93.5 us; the launch traced here: 93.1 us
  starting transfers between devices  54.3 us (58%)
  Pallas kernels  19.3 us (21%)
  waiting for transfers between devices  18.6 us (20%)
    ppermute x23, starting transfers between devices, exchange(): return lax.ppermute(block, axis, [(i, i ^ step) for i in range(count)])  45.1 us
    pallas_call x18, Pallas kernels, call(): pl.pallas_call(kernel, out_shape=outs, compiler_params=PARAMS, name=name,...  19.3 us
    ppermute x23, waiting for transfers between devices, exchange(): return lax.ppermute(block, axis, [(i, i ^ step) for i in range(count)])  18.6 us
    ppermute x6, starting transfers between devices, swap(): return lax.ppermute(block, axis, route)  9.16 us
  transfers between devices with their start and end apart: 29, of which 14 were waited for; matrix products, arithmetic and copies ran while one was open for 0% of the time, Pallas kernels for 14%

profile of v6, /device:TPU:0, one launch (start us, length us, event | category | flops | bytes accessed | tf_op | source)
XLA Modules:
  0.0 93.1 jit_solution(2625824243885828174)
XLA Ops:
  0.7 2.3 %curve_order.1 = (f32[8,4096]{1,0:T(8,128)S(1)}, bf16[8,4096]{1,0:T(8,128)(2,1)S(1)}) custom-call(f32[8,4096]{1,0:T(8,128)} %right_in.1, s32[1,4096]{1,0:T(1,128)} %order_in.1), custom_call_target="tpu_custom_call" | custom-call | flops 10000000000 | tf_op jit(solution)/shard_map/curve_order/pallas_call | solution.py:335
  3.0 5.1 %collective-permute-start.2 = (bf16[8,4096]{1,0:T(8,128)(2,1)S(1)}, bf16[8,4096]{1,0:T(8,128)(2,1)S(1)}, u32[]{:S(2)}, u32[]{:S(2)}) collective-permute-start(bf16[8,4096]{1,0:T(8,128)(2,1)S(1)} %get-tuple-element.44.rounded_ref.refs_0_), channel_id=1, source_target_pairs={{0,3},{1,2},{2,1},{3,0},{4,7},{5,6},{6,5},{7,4},{8,11},{9,10},{10,... | collective-permute-start | bytes 196616 | tf_op jit(solution)/shard_map/ppermute | solution.py:319
  11.8 1.9 %collective-permute-done.1.refs_2_ = bf16[8,4096]{1,0:T(8,128)(2,1)S(1)} collective-permute-done((bf16[8,4096]{1,0:T(8,128)(2,1)S(1)}, bf16[8,4096]{1,0:T(8,128)(2,1)S(1)}, u32[]{:S(2)}, u32[]{:S(2)}) %collective-permute-start.1) | collective-permute-done | bytes 65568 | tf_op jit(solution)/shard_map/ppermute | solution.py:319
  14.8 1.8 %late.3.begun_ref = f32[81,8,256]{2,1,0:T(8,128)S(1)} custom-call(s32[1,1280]{1,0:T(1,128)S(4)} %lists.1.lists_ref, bf16[96,256,256]{2,1,0:T(8,128)(2,1)S(1)} %copy-done, f32[81,8,256]{2,1,0:T(8,128)S(1)} %early.3.begun_ref, f32[64,8,256]{2,1,0:T(8,128)S(1)} %get-tuple-element.45.field_ref), custom_call_target="tpu_custom_call" | custom-call | flops 3000000000 | tf_op jit(solution)/shard_map/late/pallas_call | solution.py:335
  17.1 3.9 %collective-permute-start.5 = (bf16[8,4096]{1,0:T(8,128)(2,1)S(1)}, bf16[8,4096]{1,0:T(8,128)(2,1)S(1)}, u32[]{:S(2)}, u32[]{:S(2)}) collective-permute-start(bf16[8,4096]{1,0:T(8,128)(2,1)S(1)} %get-tuple-element.50), channel_id=1, source_target_pairs={{0,3},{1,2},{2,1},{3,0},{4,7},{5,6},{6,5},{7,4},{8,11},{9,10},{10,... | collective-permute-start | bytes 196616 | tf_op jit(solution)/shard_map/ppermute | solution.py:319
  21.0 1.9 %collective-permute-start.6 = (bf16[8,4096]{1,0:T(8,128)(2,1)S(1)}, bf16[8,4096]{1,0:T(8,128)(2,1)S(1)}, u32[]{:S(2)}, u32[]{:S(2)}) collective-permute-start(bf16[8,4096]{1,0:T(8,128)(2,1)S(1)} %get-tuple-element.51), channel_id=1, source_target_pairs={{0,2},{1,3},{2,0},{3,1},{4,6},{5,7},{6,4},{7,5},{8,10},{9,11},{10,... | collective-permute-start | bytes 196616 | tf_op jit(solution)/shard_map/ppermute | solution.py:319
  22.9 5.4 %turn.1.after_ref.blocks_ref = bf16[192,256,256]{2,1,0:T(8,128)(2,1)S(1)} custom-call(bf16[96,256,256]{2,1,0:T(8,128)(2,1)S(1)} %copy-done, f32[8,128]{1,0:T(8,128)S(1)} %get-tuple-element.48.after_ref.moments_in_ref), custom_call_target="tpu_custom_call" | custom-call | flops 4000000000 | tf_op jit(solution)/shard_map/turn/pallas_call | solution.py:335
  28.6 2.4 %collective-permute-start.10 = (bf16[8,4096]{1,0:T(8,128)(2,1)S(1)}, bf16[8,4096]{1,0:T(8,128)(2,1)S(1)}, u32[]{:S(2)}, u32[]{:S(2)}) collective-permute-start(bf16[8,4096]{1,0:T(8,128)(2,1)S(1)} %get-tuple-element.54.rounded_ref.refs_0_), channel_id=1, source_target_pairs={{0,3},{1,2},{2,1},{3,0},{4,7},{5,6},{6,5},{7,4},{8,11},{9,10},{10,... | collective-permute-start | bytes 196616 | tf_op jit(solution)/shard_map/ppermute | solution.py:319
  34.7 3.0 %collective-permute-done.9.refs_2_ = bf16[8,4096]{1,0:T(8,128)(2,1)S(1)} collective-permute-done((bf16[8,4096]{1,0:T(8,128)(2,1)S(1)}, bf16[8,4096]{1,0:T(8,128)(2,1)S(1)}, u32[]{:S(2)}, u32[]{:S(2)}) %collective-permute-start.9) | collective-permute-done | bytes 65568 | tf_op jit(solution)/shard_map/ppermute | solution.py:319
  38.1 1.8 %collective-permute-start.11 = (bf16[8,4096]{1,0:T(8,128)(2,1)S(1)}, bf16[8,4096]{1,0:T(8,128)(2,1)S(1)}, u32[]{:S(2)}, u32[]{:S(2)}) collective-permute-start(bf16[8,4096]{1,0:T(8,128)(2,1)S(1)} %get-tuple-element.56), channel_id=1, source_target_pairs={{0,4},{4,0},{8,12},{12,8},{16,20},{20,16},{24,28},{28,24},{1,5},{5... | collective-permute-start | bytes 196616 | tf_op jit(solution)/shard_map/ppermute | solution.py:327
  41.7 2.5 %collective-permute-start.13 = (bf16[8,4096]{1,0:T(8,128)(2,1)S(1)}, bf16[8,4096]{1,0:T(8,128)(2,1)S(1)}, u32[]{:S(2)}, u32[]{:S(2)}) collective-permute-start(bf16[8,4096]{1,0:T(8,128)(2,1)S(1)} %get-tuple-element.61), channel_id=1, source_target_pairs={{0,3},{1,2},{2,1},{3,0},{4,7},{5,6},{6,5},{7,4},{8,11},{9,10},{10,... | collective-permute-start | bytes 196616 | tf_op jit(solution)/shard_map/ppermute | solution.py:319
  44.3 1.9 %collective-permute-start.14 = (bf16[8,4096]{1,0:T(8,128)(2,1)S(1)}, bf16[8,4096]{1,0:T(8,128)(2,1)S(1)}, u32[]{:S(2)}, u32[]{:S(2)}) collective-permute-start(bf16[8,4096]{1,0:T(8,128)(2,1)S(1)} %get-tuple-element.62), channel_id=1, source_target_pairs={{0,2},{1,3},{2,0},{3,1},{4,6},{5,7},{6,4},{7,5},{8,10},{9,11},{10,... | collective-permute-start | bytes 196616 | tf_op jit(solution)/shard_map/ppermute | solution.py:319
  46.2 1.7 %collective-permute-done.13.refs_0_ = bf16[8,4096]{1,0:T(8,128)(2,1)S(1)} collective-permute-done((bf16[8,4096]{1,0:T(8,128)(2,1)S(1)}, bf16[8,4096]{1,0:T(8,128)(2,1)S(1)}, u32[]{:S(2)}, u32[]{:S(2)}) %collective-permute-start.13) | collective-permute-done | bytes 65568 | tf_op jit(solution)/shard_map/ppermute | solution.py:319
  47.9 2.4 %collective-permute-done.14.refs_1_ = bf16[8,4096]{1,0:T(8,128)(2,1)S(1)} collective-permute-done((bf16[8,4096]{1,0:T(8,128)(2,1)S(1)}, bf16[8,4096]{1,0:T(8,128)(2,1)S(1)}, u32[]{:S(2)}, u32[]{:S(2)}) %collective-permute-start.14) | collective-permute-done | bytes 65568 | tf_op jit(solution)/shard_map/ppermute | solution.py:319
  52.7 2.5 %collective-permute-start.16 = (bf16[8,4096]{1,0:T(8,128)(2,1)S(1)}, bf16[8,4096]{1,0:T(8,128)(2,1)S(1)}, u32[]{:S(2)}, u32[]{:S(2)}) collective-permute-start(bf16[8,4096]{1,0:T(8,128)(2,1)S(1)} %get-tuple-element.65.rounded_ref.refs_0_), channel_id=1, source_target_pairs={{0,1},{1,0},{2,3},{3,2},{4,5},{5,4},{6,7},{7,6},{8,9},{9,8},{10,11... | collective-permute-start | bytes 196616 | tf_op jit(solution)/shard_map/ppermute | solution.py:319
  58.7 5.3 %collective-permute-start.19 = (bf16[8,4096]{1,0:T(8,128)(2,1)S(1)}, bf16[8,4096]{1,0:T(8,128)(2,1)S(1)}, u32[]{:S(2)}, u32[]{:S(2)}) collective-permute-start(bf16[8,4096]{1,0:T(8,128)(2,1)S(1)} %get-tuple-element.67), channel_id=1, source_target_pairs={{0,4},{4,0},{8,12},{12,8},{16,20},{20,16},{24,28},{28,24},{1,5},{5... | collective-permute-start | bytes 196616 | tf_op jit(solution)/shard_map/ppermute | solution.py:327
  66.0 3.0 %collective-permute-start.21 = (f32[8,128]{1,0:T(8,128)S(1)}, f32[8,128]{1,0:T(8,128)S(1)}, u32[]{:S(2)}, u32[]{:S(2)}) collective-permute-start(f32[8,128]{1,0:T(8,128)S(1)} %get-tuple-element.70), channel_id=1, source_target_pairs={{0,1},{1,0},{2,3},{3,2},{4,5},{5,4},{6,7},{7,6},{8,9},{9,8},{10,11... | collective-permute-start | bytes 12296 | tf_op jit(solution)/shard_map/ppermute | solution.py:319
  69.0 1.6 %collective-permute-done.21 = f32[8,128]{1,0:T(8,128)S(1)} collective-permute-done((f32[8,128]{1,0:T(8,128)S(1)}, f32[8,128]{1,0:T(8,128)S(1)}, u32[]{:S(2)}, u32[]{:S(2)}) %collective-permute-start.21) | collective-permute-done | bytes 4128 | tf_op jit(solution)/shard_map/ppermute | solution.py:319
  70.6 1.9 %collective-permute-start.22 = (f32[8,128]{1,0:T(8,128)S(1)}, f32[8,128]{1,0:T(8,128)S(1)}, u32[]{:S(2)}, u32[]{:S(2)}) collective-permute-start(f32[8,128]{1,0:T(8,128)S(1)} %add.15), channel_id=1, source_target_pairs={{0,2},{1,3},{2,0},{3,1},{4,6},{5,7},{6,4},{7,5},{8,10},{9,11},{10,... | collective-permute-start | bytes 12296 | tf_op jit(solution)/shard_map/ppermute | solution.py:319
  72.6 2.4 %collective-permute-start.26 = (f32[8,4096]{1,0:T(8,128)S(1)}, f32[8,4096]{1,0:T(8,128)S(1)}, u32[]{:S(2)}, u32[]{:S(2)}) collective-permute-start(f32[8,4096]{1,0:T(8,128)S(1)} %get-tuple-element.74), channel_id=1, source_target_pairs={{0,3},{1,2},{2,1},{3,0},{4,7},{5,6},{6,5},{7,4},{8,11},{9,10},{10,... | collective-permute-start | bytes 393224 | tf_op jit(solution)/shard_map/ppermute | solution.py:319
  75.1 2.1 %collective-permute-start.28 = (f32[8,4096]{1,0:T(8,128)S(1)}, f32[8,4096]{1,0:T(8,128)S(1)}, u32[]{:S(2)}, u32[]{:S(2)}) collective-permute-start(f32[8,4096]{1,0:T(8,128)S(1)} %get-tuple-element.81), channel_id=1, source_target_pairs={{0,1},{1,0},{2,3},{3,2},{4,5},{5,4},{6,7},{7,6},{8,9},{9,8},{10,11... | collective-permute-start | bytes 393224 | tf_op jit(solution)/shard_map/ppermute | solution.py:319
  77.3 3.8 %collective-permute-start.23 = (f32[8,128]{1,0:T(8,128)S(1)}, f32[8,128]{1,0:T(8,128)S(1)}, u32[]{:S(2)}, u32[]{:S(2)}) collective-permute-start(f32[8,128]{1,0:T(8,128)S(1)} %add.16), channel_id=1, source_target_pairs={{0,4},{4,0},{8,12},{12,8},{16,20},{20,16},{24,28},{28,24},{1,5},{5... | collective-permute-start | bytes 12296 | tf_op jit(solution)/shard_map/ppermute | solution.py:319
  81.9 2.8 %collective-permute-start.24 = (f32[8,128]{1,0:T(8,128)S(1)}, f32[8,128]{1,0:T(8,128)S(1)}, u32[]{:S(2)}, u32[]{:S(2)}) collective-permute-start(f32[8,128]{1,0:T(8,128)S(1)} %add.17), channel_id=1, source_target_pairs={{0,8},{4,12},{8,0},{12,4},{16,24},{20,28},{24,16},{28,20},{1,9},{5... | collective-permute-start | bytes 12296 | tf_op jit(solution)/shard_map/ppermute | solution.py:319
  86.3 4.3 %collective-permute-start.25 = (f32[8,128]{1,0:T(8,128)S(1)}, f32[8,128]{1,0:T(8,128)S(1)}, u32[]{:S(2)}, u32[]{:S(2)}) collective-permute-start(f32[8,128]{1,0:T(8,128)S(1)} %add.18), channel_id=1, source_target_pairs={{0,16},{4,20},{8,24},{12,28},{16,0},{20,4},{24,8},{28,12},{1,17},{... | collective-permute-start | bytes 12296 | tf_op jit(solution)/shard_map/ppermute | solution.py:319
  (66 shorter events, 24.4 us)
Async XLA Ops:
  3.0 8.8 %collective-permute-start.2 = (bf16[8,4096]{1,0:T(8,128)(2,1)S(1)}, bf16[8,4096]{1,0:T(8,128)(2,1)S(1)}, u32[]{:S(2)}, u32[]{:S(2)}) collective-permute-start(bf16[8,4096]{1,0:T(8,128)(2,1)S(1)} %get-tuple-element.44.rounded_ref.refs_0_), channel_id=1, source_target_pairs={{0,3},{1,2},{2,1},{3,0},{4,7},{5,6},{6,5},{7,4},{8,11},{9,10},{10,... | collective-permute-start | bytes 196616 | tf_op jit(solution)/shard_map/ppermute | solution.py:319
  8.1 5.6 %collective-permute-start.1 = (bf16[8,4096]{1,0:T(8,128)(2,1)S(1)}, bf16[8,4096]{1,0:T(8,128)(2,1)S(1)}, u32[]{:S(2)}, u32[]{:S(2)}) collective-permute-start(bf16[8,4096]{1,0:T(8,128)(2,1)S(1)} %get-tuple-element.44.rounded_ref.refs_0_), channel_id=1, source_target_pairs={{0,2},{1,3},{2,0},{3,1},{4,6},{5,7},{6,4},{7,5},{8,10},{9,11},{10,... | collective-permute-start | bytes 196616 | tf_op jit(solution)/shard_map/ppermute | solution.py:319
  8.1 5.6 %collective-permute-start = (bf16[8,4096]{1,0:T(8,128)(2,1)S(1)}, bf16[8,4096]{1,0:T(8,128)(2,1)S(1)}, u32[]{:S(2)}, u32[]{:S(2)}) collective-permute-start(bf16[8,4096]{1,0:T(8,128)(2,1)S(1)} %get-tuple-element.44.rounded_ref.refs_0_), channel_id=1, source_target_pairs={{0,1},{1,0},{2,3},{3,2},{4,5},{5,4},{6,7},{7,6},{8,9},{9,8},{10,11... | collective-permute-start | bytes 196616 | tf_op jit(solution)/shard_map/ppermute | solution.py:319
  17.1 11.2 %collective-permute-start.5 = (bf16[8,4096]{1,0:T(8,128)(2,1)S(1)}, bf16[8,4096]{1,0:T(8,128)(2,1)S(1)}, u32[]{:S(2)}, u32[]{:S(2)}) collective-permute-start(bf16[8,4096]{1,0:T(8,128)(2,1)S(1)} %get-tuple-element.50), channel_id=1, source_target_pairs={{0,3},{1,2},{2,1},{3,0},{4,7},{5,6},{6,5},{7,4},{8,11},{9,10},{10,... | collective-permute-start | bytes 196616 | tf_op jit(solution)/shard_map/ppermute | solution.py:319
  21.0 7.3 %collective-permute-start.6 = (bf16[8,4096]{1,0:T(8,128)(2,1)S(1)}, bf16[8,4096]{1,0:T(8,128)(2,1)S(1)}, u32[]{:S(2)}, u32[]{:S(2)}) collective-permute-start(bf16[8,4096]{1,0:T(8,128)(2,1)S(1)} %get-tuple-element.51), channel_id=1, source_target_pairs={{0,2},{1,3},{2,0},{3,1},{4,6},{5,7},{6,4},{7,5},{8,10},{9,11},{10,... | collective-permute-start | bytes 196616 | tf_op jit(solution)/shard_map/ppermute | solution.py:319
  22.9 5.5 %collective-permute-start.7 = (bf16[8,4096]{1,0:T(8,128)(2,1)S(1)}, bf16[8,4096]{1,0:T(8,128)(2,1)S(1)}, u32[]{:S(2)}, u32[]{:S(2)}) collective-permute-start(bf16[8,4096]{1,0:T(8,128)(2,1)S(1)} %get-tuple-element.52), channel_id=1, source_target_pairs={{0,1},{1,0},{2,3},{3,2},{4,5},{5,4},{6,7},{7,6},{8,9},{9,8},{10,11... | collective-permute-start | bytes 196616 | tf_op jit(solution)/shard_map/ppermute | solution.py:319
  28.6 6.2 %collective-permute-start.10 = (bf16[8,4096]{1,0:T(8,128)(2,1)S(1)}, bf16[8,4096]{1,0:T(8,128)(2,1)S(1)}, u32[]{:S(2)}, u32[]{:S(2)}) collective-permute-start(bf16[8,4096]{1,0:T(8,128)(2,1)S(1)} %get-tuple-element.54.rounded_ref.refs_0_), channel_id=1, source_target_pairs={{0,3},{1,2},{2,1},{3,0},{4,7},{5,6},{6,5},{7,4},{8,11},{9,10},{10,... | collective-permute-start | bytes 196616 | tf_op jit(solution)/shard_map/ppermute | solution.py:319
  31.0 6.8 %collective-permute-start.9 = (bf16[8,4096]{1,0:T(8,128)(2,1)S(1)}, bf16[8,4096]{1,0:T(8,128)(2,1)S(1)}, u32[]{:S(2)}, u32[]{:S(2)}) collective-permute-start(bf16[8,4096]{1,0:T(8,128)(2,1)S(1)} %get-tuple-element.54.rounded_ref.refs_0_), channel_id=1, source_target_pairs={{0,2},{1,3},{2,0},{3,1},{4,6},{5,7},{6,4},{7,5},{8,10},{9,11},{10,... | collective-permute-start | bytes 196616 | tf_op jit(solution)/shard_map/ppermute | solution.py:319
  32.0 5.8 %collective-permute-start.8 = (bf16[8,4096]{1,0:T(8,128)(2,1)S(1)}, bf16[8,4096]{1,0:T(8,128)(2,1)S(1)}, u32[]{:S(2)}, u32[]{:S(2)}) collective-permute-start(bf16[8,4096]{1,0:T(8,128)(2,1)S(1)} %get-tuple-element.54.rounded_ref.refs_0_), channel_id=1, source_target_pairs={{0,1},{1,0},{2,3},{3,2},{4,5},{5,4},{6,7},{7,6},{8,9},{9,8},{10,11... | collective-permute-start | bytes 196616 | tf_op jit(solution)/shard_map/ppermute | solution.py:319
  41.7 6.1 %collective-permute-start.13 = (bf16[8,4096]{1,0:T(8,128)(2,1)S(1)}, bf16[8,4096]{1,0:T(8,128)(2,1)S(1)}, u32[]{:S(2)}, u32[]{:S(2)}) collective-permute-start(bf16[8,4096]{1,0:T(8,128)(2,1)S(1)} %get-tuple-element.61), channel_id=1, source_target_pairs={{0,3},{1,2},{2,1},{3,0},{4,7},{5,6},{6,5},{7,4},{8,11},{9,10},{10,... | collective-permute-start | bytes 196616 | tf_op jit(solution)/shard_map/ppermute | solution.py:319
  44.3 6.0 %collective-permute-start.14 = (bf16[8,4096]{1,0:T(8,128)(2,1)S(1)}, bf16[8,4096]{1,0:T(8,128)(2,1)S(1)}, u32[]{:S(2)}, u32[]{:S(2)}) collective-permute-start(bf16[8,4096]{1,0:T(8,128)(2,1)S(1)} %get-tuple-element.62), channel_id=1, source_target_pairs={{0,2},{1,3},{2,0},{3,1},{4,6},{5,7},{6,4},{7,5},{8,10},{9,11},{10,... | collective-permute-start | bytes 196616 | tf_op jit(solution)/shard_map/ppermute | solution.py:319
  46.1 4.6 %collective-permute-start.15 = (bf16[8,4096]{1,0:T(8,128)(2,1)S(1)}, bf16[8,4096]{1,0:T(8,128)(2,1)S(1)}, u32[]{:S(2)}, u32[]{:S(2)}) collective-permute-start(bf16[8,4096]{1,0:T(8,128)(2,1)S(1)} %get-tuple-element.63), channel_id=1, source_target_pairs={{0,1},{1,0},{2,3},{3,2},{4,5},{5,4},{6,7},{7,6},{8,9},{9,8},{10,11... | collective-permute-start | bytes 196616 | tf_op jit(solution)/shard_map/ppermute | solution.py:319
  50.8 6.1 %collective-permute-start.18 = (bf16[8,4096]{1,0:T(8,128)(2,1)S(1)}, bf16[8,4096]{1,0:T(8,128)(2,1)S(1)}, u32[]{:S(2)}, u32[]{:S(2)}) collective-permute-start(bf16[8,4096]{1,0:T(8,128)(2,1)S(1)} %get-tuple-element.65.rounded_ref.refs_0_), channel_id=1, source_target_pairs={{0,3},{1,2},{2,1},{3,0},{4,7},{5,6},{6,5},{7,4},{8,11},{9,10},{10,... | collective-permute-start | bytes 196616 | tf_op jit(solution)/shard_map/ppermute | solution.py:319
  52.0 6.3 %collective-permute-start.17 = (bf16[8,4096]{1,0:T(8,128)(2,1)S(1)}, bf16[8,4096]{1,0:T(8,128)(2,1)S(1)}, u32[]{:S(2)}, u32[]{:S(2)}) collective-permute-start(bf16[8,4096]{1,0:T(8,128)(2,1)S(1)} %get-tuple-element.65.rounded_ref.refs_0_), channel_id=1, source_target_pairs={{0,2},{1,3},{2,0},{3,1},{4,6},{5,7},{6,4},{7,5},{8,10},{9,11},{10,... | collective-permute-start | bytes 196616 | tf_op jit(solution)/shard_map/ppermute | solution.py:319
  52.7 5.6 %collective-permute-start.16 = (bf16[8,4096]{1,0:T(8,128)(2,1)S(1)}, bf16[8,4096]{1,0:T(8,128)(2,1)S(1)}, u32[]{:S(2)}, u32[]{:S(2)}) collective-permute-start(bf16[8,4096]{1,0:T(8,128)(2,1)S(1)} %get-tuple-element.65.rounded_ref.refs_0_), channel_id=1, source_target_pairs={{0,1},{1,0},{2,3},{3,2},{4,5},{5,4},{6,7},{7,6},{8,9},{9,8},{10,11... | collective-permute-start | bytes 196616 | tf_op jit(solution)/shard_map/ppermute | solution.py:319
  58.7 6.8 %collective-permute-start.19 = (bf16[8,4096]{1,0:T(8,128)(2,1)S(1)}, bf16[8,4096]{1,0:T(8,128)(2,1)S(1)}, u32[]{:S(2)}, u32[]{:S(2)}) collective-permute-start(bf16[8,4096]{1,0:T(8,128)(2,1)S(1)} %get-tuple-element.67), channel_id=1, source_target_pairs={{0,4},{4,0},{8,12},{12,8},{16,20},{20,16},{24,28},{28,24},{1,5},{5... | collective-permute-start | bytes 196616 | tf_op jit(solution)/shard_map/ppermute | solution.py:327
  66.0 4.6 %collective-permute-start.21 = (f32[8,128]{1,0:T(8,128)S(1)}, f32[8,128]{1,0:T(8,128)S(1)}, u32[]{:S(2)}, u32[]{:S(2)}) collective-permute-start(f32[8,128]{1,0:T(8,128)S(1)} %get-tuple-element.70), channel_id=1, source_target_pairs={{0,1},{1,0},{2,3},{3,2},{4,5},{5,4},{6,7},{7,6},{8,9},{9,8},{10,11... | collective-permute-start | bytes 12296 | tf_op jit(solution)/shard_map/ppermute | solution.py:319
  70.6 4.5 %collective-permute-start.22 = (f32[8,128]{1,0:T(8,128)S(1)}, f32[8,128]{1,0:T(8,128)S(1)}, u32[]{:S(2)}, u32[]{:S(2)}) collective-permute-start(f32[8,128]{1,0:T(8,128)S(1)} %add.15), channel_id=1, source_target_pairs={{0,2},{1,3},{2,0},{3,1},{4,6},{5,7},{6,4},{7,5},{8,10},{9,11},{10,... | collective-permute-start | bytes 12296 | tf_op jit(solution)/shard_map/ppermute | solution.py:319
  72.6 19.6 %collective-permute-start.26 = (f32[8,4096]{1,0:T(8,128)S(1)}, f32[8,4096]{1,0:T(8,128)S(1)}, u32[]{:S(2)}, u32[]{:S(2)}) collective-permute-start(f32[8,4096]{1,0:T(8,128)S(1)} %get-tuple-element.74), channel_id=1, source_target_pairs={{0,3},{1,2},{2,1},{3,0},{4,7},{5,6},{6,5},{7,4},{8,11},{9,10},{10,... | collective-permute-start | bytes 393224 | tf_op jit(solution)/shard_map/ppermute | solution.py:319
  75.0 17.1 %collective-permute-start.27 = (f32[8,4096]{1,0:T(8,128)S(1)}, f32[8,4096]{1,0:T(8,128)S(1)}, u32[]{:S(2)}, u32[]{:S(2)}) collective-permute-start(f32[8,4096]{1,0:T(8,128)S(1)} %get-tuple-element.78), channel_id=1, source_target_pairs={{0,2},{1,3},{2,0},{3,1},{4,6},{5,7},{6,4},{7,5},{8,10},{9,11},{10,... | collective-permute-start | bytes 393224 | tf_op jit(solution)/shard_map/ppermute | solution.py:319
  75.1 17.0 %collective-permute-start.28 = (f32[8,4096]{1,0:T(8,128)S(1)}, f32[8,4096]{1,0:T(8,128)S(1)}, u32[]{:S(2)}, u32[]{:S(2)}) collective-permute-start(f32[8,4096]{1,0:T(8,128)S(1)} %get-tuple-element.81), channel_id=1, source_target_pairs={{0,1},{1,0},{2,3},{3,2},{4,5},{5,4},{6,7},{7,6},{8,9},{9,8},{10,11... | collective-permute-start | bytes 393224 | tf_op jit(solution)/shard_map/ppermute | solution.py:319
  77.3 4.6 %collective-permute-start.23 = (f32[8,128]{1,0:T(8,128)S(1)}, f32[8,128]{1,0:T(8,128)S(1)}, u32[]{:S(2)}, u32[]{:S(2)}) collective-permute-start(f32[8,128]{1,0:T(8,128)S(1)} %add.16), channel_id=1, source_target_pairs={{0,4},{4,0},{8,12},{12,8},{16,20},{20,16},{24,28},{28,24},{1,5},{5... | collective-permute-start | bytes 12296 | tf_op jit(solution)/shard_map/ppermute | solution.py:319
  81.9 4.4 %collective-permute-start.24 = (f32[8,128]{1,0:T(8,128)S(1)}, f32[8,128]{1,0:T(8,128)S(1)}, u32[]{:S(2)}, u32[]{:S(2)}) collective-permute-start(f32[8,128]{1,0:T(8,128)S(1)} %add.17), channel_id=1, source_target_pairs={{0,8},{4,12},{8,0},{12,4},{16,24},{20,28},{24,16},{28,20},{1,9},{5... | collective-permute-start | bytes 12296 | tf_op jit(solution)/shard_map/ppermute | solution.py:319
  86.3 5.8 %collective-permute-start.25 = (f32[8,128]{1,0:T(8,128)S(1)}, f32[8,128]{1,0:T(8,128)S(1)}, u32[]{:S(2)}, u32[]{:S(2)}) collective-permute-start(f32[8,128]{1,0:T(8,128)S(1)} %add.18), channel_id=1, source_target_pairs={{0,16},{4,20},{8,24},{12,28},{16,0},{20,4},{24,8},{28,12},{1,17},{... | collective-permute-start | bytes 12296 | tf_op jit(solution)/shard_map/ppermute | solution.py:319
  (9 other events, 48.3 us)

commit v7 on v6

--- a/solution.py
+++ b/solution.py
@@ -174,18 +174,36 @@
         add_part(column_count, count, times_transposed, True, False)
 
 
-def lay_out(row_ref, field, first, block_len):
-    for block in range(row_ref.shape[1] // block_len):
-        piece = row_ref[:, block * block_len : (block + 1) * block_len]
-        field[first + block] = piece.astype(F32)
+def raised(value, exponent):
+    result = value
+    for _ in range(exponent - 1):
+        result = result * value
+    return result
+
+
+def widen(tile, columns):
+    return jnp.concatenate([tile] * (columns // LANES), axis=1)
+
+
+def lay_out(row_ref, field, first, blocks_dev, block_len, factor=None):
+    for block in range(blocks_dev):
+        piece = row_ref[:, block * block_len : (block + 1) * block_len].astype(F32)
+        field[first + block] = piece if factor is None else piece * factor
 
 
 def early_kernel(
-    sub_count, slot_count, lists_ref, blocks_ref, diag_ref, noise_ref, own_ref, rounded_ref, total, field
+    index, sub_count, slot_count, lists_ref, blocks_ref, diag_ref, noise_ref, own_ref, rounded_ref, total,
+    *refs
 ):
+    field = refs[-1]
     block_len = blocks_ref.shape[1]
     sub_index, blocks_dev, own_first, _ = device_place(block_len, own_ref, sub_count)
-    lay_out(rounded_ref, field, own_first, block_len)
+    if index == 0:
+        largest = diag_ref[0].astype(F32)
+        for block in range(1, blocks_dev):
+            largest = jnp.maximum(largest, diag_ref[block].astype(F32))
+        refs[0][...] = jnp.full(refs[0].shape, jnp.maximum(jnp.max(largest), 1.0))
+    lay_out(rounded_ref, field, own_first, blocks_dev, block_len)
     for block in range(total.shape[0]):
         total[block] = jnp.zeros(total.shape[1:], F32)
     for block in range(blocks_dev):
@@ -195,15 +213,31 @@
     add_products(lists_ref, blocks_ref, slot_count, field, total, EARLY, LONG_GROUP)
 
 
-def ahead_kernel(sub_count, slot_count, lists_ref, blocks_ref, begun_ref, *refs):
-    row_refs = refs[:sub_count]
-    even_ref, odd_ref, field_ref, total = refs[sub_count:]
+def ahead_kernel(index, sub_count, slot_count, lists_ref, blocks_ref, begun_ref, *refs):
+    if index == 1:
+        *refs, ratios_ref, total = refs
+        row_refs, (even_ref, odd_ref, field_ref) = refs[:-3], refs[-3:]
+        points_dev = even_ref.shape[1] - LANES
+        units = [row_ref[:, points_dev:].astype(F32) for row_ref in row_refs]
+        tile_unit = functools.reduce(jnp.maximum, units)
+        ratios = [unit / tile_unit for unit in units]
+        ratios_ref[...] = jnp.concatenate(ratios + [tile_unit], axis=1)
+    else:
+        row_refs, (even_ref, odd_ref, field_ref, total) = refs[:-4], refs[-4:]
+        points_dev = even_ref.shape[1]
+        if index:
+            ratios_ref, *row_refs = row_refs
+            ratios = [ratios_ref[:, step * LANES : (step + 1) * LANES] for step in range(sub_count)]
     block_len = blocks_ref.shape[1]
-    sub_index, blocks_dev, _, tile_blocks = device_place(block_len, even_ref, sub_count)
+    blocks_dev = points_dev // block_len
+    tile_blocks = blocks_dev * sub_count
+    sub_index = lax.axis_index("sub")
     for step, row_ref in enumerate(row_refs):
-        lay_out(row_ref, field_ref, (sub_index ^ step) * blocks_dev, block_len)
+        factor = widen(raised(ratios[step], index), block_len) if index else None
+        lay_out(row_ref, field_ref, (sub_index ^ step) * blocks_dev, blocks_dev, block_len, factor)
     for block in range(blocks_dev):
-        total[block] = begun_ref[tile_blocks + block]
+        value = begun_ref[tile_blocks + block]
+        total[block] = value * widen(raised(ratios[0], index), block_len) if index else value
     total[blocks_dev] = jnp.zeros(total.shape[1:], F32)
     add_products(lists_ref, blocks_ref, slot_count, field_ref, total, AHEAD, SHORT_GROUP, 0, tile_blocks)
     is_odd = lax.axis_index("tile") % 2 == 1
@@ -213,28 +247,56 @@
         first_row = field_ref[block]
         even_ref[:, span] = jnp.where(is_odd, first_row, products).astype(BF16)
         odd_ref[:, span] = jnp.where(is_odd, products, first_row).astype(BF16)
-
-
-def late_kernel(slot_count, lists_ref, blocks_ref, begun_ref, field_ref, total):
-    total[...] = begun_ref[...]
+    if index == 1:
+        even_ref[:, points_dev:] = tile_unit.astype(BF16)
+        odd_ref[:, points_dev:] = tile_unit.astype(BF16)
+
+
+def late_kernel(index, slot_count, lists_ref, blocks_ref, begun_ref, field_ref, *refs):
+    total = refs[-1]
+    if index:
+        factor = widen(raised(refs[0][:, :LANES], index), total.shape[2])
+        for block in range(total.shape[0]):
+            total[block] = begun_ref[block] * factor
+    else:
+        total[...] = begun_ref[...]
     add_products(lists_ref, blocks_ref, slot_count, field_ref, total, LATE, LONG_GROUP)
 
 
 def part_kernel(
-    sub_count, slot_count, is_last, lists_ref, blocks_ref, begun_ref, field_ref, even_ref, odd_ref,
-    moments_in_ref, *refs
+    index, sub_count, slot_count, lists_ref, blocks_ref, begun_ref, field_ref, even_ref, odd_ref,
+    moments_in_ref, unit_ref, *refs
 ):
-    part_refs = refs[:sub_count]
-    moments_ref, total, ahead = refs[sub_count:]
+    if index == 1:
+        ratios_ref, *refs = refs
+        *refs, sides_ref, total, ahead = refs
+    else:
+        if index:
+            ratios_ref, sides_ref, *refs = refs
+        *refs, total, ahead = refs
+    part_refs, moments_ref = refs[:-1], refs[-1]
     block_len = blocks_ref.shape[1]
-    sub_index, blocks_dev, own_first, tile_blocks = device_place(block_len, even_ref, sub_count)
+    sub_index, blocks_dev, own_first, tile_blocks = device_place(block_len, part_refs[0], sub_count)
     is_odd = lax.axis_index("tile") % 2 == 1
+    if index == 1:
+        points_dev = blocks_dev * block_len
+        even = even_ref[:, points_dev:].astype(F32)
+        odd = odd_ref[:, points_dev:].astype(F32)
+        tile_unit = ratios_ref[:, sub_count * LANES :]
+        sides = [jnp.where(is_odd, even, odd) / tile_unit, jnp.where(is_odd, odd, even) / tile_unit]
+        sides_ref[...] = jnp.concatenate(sides, axis=1)
+    elif index:
+        sides = [sides_ref[:, :LANES], sides_ref[:, LANES:]]
+    if index:
+        before, after = [widen(raised(side, index), block_len) for side in sides]
     for block in range(blocks_dev):
         span = slice(block * block_len, (block + 1) * block_len)
         even = even_ref[:, span].astype(F32)
         odd = odd_ref[:, span].astype(F32)
-        ahead[block] = jnp.where(is_odd, odd, even)
-        total[block] = begun_ref[block] + jnp.where(is_odd, even, odd)
+        products = jnp.where(is_odd, even, odd)
+        first_row = jnp.where(is_odd, odd, even)
+        ahead[block] = first_row * after if index else first_row
+        total[block] = begun_ref[block] + (products * before if index else products)
     for block in range(blocks_dev, tile_blocks):
         total[block] = begun_ref[block]
     total[begun_ref.shape[0] - 1] = jnp.zeros(total.shape[1:], F32)
@@ -245,23 +307,33 @@
             span = slice(block * block_len, (block + 1) * block_len)
             part_refs[step][:, span] = total[first + block].astype(part_refs[step].dtype)
     moments = moments_in_ref[...]
-    if is_last:
+    if index + 1 == ITERS:
         product = jnp.zeros(total.shape[1:], F32)
         for block in range(tile_blocks):
             product += field_ref[block] * total[block]
+        last = jnp.sum(product, axis=1, keepdims=True)
+        unit = unit_ref[...]
+        last = last / (raised(ratios_ref[:, :LANES], 2 * index) * unit)
         lane = lax.broadcasted_iota(jnp.int32, moments.shape, 1)
-        moments = jnp.where(lane == 2 * ITERS - 1, jnp.sum(product, axis=1, keepdims=True), moments)
+        moments = jnp.where(lane == 2 * ITERS - 1, last, moments)
+        moments = jnp.where(lane == 2 * ITERS, unit, moments)
     moments_ref[...] = moments
 
 
-def join_kernel(index, after_ref, own_ref, old_ref, moments_in_ref, *refs):
+def join_kernel(index, after_ref, unit_ref, ratios_ref, own_ref, old_ref, moments_in_ref, *refs):
     part_refs = refs[:-3]
     next_ref, rounded_ref, moments_ref = refs[-3:]
+    points_dev = own_ref.shape[1]
     value = own_ref[...]
     for part_ref in part_refs:
         value += part_ref[...].astype(F32)
+    unit = unit_ref[...]
+    divisor = raised(ratios_ref[:, :LANES], index) * unit if index else unit
+    value = value * widen(1.0 / divisor, points_dev)
     next_ref[...] = value
-    rounded_ref[...] = value.astype(BF16)
+    rounded_ref[:, :points_dev] = value.astype(BF16)
+    if index == 0:
+        rounded_ref[:, points_dev:] = unit.astype(BF16)
     old = old_ref[...]
     lane = lax.broadcasted_iota(jnp.int32, moments_ref.shape, 1)
     moments = moments_in_ref[...] if index else jnp.zeros(moments_ref.shape, F32)
@@ -273,10 +345,28 @@
     moments_ref[...] = moments
 
 
-def finish_kernel(sub_count, moments_ref, *refs):
+def add_moments_kernel(first_ref, second_ref, sum_ref):
+    unit_lane = 2 * ITERS
+    lane = lax.broadcasted_iota(jnp.int32, sum_ref.shape, 1)
+    units = [ref[:, unit_lane : unit_lane + 1] for ref in (first_ref, second_ref)]
+    larger = jnp.maximum(units[0], units[1])
+    result = jnp.zeros(sum_ref.shape, F32)
+    for ref, unit in zip((first_ref, second_ref), units):
+        ratio = unit / larger
+        value = ref[...]
+        for order in range(1, unit_lane):
+            value = jnp.where(lane >= order, value * ratio, value)
+        result += value
+    sum_ref[...] = jnp.where(lane == unit_lane, larger, result)
+
+
+def finish_kernel(sub_count, moments_ref, unit_ref, ratios_ref, *refs):
     part_refs, basis_refs = refs[:sub_count], refs[sub_count:-2]
     solution_ref, residual_ref = refs[-2:]
     moments = [moments_ref[:, order : order + 1] for order in range(2 * ITERS)]
+    largest = moments_ref[:, 2 * ITERS : 2 * ITERS + 1]
+    unit = unit_ref[:, :1]
+    ratio = unit / largest
 
     def inner(first, second, shift):
         value = 0.0
@@ -306,6 +396,14 @@
             norm_now = norm_next
     fields = [basis_ref[...] for basis_ref in basis_refs]
     fields.append(sum(part_ref[...].astype(F32) for part_ref in part_refs))
+    for order in range(1, ITERS + 1):
+        scale = raised(ratio, order)
+        if order < ITERS:
+            answer[order] = answer[order] * scale
+        else:
+            scale = scale / (raised(ratios_ref[:, :1], ITERS - 1) * unit)
+        residual[order] = residual[order] * scale
+    answer = [weight / largest for weight in answer]
     solution_ref[...] = sum(weight * field for weight, field in zip(answer, fields))
     residual_ref[...] = sum(weight * field for weight, field in zip(residual, fields))
 
@@ -390,38 +488,57 @@
         ],
     )
     basis = [field]
-    moments = jnp.zeros(scalars.shape, F32)
+    moments = unit = jnp.zeros(scalars.shape, F32)
+    ratios = sides = ()
     for index in range(ITERS):
         is_last = index + 1 == ITERS
         rows = [exchange(rounded, "sub", step) for step in range(1, sub_count)]
         begun = call(
-            functools.partial(early_kernel, sub_count, slot_count),
-            sums,
+            functools.partial(early_kernel, index, sub_count, slot_count),
+            (sums,) if index else (sums, scalars),
             (lists, blocks, diag_blocks, noise, field, rounded),
             "early",
             3,
             scratch_shapes=[scratch(extended)],
         )
-        even, odd, tile_field = call(
-            functools.partial(ahead_kernel, sub_count, slot_count),
-            (half, half, jax.ShapeDtypeStruct((sub_count * blocks_dev, rhs_count, block_len), F32)),
-            (lists, blocks, begun, rounded, *rows),
+        if index == 0:
+            begun, unit = begun
+        else:
+            (begun,) = begun
+        message = shape(rhs_count, points_dev + LANES, BF16) if index == 1 else half
+        even, odd, tile_field, *found = call(
+            functools.partial(ahead_kernel, index, sub_count, slot_count),
+            (message, message, jax.ShapeDtypeStruct((sub_count * blocks_dev, rhs_count, block_len), F32))
+            + ((shape(rhs_count, (sub_count + 1) * LANES, F32),) if index == 1 else ()),
+            (lists, blocks, begun, *ratios, rounded, *rows),
             "ahead",
             1,
             scratch_shapes=[scratch(blocks_dev + 1)],
         )
+        ratios = ratios or tuple(found)
         even = swap(even, "tile", 0)
         odd = swap(odd, "tile", 1)
-        begun = call(functools.partial(late_kernel, slot_count), sums, (lists, blocks, begun, tile_field), "late", 3)
+        begun = call(
+            functools.partial(late_kernel, index, slot_count),
+            sums,
+            (lists, blocks, begun, tile_field, *ratios),
+            "late",
+            3,
+        )
         part = shape(rhs_count, points_dev, F32 if is_last else BF16)
-        *parts, moments = call(
-            functools.partial(part_kernel, sub_count, slot_count, is_last),
-            (full,) + (part,) * (sub_count - 1) + (scalars,),
-            (lists, blocks, begun, tile_field, even, odd, moments),
+        found = call(
+            functools.partial(part_kernel, index, sub_count, slot_count),
+            (full,)
+            + (part,) * (sub_count - 1)
+            + (scalars,)
+            + ((shape(rhs_count, 2 * LANES, F32),) if index == 1 else ()),
+            (lists, blocks, begun, tile_field, even, odd, moments, unit, *ratios, *sides),
             "parts",
             1,
             scratch_shapes=[scratch(extended + 1), scratch(blocks_dev)],
         )
+        parts, moments = list(found[:sub_count]), found[sub_count]
+        sides = sides or tuple(found[sub_count + 1 :])
         if is_last:
             break
         if index == 0:
@@ -436,8 +553,8 @@
         arrived = [exchange(parts[step], "sub", step) for step in range(sub_count - 1, 0, -1)]
         field, rounded, moments = call(
             functools.partial(join_kernel, index),
-            (full, half, scalars),
-            (blocks, parts[0], field, moments, *arrived),
+            (full, half if index else shape(rhs_count, points_dev + LANES, BF16), scalars),
+            (blocks, unit, *(ratios or (unit,)), parts[0], field, moments, *arrived),
             "join",
         )
         basis.append(field)
@@ -445,7 +562,7 @@
     for axis, count in (("sub", sub_count), ("tile", tile_count)):
         step = 1
         while step < count:
-            moments = moments + exchange(moments, axis, step)
+            moments = call(add_moments_kernel, scalars, (moments, exchange(moments, axis, step)), "add_moments")
             if len(arrived) < sub_count - 1:
                 far = sub_count - 1 - len(arrived)
                 arrived.append(exchange(parts[far], "sub", far))
@@ -456,7 +573,7 @@
     return call(
         functools.partial(finish_kernel, sub_count),
         (full, full),
-        (moments, parts[0], *arrived, *basis),
+        (moments, unit, *ratios, parts[0], *arrived, *basis),
         "finish",
     )
 

time: 93.5 us -> 95.1 us (1.017)
  Pallas kernels: 19.3 us -> 33.2 us
  starting transfers between devices: 54.3 us -> 40.4 us
  waiting for transfers between devices: 18.6 us -> 20.1 us
    pallas_call x18 -> x23, Pallas kernels: 19.3 us -> 33.2 us  [call(): pl.pallas_call(kernel, out_shape=outs, compiler_params=PARAMS, name=name,...]
    ppermute x23, starting transfers between devices: 45.1 us -> 38.2 us  [exchange(): return lax.ppermute(block, axis, [(i, i ^ step) for i in range(count)])]
    ppermute x6, starting transfers between devices: 9.16 us -> 2.21 us  [swap(): return lax.ppermute(block, axis, route)]
    ppermute x23, waiting for transfers between devices: 18.6 us -> 20.1 us  [exchange(): return lax.ppermute(block, axis, [(i, i ^ step) for i in range(count)])]
  transfers between devices with their start and end apart: 29 -> 29, of which waited for: 14 -> 12; matrix products, arithmetic and copies ran while one was open for 0% -> 0% of each run, Pallas kernels for 14% -> 25%
where the time goes in v7:
time: 95.1 us; the launch traced here: 94.7 us
  starting transfers between devices  40.4 us (42%)
  Pallas kernels  33.2 us (35%)
  waiting for transfers between devices  20.1 us (21%)
  between operations  0.97 us (1%)
    ppermute x23, starting transfers between devices, exchange(): return lax.ppermute(block, axis, [(i, i ^ step) for i in range(count)])  38.2 us
    pallas_call x23, Pallas kernels, call(): pl.pallas_call(kernel, out_shape=outs, compiler_params=PARAMS, name=name,...  33.2 us
    ppermute x23, waiting for transfers between devices, exchange(): return lax.ppermute(block, axis, [(i, i ^ step) for i in range(count)])  20.1 us
    ppermute x6, starting transfers between devices, swap(): return lax.ppermute(block, axis, route)  2.21 us
  transfers between devices with their start and end apart: 29, of which 12 were waited for; matrix products, arithmetic and copies ran while one was open for 0% of the time, Pallas kernels for 25%

profile of v7, /device:TPU:0, one launch (start us, length us, event | category | flops | bytes accessed | tf_op | source)
XLA Modules:
  0.0 94.7 jit_solution(11489345395247761817)
XLA Ops:
  0.7 2.3 %curve_order.1 = (f32[8,4096]{1,0:T(8,128)S(1)}, bf16[8,4096]{1,0:T(8,128)(2,1)S(1)}) custom-call(f32[8,4096]{1,0:T(8,128)} %right_in.1, s32[1,4096]{1,0:T(1,128)} %order_in.1), custom_call_target="tpu_custom_call" | custom-call | flops 10000000000 | tf_op jit(solution)/shard_map/curve_order/pallas_call | solution.py:433
  3.0 5.1 %collective-permute-start.2 = (bf16[8,4096]{1,0:T(8,128)(2,1)S(1)}, bf16[8,4096]{1,0:T(8,128)(2,1)S(1)}, u32[]{:S(2)}, u32[]{:S(2)}) collective-permute-start(bf16[8,4096]{1,0:T(8,128)(2,1)S(1)} %get-tuple-element.48.rounded_ref.refs_0_), channel_id=1, source_target_pairs={{0,3},{1,2},{2,1},{3,0},{4,7},{5,6},{6,5},{7,4},{8,11},{9,10},{10,... | collective-permute-start | bytes 196616 | tf_op jit(solution)/shard_map/ppermute | solution.py:417
  8.8 1.5 %lists.1.lists_ref = s32[1,1280]{1,0:T(1,128)S(4)} custom-call(s32[2,96]{1,0:T(2,128)S(1)} %bitcast.5), custom_call_target="tpu_custom_call" | custom-call | flops 1000000000 | tf_op jit(solution)/shard_map/lists/pallas_call | solution.py:433
  10.3 2.9 %early.3 = (f32[81,8,256]{2,1,0:T(8,128)S(1)}, f32[8,128]{1,0:T(8,128)S(1)}) custom-call(s32[1,1280]{1,0:T(1,128)S(4)} %lists.1.lists_ref, bf16[96,256,256]{2,1,0:T(8,128)(2,1)S(1)} %copy-done, bf16[16,256,256]{2,1,0:T(8,128)(2,1)S(1)} %copy-done.1, f32[1,4096]{1,0:T(1,128)S(1)} %bitcast.2, f32[8,4096]{1,0:T(8,128)S(1)} %get-tuple-element.47.own_ref.old_ref.refs_4_, ...), custom_call_target="tpu_custom_call" | custom-call | flops 3000000000 | tf_op jit(solution)/shard_map/early/pallas_call | solution.py:433
  15.3 4.9 %late.3.begun_ref = f32[81,8,256]{2,1,0:T(8,128)S(1)} custom-call(s32[1,1280]{1,0:T(1,128)S(4)} %lists.1.lists_ref, bf16[96,256,256]{2,1,0:T(8,128)(2,1)S(1)} %copy-done, f32[81,8,256]{2,1,0:T(8,128)S(1)} %get-tuple-element.49.begun_ref, f32[64,8,256]{2,1,0:T(8,128)S(1)} %get-tuple-element.50.field_ref), custom_call_target="tpu_custom_call" | custom-call | flops 3000000000 | tf_op jit(solution)/shard_map/late/pallas_call | solution.py:433
  21.9 4.2 %collective-permute-start.7 = (bf16[8,4096]{1,0:T(8,128)(2,1)S(1)}, bf16[8,4096]{1,0:T(8,128)(2,1)S(1)}, u32[]{:S(2)}, u32[]{:S(2)}) collective-permute-start(bf16[8,4096]{1,0:T(8,128)(2,1)S(1)} %get-tuple-element.58), channel_id=1, source_target_pairs={{0,1},{1,0},{2,3},{3,2},{4,5},{5,4},{6,7},{7,6},{8,9},{9,8},{10,11... | collective-permute-start | bytes 196616 | tf_op jit(solution)/shard_map/ppermute | solution.py:417
  26.0 5.4 %turn.1.after_ref.blocks_ref = bf16[192,256,256]{2,1,0:T(8,128)(2,1)S(1)} custom-call(bf16[96,256,256]{2,1,0:T(8,128)(2,1)S(1)} %copy-done, f32[8,128]{1,0:T(8,128)S(1)} %get-tuple-element.54.after_ref.moments_in_ref), custom_call_target="tpu_custom_call" | custom-call | flops 4000000000 | tf_op jit(solution)/shard_map/turn/pallas_call | solution.py:433
  33.1 2.9 %collective-permute-start.8 = (bf16[8,4224]{1,0:T(8,128)(2,1)S(1)}, bf16[8,4224]{1,0:T(8,128)(2,1)S(1)}, u32[]{:S(2)}, u32[]{:S(2)}) collective-permute-start(bf16[8,4224]{1,0:T(8,128)(2,1)S(1)} %get-tuple-element.60.rounded_ref.refs_0_), channel_id=1, source_target_pairs={{0,1},{1,0},{2,3},{3,2},{4,5},{5,4},{6,7},{7,6},{8,9},{9,8},{10,11... | collective-permute-start | bytes 202760 | tf_op jit(solution)/shard_map/ppermute | solution.py:417
  37.9 2.2 %collective-permute-done.9.refs_2_ = bf16[8,4224]{1,0:T(8,128)(2,1)S(1)} collective-permute-done((bf16[8,4224]{1,0:T(8,128)(2,1)S(1)}, bf16[8,4224]{1,0:T(8,128)(2,1)S(1)}, u32[]{:S(2)}, u32[]{:S(2)}) %collective-permute-start.9) | collective-permute-done | bytes 67616 | tf_op jit(solution)/shard_map/ppermute | solution.py:417
  41.8 3.2 %late.4.begun_ref = f32[81,8,256]{2,1,0:T(8,128)S(1)} custom-call(s32[1,1280]{1,0:T(1,128)S(4)} %lists.1.lists_ref, bf16[192,256,256]{2,1,0:T(8,128)(2,1)S(1)} %turn.1.after_ref.blocks_ref, f32[81,8,256]{2,1,0:T(8,128)S(1)} %early.4.begun_ref, f32[64,8,256]{2,1,0:T(8,128)S(1)} %get-tuple-element.62.field_ref, f32[8,640]{1,0:T(8,128)S(1)} %get-tuple-element.61.refs_0_.ratios_ref), custom_call_target="tpu_custom_call" | custom-call | flops 3000000000 | tf_op jit(solution)/shard_map/late/pallas_call | solution.py:433
  46.0 4.3 %collective-permute-start.15 = (bf16[8,4096]{1,0:T(8,128)(2,1)S(1)}, bf16[8,4096]{1,0:T(8,128)(2,1)S(1)}, u32[]{:S(2)}, u32[]{:S(2)}) collective-permute-start(bf16[8,4096]{1,0:T(8,128)(2,1)S(1)} %get-tuple-element.70), channel_id=1, source_target_pairs={{0,1},{1,0},{2,3},{3,2},{4,5},{5,4},{6,7},{7,6},{8,9},{9,8},{10,11... | collective-permute-start | bytes 196616 | tf_op jit(solution)/shard_map/ppermute | solution.py:417
  50.3 1.8 %collective-permute-done.13.refs_0_ = bf16[8,4096]{1,0:T(8,128)(2,1)S(1)} collective-permute-done((bf16[8,4096]{1,0:T(8,128)(2,1)S(1)}, bf16[8,4096]{1,0:T(8,128)(2,1)S(1)}, u32[]{:S(2)}, u32[]{:S(2)}) %collective-permute-start.13) | collective-permute-done | bytes 65568 | tf_op jit(solution)/shard_map/ppermute | solution.py:417
  52.1 1.5 %collective-permute-done.15.refs_2_ = bf16[8,4096]{1,0:T(8,128)(2,1)S(1)} collective-permute-done((bf16[8,4096]{1,0:T(8,128)(2,1)S(1)}, bf16[8,4096]{1,0:T(8,128)(2,1)S(1)}, u32[]{:S(2)}, u32[]{:S(2)}) %collective-permute-start.15) | collective-permute-done | bytes 65568 | tf_op jit(solution)/shard_map/ppermute | solution.py:417
  53.7 3.3 %collective-permute-start.18 = (bf16[8,4096]{1,0:T(8,128)(2,1)S(1)}, bf16[8,4096]{1,0:T(8,128)(2,1)S(1)}, u32[]{:S(2)}, u32[]{:S(2)}) collective-permute-start(bf16[8,4096]{1,0:T(8,128)(2,1)S(1)} %get-tuple-element.72.rounded_ref.refs_1_), channel_id=1, source_target_pairs={{0,3},{1,2},{2,1},{3,0},{4,7},{5,6},{6,5},{7,4},{8,11},{9,10},{10,... | collective-permute-start | bytes 196616 | tf_op jit(solution)/shard_map/ppermute | solution.py:417
  59.8 3.7 %collective-permute-done.17.refs_3_ = bf16[8,4096]{1,0:T(8,128)(2,1)S(1)} collective-permute-done((bf16[8,4096]{1,0:T(8,128)(2,1)S(1)}, bf16[8,4096]{1,0:T(8,128)(2,1)S(1)}, u32[]{:S(2)}, u32[]{:S(2)}) %collective-permute-start.17) | collective-permute-done | bytes 65568 | tf_op jit(solution)/shard_map/ppermute | solution.py:417
  65.0 3.2 %late.5.begun_ref = f32[81,8,256]{2,1,0:T(8,128)S(1)} custom-call(s32[1,1280]{1,0:T(1,128)S(4)} %lists.1.lists_ref, bf16[192,256,256]{2,1,0:T(8,128)(2,1)S(1)} %turn.1.after_ref.blocks_ref, f32[81,8,256]{2,1,0:T(8,128)S(1)} %early.5.begun_ref, f32[64,8,256]{2,1,0:T(8,128)S(1)} %get-tuple-element.73.field_ref, f32[8,640]{1,0:T(8,128)S(1)} %get-tuple-element.61.refs_0_.ratios_ref), custom_call_target="tpu_custom_call" | custom-call | flops 3000000000 | tf_op jit(solution)/shard_map/late/pallas_call | solution.py:433
  69.3 3.6 %collective-permute-done.21.second_ref = f32[8,128]{1,0:T(8,128)S(1)} collective-permute-done((f32[8,128]{1,0:T(8,128)S(1)}, f32[8,128]{1,0:T(8,128)S(1)}, u32[]{:S(2)}, u32[]{:S(2)}) %collective-permute-start.21) | collective-permute-done | bytes 4128 | tf_op jit(solution)/shard_map/ppermute | solution.py:417
  73.1 2.4 %collective-permute-start.26 = (f32[8,4096]{1,0:T(8,128)S(1)}, f32[8,4096]{1,0:T(8,128)S(1)}, u32[]{:S(2)}, u32[]{:S(2)}) collective-permute-start(f32[8,4096]{1,0:T(8,128)S(1)} %get-tuple-element.82), channel_id=1, source_target_pairs={{0,3},{1,2},{2,1},{3,0},{4,7},{5,6},{6,5},{7,4},{8,11},{9,10},{10,... | collective-permute-start | bytes 393224 | tf_op jit(solution)/shard_map/ppermute | solution.py:417
  76.0 1.6 %collective-permute-done.22.second_ref = f32[8,128]{1,0:T(8,128)S(1)} collective-permute-done((f32[8,128]{1,0:T(8,128)S(1)}, f32[8,128]{1,0:T(8,128)S(1)}, u32[]{:S(2)}, u32[]{:S(2)}) %collective-permute-start.22) | collective-permute-done | bytes 4128 | tf_op jit(solution)/shard_map/ppermute | solution.py:417
  77.7 3.3 %collective-permute-start.23 = (f32[8,128]{1,0:T(8,128)S(1)}, f32[8,128]{1,0:T(8,128)S(1)}, u32[]{:S(2)}, u32[]{:S(2)}) collective-permute-start(f32[8,128]{1,0:T(8,128)S(1)} %add_moments.6.first_ref), channel_id=1, source_target_pairs={{0,4},{4,0},{8,12},{12,8},{16,20},{20,16},{24,28},{28,24},{1,5},{5... | collective-permute-start | bytes 12296 | tf_op jit(solution)/shard_map/ppermute | solution.py:417
  82.0 3.0 %collective-permute-start.24 = (f32[8,128]{1,0:T(8,128)S(1)}, f32[8,128]{1,0:T(8,128)S(1)}, u32[]{:S(2)}, u32[]{:S(2)}) collective-permute-start(f32[8,128]{1,0:T(8,128)S(1)} %add_moments.7.first_ref), channel_id=1, source_target_pairs={{0,8},{4,12},{8,0},{12,4},{16,24},{20,28},{24,16},{28,20},{1,9},{5... | collective-permute-start | bytes 12296 | tf_op jit(solution)/shard_map/ppermute | solution.py:417
  84.9 1.6 %collective-permute-done.24.second_ref = f32[8,128]{1,0:T(8,128)S(1)} collective-permute-done((f32[8,128]{1,0:T(8,128)S(1)}, f32[8,128]{1,0:T(8,128)S(1)}, u32[]{:S(2)}, u32[]{:S(2)}) %collective-permute-start.24) | collective-permute-done | bytes 4128 | tf_op jit(solution)/shard_map/ppermute | solution.py:417
  86.6 5.4 %collective-permute-start.25 = (f32[8,128]{1,0:T(8,128)S(1)}, f32[8,128]{1,0:T(8,128)S(1)}, u32[]{:S(2)}, u32[]{:S(2)}) collective-permute-start(f32[8,128]{1,0:T(8,128)S(1)} %add_moments.8.first_ref), channel_id=1, source_target_pairs={{0,16},{4,20},{8,24},{12,28},{16,0},{20,4},{24,8},{28,12},{1,17},{... | collective-permute-start | bytes 12296 | tf_op jit(solution)/shard_map/ppermute | solution.py:417
  92.0 1.6 %collective-permute-done.25.second_ref = f32[8,128]{1,0:T(8,128)S(1)} collective-permute-done((f32[8,128]{1,0:T(8,128)S(1)}, f32[8,128]{1,0:T(8,128)S(1)}, u32[]{:S(2)}, u32[]{:S(2)}) %collective-permute-start.25) | collective-permute-done | bytes 4128 | tf_op jit(solution)/shard_map/ppermute | solution.py:417
  (66 shorter events, 19.0 us)
Async XLA Ops:
  3.0 10.2 %collective-permute-start.2 = (bf16[8,4096]{1,0:T(8,128)(2,1)S(1)}, bf16[8,4096]{1,0:T(8,128)(2,1)S(1)}, u32[]{:S(2)}, u32[]{:S(2)}) collective-permute-start(bf16[8,4096]{1,0:T(8,128)(2,1)S(1)} %get-tuple-element.48.rounded_ref.refs_0_), channel_id=1, source_target_pairs={{0,3},{1,2},{2,1},{3,0},{4,7},{5,6},{6,5},{7,4},{8,11},{9,10},{10,... | collective-permute-start | bytes 196616 | tf_op jit(solution)/shard_map/ppermute | solution.py:417
  8.1 5.6 %collective-permute-start.1 = (bf16[8,4096]{1,0:T(8,128)(2,1)S(1)}, bf16[8,4096]{1,0:T(8,128)(2,1)S(1)}, u32[]{:S(2)}, u32[]{:S(2)}) collective-permute-start(bf16[8,4096]{1,0:T(8,128)(2,1)S(1)} %get-tuple-element.48.rounded_ref.refs_0_), channel_id=1, source_target_pairs={{0,2},{1,3},{2,0},{3,1},{4,6},{5,7},{6,4},{7,5},{8,10},{9,11},{10,... | collective-permute-start | bytes 196616 | tf_op jit(solution)/shard_map/ppermute | solution.py:417
  8.1 5.6 %collective-permute-start = (bf16[8,4096]{1,0:T(8,128)(2,1)S(1)}, bf16[8,4096]{1,0:T(8,128)(2,1)S(1)}, u32[]{:S(2)}, u32[]{:S(2)}) collective-permute-start(bf16[8,4096]{1,0:T(8,128)(2,1)S(1)} %get-tuple-element.48.rounded_ref.refs_0_), channel_id=1, source_target_pairs={{0,1},{1,0},{2,3},{3,2},{4,5},{5,4},{6,7},{7,6},{8,9},{9,8},{10,11... | collective-permute-start | bytes 196616 | tf_op jit(solution)/shard_map/ppermute | solution.py:417
  14.6 5.7 %collective-permute-start.3 = (bf16[8,4096]{1,0:T(8,128)(2,1)S(1)}, bf16[8,4096]{1,0:T(8,128)(2,1)S(1)}, u32[]{:S(2)}, u32[]{:S(2)}) collective-permute-start(bf16[8,4096]{1,0:T(8,128)(2,1)S(1)} %get-tuple-element.51), channel_id=1, source_target_pairs={{0,4},{4,0},{8,12},{12,8},{16,20},{20,16},{24,28},{28,24},{1,5},{5... | collective-permute-start | bytes 196616 | tf_op jit(solution)/shard_map/ppermute | solution.py:425
  14.7 5.6 %collective-permute-start.4 = (bf16[8,4096]{1,0:T(8,128)(2,1)S(1)}, bf16[8,4096]{1,0:T(8,128)(2,1)S(1)}, u32[]{:S(2)}, u32[]{:S(2)}) collective-permute-start(bf16[8,4096]{1,0:T(8,128)(2,1)S(1)} %get-tuple-element.52), channel_id=1, source_target_pairs={{4,8},{8,4},{12,16},{16,12},{20,24},{24,20},{5,9},{9,5},{13,17},{1... | collective-permute-start | bytes 196616 | tf_op jit(solution)/shard_map/ppermute | solution.py:425
  21.6 9.9 %collective-permute-start.5 = (bf16[8,4096]{1,0:T(8,128)(2,1)S(1)}, bf16[8,4096]{1,0:T(8,128)(2,1)S(1)}, u32[]{:S(2)}, u32[]{:S(2)}) collective-permute-start(bf16[8,4096]{1,0:T(8,128)(2,1)S(1)} %get-tuple-element.56), channel_id=1, source_target_pairs={{0,3},{1,2},{2,1},{3,0},{4,7},{5,6},{6,5},{7,4},{8,11},{9,10},{10,... | collective-permute-start | bytes 196616 | tf_op jit(solution)/shard_map/ppermute | solution.py:417
  21.7 9.8 %collective-permute-start.6 = (bf16[8,4096]{1,0:T(8,128)(2,1)S(1)}, bf16[8,4096]{1,0:T(8,128)(2,1)S(1)}, u32[]{:S(2)}, u32[]{:S(2)}) collective-permute-start(bf16[8,4096]{1,0:T(8,128)(2,1)S(1)} %get-tuple-element.57), channel_id=1, source_target_pairs={{0,2},{1,3},{2,0},{3,1},{4,6},{5,7},{6,4},{7,5},{8,10},{9,11},{10,... | collective-permute-start | bytes 196616 | tf_op jit(solution)/shard_map/ppermute | solution.py:417
  21.9 9.6 %collective-permute-start.7 = (bf16[8,4096]{1,0:T(8,128)(2,1)S(1)}, bf16[8,4096]{1,0:T(8,128)(2,1)S(1)}, u32[]{:S(2)}, u32[]{:S(2)}) collective-permute-start(bf16[8,4096]{1,0:T(8,128)(2,1)S(1)} %get-tuple-element.58), channel_id=1, source_target_pairs={{0,1},{1,0},{2,3},{3,2},{4,5},{5,4},{6,7},{7,6},{8,9},{9,8},{10,11... | collective-permute-start | bytes 196616 | tf_op jit(solution)/shard_map/ppermute | solution.py:417
  31.6 6.2 %collective-permute-start.10 = (bf16[8,4224]{1,0:T(8,128)(2,1)S(1)}, bf16[8,4224]{1,0:T(8,128)(2,1)S(1)}, u32[]{:S(2)}, u32[]{:S(2)}) collective-permute-start(bf16[8,4224]{1,0:T(8,128)(2,1)S(1)} %get-tuple-element.60.rounded_ref.refs_0_), channel_id=1, source_target_pairs={{0,3},{1,2},{2,1},{3,0},{4,7},{5,6},{6,5},{7,4},{8,11},{9,10},{10,... | collective-permute-start | bytes 202760 | tf_op jit(solution)/shard_map/ppermute | solution.py:417
  32.5 7.6 %collective-permute-start.9 = (bf16[8,4224]{1,0:T(8,128)(2,1)S(1)}, bf16[8,4224]{1,0:T(8,128)(2,1)S(1)}, u32[]{:S(2)}, u32[]{:S(2)}) collective-permute-start(bf16[8,4224]{1,0:T(8,128)(2,1)S(1)} %get-tuple-element.60.rounded_ref.refs_0_), channel_id=1, source_target_pairs={{0,2},{1,3},{2,0},{3,1},{4,6},{5,7},{6,4},{7,5},{8,10},{9,11},{10,... | collective-permute-start | bytes 202760 | tf_op jit(solution)/shard_map/ppermute | solution.py:417
  33.1 7.0 %collective-permute-start.8 = (bf16[8,4224]{1,0:T(8,128)(2,1)S(1)}, bf16[8,4224]{1,0:T(8,128)(2,1)S(1)}, u32[]{:S(2)}, u32[]{:S(2)}) collective-permute-start(bf16[8,4224]{1,0:T(8,128)(2,1)S(1)} %get-tuple-element.60.rounded_ref.refs_0_), channel_id=1, source_target_pairs={{0,1},{1,0},{2,3},{3,2},{4,5},{5,4},{6,7},{7,6},{8,9},{9,8},{10,11... | collective-permute-start | bytes 202760 | tf_op jit(solution)/shard_map/ppermute | solution.py:417
  45.8 6.3 %collective-permute-start.13 = (bf16[8,4096]{1,0:T(8,128)(2,1)S(1)}, bf16[8,4096]{1,0:T(8,128)(2,1)S(1)}, u32[]{:S(2)}, u32[]{:S(2)}) collective-permute-start(bf16[8,4096]{1,0:T(8,128)(2,1)S(1)} %get-tuple-element.68), channel_id=1, source_target_pairs={{0,3},{1,2},{2,1},{3,0},{4,7},{5,6},{6,5},{7,4},{8,11},{9,10},{10,... | collective-permute-start | bytes 196616 | tf_op jit(solution)/shard_map/ppermute | solution.py:417
  45.9 6.2 %collective-permute-start.14 = (bf16[8,4096]{1,0:T(8,128)(2,1)S(1)}, bf16[8,4096]{1,0:T(8,128)(2,1)S(1)}, u32[]{:S(2)}, u32[]{:S(2)}) collective-permute-start(bf16[8,4096]{1,0:T(8,128)(2,1)S(1)} %get-tuple-element.69), channel_id=1, source_target_pairs={{0,2},{1,3},{2,0},{3,1},{4,6},{5,7},{6,4},{7,5},{8,10},{9,11},{10,... | collective-permute-start | bytes 196616 | tf_op jit(solution)/shard_map/ppermute | solution.py:417
  46.0 7.6 %collective-permute-start.15 = (bf16[8,4096]{1,0:T(8,128)(2,1)S(1)}, bf16[8,4096]{1,0:T(8,128)(2,1)S(1)}, u32[]{:S(2)}, u32[]{:S(2)}) collective-permute-start(bf16[8,4096]{1,0:T(8,128)(2,1)S(1)} %get-tuple-element.70), channel_id=1, source_target_pairs={{0,1},{1,0},{2,3},{3,2},{4,5},{5,4},{6,7},{7,6},{8,9},{9,8},{10,11... | collective-permute-start | bytes 196616 | tf_op jit(solution)/shard_map/ppermute | solution.py:417
  53.7 6.1 %collective-permute-start.18 = (bf16[8,4096]{1,0:T(8,128)(2,1)S(1)}, bf16[8,4096]{1,0:T(8,128)(2,1)S(1)}, u32[]{:S(2)}, u32[]{:S(2)}) collective-permute-start(bf16[8,4096]{1,0:T(8,128)(2,1)S(1)} %get-tuple-element.72.rounded_ref.refs_1_), channel_id=1, source_target_pairs={{0,3},{1,2},{2,1},{3,0},{4,7},{5,6},{6,5},{7,4},{8,11},{9,10},{10,... | collective-permute-start | bytes 196616 | tf_op jit(solution)/shard_map/ppermute | solution.py:417
  57.0 6.4 %collective-permute-start.17 = (bf16[8,4096]{1,0:T(8,128)(2,1)S(1)}, bf16[8,4096]{1,0:T(8,128)(2,1)S(1)}, u32[]{:S(2)}, u32[]{:S(2)}) collective-permute-start(bf16[8,4096]{1,0:T(8,128)(2,1)S(1)} %get-tuple-element.72.rounded_ref.refs_1_), channel_id=1, source_target_pairs={{0,2},{1,3},{2,0},{3,1},{4,6},{5,7},{6,4},{7,5},{8,10},{9,11},{10,... | collective-permute-start | bytes 196616 | tf_op jit(solution)/shard_map/ppermute | solution.py:417
  57.0 6.4 %collective-permute-start.16 = (bf16[8,4096]{1,0:T(8,128)(2,1)S(1)}, bf16[8,4096]{1,0:T(8,128)(2,1)S(1)}, u32[]{:S(2)}, u32[]{:S(2)}) collective-permute-start(bf16[8,4096]{1,0:T(8,128)(2,1)S(1)} %get-tuple-element.72.rounded_ref.refs_1_), channel_id=1, source_target_pairs={{0,1},{1,0},{2,3},{3,2},{4,5},{5,4},{6,7},{7,6},{8,9},{9,8},{10,11... | collective-permute-start | bytes 196616 | tf_op jit(solution)/shard_map/ppermute | solution.py:417
  73.0 4.6 %collective-permute-start.22 = (f32[8,128]{1,0:T(8,128)S(1)}, f32[8,128]{1,0:T(8,128)S(1)}, u32[]{:S(2)}, u32[]{:S(2)}) collective-permute-start(f32[8,128]{1,0:T(8,128)S(1)} %add_moments.5.first_ref), channel_id=1, source_target_pairs={{0,2},{1,3},{2,0},{3,1},{4,6},{5,7},{6,4},{7,5},{8,10},{9,11},{10,... | collective-permute-start | bytes 12296 | tf_op jit(solution)/shard_map/ppermute | solution.py:417
  73.1 20.6 %collective-permute-start.26 = (f32[8,4096]{1,0:T(8,128)S(1)}, f32[8,4096]{1,0:T(8,128)S(1)}, u32[]{:S(2)}, u32[]{:S(2)}) collective-permute-start(f32[8,4096]{1,0:T(8,128)S(1)} %get-tuple-element.82), channel_id=1, source_target_pairs={{0,3},{1,2},{2,1},{3,0},{4,7},{5,6},{6,5},{7,4},{8,11},{9,10},{10,... | collective-permute-start | bytes 393224 | tf_op jit(solution)/shard_map/ppermute | solution.py:417
  75.4 18.3 %collective-permute-start.27 = (f32[8,4096]{1,0:T(8,128)S(1)}, f32[8,4096]{1,0:T(8,128)S(1)}, u32[]{:S(2)}, u32[]{:S(2)}) collective-permute-start(f32[8,4096]{1,0:T(8,128)S(1)} %get-tuple-element.86), channel_id=1, source_target_pairs={{0,2},{1,3},{2,0},{3,1},{4,6},{5,7},{6,4},{7,5},{8,10},{9,11},{10,... | collective-permute-start | bytes 393224 | tf_op jit(solution)/shard_map/ppermute | solution.py:417
  77.7 16.1 %collective-permute-start.28 = (f32[8,4096]{1,0:T(8,128)S(1)}, f32[8,4096]{1,0:T(8,128)S(1)}, u32[]{:S(2)}, u32[]{:S(2)}) collective-permute-start(f32[8,4096]{1,0:T(8,128)S(1)} %get-tuple-element.89), channel_id=1, source_target_pairs={{0,1},{1,0},{2,3},{3,2},{4,5},{5,4},{6,7},{7,6},{8,9},{9,8},{10,11... | collective-permute-start | bytes 393224 | tf_op jit(solution)/shard_map/ppermute | solution.py:417
  77.7 4.1 %collective-permute-start.23 = (f32[8,128]{1,0:T(8,128)S(1)}, f32[8,128]{1,0:T(8,128)S(1)}, u32[]{:S(2)}, u32[]{:S(2)}) collective-permute-start(f32[8,128]{1,0:T(8,128)S(1)} %add_moments.6.first_ref), channel_id=1, source_target_pairs={{0,4},{4,0},{8,12},{12,8},{16,20},{20,16},{24,28},{28,24},{1,5},{5... | collective-permute-start | bytes 12296 | tf_op jit(solution)/shard_map/ppermute | solution.py:417
  82.0 4.5 %collective-permute-start.24 = (f32[8,128]{1,0:T(8,128)S(1)}, f32[8,128]{1,0:T(8,128)S(1)}, u32[]{:S(2)}, u32[]{:S(2)}) collective-permute-start(f32[8,128]{1,0:T(8,128)S(1)} %add_moments.7.first_ref), channel_id=1, source_target_pairs={{0,8},{4,12},{8,0},{12,4},{16,24},{20,28},{24,16},{28,20},{1,9},{5... | collective-permute-start | bytes 12296 | tf_op jit(solution)/shard_map/ppermute | solution.py:417
  86.6 7.0 %collective-permute-start.25 = (f32[8,128]{1,0:T(8,128)S(1)}, f32[8,128]{1,0:T(8,128)S(1)}, u32[]{:S(2)}, u32[]{:S(2)}) collective-permute-start(f32[8,128]{1,0:T(8,128)S(1)} %add_moments.8.first_ref), channel_id=1, source_target_pairs={{0,16},{4,20},{8,24},{12,28},{16,0},{20,4},{24,8},{28,12},{1,17},{... | collective-permute-start | bytes 12296 | tf_op jit(solution)/shard_map/ppermute | solution.py:417
  (9 other events, 56.3 us)

commit v8 on v7

--- a/solution.py
+++ b/solution.py
@@ -202,7 +202,7 @@
         largest = diag_ref[0].astype(F32)
         for block in range(1, blocks_dev):
             largest = jnp.maximum(largest, diag_ref[block].astype(F32))
-        refs[0][...] = jnp.full(refs[0].shape, jnp.maximum(jnp.max(largest), 1.0))
+        refs[0][...] = jnp.full(refs[0].shape, jnp.maximum(jnp.max(largest) * block_len, 1.0))
     lay_out(rounded_ref, field, own_first, blocks_dev, block_len)
     for block in range(total.shape[0]):
         total[block] = jnp.zeros(total.shape[1:], F32)
@@ -263,18 +263,27 @@
     add_products(lists_ref, blocks_ref, slot_count, field_ref, total, LATE, LONG_GROUP)
 
 
+def lost_weight(moments):
+    inner = [moments[:, order : order + 1] for order in range(4)]
+    first = inner[1] / inner[0]
+    norm = inner[2] - first * inner[1]
+    second = (inner[3] - 2.0 * first * inner[2] + first * first * inner[1]) / norm
+    trace = first + 2.0 * second
+    return jnp.where((norm > 0.0) & (trace > 0.0) & (trace < 30.0), -trace, 0.0)
+
+
 def part_kernel(
     index, sub_count, slot_count, lists_ref, blocks_ref, begun_ref, field_ref, even_ref, odd_ref,
     moments_in_ref, unit_ref, *refs
 ):
+    *refs, total, ahead = refs
     if index == 1:
-        ratios_ref, *refs = refs
-        *refs, sides_ref, total, ahead = refs
-    else:
-        if index:
-            ratios_ref, sides_ref, *refs = refs
-        *refs, total, ahead = refs
-    part_refs, moments_ref = refs[:-1], refs[-1]
+        ratios_ref, *refs, sides_ref = refs
+    elif index:
+        ratios_ref, sides_ref, *refs = refs
+    if index + 1 == ITERS:
+        lost_refs, refs = refs[: sub_count - 1], refs[sub_count - 1 :]
+    part_refs, moments_ref, *kept_refs = refs[:sub_count], *refs[sub_count:]
     block_len = blocks_ref.shape[1]
     sub_index, blocks_dev, own_first, tile_blocks = device_place(block_len, part_refs[0], sub_count)
     is_odd = lax.axis_index("tile") % 2 == 1
@@ -301,19 +310,27 @@
         total[block] = begun_ref[block]
     total[begun_ref.shape[0] - 1] = jnp.zeros(total.shape[1:], F32)
     add_products(lists_ref, blocks_ref, slot_count, ahead, total, FROM_AHEAD, SHORT_GROUP, tile_blocks, 0)
+    moments = moments_in_ref[...]
+    if index + 1 == ITERS:
+        weight = lost_weight(moments) * ratios_ref[:, :1]
     for step in range(sub_count):
         first = (sub_index ^ step) * blocks_dev
         for block in range(blocks_dev):
             span = slice(block * block_len, (block + 1) * block_len)
-            part_refs[step][:, span] = total[first + block].astype(part_refs[step].dtype)
-    moments = moments_in_ref[...]
+            value = total[first + block]
+            if step and index + 1 == ITERS:
+                value += weight * lost_refs[step - 1][:, span]
+            rounded = value.astype(part_refs[step].dtype)
+            part_refs[step][:, span] = rounded
+            if step and kept_refs:
+                kept_refs[step - 1][:, span] = value - rounded.astype(F32)
     if index + 1 == ITERS:
         product = jnp.zeros(total.shape[1:], F32)
+        unit = unit_ref[...]
+        scale = widen(1.0 / (raised(ratios_ref[:, :LANES], 2 * index) * unit), block_len)
         for block in range(tile_blocks):
-            product += field_ref[block] * total[block]
+            product += field_ref[block] * (total[block] * scale)
         last = jnp.sum(product, axis=1, keepdims=True)
-        unit = unit_ref[...]
-        last = last / (raised(ratios_ref[:, :LANES], 2 * index) * unit)
         lane = lax.broadcasted_iota(jnp.int32, moments.shape, 1)
         moments = jnp.where(lane == 2 * ITERS - 1, last, moments)
         moments = jnp.where(lane == 2 * ITERS, unit, moments)
@@ -531,14 +548,17 @@
             (full,)
             + (part,) * (sub_count - 1)
             + (scalars,)
+            + ((full,) * (sub_count - 1) if index + 2 == ITERS else ())
             + ((shape(rhs_count, 2 * LANES, F32),) if index == 1 else ()),
-            (lists, blocks, begun, tile_field, even, odd, moments, unit, *ratios, *sides),
+            (lists, blocks, begun, tile_field, even, odd, moments, unit, *ratios, *sides, *(lost if is_last else ())),
             "parts",
             1,
             scratch_shapes=[scratch(extended + 1), scratch(blocks_dev)],
         )
         parts, moments = list(found[:sub_count]), found[sub_count]
-        sides = sides or tuple(found[sub_count + 1 :])
+        if index == 1:
+            sides = (found[-1],)
+        lost = found[sub_count + 1 : 2 * sub_count]
         if is_last:
             break
         if index == 0:

time: 95.1 us -> 96.3 us (1.013)
  Pallas kernels: 33.2 us -> 25.7 us
  starting transfers between devices: 40.4 us -> 47.7 us
  waiting for transfers between devices: 20.1 us -> 22.2 us
    pallas_call x23, Pallas kernels: 33.2 us -> 25.7 us  [call(): pl.pallas_call(kernel, out_shape=outs, compiler_params=PARAMS, name=name,...]
    ppermute x23, starting transfers between devices: 38.2 us -> 44.4 us  [exchange(): return lax.ppermute(block, axis, [(i, i ^ step) for i in range(count)])]
    ppermute x23, waiting for transfers between devices: 20.1 us -> 22.1 us  [exchange(): return lax.ppermute(block, axis, [(i, i ^ step) for i in range(count)])]
    ppermute x6, starting transfers between devices: 2.21 us -> 3.3 us  [swap(): return lax.ppermute(block, axis, route)]
  transfers between devices with their start and end apart: 29 -> 29, of which waited for: 12 -> 12; matrix products, arithmetic and copies ran while one was open for 0% -> 0% of each run, Pallas kernels for 25% -> 20%
where the time goes in v8:
time: 96.3 us; the launch traced here: 96.5 us
  starting transfers between devices  47.7 us (50%)
  Pallas kernels  25.7 us (27%)
  waiting for transfers between devices  22.2 us (23%)
    ppermute x23, starting transfers between devices, exchange(): return lax.ppermute(block, axis, [(i, i ^ step) for i in range(count)])  44.4 us
    pallas_call x23, Pallas kernels, call(): pl.pallas_call(kernel, out_shape=outs, compiler_params=PARAMS, name=name,...  25.7 us
    ppermute x23, waiting for transfers between devices, exchange(): return lax.ppermute(block, axis, [(i, i ^ step) for i in range(count)])  22.1 us
    ppermute x6, starting transfers between devices, swap(): return lax.ppermute(block, axis, route)  3.3 us
  transfers between devices with their start and end apart: 29, of which 12 were waited for; matrix products, arithmetic and copies ran while one was open for 0% of the time, Pallas kernels for 20%

profile of v8, /device:TPU:0, one launch (start us, length us, event | category | flops | bytes accessed | tf_op | source)
XLA Modules:
  0.0 96.5 jit_solution(5025250192220972723)
XLA Ops:
  0.7 2.3 %curve_order.1 = (f32[8,4096]{1,0:T(8,128)S(1)}, bf16[8,4096]{1,0:T(8,128)(2,1)S(1)}) custom-call(f32[8,4096]{1,0:T(8,128)} %right_in.1, s32[1,4096]{1,0:T(1,128)} %order_in.1), custom_call_target="tpu_custom_call" | custom-call | flops 10000000000 | tf_op jit(solution)/shard_map/curve_order/pallas_call | solution.py:450
  3.0 5.1 %collective-permute-start.2 = (bf16[8,4096]{1,0:T(8,128)(2,1)S(1)}, bf16[8,4096]{1,0:T(8,128)(2,1)S(1)}, u32[]{:S(2)}, u32[]{:S(2)}) collective-permute-start(bf16[8,4096]{1,0:T(8,128)(2,1)S(1)} %get-tuple-element.51.rounded_ref.refs_0_), channel_id=1, source_target_pairs={{0,3},{1,2},{2,1},{3,0},{4,7},{5,6},{6,5},{7,4},{8,11},{9,10},{10,... | collective-permute-start | bytes 196616 | tf_op jit(solution)/shard_map/ppermute | solution.py:434
  10.3 2.9 %early.3 = (f32[81,8,256]{2,1,0:T(8,128)S(1)}, f32[8,128]{1,0:T(8,128)S(1)}) custom-call(s32[1,1280]{1,0:T(1,128)S(4)} %lists.1.lists_ref, bf16[96,256,256]{2,1,0:T(8,128)(2,1)S(1)} %copy-done, bf16[16,256,256]{2,1,0:T(8,128)(2,1)S(1)} %copy-done.1, f32[1,4096]{1,0:T(1,128)S(1)} %bitcast.2, f32[8,4096]{1,0:T(8,128)S(1)} %get-tuple-element.50.own_ref.old_ref.refs_4_, ...), custom_call_target="tpu_custom_call" | custom-call | flops 3000000000 | tf_op jit(solution)/shard_map/early/pallas_call | solution.py:450
  14.8 2.8 %late.3.begun_ref = f32[81,8,256]{2,1,0:T(8,128)S(1)} custom-call(s32[1,1280]{1,0:T(1,128)S(4)} %lists.1.lists_ref, bf16[96,256,256]{2,1,0:T(8,128)(2,1)S(1)} %copy-done, f32[81,8,256]{2,1,0:T(8,128)S(1)} %get-tuple-element.52.begun_ref, f32[64,8,256]{2,1,0:T(8,128)S(1)} %get-tuple-element.53.field_ref), custom_call_target="tpu_custom_call" | custom-call | flops 3000000000 | tf_op jit(solution)/shard_map/late/pallas_call | solution.py:450
  18.2 3.9 %collective-permute-start.5 = (bf16[8,4096]{1,0:T(8,128)(2,1)S(1)}, bf16[8,4096]{1,0:T(8,128)(2,1)S(1)}, u32[]{:S(2)}, u32[]{:S(2)}) collective-permute-start(bf16[8,4096]{1,0:T(8,128)(2,1)S(1)} %get-tuple-element.59), channel_id=1, source_target_pairs={{0,3},{1,2},{2,1},{3,0},{4,7},{5,6},{6,5},{7,4},{8,11},{9,10},{10,... | collective-permute-start | bytes 196616 | tf_op jit(solution)/shard_map/ppermute | solution.py:434
  24.0 5.4 %turn.1.after_ref.blocks_ref = bf16[192,256,256]{2,1,0:T(8,128)(2,1)S(1)} custom-call(bf16[96,256,256]{2,1,0:T(8,128)(2,1)S(1)} %copy-done, f32[8,128]{1,0:T(8,128)S(1)} %get-tuple-element.57.after_ref.moments_in_ref), custom_call_target="tpu_custom_call" | custom-call | flops 4000000000 | tf_op jit(solution)/shard_map/turn/pallas_call | solution.py:450
  29.6 3.3 %collective-permute-start.10 = (bf16[8,4224]{1,0:T(8,128)(2,1)S(1)}, bf16[8,4224]{1,0:T(8,128)(2,1)S(1)}, u32[]{:S(2)}, u32[]{:S(2)}) collective-permute-start(bf16[8,4224]{1,0:T(8,128)(2,1)S(1)} %get-tuple-element.63.rounded_ref.refs_0_), channel_id=1, source_target_pairs={{0,3},{1,2},{2,1},{3,0},{4,7},{5,6},{6,5},{7,4},{8,11},{9,10},{10,... | collective-permute-start | bytes 202760 | tf_op jit(solution)/shard_map/ppermute | solution.py:434
  35.7 4.7 %collective-permute-done.9.refs_2_ = bf16[8,4224]{1,0:T(8,128)(2,1)S(1)} collective-permute-done((bf16[8,4224]{1,0:T(8,128)(2,1)S(1)}, bf16[8,4224]{1,0:T(8,128)(2,1)S(1)}, u32[]{:S(2)}, u32[]{:S(2)}) %collective-permute-start.9) | collective-permute-done | bytes 67616 | tf_op jit(solution)/shard_map/ppermute | solution.py:434
  41.9 2.0 %late.4.begun_ref = f32[81,8,256]{2,1,0:T(8,128)S(1)} custom-call(s32[1,1280]{1,0:T(1,128)S(4)} %lists.1.lists_ref, bf16[192,256,256]{2,1,0:T(8,128)(2,1)S(1)} %turn.1.after_ref.blocks_ref, f32[81,8,256]{2,1,0:T(8,128)S(1)} %early.4.begun_ref, f32[64,8,256]{2,1,0:T(8,128)S(1)} %get-tuple-element.65.field_ref, f32[8,640]{1,0:T(8,128)S(1)} %get-tuple-element.64.refs_0_.ratios_ref), custom_call_target="tpu_custom_call" | custom-call | flops 3000000000 | tf_op jit(solution)/shard_map/late/pallas_call | solution.py:450
  44.3 2.5 %collective-permute-start.13 = (bf16[8,4096]{1,0:T(8,128)(2,1)S(1)}, bf16[8,4096]{1,0:T(8,128)(2,1)S(1)}, u32[]{:S(2)}, u32[]{:S(2)}) collective-permute-start(bf16[8,4096]{1,0:T(8,128)(2,1)S(1)} %get-tuple-element.71), channel_id=1, source_target_pairs={{0,3},{1,2},{2,1},{3,0},{4,7},{5,6},{6,5},{7,4},{8,11},{9,10},{10,... | collective-permute-start | bytes 196616 | tf_op jit(solution)/shard_map/ppermute | solution.py:434
  46.7 2.0 %collective-permute-start.15 = (bf16[8,4096]{1,0:T(8,128)(2,1)S(1)}, bf16[8,4096]{1,0:T(8,128)(2,1)S(1)}, u32[]{:S(2)}, u32[]{:S(2)}) collective-permute-start(bf16[8,4096]{1,0:T(8,128)(2,1)S(1)} %get-tuple-element.73), channel_id=1, source_target_pairs={{0,1},{1,0},{2,3},{3,2},{4,5},{5,4},{6,7},{7,6},{8,9},{9,8},{10,11... | collective-permute-start | bytes 196616 | tf_op jit(solution)/shard_map/ppermute | solution.py:434
  48.7 1.7 %collective-permute-done.13.refs_0_ = bf16[8,4096]{1,0:T(8,128)(2,1)S(1)} collective-permute-done((bf16[8,4096]{1,0:T(8,128)(2,1)S(1)}, bf16[8,4096]{1,0:T(8,128)(2,1)S(1)}, u32[]{:S(2)}, u32[]{:S(2)}) %collective-permute-start.13) | collective-permute-done | bytes 65568 | tf_op jit(solution)/shard_map/ppermute | solution.py:434
  50.4 2.6 %collective-permute-done.14.refs_1_ = bf16[8,4096]{1,0:T(8,128)(2,1)S(1)} collective-permute-done((bf16[8,4096]{1,0:T(8,128)(2,1)S(1)}, bf16[8,4096]{1,0:T(8,128)(2,1)S(1)}, u32[]{:S(2)}, u32[]{:S(2)}) %collective-permute-start.14) | collective-permute-done | bytes 65568 | tf_op jit(solution)/shard_map/ppermute | solution.py:434
  53.1 1.9 %collective-permute-start.18 = (bf16[8,4096]{1,0:T(8,128)(2,1)S(1)}, bf16[8,4096]{1,0:T(8,128)(2,1)S(1)}, u32[]{:S(2)}, u32[]{:S(2)}) collective-permute-start(bf16[8,4096]{1,0:T(8,128)(2,1)S(1)} %get-tuple-element.75.rounded_ref.refs_1_), channel_id=1, source_target_pairs={{0,3},{1,2},{2,1},{3,0},{4,7},{5,6},{6,5},{7,4},{8,11},{9,10},{10,... | collective-permute-start | bytes 196616 | tf_op jit(solution)/shard_map/ppermute | solution.py:434
  55.0 2.5 %collective-permute-start.16 = (bf16[8,4096]{1,0:T(8,128)(2,1)S(1)}, bf16[8,4096]{1,0:T(8,128)(2,1)S(1)}, u32[]{:S(2)}, u32[]{:S(2)}) collective-permute-start(bf16[8,4096]{1,0:T(8,128)(2,1)S(1)} %get-tuple-element.75.rounded_ref.refs_1_), channel_id=1, source_target_pairs={{0,1},{1,0},{2,3},{3,2},{4,5},{5,4},{6,7},{7,6},{8,9},{9,8},{10,11... | collective-permute-start | bytes 196616 | tf_op jit(solution)/shard_map/ppermute | solution.py:434
  59.2 3.5 %collective-permute-done.17.refs_3_ = bf16[8,4096]{1,0:T(8,128)(2,1)S(1)} collective-permute-done((bf16[8,4096]{1,0:T(8,128)(2,1)S(1)}, bf16[8,4096]{1,0:T(8,128)(2,1)S(1)}, u32[]{:S(2)}, u32[]{:S(2)}) %collective-permute-start.17) | collective-permute-done | bytes 65568 | tf_op jit(solution)/shard_map/ppermute | solution.py:434
  64.5 2.0 %late.5.begun_ref = f32[81,8,256]{2,1,0:T(8,128)S(1)} custom-call(s32[1,1280]{1,0:T(1,128)S(4)} %lists.1.lists_ref, bf16[192,256,256]{2,1,0:T(8,128)(2,1)S(1)} %turn.1.after_ref.blocks_ref, f32[81,8,256]{2,1,0:T(8,128)S(1)} %early.5.begun_ref, f32[64,8,256]{2,1,0:T(8,128)S(1)} %get-tuple-element.76.field_ref, f32[8,640]{1,0:T(8,128)S(1)} %get-tuple-element.64.refs_0_.ratios_ref), custom_call_target="tpu_custom_call" | custom-call | flops 3000000000 | tf_op jit(solution)/shard_map/late/pallas_call | solution.py:450
  67.5 3.6 %collective-permute-done.21.second_ref = f32[8,128]{1,0:T(8,128)S(1)} collective-permute-done((f32[8,128]{1,0:T(8,128)S(1)}, f32[8,128]{1,0:T(8,128)S(1)}, u32[]{:S(2)}, u32[]{:S(2)}) %collective-permute-start.21) | collective-permute-done | bytes 4128 | tf_op jit(solution)/shard_map/ppermute | solution.py:434
  71.1 1.6 %collective-permute-start.22 = (f32[8,128]{1,0:T(8,128)S(1)}, f32[8,128]{1,0:T(8,128)S(1)}, u32[]{:S(2)}, u32[]{:S(2)}) collective-permute-start(f32[8,128]{1,0:T(8,128)S(1)} %add_moments.5.first_ref), channel_id=1, source_target_pairs={{0,2},{1,3},{2,0},{3,1},{4,6},{5,7},{6,4},{7,5},{8,10},{9,11},{10,... | collective-permute-start | bytes 12296 | tf_op jit(solution)/shard_map/ppermute | solution.py:434
  73.6 1.7 %collective-permute-start.27 = (f32[8,4096]{1,0:T(8,128)S(1)}, f32[8,4096]{1,0:T(8,128)S(1)}, u32[]{:S(2)}, u32[]{:S(2)}) collective-permute-start(f32[8,4096]{1,0:T(8,128)S(1)} %get-tuple-element.92), channel_id=1, source_target_pairs={{0,2},{1,3},{2,0},{3,1},{4,6},{5,7},{6,4},{7,5},{8,10},{9,11},{10,... | collective-permute-start | bytes 393224 | tf_op jit(solution)/shard_map/ppermute | solution.py:434
  77.3 5.2 %collective-permute-start.23 = (f32[8,128]{1,0:T(8,128)S(1)}, f32[8,128]{1,0:T(8,128)S(1)}, u32[]{:S(2)}, u32[]{:S(2)}) collective-permute-start(f32[8,128]{1,0:T(8,128)S(1)} %add_moments.6.first_ref), channel_id=1, source_target_pairs={{0,4},{4,0},{8,12},{12,8},{16,20},{20,16},{24,28},{28,24},{1,5},{5... | collective-permute-start | bytes 12296 | tf_op jit(solution)/shard_map/ppermute | solution.py:434
  83.4 3.1 %collective-permute-start.24 = (f32[8,128]{1,0:T(8,128)S(1)}, f32[8,128]{1,0:T(8,128)S(1)}, u32[]{:S(2)}, u32[]{:S(2)}) collective-permute-start(f32[8,128]{1,0:T(8,128)S(1)} %add_moments.7.first_ref), channel_id=1, source_target_pairs={{0,8},{4,12},{8,0},{12,4},{16,24},{20,28},{24,16},{28,20},{1,9},{5... | collective-permute-start | bytes 12296 | tf_op jit(solution)/shard_map/ppermute | solution.py:434
  86.5 1.6 %collective-permute-done.24.second_ref = f32[8,128]{1,0:T(8,128)S(1)} collective-permute-done((f32[8,128]{1,0:T(8,128)S(1)}, f32[8,128]{1,0:T(8,128)S(1)}, u32[]{:S(2)}, u32[]{:S(2)}) %collective-permute-start.24) | collective-permute-done | bytes 4128 | tf_op jit(solution)/shard_map/ppermute | solution.py:434
  88.2 5.6 %collective-permute-start.25 = (f32[8,128]{1,0:T(8,128)S(1)}, f32[8,128]{1,0:T(8,128)S(1)}, u32[]{:S(2)}, u32[]{:S(2)}) collective-permute-start(f32[8,128]{1,0:T(8,128)S(1)} %add_moments.8.first_ref), channel_id=1, source_target_pairs={{0,16},{4,20},{8,24},{12,28},{16,0},{20,4},{24,8},{28,12},{1,17},{... | collective-permute-start | bytes 12296 | tf_op jit(solution)/shard_map/ppermute | solution.py:434
  (66 shorter events, 22.1 us)
Async XLA Ops:
  3.0 10.2 %collective-permute-start.2 = (bf16[8,4096]{1,0:T(8,128)(2,1)S(1)}, bf16[8,4096]{1,0:T(8,128)(2,1)S(1)}, u32[]{:S(2)}, u32[]{:S(2)}) collective-permute-start(bf16[8,4096]{1,0:T(8,128)(2,1)S(1)} %get-tuple-element.51.rounded_ref.refs_0_), channel_id=1, source_target_pairs={{0,3},{1,2},{2,1},{3,0},{4,7},{5,6},{6,5},{7,4},{8,11},{9,10},{10,... | collective-permute-start | bytes 196616 | tf_op jit(solution)/shard_map/ppermute | solution.py:434
  8.1 5.6 %collective-permute-start.1 = (bf16[8,4096]{1,0:T(8,128)(2,1)S(1)}, bf16[8,4096]{1,0:T(8,128)(2,1)S(1)}, u32[]{:S(2)}, u32[]{:S(2)}) collective-permute-start(bf16[8,4096]{1,0:T(8,128)(2,1)S(1)} %get-tuple-element.51.rounded_ref.refs_0_), channel_id=1, source_target_pairs={{0,2},{1,3},{2,0},{3,1},{4,6},{5,7},{6,4},{7,5},{8,10},{9,11},{10,... | collective-permute-start | bytes 196616 | tf_op jit(solution)/shard_map/ppermute | solution.py:434
  8.1 5.6 %collective-permute-start = (bf16[8,4096]{1,0:T(8,128)(2,1)S(1)}, bf16[8,4096]{1,0:T(8,128)(2,1)S(1)}, u32[]{:S(2)}, u32[]{:S(2)}) collective-permute-start(bf16[8,4096]{1,0:T(8,128)(2,1)S(1)} %get-tuple-element.51.rounded_ref.refs_0_), channel_id=1, source_target_pairs={{0,1},{1,0},{2,3},{3,2},{4,5},{5,4},{6,7},{7,6},{8,9},{9,8},{10,11... | collective-permute-start | bytes 196616 | tf_op jit(solution)/shard_map/ppermute | solution.py:434
  14.1 3.6 %collective-permute-start.3 = (bf16[8,4096]{1,0:T(8,128)(2,1)S(1)}, bf16[8,4096]{1,0:T(8,128)(2,1)S(1)}, u32[]{:S(2)}, u32[]{:S(2)}) collective-permute-start(bf16[8,4096]{1,0:T(8,128)(2,1)S(1)} %get-tuple-element.54), channel_id=1, source_target_pairs={{0,4},{4,0},{8,12},{12,8},{16,20},{20,16},{24,28},{28,24},{1,5},{5... | collective-permute-start | bytes 196616 | tf_op jit(solution)/shard_map/ppermute | solution.py:442
  18.2 11.2 %collective-permute-start.5 = (bf16[8,4096]{1,0:T(8,128)(2,1)S(1)}, bf16[8,4096]{1,0:T(8,128)(2,1)S(1)}, u32[]{:S(2)}, u32[]{:S(2)}) collective-permute-start(bf16[8,4096]{1,0:T(8,128)(2,1)S(1)} %get-tuple-element.59), channel_id=1, source_target_pairs={{0,3},{1,2},{2,1},{3,0},{4,7},{5,6},{6,5},{7,4},{8,11},{9,10},{10,... | collective-permute-start | bytes 196616 | tf_op jit(solution)/shard_map/ppermute | solution.py:434
  22.0 7.4 %collective-permute-start.6 = (bf16[8,4096]{1,0:T(8,128)(2,1)S(1)}, bf16[8,4096]{1,0:T(8,128)(2,1)S(1)}, u32[]{:S(2)}, u32[]{:S(2)}) collective-permute-start(bf16[8,4096]{1,0:T(8,128)(2,1)S(1)} %get-tuple-element.60), channel_id=1, source_target_pairs={{0,2},{1,3},{2,0},{3,1},{4,6},{5,7},{6,4},{7,5},{8,10},{9,11},{10,... | collective-permute-start | bytes 196616 | tf_op jit(solution)/shard_map/ppermute | solution.py:434
  23.5 5.9 %collective-permute-start.7 = (bf16[8,4096]{1,0:T(8,128)(2,1)S(1)}, bf16[8,4096]{1,0:T(8,128)(2,1)S(1)}, u32[]{:S(2)}, u32[]{:S(2)}) collective-permute-start(bf16[8,4096]{1,0:T(8,128)(2,1)S(1)} %get-tuple-element.61), channel_id=1, source_target_pairs={{0,1},{1,0},{2,3},{3,2},{4,5},{5,4},{6,7},{7,6},{8,9},{9,8},{10,11... | collective-permute-start | bytes 196616 | tf_op jit(solution)/shard_map/ppermute | solution.py:434
  29.6 6.1 %collective-permute-start.10 = (bf16[8,4224]{1,0:T(8,128)(2,1)S(1)}, bf16[8,4224]{1,0:T(8,128)(2,1)S(1)}, u32[]{:S(2)}, u32[]{:S(2)}) collective-permute-start(bf16[8,4224]{1,0:T(8,128)(2,1)S(1)} %get-tuple-element.63.rounded_ref.refs_0_), channel_id=1, source_target_pairs={{0,3},{1,2},{2,1},{3,0},{4,7},{5,6},{6,5},{7,4},{8,11},{9,10},{10,... | collective-permute-start | bytes 202760 | tf_op jit(solution)/shard_map/ppermute | solution.py:434
  32.9 7.5 %collective-permute-start.9 = (bf16[8,4224]{1,0:T(8,128)(2,1)S(1)}, bf16[8,4224]{1,0:T(8,128)(2,1)S(1)}, u32[]{:S(2)}, u32[]{:S(2)}) collective-permute-start(bf16[8,4224]{1,0:T(8,128)(2,1)S(1)} %get-tuple-element.63.rounded_ref.refs_0_), channel_id=1, source_target_pairs={{0,2},{1,3},{2,0},{3,1},{4,6},{5,7},{6,4},{7,5},{8,10},{9,11},{10,... | collective-permute-start | bytes 202760 | tf_op jit(solution)/shard_map/ppermute | solution.py:434
  32.9 7.5 %collective-permute-start.8 = (bf16[8,4224]{1,0:T(8,128)(2,1)S(1)}, bf16[8,4224]{1,0:T(8,128)(2,1)S(1)}, u32[]{:S(2)}, u32[]{:S(2)}) collective-permute-start(bf16[8,4224]{1,0:T(8,128)(2,1)S(1)} %get-tuple-element.63.rounded_ref.refs_0_), channel_id=1, source_target_pairs={{0,1},{1,0},{2,3},{3,2},{4,5},{5,4},{6,7},{7,6},{8,9},{9,8},{10,11... | collective-permute-start | bytes 202760 | tf_op jit(solution)/shard_map/ppermute | solution.py:434
  44.3 6.1 %collective-permute-start.13 = (bf16[8,4096]{1,0:T(8,128)(2,1)S(1)}, bf16[8,4096]{1,0:T(8,128)(2,1)S(1)}, u32[]{:S(2)}, u32[]{:S(2)}) collective-permute-start(bf16[8,4096]{1,0:T(8,128)(2,1)S(1)} %get-tuple-element.71), channel_id=1, source_target_pairs={{0,3},{1,2},{2,1},{3,0},{4,7},{5,6},{6,5},{7,4},{8,11},{9,10},{10,... | collective-permute-start | bytes 196616 | tf_op jit(solution)/shard_map/ppermute | solution.py:434
  46.7 6.3 %collective-permute-start.14 = (bf16[8,4096]{1,0:T(8,128)(2,1)S(1)}, bf16[8,4096]{1,0:T(8,128)(2,1)S(1)}, u32[]{:S(2)}, u32[]{:S(2)}) collective-permute-start(bf16[8,4096]{1,0:T(8,128)(2,1)S(1)} %get-tuple-element.72), channel_id=1, source_target_pairs={{0,2},{1,3},{2,0},{3,1},{4,6},{5,7},{6,4},{7,5},{8,10},{9,11},{10,... | collective-permute-start | bytes 196616 | tf_op jit(solution)/shard_map/ppermute | solution.py:434
  46.7 6.3 %collective-permute-start.15 = (bf16[8,4096]{1,0:T(8,128)(2,1)S(1)}, bf16[8,4096]{1,0:T(8,128)(2,1)S(1)}, u32[]{:S(2)}, u32[]{:S(2)}) collective-permute-start(bf16[8,4096]{1,0:T(8,128)(2,1)S(1)} %get-tuple-element.73), channel_id=1, source_target_pairs={{0,1},{1,0},{2,3},{3,2},{4,5},{5,4},{6,7},{7,6},{8,9},{9,8},{10,11... | collective-permute-start | bytes 196616 | tf_op jit(solution)/shard_map/ppermute | solution.py:434
  53.1 6.1 %collective-permute-start.18 = (bf16[8,4096]{1,0:T(8,128)(2,1)S(1)}, bf16[8,4096]{1,0:T(8,128)(2,1)S(1)}, u32[]{:S(2)}, u32[]{:S(2)}) collective-permute-start(bf16[8,4096]{1,0:T(8,128)(2,1)S(1)} %get-tuple-element.75.rounded_ref.refs_1_), channel_id=1, source_target_pairs={{0,3},{1,2},{2,1},{3,0},{4,7},{5,6},{6,5},{7,4},{8,11},{9,10},{10,... | collective-permute-start | bytes 196616 | tf_op jit(solution)/shard_map/ppermute | solution.py:434
  55.0 7.7 %collective-permute-start.17 = (bf16[8,4096]{1,0:T(8,128)(2,1)S(1)}, bf16[8,4096]{1,0:T(8,128)(2,1)S(1)}, u32[]{:S(2)}, u32[]{:S(2)}) collective-permute-start(bf16[8,4096]{1,0:T(8,128)(2,1)S(1)} %get-tuple-element.75.rounded_ref.refs_1_), channel_id=1, source_target_pairs={{0,2},{1,3},{2,0},{3,1},{4,6},{5,7},{6,4},{7,5},{8,10},{9,11},{10,... | collective-permute-start | bytes 196616 | tf_op jit(solution)/shard_map/ppermute | solution.py:434
  55.0 7.7 %collective-permute-start.16 = (bf16[8,4096]{1,0:T(8,128)(2,1)S(1)}, bf16[8,4096]{1,0:T(8,128)(2,1)S(1)}, u32[]{:S(2)}, u32[]{:S(2)}) collective-permute-start(bf16[8,4096]{1,0:T(8,128)(2,1)S(1)} %get-tuple-element.75.rounded_ref.refs_1_), channel_id=1, source_target_pairs={{0,1},{1,0},{2,3},{3,2},{4,5},{5,4},{6,7},{7,6},{8,9},{9,8},{10,11... | collective-permute-start | bytes 196616 | tf_op jit(solution)/shard_map/ppermute | solution.py:434
  67.4 3.7 %collective-permute-start.21 = (f32[8,128]{1,0:T(8,128)S(1)}, f32[8,128]{1,0:T(8,128)S(1)}, u32[]{:S(2)}, u32[]{:S(2)}) collective-permute-start(f32[8,128]{1,0:T(8,128)S(1)} %get-tuple-element.84.first_ref), channel_id=1, source_target_pairs={{0,1},{1,0},{2,3},{3,2},{4,5},{5,4},{6,7},{7,6},{8,9},{9,8},{10,11... | collective-permute-start | bytes 12296 | tf_op jit(solution)/shard_map/ppermute | solution.py:434
  71.1 4.6 %collective-permute-start.22 = (f32[8,128]{1,0:T(8,128)S(1)}, f32[8,128]{1,0:T(8,128)S(1)}, u32[]{:S(2)}, u32[]{:S(2)}) collective-permute-start(f32[8,128]{1,0:T(8,128)S(1)} %add_moments.5.first_ref), channel_id=1, source_target_pairs={{0,2},{1,3},{2,0},{3,1},{4,6},{5,7},{6,4},{7,5},{8,10},{9,11},{10,... | collective-permute-start | bytes 12296 | tf_op jit(solution)/shard_map/ppermute | solution.py:434
  72.8 22.7 %collective-permute-start.26 = (f32[8,4096]{1,0:T(8,128)S(1)}, f32[8,4096]{1,0:T(8,128)S(1)}, u32[]{:S(2)}, u32[]{:S(2)}) collective-permute-start(f32[8,4096]{1,0:T(8,128)S(1)} %get-tuple-element.88), channel_id=1, source_target_pairs={{0,3},{1,2},{2,1},{3,0},{4,7},{5,6},{6,5},{7,4},{8,11},{9,10},{10,... | collective-permute-start | bytes 393224 | tf_op jit(solution)/shard_map/ppermute | solution.py:434
  73.6 21.9 %collective-permute-start.27 = (f32[8,4096]{1,0:T(8,128)S(1)}, f32[8,4096]{1,0:T(8,128)S(1)}, u32[]{:S(2)}, u32[]{:S(2)}) collective-permute-start(f32[8,4096]{1,0:T(8,128)S(1)} %get-tuple-element.92), channel_id=1, source_target_pairs={{0,2},{1,3},{2,0},{3,1},{4,6},{5,7},{6,4},{7,5},{8,10},{9,11},{10,... | collective-permute-start | bytes 393224 | tf_op jit(solution)/shard_map/ppermute | solution.py:434
  75.8 19.7 %collective-permute-start.28 = (f32[8,4096]{1,0:T(8,128)S(1)}, f32[8,4096]{1,0:T(8,128)S(1)}, u32[]{:S(2)}, u32[]{:S(2)}) collective-permute-start(f32[8,4096]{1,0:T(8,128)S(1)} %get-tuple-element.95), channel_id=1, source_target_pairs={{0,1},{1,0},{2,3},{3,2},{4,5},{5,4},{6,7},{7,6},{8,9},{9,8},{10,11... | collective-permute-start | bytes 393224 | tf_op jit(solution)/shard_map/ppermute | solution.py:434
  77.3 6.0 %collective-permute-start.23 = (f32[8,128]{1,0:T(8,128)S(1)}, f32[8,128]{1,0:T(8,128)S(1)}, u32[]{:S(2)}, u32[]{:S(2)}) collective-permute-start(f32[8,128]{1,0:T(8,128)S(1)} %add_moments.6.first_ref), channel_id=1, source_target_pairs={{0,4},{4,0},{8,12},{12,8},{16,20},{20,16},{24,28},{28,24},{1,5},{5... | collective-permute-start | bytes 12296 | tf_op jit(solution)/shard_map/ppermute | solution.py:434
  83.4 4.7 %collective-permute-start.24 = (f32[8,128]{1,0:T(8,128)S(1)}, f32[8,128]{1,0:T(8,128)S(1)}, u32[]{:S(2)}, u32[]{:S(2)}) collective-permute-start(f32[8,128]{1,0:T(8,128)S(1)} %add_moments.7.first_ref), channel_id=1, source_target_pairs={{0,8},{4,12},{8,0},{12,4},{16,24},{20,28},{24,16},{28,20},{1,9},{5... | collective-permute-start | bytes 12296 | tf_op jit(solution)/shard_map/ppermute | solution.py:434
  88.2 7.2 %collective-permute-start.25 = (f32[8,128]{1,0:T(8,128)S(1)}, f32[8,128]{1,0:T(8,128)S(1)}, u32[]{:S(2)}, u32[]{:S(2)}) collective-permute-start(f32[8,128]{1,0:T(8,128)S(1)} %add_moments.8.first_ref), channel_id=1, source_target_pairs={{0,16},{4,20},{8,24},{12,28},{16,0},{20,4},{24,8},{28,12},{1,17},{... | collective-permute-start | bytes 12296 | tf_op jit(solution)/shard_map/ppermute | solution.py:434
  (9 other events, 52.5 us)

commit v9 on v8

--- a/solution.py
+++ b/solution.py
@@ -263,6 +263,35 @@
     add_products(lists_ref, blocks_ref, slot_count, field_ref, total, LATE, LONG_GROUP)
 
 
+def neighbours(is_odd, even, odd):
+    return jnp.where(is_odd, even, odd), jnp.where(is_odd, odd, even)
+
+
+def curvature_kernel(
+    begun_ref, field_ref, even_ref, odd_ref, moments_in_ref, unit_ref, ratios_ref, sides_ref, moments_ref
+):
+    index = ITERS - 1
+    block_len = begun_ref.shape[2]
+    blocks_dev = even_ref.shape[1] // block_len
+    is_odd = lax.axis_index("tile") % 2 == 1
+    unit = unit_ref[...]
+    scale = widen(1.0 / (raised(ratios_ref[:, :LANES], 2 * index) * unit), block_len)
+    before = widen(2.0 * raised(sides_ref[:, :LANES], index), block_len)
+    product = jnp.zeros(begun_ref.shape[1:], F32)
+    for block in range(field_ref.shape[0]):
+        value = begun_ref[block]
+        if block < blocks_dev:
+            span = slice(block * block_len, (block + 1) * block_len)
+            arrived, _ = neighbours(is_odd, even_ref[:, span].astype(F32), odd_ref[:, span].astype(F32))
+            value += arrived * before
+        product += field_ref[block] * (value * scale)
+    last = jnp.sum(product, axis=1, keepdims=True)
+    moments = moments_in_ref[...]
+    lane = lax.broadcasted_iota(jnp.int32, moments.shape, 1)
+    moments = jnp.where(lane == 2 * ITERS - 1, last, moments)
+    moments_ref[...] = jnp.where(lane == 2 * ITERS, unit, moments)
+
+
 def lost_weight(moments):
     inner = [moments[:, order : order + 1] for order in range(4)]
     first = inner[1] / inner[0]
@@ -274,7 +303,7 @@
 
 def part_kernel(
     index, sub_count, slot_count, lists_ref, blocks_ref, begun_ref, field_ref, even_ref, odd_ref,
-    moments_in_ref, unit_ref, *refs
+    moments_in_ref, *refs
 ):
     *refs, total, ahead = refs
     if index == 1:
@@ -292,7 +321,7 @@
         even = even_ref[:, points_dev:].astype(F32)
         odd = odd_ref[:, points_dev:].astype(F32)
         tile_unit = ratios_ref[:, sub_count * LANES :]
-        sides = [jnp.where(is_odd, even, odd) / tile_unit, jnp.where(is_odd, odd, even) / tile_unit]
+        sides = [side / tile_unit for side in neighbours(is_odd, even, odd)]
         sides_ref[...] = jnp.concatenate(sides, axis=1)
     elif index:
         sides = [sides_ref[:, :LANES], sides_ref[:, LANES:]]
@@ -302,8 +331,7 @@
         span = slice(block * block_len, (block + 1) * block_len)
         even = even_ref[:, span].astype(F32)
         odd = odd_ref[:, span].astype(F32)
-        products = jnp.where(is_odd, even, odd)
-        first_row = jnp.where(is_odd, odd, even)
+        products, first_row = neighbours(is_odd, even, odd)
         ahead[block] = first_row * after if index else first_row
         total[block] = begun_ref[block] + (products * before if index else products)
     for block in range(blocks_dev, tile_blocks):
@@ -324,16 +352,6 @@
             part_refs[step][:, span] = rounded
             if step and kept_refs:
                 kept_refs[step - 1][:, span] = value - rounded.astype(F32)
-    if index + 1 == ITERS:
-        product = jnp.zeros(total.shape[1:], F32)
-        unit = unit_ref[...]
-        scale = widen(1.0 / (raised(ratios_ref[:, :LANES], 2 * index) * unit), block_len)
-        for block in range(tile_blocks):
-            product += field_ref[block] * (total[block] * scale)
-        last = jnp.sum(product, axis=1, keepdims=True)
-        lane = lax.broadcasted_iota(jnp.int32, moments.shape, 1)
-        moments = jnp.where(lane == 2 * ITERS - 1, last, moments)
-        moments = jnp.where(lane == 2 * ITERS, unit, moments)
     moments_ref[...] = moments
 
 
@@ -542,6 +560,13 @@
             "late",
             3,
         )
+        if is_last:
+            curved = call(
+                curvature_kernel,
+                scalars,
+                (begun, tile_field, even, odd, moments, unit, *ratios, *sides),
+                "curvature",
+            )
         part = shape(rhs_count, points_dev, F32 if is_last else BF16)
         found = call(
             functools.partial(part_kernel, index, sub_count, slot_count),
@@ -550,7 +575,7 @@
             + (scalars,)
             + ((full,) * (sub_count - 1) if index + 2 == ITERS else ())
             + ((shape(rhs_count, 2 * LANES, F32),) if index == 1 else ()),
-            (lists, blocks, begun, tile_field, even, odd, moments, unit, *ratios, *sides, *(lost if is_last else ())),
+            (lists, blocks, begun, tile_field, even, odd, moments, *ratios, *sides, *(lost if is_last else ())),
             "parts",
             1,
             scratch_shapes=[scratch(extended + 1), scratch(blocks_dev)],
@@ -578,6 +603,7 @@
             "join",
         )
         basis.append(field)
+    moments = curved
     arrived = []
     for axis, count in (("sub", sub_count), ("tile", tile_count)):
         step = 1

time: 96.3 us -> 95 us (0.987)
  starting transfers between devices: 47.7 us -> 45.8 us
  Pallas kernels: 25.7 us -> 26.9 us
    ppermute x23, starting transfers between devices: 44.4 us -> 43.1 us  [exchange(): return lax.ppermute(block, axis, [(i, i ^ step) for i in range(count)])]
    pallas_call x23 -> x24, Pallas kernels: 25.7 us -> 26.9 us  [call(): pl.pallas_call(kernel, out_shape=outs, compiler_params=PARAMS, name=name,...]
  transfers between devices with their start and end apart: 29 -> 29, of which waited for: 12 -> 12; matrix products, arithmetic and copies ran while one was open for 0% -> 0% of each run, Pallas kernels for 20% -> 21%
where the time goes in v9:
time: 95 us; the launch traced here: 95.6 us
  starting transfers between devices  45.8 us (48%)
  Pallas kernels  26.9 us (28%)
  waiting for transfers between devices  21.9 us (23%)
    ppermute x23, starting transfers between devices, exchange(): return lax.ppermute(block, axis, [(i, i ^ step) for i in range(count)])  43.1 us
    pallas_call x24, Pallas kernels, call(): pl.pallas_call(kernel, out_shape=outs, compiler_params=PARAMS, name=name,...  26.9 us
    ppermute x23, waiting for transfers between devices, exchange(): return lax.ppermute(block, axis, [(i, i ^ step) for i in range(count)])  21.9 us
    ppermute x6, starting transfers between devices, swap(): return lax.ppermute(block, axis, route)  2.7 us
  transfers between devices with their start and end apart: 29, of which 12 were waited for; matrix products, arithmetic and copies ran while one was open for 0% of the time, Pallas kernels for 21%

profile of v9, /device:TPU:0, one launch (start us, length us, event | category | flops | bytes accessed | tf_op | source)
XLA Modules:
  0.0 95.6 jit_solution(14332335854263053828)
XLA Ops:
  0.7 2.3 %curve_order.1 = (f32[8,4096]{1,0:T(8,128)S(1)}, bf16[8,4096]{1,0:T(8,128)(2,1)S(1)}) custom-call(f32[8,4096]{1,0:T(8,128)} %right_in.1, s32[1,4096]{1,0:T(1,128)} %order_in.1), custom_call_target="tpu_custom_call" | custom-call | flops 10000000000 | tf_op jit(solution)/shard_map/curve_order/pallas_call | solution.py:468
  3.0 5.1 %collective-permute-start.2 = (bf16[8,4096]{1,0:T(8,128)(2,1)S(1)}, bf16[8,4096]{1,0:T(8,128)(2,1)S(1)}, u32[]{:S(2)}, u32[]{:S(2)}) collective-permute-start(bf16[8,4096]{1,0:T(8,128)(2,1)S(1)} %get-tuple-element.50.rounded_ref.refs_0_), channel_id=1, source_target_pairs={{0,3},{1,2},{2,1},{3,0},{4,7},{5,6},{6,5},{7,4},{8,11},{9,10},{10,... | collective-permute-start | bytes 196616 | tf_op jit(solution)/shard_map/ppermute | solution.py:452
  10.3 2.5 %early.3 = (f32[81,8,256]{2,1,0:T(8,128)S(1)}, f32[8,128]{1,0:T(8,128)S(1)}) custom-call(s32[1,1280]{1,0:T(1,128)S(4)} %lists.1.lists_ref, bf16[96,256,256]{2,1,0:T(8,128)(2,1)S(1)} %copy-done, bf16[16,256,256]{2,1,0:T(8,128)(2,1)S(1)} %copy-done.1, f32[1,4096]{1,0:T(1,128)S(1)} %bitcast.2, f32[8,4096]{1,0:T(8,128)S(1)} %get-tuple-element.49.own_ref.old_ref.refs_4_, ...), custom_call_target="tpu_custom_call" | custom-call | flops 3000000000 | tf_op jit(solution)/shard_map/early/pallas_call | solution.py:468
  15.1 3.2 %late.3.begun_ref = f32[81,8,256]{2,1,0:T(8,128)S(1)} custom-call(s32[1,1280]{1,0:T(1,128)S(4)} %lists.1.lists_ref, bf16[96,256,256]{2,1,0:T(8,128)(2,1)S(1)} %copy-done, f32[81,8,256]{2,1,0:T(8,128)S(1)} %get-tuple-element.51.begun_ref, f32[64,8,256]{2,1,0:T(8,128)S(1)} %get-tuple-element.52.field_ref), custom_call_target="tpu_custom_call" | custom-call | flops 3000000000 | tf_op jit(solution)/shard_map/late/pallas_call | solution.py:468
  19.2 2.8 %collective-permute-start.5 = (bf16[8,4096]{1,0:T(8,128)(2,1)S(1)}, bf16[8,4096]{1,0:T(8,128)(2,1)S(1)}, u32[]{:S(2)}, u32[]{:S(2)}) collective-permute-start(bf16[8,4096]{1,0:T(8,128)(2,1)S(1)} %get-tuple-element.58), channel_id=1, source_target_pairs={{0,3},{1,2},{2,1},{3,0},{4,7},{5,6},{6,5},{7,4},{8,11},{9,10},{10,... | collective-permute-start | bytes 196616 | tf_op jit(solution)/shard_map/ppermute | solution.py:452
  24.0 5.4 %turn.1.after_ref.blocks_ref = bf16[192,256,256]{2,1,0:T(8,128)(2,1)S(1)} custom-call(bf16[96,256,256]{2,1,0:T(8,128)(2,1)S(1)} %copy-done, f32[8,128]{1,0:T(8,128)S(1)} %get-tuple-element.55.after_ref.moments_in_ref), custom_call_target="tpu_custom_call" | custom-call | flops 4000000000 | tf_op jit(solution)/shard_map/turn/pallas_call | solution.py:468
  29.6 3.6 %collective-permute-start.10 = (bf16[8,4224]{1,0:T(8,128)(2,1)S(1)}, bf16[8,4224]{1,0:T(8,128)(2,1)S(1)}, u32[]{:S(2)}, u32[]{:S(2)}) collective-permute-start(bf16[8,4224]{1,0:T(8,128)(2,1)S(1)} %get-tuple-element.62.rounded_ref.refs_0_), channel_id=1, source_target_pairs={{0,3},{1,2},{2,1},{3,0},{4,7},{5,6},{6,5},{7,4},{8,11},{9,10},{10,... | collective-permute-start | bytes 202760 | tf_op jit(solution)/shard_map/ppermute | solution.py:452
  35.7 4.8 %collective-permute-done.9.refs_2_ = bf16[8,4224]{1,0:T(8,128)(2,1)S(1)} collective-permute-done((bf16[8,4224]{1,0:T(8,128)(2,1)S(1)}, bf16[8,4224]{1,0:T(8,128)(2,1)S(1)}, u32[]{:S(2)}, u32[]{:S(2)}) %collective-permute-start.9) | collective-permute-done | bytes 67616 | tf_op jit(solution)/shard_map/ppermute | solution.py:452
  41.8 2.0 %late.4.begun_ref = f32[81,8,256]{2,1,0:T(8,128)S(1)} custom-call(s32[1,1280]{1,0:T(1,128)S(4)} %lists.1.lists_ref, bf16[192,256,256]{2,1,0:T(8,128)(2,1)S(1)} %turn.1.after_ref.blocks_ref, f32[81,8,256]{2,1,0:T(8,128)S(1)} %early.4.begun_ref, f32[64,8,256]{2,1,0:T(8,128)S(1)} %get-tuple-element.64.field_ref, f32[8,640]{1,0:T(8,128)S(1)} %get-tuple-element.63.refs_0_.ratios_ref), custom_call_target="tpu_custom_call" | custom-call | flops 3000000000 | tf_op jit(solution)/shard_map/late/pallas_call | solution.py:468
  44.5 2.3 %collective-permute-start.13 = (bf16[8,4096]{1,0:T(8,128)(2,1)S(1)}, bf16[8,4096]{1,0:T(8,128)(2,1)S(1)}, u32[]{:S(2)}, u32[]{:S(2)}) collective-permute-start(bf16[8,4096]{1,0:T(8,128)(2,1)S(1)} %get-tuple-element.70), channel_id=1, source_target_pairs={{0,3},{1,2},{2,1},{3,0},{4,7},{5,6},{6,5},{7,4},{8,11},{9,10},{10,... | collective-permute-start | bytes 196616 | tf_op jit(solution)/shard_map/ppermute | solution.py:452
  47.0 1.9 %collective-permute-start.15 = (bf16[8,4096]{1,0:T(8,128)(2,1)S(1)}, bf16[8,4096]{1,0:T(8,128)(2,1)S(1)}, u32[]{:S(2)}, u32[]{:S(2)}) collective-permute-start(bf16[8,4096]{1,0:T(8,128)(2,1)S(1)} %get-tuple-element.72), channel_id=1, source_target_pairs={{0,1},{1,0},{2,3},{3,2},{4,5},{5,4},{6,7},{7,6},{8,9},{9,8},{10,11... | collective-permute-start | bytes 196616 | tf_op jit(solution)/shard_map/ppermute | solution.py:452
  48.9 1.7 %collective-permute-done.13.refs_0_ = bf16[8,4096]{1,0:T(8,128)(2,1)S(1)} collective-permute-done((bf16[8,4096]{1,0:T(8,128)(2,1)S(1)}, bf16[8,4096]{1,0:T(8,128)(2,1)S(1)}, u32[]{:S(2)}, u32[]{:S(2)}) %collective-permute-start.13) | collective-permute-done | bytes 65568 | tf_op jit(solution)/shard_map/ppermute | solution.py:452
  50.6 2.3 %collective-permute-done.14.refs_1_ = bf16[8,4096]{1,0:T(8,128)(2,1)S(1)} collective-permute-done((bf16[8,4096]{1,0:T(8,128)(2,1)S(1)}, bf16[8,4096]{1,0:T(8,128)(2,1)S(1)}, u32[]{:S(2)}, u32[]{:S(2)}) %collective-permute-start.14) | collective-permute-done | bytes 65568 | tf_op jit(solution)/shard_map/ppermute | solution.py:452
  53.1 2.2 %collective-permute-start.18 = (bf16[8,4096]{1,0:T(8,128)(2,1)S(1)}, bf16[8,4096]{1,0:T(8,128)(2,1)S(1)}, u32[]{:S(2)}, u32[]{:S(2)}) collective-permute-start(bf16[8,4096]{1,0:T(8,128)(2,1)S(1)} %get-tuple-element.74.rounded_ref.refs_1_), channel_id=1, source_target_pairs={{0,3},{1,2},{2,1},{3,0},{4,7},{5,6},{6,5},{7,4},{8,11},{9,10},{10,... | collective-permute-start | bytes 196616 | tf_op jit(solution)/shard_map/ppermute | solution.py:452
  55.3 2.2 %collective-permute-start.16 = (bf16[8,4096]{1,0:T(8,128)(2,1)S(1)}, bf16[8,4096]{1,0:T(8,128)(2,1)S(1)}, u32[]{:S(2)}, u32[]{:S(2)}) collective-permute-start(bf16[8,4096]{1,0:T(8,128)(2,1)S(1)} %get-tuple-element.74.rounded_ref.refs_1_), channel_id=1, source_target_pairs={{0,1},{1,0},{2,3},{3,2},{4,5},{5,4},{6,7},{7,6},{8,9},{9,8},{10,11... | collective-permute-start | bytes 196616 | tf_op jit(solution)/shard_map/ppermute | solution.py:452
  59.2 3.5 %collective-permute-done.17.refs_3_ = bf16[8,4096]{1,0:T(8,128)(2,1)S(1)} collective-permute-done((bf16[8,4096]{1,0:T(8,128)(2,1)S(1)}, bf16[8,4096]{1,0:T(8,128)(2,1)S(1)}, u32[]{:S(2)}, u32[]{:S(2)}) %collective-permute-start.17) | collective-permute-done | bytes 65568 | tf_op jit(solution)/shard_map/ppermute | solution.py:452
  64.5 2.0 %late.5.begun_ref = f32[81,8,256]{2,1,0:T(8,128)S(1)} custom-call(s32[1,1280]{1,0:T(1,128)S(4)} %lists.1.lists_ref, bf16[192,256,256]{2,1,0:T(8,128)(2,1)S(1)} %turn.1.after_ref.blocks_ref, f32[81,8,256]{2,1,0:T(8,128)S(1)} %early.5.begun_ref, f32[64,8,256]{2,1,0:T(8,128)S(1)} %get-tuple-element.75.field_ref, f32[8,640]{1,0:T(8,128)S(1)} %get-tuple-element.63.refs_0_.ratios_ref), custom_call_target="tpu_custom_call" | custom-call | flops 3000000000 | tf_op jit(solution)/shard_map/late/pallas_call | solution.py:468
  67.9 2.4 %collective-permute-done.21.second_ref = f32[8,128]{1,0:T(8,128)S(1)} collective-permute-done((f32[8,128]{1,0:T(8,128)S(1)}, f32[8,128]{1,0:T(8,128)S(1)}, u32[]{:S(2)}, u32[]{:S(2)}) %collective-permute-start.21) | collective-permute-done | bytes 4128 | tf_op jit(solution)/shard_map/ppermute | solution.py:452
  70.4 1.8 %collective-permute-start.22 = (f32[8,128]{1,0:T(8,128)S(1)}, f32[8,128]{1,0:T(8,128)S(1)}, u32[]{:S(2)}, u32[]{:S(2)}) collective-permute-start(f32[8,128]{1,0:T(8,128)S(1)} %add_moments.5.first_ref), channel_id=1, source_target_pairs={{0,2},{1,3},{2,0},{3,1},{4,6},{5,7},{6,4},{7,5},{8,10},{9,11},{10,... | collective-permute-start | bytes 12296 | tf_op jit(solution)/shard_map/ppermute | solution.py:452
  72.8 1.7 %collective-permute-start.27 = (f32[8,4096]{1,0:T(8,128)S(1)}, f32[8,4096]{1,0:T(8,128)S(1)}, u32[]{:S(2)}, u32[]{:S(2)}) collective-permute-start(f32[8,4096]{1,0:T(8,128)S(1)} %get-tuple-element.90), channel_id=1, source_target_pairs={{0,2},{1,3},{2,0},{3,1},{4,6},{5,7},{6,4},{7,5},{8,10},{9,11},{10,... | collective-permute-start | bytes 393224 | tf_op jit(solution)/shard_map/ppermute | solution.py:452
  75.1 1.7 %collective-permute-start.28 = (f32[8,4096]{1,0:T(8,128)S(1)}, f32[8,4096]{1,0:T(8,128)S(1)}, u32[]{:S(2)}, u32[]{:S(2)}) collective-permute-start(f32[8,4096]{1,0:T(8,128)S(1)} %get-tuple-element.93), channel_id=1, source_target_pairs={{0,1},{1,0},{2,3},{3,2},{4,5},{5,4},{6,7},{7,6},{8,9},{9,8},{10,11... | collective-permute-start | bytes 393224 | tf_op jit(solution)/shard_map/ppermute | solution.py:452
  76.8 4.6 %collective-permute-start.23 = (f32[8,128]{1,0:T(8,128)S(1)}, f32[8,128]{1,0:T(8,128)S(1)}, u32[]{:S(2)}, u32[]{:S(2)}) collective-permute-start(f32[8,128]{1,0:T(8,128)S(1)} %add_moments.6.first_ref), channel_id=1, source_target_pairs={{0,4},{4,0},{8,12},{12,8},{16,20},{20,16},{24,28},{28,24},{1,5},{5... | collective-permute-start | bytes 12296 | tf_op jit(solution)/shard_map/ppermute | solution.py:452
  82.3 2.4 %collective-permute-start.24 = (f32[8,128]{1,0:T(8,128)S(1)}, f32[8,128]{1,0:T(8,128)S(1)}, u32[]{:S(2)}, u32[]{:S(2)}) collective-permute-start(f32[8,128]{1,0:T(8,128)S(1)} %add_moments.7.first_ref), channel_id=1, source_target_pairs={{0,8},{4,12},{8,0},{12,4},{16,24},{20,28},{24,16},{28,20},{1,9},{5... | collective-permute-start | bytes 12296 | tf_op jit(solution)/shard_map/ppermute | solution.py:452
  86.3 6.6 %collective-permute-start.25 = (f32[8,128]{1,0:T(8,128)S(1)}, f32[8,128]{1,0:T(8,128)S(1)}, u32[]{:S(2)}, u32[]{:S(2)}) collective-permute-start(f32[8,128]{1,0:T(8,128)S(1)} %add_moments.8.first_ref), channel_id=1, source_target_pairs={{0,16},{4,20},{8,24},{12,28},{16,0},{20,4},{24,8},{28,12},{1,17},{... | collective-permute-start | bytes 12296 | tf_op jit(solution)/shard_map/ppermute | solution.py:452
  (67 shorter events, 23.7 us)
Async XLA Ops:
  3.0 9.8 %collective-permute-start.2 = (bf16[8,4096]{1,0:T(8,128)(2,1)S(1)}, bf16[8,4096]{1,0:T(8,128)(2,1)S(1)}, u32[]{:S(2)}, u32[]{:S(2)}) collective-permute-start(bf16[8,4096]{1,0:T(8,128)(2,1)S(1)} %get-tuple-element.50.rounded_ref.refs_0_), channel_id=1, source_target_pairs={{0,3},{1,2},{2,1},{3,0},{4,7},{5,6},{6,5},{7,4},{8,11},{9,10},{10,... | collective-permute-start | bytes 196616 | tf_op jit(solution)/shard_map/ppermute | solution.py:452
  8.1 5.6 %collective-permute-start.1 = (bf16[8,4096]{1,0:T(8,128)(2,1)S(1)}, bf16[8,4096]{1,0:T(8,128)(2,1)S(1)}, u32[]{:S(2)}, u32[]{:S(2)}) collective-permute-start(bf16[8,4096]{1,0:T(8,128)(2,1)S(1)} %get-tuple-element.50.rounded_ref.refs_0_), channel_id=1, source_target_pairs={{0,2},{1,3},{2,0},{3,1},{4,6},{5,7},{6,4},{7,5},{8,10},{9,11},{10,... | collective-permute-start | bytes 196616 | tf_op jit(solution)/shard_map/ppermute | solution.py:452
  8.1 5.6 %collective-permute-start = (bf16[8,4096]{1,0:T(8,128)(2,1)S(1)}, bf16[8,4096]{1,0:T(8,128)(2,1)S(1)}, u32[]{:S(2)}, u32[]{:S(2)}) collective-permute-start(bf16[8,4096]{1,0:T(8,128)(2,1)S(1)} %get-tuple-element.50.rounded_ref.refs_0_), channel_id=1, source_target_pairs={{0,1},{1,0},{2,3},{3,2},{4,5},{5,4},{6,7},{7,6},{8,9},{9,8},{10,11... | collective-permute-start | bytes 196616 | tf_op jit(solution)/shard_map/ppermute | solution.py:452
  14.3 4.0 %collective-permute-start.3 = (bf16[8,4096]{1,0:T(8,128)(2,1)S(1)}, bf16[8,4096]{1,0:T(8,128)(2,1)S(1)}, u32[]{:S(2)}, u32[]{:S(2)}) collective-permute-start(bf16[8,4096]{1,0:T(8,128)(2,1)S(1)} %get-tuple-element.53), channel_id=1, source_target_pairs={{0,4},{4,0},{8,12},{12,8},{16,20},{20,16},{24,28},{28,24},{1,5},{5... | collective-permute-start | bytes 196616 | tf_op jit(solution)/shard_map/ppermute | solution.py:460
  14.4 3.9 %collective-permute-start.4 = (bf16[8,4096]{1,0:T(8,128)(2,1)S(1)}, bf16[8,4096]{1,0:T(8,128)(2,1)S(1)}, u32[]{:S(2)}, u32[]{:S(2)}) collective-permute-start(bf16[8,4096]{1,0:T(8,128)(2,1)S(1)} %get-tuple-element.54), channel_id=1, source_target_pairs={{4,8},{8,4},{12,16},{16,12},{20,24},{24,20},{5,9},{9,5},{13,17},{1... | collective-permute-start | bytes 196616 | tf_op jit(solution)/shard_map/ppermute | solution.py:460
  19.2 10.2 %collective-permute-start.5 = (bf16[8,4096]{1,0:T(8,128)(2,1)S(1)}, bf16[8,4096]{1,0:T(8,128)(2,1)S(1)}, u32[]{:S(2)}, u32[]{:S(2)}) collective-permute-start(bf16[8,4096]{1,0:T(8,128)(2,1)S(1)} %get-tuple-element.58), channel_id=1, source_target_pairs={{0,3},{1,2},{2,1},{3,0},{4,7},{5,6},{6,5},{7,4},{8,11},{9,10},{10,... | collective-permute-start | bytes 196616 | tf_op jit(solution)/shard_map/ppermute | solution.py:452
  22.0 7.4 %collective-permute-start.6 = (bf16[8,4096]{1,0:T(8,128)(2,1)S(1)}, bf16[8,4096]{1,0:T(8,128)(2,1)S(1)}, u32[]{:S(2)}, u32[]{:S(2)}) collective-permute-start(bf16[8,4096]{1,0:T(8,128)(2,1)S(1)} %get-tuple-element.59), channel_id=1, source_target_pairs={{0,2},{1,3},{2,0},{3,1},{4,6},{5,7},{6,4},{7,5},{8,10},{9,11},{10,... | collective-permute-start | bytes 196616 | tf_op jit(solution)/shard_map/ppermute | solution.py:452
  23.5 5.9 %collective-permute-start.7 = (bf16[8,4096]{1,0:T(8,128)(2,1)S(1)}, bf16[8,4096]{1,0:T(8,128)(2,1)S(1)}, u32[]{:S(2)}, u32[]{:S(2)}) collective-permute-start(bf16[8,4096]{1,0:T(8,128)(2,1)S(1)} %get-tuple-element.60), channel_id=1, source_target_pairs={{0,1},{1,0},{2,3},{3,2},{4,5},{5,4},{6,7},{7,6},{8,9},{9,8},{10,11... | collective-permute-start | bytes 196616 | tf_op jit(solution)/shard_map/ppermute | solution.py:452
  29.6 6.1 %collective-permute-start.10 = (bf16[8,4224]{1,0:T(8,128)(2,1)S(1)}, bf16[8,4224]{1,0:T(8,128)(2,1)S(1)}, u32[]{:S(2)}, u32[]{:S(2)}) collective-permute-start(bf16[8,4224]{1,0:T(8,128)(2,1)S(1)} %get-tuple-element.62.rounded_ref.refs_0_), channel_id=1, source_target_pairs={{0,3},{1,2},{2,1},{3,0},{4,7},{5,6},{6,5},{7,4},{8,11},{9,10},{10,... | collective-permute-start | bytes 202760 | tf_op jit(solution)/shard_map/ppermute | solution.py:452
  33.1 7.3 %collective-permute-start.9 = (bf16[8,4224]{1,0:T(8,128)(2,1)S(1)}, bf16[8,4224]{1,0:T(8,128)(2,1)S(1)}, u32[]{:S(2)}, u32[]{:S(2)}) collective-permute-start(bf16[8,4224]{1,0:T(8,128)(2,1)S(1)} %get-tuple-element.62.rounded_ref.refs_0_), channel_id=1, source_target_pairs={{0,2},{1,3},{2,0},{3,1},{4,6},{5,7},{6,4},{7,5},{8,10},{9,11},{10,... | collective-permute-start | bytes 202760 | tf_op jit(solution)/shard_map/ppermute | solution.py:452
  33.1 7.3 %collective-permute-start.8 = (bf16[8,4224]{1,0:T(8,128)(2,1)S(1)}, bf16[8,4224]{1,0:T(8,128)(2,1)S(1)}, u32[]{:S(2)}, u32[]{:S(2)}) collective-permute-start(bf16[8,4224]{1,0:T(8,128)(2,1)S(1)} %get-tuple-element.62.rounded_ref.refs_0_), channel_id=1, source_target_pairs={{0,1},{1,0},{2,3},{3,2},{4,5},{5,4},{6,7},{7,6},{8,9},{9,8},{10,11... | collective-permute-start | bytes 202760 | tf_op jit(solution)/shard_map/ppermute | solution.py:452
  44.5 6.1 %collective-permute-start.13 = (bf16[8,4096]{1,0:T(8,128)(2,1)S(1)}, bf16[8,4096]{1,0:T(8,128)(2,1)S(1)}, u32[]{:S(2)}, u32[]{:S(2)}) collective-permute-start(bf16[8,4096]{1,0:T(8,128)(2,1)S(1)} %get-tuple-element.70), channel_id=1, source_target_pairs={{0,3},{1,2},{2,1},{3,0},{4,7},{5,6},{6,5},{7,4},{8,11},{9,10},{10,... | collective-permute-start | bytes 196616 | tf_op jit(solution)/shard_map/ppermute | solution.py:452
  46.8 6.2 %collective-permute-start.14 = (bf16[8,4096]{1,0:T(8,128)(2,1)S(1)}, bf16[8,4096]{1,0:T(8,128)(2,1)S(1)}, u32[]{:S(2)}, u32[]{:S(2)}) collective-permute-start(bf16[8,4096]{1,0:T(8,128)(2,1)S(1)} %get-tuple-element.71), channel_id=1, source_target_pairs={{0,2},{1,3},{2,0},{3,1},{4,6},{5,7},{6,4},{7,5},{8,10},{9,11},{10,... | collective-permute-start | bytes 196616 | tf_op jit(solution)/shard_map/ppermute | solution.py:452
  47.0 5.9 %collective-permute-start.15 = (bf16[8,4096]{1,0:T(8,128)(2,1)S(1)}, bf16[8,4096]{1,0:T(8,128)(2,1)S(1)}, u32[]{:S(2)}, u32[]{:S(2)}) collective-permute-start(bf16[8,4096]{1,0:T(8,128)(2,1)S(1)} %get-tuple-element.72), channel_id=1, source_target_pairs={{0,1},{1,0},{2,3},{3,2},{4,5},{5,4},{6,7},{7,6},{8,9},{9,8},{10,11... | collective-permute-start | bytes 196616 | tf_op jit(solution)/shard_map/ppermute | solution.py:452
  53.1 6.1 %collective-permute-start.18 = (bf16[8,4096]{1,0:T(8,128)(2,1)S(1)}, bf16[8,4096]{1,0:T(8,128)(2,1)S(1)}, u32[]{:S(2)}, u32[]{:S(2)}) collective-permute-start(bf16[8,4096]{1,0:T(8,128)(2,1)S(1)} %get-tuple-element.74.rounded_ref.refs_1_), channel_id=1, source_target_pairs={{0,3},{1,2},{2,1},{3,0},{4,7},{5,6},{6,5},{7,4},{8,11},{9,10},{10,... | collective-permute-start | bytes 196616 | tf_op jit(solution)/shard_map/ppermute | solution.py:452
  55.3 7.4 %collective-permute-start.17 = (bf16[8,4096]{1,0:T(8,128)(2,1)S(1)}, bf16[8,4096]{1,0:T(8,128)(2,1)S(1)}, u32[]{:S(2)}, u32[]{:S(2)}) collective-permute-start(bf16[8,4096]{1,0:T(8,128)(2,1)S(1)} %get-tuple-element.74.rounded_ref.refs_1_), channel_id=1, source_target_pairs={{0,2},{1,3},{2,0},{3,1},{4,6},{5,7},{6,4},{7,5},{8,10},{9,11},{10,... | collective-permute-start | bytes 196616 | tf_op jit(solution)/shard_map/ppermute | solution.py:452
  55.3 7.4 %collective-permute-start.16 = (bf16[8,4096]{1,0:T(8,128)(2,1)S(1)}, bf16[8,4096]{1,0:T(8,128)(2,1)S(1)}, u32[]{:S(2)}, u32[]{:S(2)}) collective-permute-start(bf16[8,4096]{1,0:T(8,128)(2,1)S(1)} %get-tuple-element.74.rounded_ref.refs_1_), channel_id=1, source_target_pairs={{0,1},{1,0},{2,3},{3,2},{4,5},{5,4},{6,7},{7,6},{8,9},{9,8},{10,11... | collective-permute-start | bytes 196616 | tf_op jit(solution)/shard_map/ppermute | solution.py:452
  70.4 4.6 %collective-permute-start.22 = (f32[8,128]{1,0:T(8,128)S(1)}, f32[8,128]{1,0:T(8,128)S(1)}, u32[]{:S(2)}, u32[]{:S(2)}) collective-permute-start(f32[8,128]{1,0:T(8,128)S(1)} %add_moments.5.first_ref), channel_id=1, source_target_pairs={{0,2},{1,3},{2,0},{3,1},{4,6},{5,7},{6,4},{7,5},{8,10},{9,11},{10,... | collective-permute-start | bytes 12296 | tf_op jit(solution)/shard_map/ppermute | solution.py:452
  72.2 22.4 %collective-permute-start.26 = (f32[8,4096]{1,0:T(8,128)S(1)}, f32[8,4096]{1,0:T(8,128)S(1)}, u32[]{:S(2)}, u32[]{:S(2)}) collective-permute-start(f32[8,4096]{1,0:T(8,128)S(1)} %get-tuple-element.86), channel_id=1, source_target_pairs={{0,3},{1,2},{2,1},{3,0},{4,7},{5,6},{6,5},{7,4},{8,11},{9,10},{10,... | collective-permute-start | bytes 393224 | tf_op jit(solution)/shard_map/ppermute | solution.py:452
  72.8 21.7 %collective-permute-start.27 = (f32[8,4096]{1,0:T(8,128)S(1)}, f32[8,4096]{1,0:T(8,128)S(1)}, u32[]{:S(2)}, u32[]{:S(2)}) collective-permute-start(f32[8,4096]{1,0:T(8,128)S(1)} %get-tuple-element.90), channel_id=1, source_target_pairs={{0,2},{1,3},{2,0},{3,1},{4,6},{5,7},{6,4},{7,5},{8,10},{9,11},{10,... | collective-permute-start | bytes 393224 | tf_op jit(solution)/shard_map/ppermute | solution.py:452
  75.1 19.5 %collective-permute-start.28 = (f32[8,4096]{1,0:T(8,128)S(1)}, f32[8,4096]{1,0:T(8,128)S(1)}, u32[]{:S(2)}, u32[]{:S(2)}) collective-permute-start(f32[8,4096]{1,0:T(8,128)S(1)} %get-tuple-element.93), channel_id=1, source_target_pairs={{0,1},{1,0},{2,3},{3,2},{4,5},{5,4},{6,7},{7,6},{8,9},{9,8},{10,11... | collective-permute-start | bytes 393224 | tf_op jit(solution)/shard_map/ppermute | solution.py:452
  76.8 5.4 %collective-permute-start.23 = (f32[8,128]{1,0:T(8,128)S(1)}, f32[8,128]{1,0:T(8,128)S(1)}, u32[]{:S(2)}, u32[]{:S(2)}) collective-permute-start(f32[8,128]{1,0:T(8,128)S(1)} %add_moments.6.first_ref), channel_id=1, source_target_pairs={{0,4},{4,0},{8,12},{12,8},{16,20},{20,16},{24,28},{28,24},{1,5},{5... | collective-permute-start | bytes 12296 | tf_op jit(solution)/shard_map/ppermute | solution.py:452
  82.3 3.9 %collective-permute-start.24 = (f32[8,128]{1,0:T(8,128)S(1)}, f32[8,128]{1,0:T(8,128)S(1)}, u32[]{:S(2)}, u32[]{:S(2)}) collective-permute-start(f32[8,128]{1,0:T(8,128)S(1)} %add_moments.7.first_ref), channel_id=1, source_target_pairs={{0,8},{4,12},{8,0},{12,4},{16,24},{20,28},{24,16},{28,20},{1,9},{5... | collective-permute-start | bytes 12296 | tf_op jit(solution)/shard_map/ppermute | solution.py:452
  86.3 8.1 %collective-permute-start.25 = (f32[8,128]{1,0:T(8,128)S(1)}, f32[8,128]{1,0:T(8,128)S(1)}, u32[]{:S(2)}, u32[]{:S(2)}) collective-permute-start(f32[8,128]{1,0:T(8,128)S(1)} %add_moments.8.first_ref), channel_id=1, source_target_pairs={{0,16},{4,20},{8,24},{12,28},{16,0},{20,4},{24,8},{28,12},{1,17},{... | collective-permute-start | bytes 12296 | tf_op jit(solution)/shard_map/ppermute | solution.py:452
  (9 other events, 52.1 us)

commit v10 on v9

--- a/solution.py
+++ b/solution.py
@@ -16,7 +16,7 @@
 BF16 = jnp.bfloat16
 VMEM = pl.BlockSpec(memory_space=pltpu.VMEM)
 SMEM = pl.BlockSpec(memory_space=pltpu.SMEM)
-EARLY, AHEAD, LATE, FROM_AHEAD = KINDS = range(4)
+EARLY, SOON, AHEAD, LATE, FROM_AHEAD = KINDS = range(5)
 PARAMS = pltpu.CompilerParams(vmem_limit_bytes=4 * 1024 * 1024)
 
 
@@ -82,9 +82,9 @@
 
     live, source, target = sides(by_row[:, 0:1], by_row[:, 1:2], 0)
     kind = jnp.where(target >= tile_blocks, AHEAD, LATE)
-    first_own = sub_index * blocks_dev
-    is_early = (source >= first_own) & (source < first_own + blocks_dev)
-    kind = jnp.where(is_early, EARLY, kind)
+    for index, step in ((EARLY, 0), (SOON, sub_count - 1)):
+        first = (sub_index ^ step) * blocks_dev
+        kind = jnp.where((source >= first) & (source < first + blocks_dev), index, kind)
     kind = jnp.where(source >= tile_blocks, FROM_AHEAD, kind)
     kind = jnp.where(live, kind, -1)
     hot = (kind == lax.broadcasted_iota(jnp.int32, (2 * width, LANES), 1)).astype(F32)
@@ -110,6 +110,7 @@
     idle = (tile_blocks + blocks_dev) * 65536
     idle_source = {
         EARLY: sub_index * blocks_dev,
+        SOON: (sub_index ^ (sub_count - 1)) * blocks_dev,
         AHEAD: tile_blocks - blocks_dev,
         LATE: 0,
         FROM_AHEAD: tile_blocks,
@@ -211,6 +212,12 @@
         value = noise_ref[:, span] * own_ref[:, span]
         total[own_first + block] = value + times(field[own_first + block].astype(BF16), diag_ref[block])
     add_products(lists_ref, blocks_ref, slot_count, field, total, EARLY, LONG_GROUP)
+
+
+def soon_kernel(index, sub_count, slot_count, blocks_dev, lists_ref, blocks_ref, begun_ref, row_ref, total, field):
+    lay_out(row_ref, field, (lax.axis_index("sub") ^ (sub_count - 1)) * blocks_dev, blocks_dev, blocks_ref.shape[1])
+    total[...] = begun_ref[...]
+    add_products(lists_ref, blocks_ref, slot_count, field, total, SOON, LONG_GROUP)
 
 
 def ahead_kernel(index, sub_count, slot_count, lists_ref, blocks_ref, begun_ref, *refs):
@@ -533,13 +540,21 @@
             (sums,) if index else (sums, scalars),
             (lists, blocks, diag_blocks, noise, field, rounded),
             "early",
-            3,
+            0.1,
             scratch_shapes=[scratch(extended)],
         )
         if index == 0:
             begun, unit = begun
         else:
             (begun,) = begun
+        begun = call(
+            functools.partial(soon_kernel, index, sub_count, slot_count, blocks_dev),
+            sums,
+            (lists, blocks, begun, rows[-1]),
+            "soon",
+            3,
+            scratch_shapes=[scratch(extended)],
+        )
         message = shape(rhs_count, points_dev + LANES, BF16) if index == 1 else half
         even, odd, tile_field, *found = call(
             functools.partial(ahead_kernel, index, sub_count, slot_count),

time: 95 us -> 95.7 us (level); the launches traced: 95.6 us -> 95.1 us
  waiting for transfers between devices: 21.9 us -> 18.8 us
  starting transfers between devices: 45.8 us -> 48.2 us
    ppermute x23, waiting for transfers between devices: 21.9 us -> 18.8 us  [exchange(): return lax.ppermute(block, axis, [(i, i ^ step) for i in range(count)])]
    ppermute x23, starting transfers between devices: 43.1 us -> 44.9 us  [exchange(): return lax.ppermute(block, axis, [(i, i ^ step) for i in range(count)])]
    pallas_call x24 -> x27, Pallas kernels: 26.9 us -> 27.1 us  [call(): pl.pallas_call(kernel, out_shape=outs, compiler_params=PARAMS, name=name,...]
  transfers between devices with their start and end apart: 29 -> 29, of which waited for: 12 -> 13; matrix products, arithmetic and copies ran while one was open for 0% -> 0% of each run, Pallas kernels for 21% -> 23%
where the time goes in v10:
time: 95.7 us; the launch traced here: 95.1 us
  starting transfers between devices  48.2 us (50%)
  Pallas kernels  27.1 us (28%)
  waiting for transfers between devices  18.8 us (20%)
    ppermute x23, starting transfers between devices, exchange(): return lax.ppermute(block, axis, [(i, i ^ step) for i in range(count)])  44.9 us
    pallas_call x27, Pallas kernels, call(): pl.pallas_call(kernel, out_shape=outs, compiler_params=PARAMS, name=name,...  27.1 us
    ppermute x23, waiting for transfers between devices, exchange(): return lax.ppermute(block, axis, [(i, i ^ step) for i in range(count)])  18.8 us
    ppermute x6, starting transfers between devices, swap(): return lax.ppermute(block, axis, route)  3.33 us
  transfers between devices with their start and end apart: 29, of which 13 were waited for; matrix products, arithmetic and copies ran while one was open for 0% of the time, Pallas kernels for 23%

profile of v10, /device:TPU:0, one launch (start us, length us, event | category | flops | bytes accessed | tf_op | source)
XLA Modules:
  0.0 95.1 jit_solution(18123492917774956355)
XLA Ops:
  0.7 2.3 %curve_order.1 = (f32[8,4096]{1,0:T(8,128)S(1)}, bf16[8,4096]{1,0:T(8,128)(2,1)S(1)}) custom-call(f32[8,4096]{1,0:T(8,128)} %right_in.1, s32[1,4096]{1,0:T(1,128)} %order_in.1), custom_call_target="tpu_custom_call" | custom-call | flops 10000000000 | tf_op jit(solution)/shard_map/curve_order/pallas_call | solution.py:475
  3.0 4.1 %collective-permute-start.2 = (bf16[8,4096]{1,0:T(8,128)(2,1)S(1)}, bf16[8,4096]{1,0:T(8,128)(2,1)S(1)}, u32[]{:S(2)}, u32[]{:S(2)}) collective-permute-start(bf16[8,4096]{1,0:T(8,128)(2,1)S(1)} %get-tuple-element.50.rounded_ref.refs_0_), channel_id=1, source_target_pairs={{0,2},{1,3},{2,0},{3,1},{4,6},{5,7},{6,4},{7,5},{8,10},{9,11},{10,... | collective-permute-start | bytes 196616 | tf_op jit(solution)/shard_map/ppermute | solution.py:459
  10.3 2.5 %early.3 = (f32[81,8,256]{2,1,0:T(8,128)S(1)}, f32[8,128]{1,0:T(8,128)S(1)}) custom-call(s32[1,1536]{1,0:T(1,128)S(4)} %lists.1.lists_ref, bf16[96,256,256]{2,1,0:T(8,128)(2,1)S(1)} %copy-done, bf16[16,256,256]{2,1,0:T(8,128)(2,1)S(1)} %copy-done.1, f32[1,4096]{1,0:T(1,128)S(1)} %bitcast.2, f32[8,4096]{1,0:T(8,128)S(1)} %get-tuple-element.49.own_ref.old_ref.refs_4_, ...), custom_call_target="tpu_custom_call" | custom-call | flops 100000000 | tf_op jit(solution)/shard_map/early/pallas_call | solution.py:475
  12.7 2.0 %collective-permute-done.row_ref.refs_3_ = bf16[8,4096]{1,0:T(8,128)(2,1)S(1)} collective-permute-done((bf16[8,4096]{1,0:T(8,128)(2,1)S(1)}, bf16[8,4096]{1,0:T(8,128)(2,1)S(1)}, u32[]{:S(2)}, u32[]{:S(2)}) %collective-permute-start) | collective-permute-done | bytes 65568 | tf_op jit(solution)/shard_map/ppermute | solution.py:459
  16.7 2.2 %late.3.begun_ref = f32[81,8,256]{2,1,0:T(8,128)S(1)} custom-call(s32[1,1536]{1,0:T(1,128)S(4)} %lists.1.lists_ref, bf16[96,256,256]{2,1,0:T(8,128)(2,1)S(1)} %copy-done, f32[81,8,256]{2,1,0:T(8,128)S(1)} %soon.3.begun_ref, f32[64,8,256]{2,1,0:T(8,128)S(1)} %get-tuple-element.52.field_ref), custom_call_target="tpu_custom_call" | custom-call | flops 3000000000 | tf_op jit(solution)/shard_map/late/pallas_call | solution.py:475
  19.8 3.2 %collective-permute-start.5 = (bf16[8,4096]{1,0:T(8,128)(2,1)S(1)}, bf16[8,4096]{1,0:T(8,128)(2,1)S(1)}, u32[]{:S(2)}, u32[]{:S(2)}) collective-permute-start(bf16[8,4096]{1,0:T(8,128)(2,1)S(1)} %get-tuple-element.58), channel_id=1, source_target_pairs={{0,3},{1,2},{2,1},{3,0},{4,7},{5,6},{6,5},{7,4},{8,11},{9,10},{10,... | collective-permute-start | bytes 196616 | tf_op jit(solution)/shard_map/ppermute | solution.py:459
  24.3 5.4 %turn.1.after_ref.blocks_ref = bf16[192,256,256]{2,1,0:T(8,128)(2,1)S(1)} custom-call(bf16[96,256,256]{2,1,0:T(8,128)(2,1)S(1)} %copy-done, f32[8,128]{1,0:T(8,128)S(1)} %get-tuple-element.55.after_ref.moments_in_ref), custom_call_target="tpu_custom_call" | custom-call | flops 4000000000 | tf_op jit(solution)/shard_map/turn/pallas_call | solution.py:475
  31.2 1.8 %collective-permute-start.8 = (bf16[8,4224]{1,0:T(8,128)(2,1)S(1)}, bf16[8,4224]{1,0:T(8,128)(2,1)S(1)}, u32[]{:S(2)}, u32[]{:S(2)}) collective-permute-start(bf16[8,4224]{1,0:T(8,128)(2,1)S(1)} %get-tuple-element.62.rounded_ref.refs_0_), channel_id=1, source_target_pairs={{0,3},{1,2},{2,1},{3,0},{4,7},{5,6},{6,5},{7,4},{8,11},{9,10},{10,... | collective-permute-start | bytes 202760 | tf_op jit(solution)/shard_map/ppermute | solution.py:459
  33.0 2.5 %collective-permute-start.9 = (bf16[8,4224]{1,0:T(8,128)(2,1)S(1)}, bf16[8,4224]{1,0:T(8,128)(2,1)S(1)}, u32[]{:S(2)}, u32[]{:S(2)}) collective-permute-start(bf16[8,4224]{1,0:T(8,128)(2,1)S(1)} %get-tuple-element.62.rounded_ref.refs_0_), channel_id=1, source_target_pairs={{0,1},{1,0},{2,3},{3,2},{4,5},{5,4},{6,7},{7,6},{8,9},{9,8},{10,11... | collective-permute-start | bytes 202760 | tf_op jit(solution)/shard_map/ppermute | solution.py:459
  38.6 2.2 %collective-permute-done.10.refs_2_ = bf16[8,4224]{1,0:T(8,128)(2,1)S(1)} collective-permute-done((bf16[8,4224]{1,0:T(8,128)(2,1)S(1)}, bf16[8,4224]{1,0:T(8,128)(2,1)S(1)}, u32[]{:S(2)}, u32[]{:S(2)}) %collective-permute-start.10) | collective-permute-done | bytes 67616 | tf_op jit(solution)/shard_map/ppermute | solution.py:459
  41.8 1.6 %late.4.begun_ref = f32[81,8,256]{2,1,0:T(8,128)S(1)} custom-call(s32[1,1536]{1,0:T(1,128)S(4)} %lists.1.lists_ref, bf16[192,256,256]{2,1,0:T(8,128)(2,1)S(1)} %turn.1.after_ref.blocks_ref, f32[81,8,256]{2,1,0:T(8,128)S(1)} %soon.4.begun_ref, f32[64,8,256]{2,1,0:T(8,128)S(1)} %get-tuple-element.64.field_ref, f32[8,640]{1,0:T(8,128)S(1)} %get-tuple-element.63.refs_0_.ratios_ref), custom_call_target="tpu_custom_call" | custom-call | flops 3000000000 | tf_op jit(solution)/shard_map/late/pallas_call | solution.py:475
  44.1 2.4 %collective-permute-start.13 = (bf16[8,4096]{1,0:T(8,128)(2,1)S(1)}, bf16[8,4096]{1,0:T(8,128)(2,1)S(1)}, u32[]{:S(2)}, u32[]{:S(2)}) collective-permute-start(bf16[8,4096]{1,0:T(8,128)(2,1)S(1)} %get-tuple-element.70), channel_id=1, source_target_pairs={{0,3},{1,2},{2,1},{3,0},{4,7},{5,6},{6,5},{7,4},{8,11},{9,10},{10,... | collective-permute-start | bytes 196616 | tf_op jit(solution)/shard_map/ppermute | solution.py:459
  46.5 2.0 %collective-permute-start.15 = (bf16[8,4096]{1,0:T(8,128)(2,1)S(1)}, bf16[8,4096]{1,0:T(8,128)(2,1)S(1)}, u32[]{:S(2)}, u32[]{:S(2)}) collective-permute-start(bf16[8,4096]{1,0:T(8,128)(2,1)S(1)} %get-tuple-element.72), channel_id=1, source_target_pairs={{0,1},{1,0},{2,3},{3,2},{4,5},{5,4},{6,7},{7,6},{8,9},{9,8},{10,11... | collective-permute-start | bytes 196616 | tf_op jit(solution)/shard_map/ppermute | solution.py:459
  48.6 1.7 %collective-permute-done.13.refs_0_ = bf16[8,4096]{1,0:T(8,128)(2,1)S(1)} collective-permute-done((bf16[8,4096]{1,0:T(8,128)(2,1)S(1)}, bf16[8,4096]{1,0:T(8,128)(2,1)S(1)}, u32[]{:S(2)}, u32[]{:S(2)}) %collective-permute-start.13) | collective-permute-done | bytes 65568 | tf_op jit(solution)/shard_map/ppermute | solution.py:459
  50.2 1.8 %collective-permute-done.14.refs_1_ = bf16[8,4096]{1,0:T(8,128)(2,1)S(1)} collective-permute-done((bf16[8,4096]{1,0:T(8,128)(2,1)S(1)}, bf16[8,4096]{1,0:T(8,128)(2,1)S(1)}, u32[]{:S(2)}, u32[]{:S(2)}) %collective-permute-start.14) | collective-permute-done | bytes 65568 | tf_op jit(solution)/shard_map/ppermute | solution.py:459
  52.2 2.0 %collective-permute-start.16 = (bf16[8,4096]{1,0:T(8,128)(2,1)S(1)}, bf16[8,4096]{1,0:T(8,128)(2,1)S(1)}, u32[]{:S(2)}, u32[]{:S(2)}) collective-permute-start(bf16[8,4096]{1,0:T(8,128)(2,1)S(1)} %get-tuple-element.74.rounded_ref.refs_1_), channel_id=1, source_target_pairs={{0,3},{1,2},{2,1},{3,0},{4,7},{5,6},{6,5},{7,4},{8,11},{9,10},{10,... | collective-permute-start | bytes 196616 | tf_op jit(solution)/shard_map/ppermute | solution.py:459
  54.4 2.2 %collective-permute-start.17 = (bf16[8,4096]{1,0:T(8,128)(2,1)S(1)}, bf16[8,4096]{1,0:T(8,128)(2,1)S(1)}, u32[]{:S(2)}, u32[]{:S(2)}) collective-permute-start(bf16[8,4096]{1,0:T(8,128)(2,1)S(1)} %get-tuple-element.74.rounded_ref.refs_1_), channel_id=1, source_target_pairs={{0,1},{1,0},{2,3},{3,2},{4,5},{5,4},{6,7},{7,6},{8,9},{9,8},{10,11... | collective-permute-start | bytes 196616 | tf_op jit(solution)/shard_map/ppermute | solution.py:459
  59.1 2.1 %collective-permute-done.18.refs_3_ = bf16[8,4096]{1,0:T(8,128)(2,1)S(1)} collective-permute-done((bf16[8,4096]{1,0:T(8,128)(2,1)S(1)}, bf16[8,4096]{1,0:T(8,128)(2,1)S(1)}, u32[]{:S(2)}, u32[]{:S(2)}) %collective-permute-start.18) | collective-permute-done | bytes 65568 | tf_op jit(solution)/shard_map/ppermute | solution.py:459
  63.1 1.6 %late.5.begun_ref = f32[81,8,256]{2,1,0:T(8,128)S(1)} custom-call(s32[1,1536]{1,0:T(1,128)S(4)} %lists.1.lists_ref, bf16[192,256,256]{2,1,0:T(8,128)(2,1)S(1)} %turn.1.after_ref.blocks_ref, f32[81,8,256]{2,1,0:T(8,128)S(1)} %soon.5.begun_ref, f32[64,8,256]{2,1,0:T(8,128)S(1)} %get-tuple-element.75.field_ref, f32[8,640]{1,0:T(8,128)S(1)} %get-tuple-element.63.refs_0_.ratios_ref), custom_call_target="tpu_custom_call" | custom-call | flops 3000000000 | tf_op jit(solution)/shard_map/late/pallas_call | solution.py:475
  66.7 1.9 %collective-permute-done.21.second_ref = f32[8,128]{1,0:T(8,128)S(1)} collective-permute-done((f32[8,128]{1,0:T(8,128)S(1)}, f32[8,128]{1,0:T(8,128)S(1)}, u32[]{:S(2)}, u32[]{:S(2)}) %collective-permute-start.21) | collective-permute-done | bytes 4128 | tf_op jit(solution)/shard_map/ppermute | solution.py:459
  70.0 1.6 %collective-permute-start.26 = (f32[8,4096]{1,0:T(8,128)S(1)}, f32[8,4096]{1,0:T(8,128)S(1)}, u32[]{:S(2)}, u32[]{:S(2)}) collective-permute-start(f32[8,4096]{1,0:T(8,128)S(1)} %get-tuple-element.86), channel_id=1, source_target_pairs={{0,3},{1,2},{2,1},{3,0},{4,7},{5,6},{6,5},{7,4},{8,11},{9,10},{10,... | collective-permute-start | bytes 393224 | tf_op jit(solution)/shard_map/ppermute | solution.py:459
  74.5 6.9 %collective-permute-start.23 = (f32[8,128]{1,0:T(8,128)S(1)}, f32[8,128]{1,0:T(8,128)S(1)}, u32[]{:S(2)}, u32[]{:S(2)}) collective-permute-start(f32[8,128]{1,0:T(8,128)S(1)} %add_moments.6.first_ref), channel_id=1, source_target_pairs={{0,4},{4,0},{8,12},{12,8},{16,20},{20,16},{24,28},{28,24},{1,5},{5... | collective-permute-start | bytes 12296 | tf_op jit(solution)/shard_map/ppermute | solution.py:459
  82.3 3.6 %collective-permute-start.24 = (f32[8,128]{1,0:T(8,128)S(1)}, f32[8,128]{1,0:T(8,128)S(1)}, u32[]{:S(2)}, u32[]{:S(2)}) collective-permute-start(f32[8,128]{1,0:T(8,128)S(1)} %add_moments.7.first_ref), channel_id=1, source_target_pairs={{0,8},{4,12},{8,0},{12,4},{16,24},{20,28},{24,16},{28,20},{1,9},{5... | collective-permute-start | bytes 12296 | tf_op jit(solution)/shard_map/ppermute | solution.py:459
  87.6 4.9 %collective-permute-start.25 = (f32[8,128]{1,0:T(8,128)S(1)}, f32[8,128]{1,0:T(8,128)S(1)}, u32[]{:S(2)}, u32[]{:S(2)}) collective-permute-start(f32[8,128]{1,0:T(8,128)S(1)} %add_moments.8.first_ref), channel_id=1, source_target_pairs={{0,16},{4,20},{8,24},{12,28},{16,0},{20,4},{24,8},{28,12},{1,17},{... | collective-permute-start | bytes 12296 | tf_op jit(solution)/shard_map/ppermute | solution.py:459
  (70 shorter events, 29.6 us)
Async XLA Ops:
  3.0 12.9 %collective-permute-start.2 = (bf16[8,4096]{1,0:T(8,128)(2,1)S(1)}, bf16[8,4096]{1,0:T(8,128)(2,1)S(1)}, u32[]{:S(2)}, u32[]{:S(2)}) collective-permute-start(bf16[8,4096]{1,0:T(8,128)(2,1)S(1)} %get-tuple-element.50.rounded_ref.refs_0_), channel_id=1, source_target_pairs={{0,2},{1,3},{2,0},{3,1},{4,6},{5,7},{6,4},{7,5},{8,10},{9,11},{10,... | collective-permute-start | bytes 196616 | tf_op jit(solution)/shard_map/ppermute | solution.py:459
  7.1 8.8 %collective-permute-start.1 = (bf16[8,4096]{1,0:T(8,128)(2,1)S(1)}, bf16[8,4096]{1,0:T(8,128)(2,1)S(1)}, u32[]{:S(2)}, u32[]{:S(2)}) collective-permute-start(bf16[8,4096]{1,0:T(8,128)(2,1)S(1)} %get-tuple-element.50.rounded_ref.refs_0_), channel_id=1, source_target_pairs={{0,1},{1,0},{2,3},{3,2},{4,5},{5,4},{6,7},{7,6},{8,9},{9,8},{10,11... | collective-permute-start | bytes 196616 | tf_op jit(solution)/shard_map/ppermute | solution.py:459
  8.7 6.1 %collective-permute-start = (bf16[8,4096]{1,0:T(8,128)(2,1)S(1)}, bf16[8,4096]{1,0:T(8,128)(2,1)S(1)}, u32[]{:S(2)}, u32[]{:S(2)}) collective-permute-start(bf16[8,4096]{1,0:T(8,128)(2,1)S(1)} %get-tuple-element.50.rounded_ref.refs_0_), channel_id=1, source_target_pairs={{0,3},{1,2},{2,1},{3,0},{4,7},{5,6},{6,5},{7,4},{8,11},{9,10},{10,... | collective-permute-start | bytes 196616 | tf_op jit(solution)/shard_map/ppermute | solution.py:459
  19.8 9.9 %collective-permute-start.5 = (bf16[8,4096]{1,0:T(8,128)(2,1)S(1)}, bf16[8,4096]{1,0:T(8,128)(2,1)S(1)}, u32[]{:S(2)}, u32[]{:S(2)}) collective-permute-start(bf16[8,4096]{1,0:T(8,128)(2,1)S(1)} %get-tuple-element.58), channel_id=1, source_target_pairs={{0,3},{1,2},{2,1},{3,0},{4,7},{5,6},{6,5},{7,4},{8,11},{9,10},{10,... | collective-permute-start | bytes 196616 | tf_op jit(solution)/shard_map/ppermute | solution.py:459
  23.1 8.0 %collective-permute-start.6 = (bf16[8,4096]{1,0:T(8,128)(2,1)S(1)}, bf16[8,4096]{1,0:T(8,128)(2,1)S(1)}, u32[]{:S(2)}, u32[]{:S(2)}) collective-permute-start(bf16[8,4096]{1,0:T(8,128)(2,1)S(1)} %get-tuple-element.59), channel_id=1, source_target_pairs={{0,2},{1,3},{2,0},{3,1},{4,6},{5,7},{6,4},{7,5},{8,10},{9,11},{10,... | collective-permute-start | bytes 196616 | tf_op jit(solution)/shard_map/ppermute | solution.py:459
  23.5 7.6 %collective-permute-start.7 = (bf16[8,4096]{1,0:T(8,128)(2,1)S(1)}, bf16[8,4096]{1,0:T(8,128)(2,1)S(1)}, u32[]{:S(2)}, u32[]{:S(2)}) collective-permute-start(bf16[8,4096]{1,0:T(8,128)(2,1)S(1)} %get-tuple-element.60), channel_id=1, source_target_pairs={{0,1},{1,0},{2,3},{3,2},{4,5},{5,4},{6,7},{7,6},{8,9},{9,8},{10,11... | collective-permute-start | bytes 196616 | tf_op jit(solution)/shard_map/ppermute | solution.py:459
  31.2 6.6 %collective-permute-start.8 = (bf16[8,4224]{1,0:T(8,128)(2,1)S(1)}, bf16[8,4224]{1,0:T(8,128)(2,1)S(1)}, u32[]{:S(2)}, u32[]{:S(2)}) collective-permute-start(bf16[8,4224]{1,0:T(8,128)(2,1)S(1)} %get-tuple-element.62.rounded_ref.refs_0_), channel_id=1, source_target_pairs={{0,3},{1,2},{2,1},{3,0},{4,7},{5,6},{6,5},{7,4},{8,11},{9,10},{10,... | collective-permute-start | bytes 202760 | tf_op jit(solution)/shard_map/ppermute | solution.py:459
  33.0 7.8 %collective-permute-start.10 = (bf16[8,4224]{1,0:T(8,128)(2,1)S(1)}, bf16[8,4224]{1,0:T(8,128)(2,1)S(1)}, u32[]{:S(2)}, u32[]{:S(2)}) collective-permute-start(bf16[8,4224]{1,0:T(8,128)(2,1)S(1)} %get-tuple-element.62.rounded_ref.refs_0_), channel_id=1, source_target_pairs={{0,2},{1,3},{2,0},{3,1},{4,6},{5,7},{6,4},{7,5},{8,10},{9,11},{10,... | collective-permute-start | bytes 202760 | tf_op jit(solution)/shard_map/ppermute | solution.py:459
  33.0 7.8 %collective-permute-start.9 = (bf16[8,4224]{1,0:T(8,128)(2,1)S(1)}, bf16[8,4224]{1,0:T(8,128)(2,1)S(1)}, u32[]{:S(2)}, u32[]{:S(2)}) collective-permute-start(bf16[8,4224]{1,0:T(8,128)(2,1)S(1)} %get-tuple-element.62.rounded_ref.refs_0_), channel_id=1, source_target_pairs={{0,1},{1,0},{2,3},{3,2},{4,5},{5,4},{6,7},{7,6},{8,9},{9,8},{10,11... | collective-permute-start | bytes 202760 | tf_op jit(solution)/shard_map/ppermute | solution.py:459
  44.1 6.1 %collective-permute-start.13 = (bf16[8,4096]{1,0:T(8,128)(2,1)S(1)}, bf16[8,4096]{1,0:T(8,128)(2,1)S(1)}, u32[]{:S(2)}, u32[]{:S(2)}) collective-permute-start(bf16[8,4096]{1,0:T(8,128)(2,1)S(1)} %get-tuple-element.70), channel_id=1, source_target_pairs={{0,3},{1,2},{2,1},{3,0},{4,7},{5,6},{6,5},{7,4},{8,11},{9,10},{10,... | collective-permute-start | bytes 196616 | tf_op jit(solution)/shard_map/ppermute | solution.py:459
  46.5 5.5 %collective-permute-start.14 = (bf16[8,4096]{1,0:T(8,128)(2,1)S(1)}, bf16[8,4096]{1,0:T(8,128)(2,1)S(1)}, u32[]{:S(2)}, u32[]{:S(2)}) collective-permute-start(bf16[8,4096]{1,0:T(8,128)(2,1)S(1)} %get-tuple-element.71), channel_id=1, source_target_pairs={{0,2},{1,3},{2,0},{3,1},{4,6},{5,7},{6,4},{7,5},{8,10},{9,11},{10,... | collective-permute-start | bytes 196616 | tf_op jit(solution)/shard_map/ppermute | solution.py:459
  46.5 5.5 %collective-permute-start.15 = (bf16[8,4096]{1,0:T(8,128)(2,1)S(1)}, bf16[8,4096]{1,0:T(8,128)(2,1)S(1)}, u32[]{:S(2)}, u32[]{:S(2)}) collective-permute-start(bf16[8,4096]{1,0:T(8,128)(2,1)S(1)} %get-tuple-element.72), channel_id=1, source_target_pairs={{0,1},{1,0},{2,3},{3,2},{4,5},{5,4},{6,7},{7,6},{8,9},{9,8},{10,11... | collective-permute-start | bytes 196616 | tf_op jit(solution)/shard_map/ppermute | solution.py:459
  52.2 6.1 %collective-permute-start.16 = (bf16[8,4096]{1,0:T(8,128)(2,1)S(1)}, bf16[8,4096]{1,0:T(8,128)(2,1)S(1)}, u32[]{:S(2)}, u32[]{:S(2)}) collective-permute-start(bf16[8,4096]{1,0:T(8,128)(2,1)S(1)} %get-tuple-element.74.rounded_ref.refs_1_), channel_id=1, source_target_pairs={{0,3},{1,2},{2,1},{3,0},{4,7},{5,6},{6,5},{7,4},{8,11},{9,10},{10,... | collective-permute-start | bytes 196616 | tf_op jit(solution)/shard_map/ppermute | solution.py:459
  54.2 7.0 %collective-permute-start.18 = (bf16[8,4096]{1,0:T(8,128)(2,1)S(1)}, bf16[8,4096]{1,0:T(8,128)(2,1)S(1)}, u32[]{:S(2)}, u32[]{:S(2)}) collective-permute-start(bf16[8,4096]{1,0:T(8,128)(2,1)S(1)} %get-tuple-element.74.rounded_ref.refs_1_), channel_id=1, source_target_pairs={{0,2},{1,3},{2,0},{3,1},{4,6},{5,7},{6,4},{7,5},{8,10},{9,11},{10,... | collective-permute-start | bytes 196616 | tf_op jit(solution)/shard_map/ppermute | solution.py:459
  54.4 6.8 %collective-permute-start.17 = (bf16[8,4096]{1,0:T(8,128)(2,1)S(1)}, bf16[8,4096]{1,0:T(8,128)(2,1)S(1)}, u32[]{:S(2)}, u32[]{:S(2)}) collective-permute-start(bf16[8,4096]{1,0:T(8,128)(2,1)S(1)} %get-tuple-element.74.rounded_ref.refs_1_), channel_id=1, source_target_pairs={{0,1},{1,0},{2,3},{3,2},{4,5},{5,4},{6,7},{7,6},{8,9},{9,8},{10,11... | collective-permute-start | bytes 196616 | tf_op jit(solution)/shard_map/ppermute | solution.py:459
  61.3 3.4 %collective-permute-start.19 = (bf16[8,4096]{1,0:T(8,128)(2,1)S(1)}, bf16[8,4096]{1,0:T(8,128)(2,1)S(1)}, u32[]{:S(2)}, u32[]{:S(2)}) collective-permute-start(bf16[8,4096]{1,0:T(8,128)(2,1)S(1)} %get-tuple-element.76), channel_id=1, source_target_pairs={{0,4},{4,0},{8,12},{12,8},{16,20},{20,16},{24,28},{28,24},{1,5},{5... | collective-permute-start | bytes 196616 | tf_op jit(solution)/shard_map/ppermute | solution.py:467
  64.9 3.6 %collective-permute-start.21 = (f32[8,128]{1,0:T(8,128)S(1)}, f32[8,128]{1,0:T(8,128)S(1)}, u32[]{:S(2)}, u32[]{:S(2)}) collective-permute-start(f32[8,128]{1,0:T(8,128)S(1)} %curvature.1.first_ref), channel_id=1, source_target_pairs={{0,1},{1,0},{2,3},{3,2},{4,5},{5,4},{6,7},{7,6},{8,9},{9,8},{10,11... | collective-permute-start | bytes 12296 | tf_op jit(solution)/shard_map/ppermute | solution.py:459
  68.6 4.6 %collective-permute-start.22 = (f32[8,128]{1,0:T(8,128)S(1)}, f32[8,128]{1,0:T(8,128)S(1)}, u32[]{:S(2)}, u32[]{:S(2)}) collective-permute-start(f32[8,128]{1,0:T(8,128)S(1)} %add_moments.5.first_ref), channel_id=1, source_target_pairs={{0,2},{1,3},{2,0},{3,1},{4,6},{5,7},{6,4},{7,5},{8,10},{9,11},{10,... | collective-permute-start | bytes 12296 | tf_op jit(solution)/shard_map/ppermute | solution.py:459
  70.0 24.1 %collective-permute-start.26 = (f32[8,4096]{1,0:T(8,128)S(1)}, f32[8,4096]{1,0:T(8,128)S(1)}, u32[]{:S(2)}, u32[]{:S(2)}) collective-permute-start(f32[8,4096]{1,0:T(8,128)S(1)} %get-tuple-element.86), channel_id=1, source_target_pairs={{0,3},{1,2},{2,1},{3,0},{4,7},{5,6},{6,5},{7,4},{8,11},{9,10},{10,... | collective-permute-start | bytes 393224 | tf_op jit(solution)/shard_map/ppermute | solution.py:459
  71.6 22.5 %collective-permute-start.27 = (f32[8,4096]{1,0:T(8,128)S(1)}, f32[8,4096]{1,0:T(8,128)S(1)}, u32[]{:S(2)}, u32[]{:S(2)}) collective-permute-start(f32[8,4096]{1,0:T(8,128)S(1)} %get-tuple-element.90), channel_id=1, source_target_pairs={{0,2},{1,3},{2,0},{3,1},{4,6},{5,7},{6,4},{7,5},{8,10},{9,11},{10,... | collective-permute-start | bytes 393224 | tf_op jit(solution)/shard_map/ppermute | solution.py:459
  73.3 20.8 %collective-permute-start.28 = (f32[8,4096]{1,0:T(8,128)S(1)}, f32[8,4096]{1,0:T(8,128)S(1)}, u32[]{:S(2)}, u32[]{:S(2)}) collective-permute-start(f32[8,4096]{1,0:T(8,128)S(1)} %get-tuple-element.93), channel_id=1, source_target_pairs={{0,1},{1,0},{2,3},{3,2},{4,5},{5,4},{6,7},{7,6},{8,9},{9,8},{10,11... | collective-permute-start | bytes 393224 | tf_op jit(solution)/shard_map/ppermute | solution.py:459
  74.5 7.7 %collective-permute-start.23 = (f32[8,128]{1,0:T(8,128)S(1)}, f32[8,128]{1,0:T(8,128)S(1)}, u32[]{:S(2)}, u32[]{:S(2)}) collective-permute-start(f32[8,128]{1,0:T(8,128)S(1)} %add_moments.6.first_ref), channel_id=1, source_target_pairs={{0,4},{4,0},{8,12},{12,8},{16,20},{20,16},{24,28},{28,24},{1,5},{5... | collective-permute-start | bytes 12296 | tf_op jit(solution)/shard_map/ppermute | solution.py:459
  82.3 5.1 %collective-permute-start.24 = (f32[8,128]{1,0:T(8,128)S(1)}, f32[8,128]{1,0:T(8,128)S(1)}, u32[]{:S(2)}, u32[]{:S(2)}) collective-permute-start(f32[8,128]{1,0:T(8,128)S(1)} %add_moments.7.first_ref), channel_id=1, source_target_pairs={{0,8},{4,12},{8,0},{12,4},{16,24},{20,28},{24,16},{28,20},{1,9},{5... | collective-permute-start | bytes 12296 | tf_op jit(solution)/shard_map/ppermute | solution.py:459
  87.6 6.5 %collective-permute-start.25 = (f32[8,128]{1,0:T(8,128)S(1)}, f32[8,128]{1,0:T(8,128)S(1)}, u32[]{:S(2)}, u32[]{:S(2)}) collective-permute-start(f32[8,128]{1,0:T(8,128)S(1)} %add_moments.8.first_ref), channel_id=1, source_target_pairs={{0,16},{4,20},{8,24},{12,28},{16,0},{20,4},{24,8},{28,12},{1,17},{... | collective-permute-start | bytes 12296 | tf_op jit(solution)/shard_map/ppermute | solution.py:459
  (9 other events, 49.7 us)

commit v11 on v9

--- a/solution.py
+++ b/solution.py
@@ -11,7 +11,8 @@
 LANES = 128
 LONG_GROUP = 16
 SHORT_GROUP = 8
-TURN_GROUP = 4
+TURN_GROUP = 24
+TURN_PRODUCTS = 6
 F32 = jnp.float32
 BF16 = jnp.bfloat16
 VMEM = pl.BlockSpec(memory_space=pltpu.VMEM)
@@ -132,10 +133,19 @@
     copy = pltpu.make_async_copy(pairs_blocks_ref, blocks_ref.at[pl.ds(0, slot_count)], sem)
     copy.start()
 
+    square = blocks_ref.shape[1:]
+    identity = lax.broadcasted_iota(jnp.int32, square, 0) == lax.broadcasted_iota(jnp.int32, square, 1)
+    identity = identity.astype(F32).astype(BF16)
+
     def one_group(group, carry):
         for step in range(TURN_GROUP):
             slot = group * TURN_GROUP + step
-            blocks_ref[slot_count + slot] = jnp.transpose(pairs_blocks_ref[slot])
+            block = pairs_blocks_ref[slot]
+            if step < TURN_GROUP - TURN_PRODUCTS:
+                turned = jnp.transpose(block)
+            else:
+                turned = times_transposed(identity, block).astype(BF16)
+            blocks_ref[slot_count + slot] = turned
         return carry
 
     lax.fori_loop(0, slot_count // TURN_GROUP, one_group, 0)
@@ -191,26 +201,35 @@
         field[first + block] = piece if factor is None else piece * factor
 
 
-def early_kernel(
-    index, sub_count, slot_count, lists_ref, blocks_ref, diag_ref, noise_ref, own_ref, rounded_ref, total,
-    *refs
-):
-    field = refs[-1]
+def own_products(diag_ref, noise_ref, own_ref, rounded, block):
+    block_len = diag_ref.shape[1]
+    span = slice(block * block_len, (block + 1) * block_len)
+    return noise_ref[:, span] * own_ref[:, span] + times(rounded, diag_ref[block])
+
+
+def early_kernel(index, sub_count, slot_count, lists_ref, blocks_ref, *refs):
+    *refs, rounded_ref, total, field = refs
     block_len = blocks_ref.shape[1]
-    sub_index, blocks_dev, own_first, _ = device_place(block_len, own_ref, sub_count)
-    if index == 0:
-        largest = diag_ref[0].astype(F32)
-        for block in range(1, blocks_dev):
-            largest = jnp.maximum(largest, diag_ref[block].astype(F32))
-        refs[0][...] = jnp.full(refs[0].shape, jnp.maximum(jnp.max(largest) * block_len, 1.0))
+    blocks_dev = rounded_ref.shape[1] // block_len
+    own_first = lax.axis_index("sub") * blocks_dev
     lay_out(rounded_ref, field, own_first, blocks_dev, block_len)
     for block in range(total.shape[0]):
         total[block] = jnp.zeros(total.shape[1:], F32)
+    if index:
+        for block in range(blocks_dev):
+            total[own_first + block] = own_products(*refs, field[own_first + block].astype(BF16), block)
+    add_products(lists_ref, blocks_ref, slot_count, field, total, EARLY, LONG_GROUP)
+
+
+def own_kernel(after_ref, diag_ref, noise_ref, own_ref, rounded_ref, sum_ref, unit_ref):
+    blocks_dev, block_len = diag_ref.shape[:2]
+    largest = diag_ref[0].astype(F32)
+    for block in range(1, blocks_dev):
+        largest = jnp.maximum(largest, diag_ref[block].astype(F32))
+    unit_ref[...] = jnp.full(unit_ref.shape, jnp.maximum(jnp.max(largest) * block_len, 1.0))
     for block in range(blocks_dev):
         span = slice(block * block_len, (block + 1) * block_len)
-        value = noise_ref[:, span] * own_ref[:, span]
-        total[own_first + block] = value + times(field[own_first + block].astype(BF16), diag_ref[block])
-    add_products(lists_ref, blocks_ref, slot_count, field, total, EARLY, LONG_GROUP)
+        sum_ref[:, span] = own_products(diag_ref, noise_ref, own_ref, rounded_ref[:, span], block)
 
 
 def ahead_kernel(index, sub_count, slot_count, lists_ref, blocks_ref, begun_ref, *refs):
@@ -523,23 +542,19 @@
         ],
     )
     basis = [field]
-    moments = unit = jnp.zeros(scalars.shape, F32)
+    moments = jnp.zeros(scalars.shape, F32)
     ratios = sides = ()
     for index in range(ITERS):
         is_last = index + 1 == ITERS
         rows = [exchange(rounded, "sub", step) for step in range(1, sub_count)]
         begun = call(
             functools.partial(early_kernel, index, sub_count, slot_count),
-            (sums,) if index else (sums, scalars),
-            (lists, blocks, diag_blocks, noise, field, rounded),
+            sums,
+            (lists, blocks, *((diag_blocks, noise, field) if index else ()), rounded),
             "early",
             3,
             scratch_shapes=[scratch(extended)],
         )
-        if index == 0:
-            begun, unit = begun
-        else:
-            (begun,) = begun
         message = shape(rhs_count, points_dev + LANES, BF16) if index == 1 else half
         even, odd, tile_field, *found = call(
             functools.partial(ahead_kernel, index, sub_count, slot_count),
@@ -595,7 +610,12 @@
                 4,
                 scratch_shapes=[pltpu.SemaphoreType.DMA(())],
             )
+            own_sum, unit = call(
+                own_kernel, (full, scalars), (moments, diag_blocks, noise, field, rounded), "own", 0.5
+            )
         arrived = [exchange(parts[step], "sub", step) for step in range(sub_count - 1, 0, -1)]
+        if index == 0:
+            arrived.append(own_sum)
         field, rounded, moments = call(
             functools.partial(join_kernel, index),
             (full, half if index else shape(rhs_count, points_dev + LANES, BF16), scalars),

time: 95 us -> 93.9 us (0.988); the launches traced: 95.6 us -> 92.9 us
  Pallas kernels: 26.9 us -> 25.1 us
    pallas_call x24 -> x25, Pallas kernels: 26.9 us -> 25.1 us  [call(): pl.pallas_call(kernel, out_shape=outs, compiler_params=PARAMS, name=name,...]
  transfers between devices with their start and end apart: 29 -> 29, of which waited for: 12 -> 13; matrix products, arithmetic and copies ran while one was open for 0% -> 0% of each run, Pallas kernels for 21% -> 19%
where the time goes in v11:
time: 93.9 us; the launch traced here: 92.9 us
  starting transfers between devices  45.5 us (48%)
  Pallas kernels  25.1 us (27%)
  waiting for transfers between devices  21.3 us (23%)
    ppermute x23, starting transfers between devices, exchange(): return lax.ppermute(block, axis, [(i, i ^ step) for i in range(count)])  42.5 us
    pallas_call x25, Pallas kernels, call(): pl.pallas_call(kernel, out_shape=outs, compiler_params=PARAMS, name=name,...  25.1 us
    ppermute x23, waiting for transfers between devices, exchange(): return lax.ppermute(block, axis, [(i, i ^ step) for i in range(count)])  21.3 us
    ppermute x6, starting transfers between devices, swap(): return lax.ppermute(block, axis, route)  3 us
  transfers between devices with their start and end apart: 29, of which 13 were waited for; matrix products, arithmetic and copies ran while one was open for 0% of the time, Pallas kernels for 19%

profile of v11, /device:TPU:0, one launch (start us, length us, event | category | flops | bytes accessed | tf_op | source)
XLA Modules:
  0.0 92.9 jit_solution(4384601293564843803)
XLA Ops:
  0.7 2.3 %curve_order.1 = (f32[8,4096]{1,0:T(8,128)S(1)}, bf16[8,4096]{1,0:T(8,128)(2,1)S(1)}) custom-call(f32[8,4096]{1,0:T(8,128)} %right_in.1, s32[1,4096]{1,0:T(1,128)} %order_in.1), custom_call_target="tpu_custom_call" | custom-call | flops 10000000000 | tf_op jit(solution)/shard_map/curve_order/pallas_call | solution.py:487
  3.0 5.1 %collective-permute-start.2 = (bf16[8,4096]{1,0:T(8,128)(2,1)S(1)}, bf16[8,4096]{1,0:T(8,128)(2,1)S(1)}, u32[]{:S(2)}, u32[]{:S(2)}) collective-permute-start(bf16[8,4096]{1,0:T(8,128)(2,1)S(1)} %get-tuple-element.49.refs_0_.rounded_ref), channel_id=1, source_target_pairs={{0,3},{1,2},{2,1},{3,0},{4,7},{5,6},{6,5},{7,4},{8,11},{9,10},{10,... | collective-permute-start | bytes 196616 | tf_op jit(solution)/shard_map/ppermute | solution.py:471
  11.4 2.3 %collective-permute-done.1.refs_2_ = bf16[8,4096]{1,0:T(8,128)(2,1)S(1)} collective-permute-done((bf16[8,4096]{1,0:T(8,128)(2,1)S(1)}, bf16[8,4096]{1,0:T(8,128)(2,1)S(1)}, u32[]{:S(2)}, u32[]{:S(2)}) %collective-permute-start.1) | collective-permute-done | bytes 65568 | tf_op jit(solution)/shard_map/ppermute | solution.py:471
  15.1 3.2 %late.3.begun_ref = f32[81,8,256]{2,1,0:T(8,128)S(1)} custom-call(s32[1,1280]{1,0:T(1,128)S(4)} %lists.1.lists_ref, bf16[96,256,256]{2,1,0:T(8,128)(2,1)S(1)} %copy-done, f32[81,8,256]{2,1,0:T(8,128)S(1)} %early.3.begun_ref, f32[64,8,256]{2,1,0:T(8,128)S(1)} %get-tuple-element.50.field_ref), custom_call_target="tpu_custom_call" | custom-call | flops 3000000000 | tf_op jit(solution)/shard_map/late/pallas_call | solution.py:487
  19.2 2.7 %collective-permute-start.5 = (bf16[8,4096]{1,0:T(8,128)(2,1)S(1)}, bf16[8,4096]{1,0:T(8,128)(2,1)S(1)}, u32[]{:S(2)}, u32[]{:S(2)}) collective-permute-start(bf16[8,4096]{1,0:T(8,128)(2,1)S(1)} %get-tuple-element.57), channel_id=1, source_target_pairs={{0,3},{1,2},{2,1},{3,0},{4,7},{5,6},{6,5},{7,4},{8,11},{9,10},{10,... | collective-permute-start | bytes 196616 | tf_op jit(solution)/shard_map/ppermute | solution.py:471
  23.7 3.6 %turn.1.after_ref.blocks_ref = bf16[192,256,256]{2,1,0:T(8,128)(2,1)S(1)} custom-call(bf16[96,256,256]{2,1,0:T(8,128)(2,1)S(1)} %copy-done, f32[8,128]{1,0:T(8,128)S(1)} %get-tuple-element.53.after_ref.moments_in_ref), custom_call_target="tpu_custom_call" | custom-call | flops 4000000000 | tf_op jit(solution)/shard_map/turn/pallas_call | solution.py:487
  29.7 2.8 %collective-permute-start.10 = (bf16[8,4224]{1,0:T(8,128)(2,1)S(1)}, bf16[8,4224]{1,0:T(8,128)(2,1)S(1)}, u32[]{:S(2)}, u32[]{:S(2)}) collective-permute-start(bf16[8,4224]{1,0:T(8,128)(2,1)S(1)} %get-tuple-element.62.refs_3_.refs_0_), channel_id=1, source_target_pairs={{0,3},{1,2},{2,1},{3,0},{4,7},{5,6},{6,5},{7,4},{8,11},{9,10},{10,... | collective-permute-start | bytes 202760 | tf_op jit(solution)/shard_map/ppermute | solution.py:471
  34.9 1.7 %collective-permute-done.10.refs_3_ = bf16[8,4224]{1,0:T(8,128)(2,1)S(1)} collective-permute-done((bf16[8,4224]{1,0:T(8,128)(2,1)S(1)}, bf16[8,4224]{1,0:T(8,128)(2,1)S(1)}, u32[]{:S(2)}, u32[]{:S(2)}) %collective-permute-start.10) | collective-permute-done | bytes 67616 | tf_op jit(solution)/shard_map/ppermute | solution.py:471
  36.6 2.6 %collective-permute-done.9.refs_2_ = bf16[8,4224]{1,0:T(8,128)(2,1)S(1)} collective-permute-done((bf16[8,4224]{1,0:T(8,128)(2,1)S(1)}, bf16[8,4224]{1,0:T(8,128)(2,1)S(1)}, u32[]{:S(2)}, u32[]{:S(2)}) %collective-permute-start.9) | collective-permute-done | bytes 67616 | tf_op jit(solution)/shard_map/ppermute | solution.py:471
  40.5 2.0 %late.4.begun_ref = f32[81,8,256]{2,1,0:T(8,128)S(1)} custom-call(s32[1,1280]{1,0:T(1,128)S(4)} %lists.1.lists_ref, bf16[192,256,256]{2,1,0:T(8,128)(2,1)S(1)} %turn.1.after_ref.blocks_ref, f32[81,8,256]{2,1,0:T(8,128)S(1)} %early.4.begun_ref, f32[64,8,256]{2,1,0:T(8,128)S(1)} %get-tuple-element.64.field_ref, f32[8,640]{1,0:T(8,128)S(1)} %get-tuple-element.63.refs_0_.ratios_ref), custom_call_target="tpu_custom_call" | custom-call | flops 3000000000 | tf_op jit(solution)/shard_map/late/pallas_call | solution.py:487
  43.2 2.2 %collective-permute-start.13 = (bf16[8,4096]{1,0:T(8,128)(2,1)S(1)}, bf16[8,4096]{1,0:T(8,128)(2,1)S(1)}, u32[]{:S(2)}, u32[]{:S(2)}) collective-permute-start(bf16[8,4096]{1,0:T(8,128)(2,1)S(1)} %get-tuple-element.70), channel_id=1, source_target_pairs={{0,3},{1,2},{2,1},{3,0},{4,7},{5,6},{6,5},{7,4},{8,11},{9,10},{10,... | collective-permute-start | bytes 196616 | tf_op jit(solution)/shard_map/ppermute | solution.py:471
  45.4 2.2 %collective-permute-start.15 = (bf16[8,4096]{1,0:T(8,128)(2,1)S(1)}, bf16[8,4096]{1,0:T(8,128)(2,1)S(1)}, u32[]{:S(2)}, u32[]{:S(2)}) collective-permute-start(bf16[8,4096]{1,0:T(8,128)(2,1)S(1)} %get-tuple-element.72), channel_id=1, source_target_pairs={{0,1},{1,0},{2,3},{3,2},{4,5},{5,4},{6,7},{7,6},{8,9},{9,8},{10,11... | collective-permute-start | bytes 196616 | tf_op jit(solution)/shard_map/ppermute | solution.py:471
  47.6 1.7 %collective-permute-done.13.refs_0_ = bf16[8,4096]{1,0:T(8,128)(2,1)S(1)} collective-permute-done((bf16[8,4096]{1,0:T(8,128)(2,1)S(1)}, bf16[8,4096]{1,0:T(8,128)(2,1)S(1)}, u32[]{:S(2)}, u32[]{:S(2)}) %collective-permute-start.13) | collective-permute-done | bytes 65568 | tf_op jit(solution)/shard_map/ppermute | solution.py:471
  49.3 1.7 %collective-permute-done.14.refs_1_ = bf16[8,4096]{1,0:T(8,128)(2,1)S(1)} collective-permute-done((bf16[8,4096]{1,0:T(8,128)(2,1)S(1)}, bf16[8,4096]{1,0:T(8,128)(2,1)S(1)}, u32[]{:S(2)}, u32[]{:S(2)}) %collective-permute-start.14) | collective-permute-done | bytes 65568 | tf_op jit(solution)/shard_map/ppermute | solution.py:471
  51.2 2.0 %collective-permute-start.18 = (bf16[8,4096]{1,0:T(8,128)(2,1)S(1)}, bf16[8,4096]{1,0:T(8,128)(2,1)S(1)}, u32[]{:S(2)}, u32[]{:S(2)}) collective-permute-start(bf16[8,4096]{1,0:T(8,128)(2,1)S(1)} %get-tuple-element.74.refs_3_.refs_1_), channel_id=1, source_target_pairs={{0,3},{1,2},{2,1},{3,0},{4,7},{5,6},{6,5},{7,4},{8,11},{9,10},{10,... | collective-permute-start | bytes 196616 | tf_op jit(solution)/shard_map/ppermute | solution.py:471
  53.9 1.7 %collective-permute-start.16 = (bf16[8,4096]{1,0:T(8,128)(2,1)S(1)}, bf16[8,4096]{1,0:T(8,128)(2,1)S(1)}, u32[]{:S(2)}, u32[]{:S(2)}) collective-permute-start(bf16[8,4096]{1,0:T(8,128)(2,1)S(1)} %get-tuple-element.74.refs_3_.refs_1_), channel_id=1, source_target_pairs={{0,1},{1,0},{2,3},{3,2},{4,5},{5,4},{6,7},{7,6},{8,9},{9,8},{10,11... | collective-permute-start | bytes 196616 | tf_op jit(solution)/shard_map/ppermute | solution.py:471
  57.2 3.0 %collective-permute-done.17.refs_3_ = bf16[8,4096]{1,0:T(8,128)(2,1)S(1)} collective-permute-done((bf16[8,4096]{1,0:T(8,128)(2,1)S(1)}, bf16[8,4096]{1,0:T(8,128)(2,1)S(1)}, u32[]{:S(2)}, u32[]{:S(2)}) %collective-permute-start.17) | collective-permute-done | bytes 65568 | tf_op jit(solution)/shard_map/ppermute | solution.py:471
  62.4 2.0 %late.5.begun_ref = f32[81,8,256]{2,1,0:T(8,128)S(1)} custom-call(s32[1,1280]{1,0:T(1,128)S(4)} %lists.1.lists_ref, bf16[192,256,256]{2,1,0:T(8,128)(2,1)S(1)} %turn.1.after_ref.blocks_ref, f32[81,8,256]{2,1,0:T(8,128)S(1)} %early.5.begun_ref, f32[64,8,256]{2,1,0:T(8,128)S(1)} %get-tuple-element.75.field_ref, f32[8,640]{1,0:T(8,128)S(1)} %get-tuple-element.63.refs_0_.ratios_ref), custom_call_target="tpu_custom_call" | custom-call | flops 3000000000 | tf_op jit(solution)/shard_map/late/pallas_call | solution.py:487
  65.9 2.3 %collective-permute-done.21.second_ref = f32[8,128]{1,0:T(8,128)S(1)} collective-permute-done((f32[8,128]{1,0:T(8,128)S(1)}, f32[8,128]{1,0:T(8,128)S(1)}, u32[]{:S(2)}, u32[]{:S(2)}) %collective-permute-start.21) | collective-permute-done | bytes 4128 | tf_op jit(solution)/shard_map/ppermute | solution.py:471
  68.3 1.8 %collective-permute-start.22 = (f32[8,128]{1,0:T(8,128)S(1)}, f32[8,128]{1,0:T(8,128)S(1)}, u32[]{:S(2)}, u32[]{:S(2)}) collective-permute-start(f32[8,128]{1,0:T(8,128)S(1)} %add_moments.5.first_ref), channel_id=1, source_target_pairs={{0,2},{1,3},{2,0},{3,1},{4,6},{5,7},{6,4},{7,5},{8,10},{9,11},{10,... | collective-permute-start | bytes 12296 | tf_op jit(solution)/shard_map/ppermute | solution.py:471
  72.9 1.7 %collective-permute-start.28 = (f32[8,4096]{1,0:T(8,128)S(1)}, f32[8,4096]{1,0:T(8,128)S(1)}, u32[]{:S(2)}, u32[]{:S(2)}) collective-permute-start(f32[8,4096]{1,0:T(8,128)S(1)} %get-tuple-element.93), channel_id=1, source_target_pairs={{0,1},{1,0},{2,3},{3,2},{4,5},{5,4},{6,7},{7,6},{8,9},{9,8},{10,11... | collective-permute-start | bytes 393224 | tf_op jit(solution)/shard_map/ppermute | solution.py:471
  74.6 5.9 %collective-permute-start.23 = (f32[8,128]{1,0:T(8,128)S(1)}, f32[8,128]{1,0:T(8,128)S(1)}, u32[]{:S(2)}, u32[]{:S(2)}) collective-permute-start(f32[8,128]{1,0:T(8,128)S(1)} %add_moments.6.first_ref), channel_id=1, source_target_pairs={{0,4},{4,0},{8,12},{12,8},{16,20},{20,16},{24,28},{28,24},{1,5},{5... | collective-permute-start | bytes 12296 | tf_op jit(solution)/shard_map/ppermute | solution.py:471
  81.4 3.1 %collective-permute-start.24 = (f32[8,128]{1,0:T(8,128)S(1)}, f32[8,128]{1,0:T(8,128)S(1)}, u32[]{:S(2)}, u32[]{:S(2)}) collective-permute-start(f32[8,128]{1,0:T(8,128)S(1)} %add_moments.7.first_ref), channel_id=1, source_target_pairs={{0,8},{4,12},{8,0},{12,4},{16,24},{20,28},{24,16},{28,20},{1,9},{5... | collective-permute-start | bytes 12296 | tf_op jit(solution)/shard_map/ppermute | solution.py:471
  86.1 4.1 %collective-permute-start.25 = (f32[8,128]{1,0:T(8,128)S(1)}, f32[8,128]{1,0:T(8,128)S(1)}, u32[]{:S(2)}, u32[]{:S(2)}) collective-permute-start(f32[8,128]{1,0:T(8,128)S(1)} %add_moments.8.first_ref), channel_id=1, source_target_pairs={{0,16},{4,20},{8,24},{12,28},{16,0},{20,4},{24,8},{28,12},{1,17},{... | collective-permute-start | bytes 12296 | tf_op jit(solution)/shard_map/ppermute | solution.py:471
  (68 shorter events, 28.4 us)
Async XLA Ops:
  3.0 8.4 %collective-permute-start.2 = (bf16[8,4096]{1,0:T(8,128)(2,1)S(1)}, bf16[8,4096]{1,0:T(8,128)(2,1)S(1)}, u32[]{:S(2)}, u32[]{:S(2)}) collective-permute-start(bf16[8,4096]{1,0:T(8,128)(2,1)S(1)} %get-tuple-element.49.refs_0_.rounded_ref), channel_id=1, source_target_pairs={{0,3},{1,2},{2,1},{3,0},{4,7},{5,6},{6,5},{7,4},{8,11},{9,10},{10,... | collective-permute-start | bytes 196616 | tf_op jit(solution)/shard_map/ppermute | solution.py:471
  8.1 5.6 %collective-permute-start.1 = (bf16[8,4096]{1,0:T(8,128)(2,1)S(1)}, bf16[8,4096]{1,0:T(8,128)(2,1)S(1)}, u32[]{:S(2)}, u32[]{:S(2)}) collective-permute-start(bf16[8,4096]{1,0:T(8,128)(2,1)S(1)} %get-tuple-element.49.refs_0_.rounded_ref), channel_id=1, source_target_pairs={{0,2},{1,3},{2,0},{3,1},{4,6},{5,7},{6,4},{7,5},{8,10},{9,11},{10,... | collective-permute-start | bytes 196616 | tf_op jit(solution)/shard_map/ppermute | solution.py:471
  8.1 5.6 %collective-permute-start = (bf16[8,4096]{1,0:T(8,128)(2,1)S(1)}, bf16[8,4096]{1,0:T(8,128)(2,1)S(1)}, u32[]{:S(2)}, u32[]{:S(2)}) collective-permute-start(bf16[8,4096]{1,0:T(8,128)(2,1)S(1)} %get-tuple-element.49.refs_0_.rounded_ref), channel_id=1, source_target_pairs={{0,1},{1,0},{2,3},{3,2},{4,5},{5,4},{6,7},{7,6},{8,9},{9,8},{10,11... | collective-permute-start | bytes 196616 | tf_op jit(solution)/shard_map/ppermute | solution.py:471
  14.3 4.0 %collective-permute-start.3 = (bf16[8,4096]{1,0:T(8,128)(2,1)S(1)}, bf16[8,4096]{1,0:T(8,128)(2,1)S(1)}, u32[]{:S(2)}, u32[]{:S(2)}) collective-permute-start(bf16[8,4096]{1,0:T(8,128)(2,1)S(1)} %get-tuple-element.51), channel_id=1, source_target_pairs={{0,4},{4,0},{8,12},{12,8},{16,20},{20,16},{24,28},{28,24},{1,5},{5... | collective-permute-start | bytes 196616 | tf_op jit(solution)/shard_map/ppermute | solution.py:479
  14.4 3.9 %collective-permute-start.4 = (bf16[8,4096]{1,0:T(8,128)(2,1)S(1)}, bf16[8,4096]{1,0:T(8,128)(2,1)S(1)}, u32[]{:S(2)}, u32[]{:S(2)}) collective-permute-start(bf16[8,4096]{1,0:T(8,128)(2,1)S(1)} %get-tuple-element.52), channel_id=1, source_target_pairs={{4,8},{8,4},{12,16},{16,12},{20,24},{24,20},{5,9},{9,5},{13,17},{1... | collective-permute-start | bytes 196616 | tf_op jit(solution)/shard_map/ppermute | solution.py:479
  19.2 9.5 %collective-permute-start.5 = (bf16[8,4096]{1,0:T(8,128)(2,1)S(1)}, bf16[8,4096]{1,0:T(8,128)(2,1)S(1)}, u32[]{:S(2)}, u32[]{:S(2)}) collective-permute-start(bf16[8,4096]{1,0:T(8,128)(2,1)S(1)} %get-tuple-element.57), channel_id=1, source_target_pairs={{0,3},{1,2},{2,1},{3,0},{4,7},{5,6},{6,5},{7,4},{8,11},{9,10},{10,... | collective-permute-start | bytes 196616 | tf_op jit(solution)/shard_map/ppermute | solution.py:471
  21.9 7.6 %collective-permute-start.6 = (bf16[8,4096]{1,0:T(8,128)(2,1)S(1)}, bf16[8,4096]{1,0:T(8,128)(2,1)S(1)}, u32[]{:S(2)}, u32[]{:S(2)}) collective-permute-start(bf16[8,4096]{1,0:T(8,128)(2,1)S(1)} %get-tuple-element.58), channel_id=1, source_target_pairs={{0,2},{1,3},{2,0},{3,1},{4,6},{5,7},{6,4},{7,5},{8,10},{9,11},{10,... | collective-permute-start | bytes 196616 | tf_op jit(solution)/shard_map/ppermute | solution.py:471
  22.6 6.9 %collective-permute-start.7 = (bf16[8,4096]{1,0:T(8,128)(2,1)S(1)}, bf16[8,4096]{1,0:T(8,128)(2,1)S(1)}, u32[]{:S(2)}, u32[]{:S(2)}) collective-permute-start(bf16[8,4096]{1,0:T(8,128)(2,1)S(1)} %get-tuple-element.59), channel_id=1, source_target_pairs={{0,1},{1,0},{2,3},{3,2},{4,5},{5,4},{6,7},{7,6},{8,9},{9,8},{10,11... | collective-permute-start | bytes 196616 | tf_op jit(solution)/shard_map/ppermute | solution.py:471
  29.7 6.9 %collective-permute-start.10 = (bf16[8,4224]{1,0:T(8,128)(2,1)S(1)}, bf16[8,4224]{1,0:T(8,128)(2,1)S(1)}, u32[]{:S(2)}, u32[]{:S(2)}) collective-permute-start(bf16[8,4224]{1,0:T(8,128)(2,1)S(1)} %get-tuple-element.62.refs_3_.refs_0_), channel_id=1, source_target_pairs={{0,3},{1,2},{2,1},{3,0},{4,7},{5,6},{6,5},{7,4},{8,11},{9,10},{10,... | collective-permute-start | bytes 202760 | tf_op jit(solution)/shard_map/ppermute | solution.py:471
  32.5 6.6 %collective-permute-start.9 = (bf16[8,4224]{1,0:T(8,128)(2,1)S(1)}, bf16[8,4224]{1,0:T(8,128)(2,1)S(1)}, u32[]{:S(2)}, u32[]{:S(2)}) collective-permute-start(bf16[8,4224]{1,0:T(8,128)(2,1)S(1)} %get-tuple-element.62.refs_3_.refs_0_), channel_id=1, source_target_pairs={{0,2},{1,3},{2,0},{3,1},{4,6},{5,7},{6,4},{7,5},{8,10},{9,11},{10,... | collective-permute-start | bytes 202760 | tf_op jit(solution)/shard_map/ppermute | solution.py:471
  32.5 6.6 %collective-permute-start.8 = (bf16[8,4224]{1,0:T(8,128)(2,1)S(1)}, bf16[8,4224]{1,0:T(8,128)(2,1)S(1)}, u32[]{:S(2)}, u32[]{:S(2)}) collective-permute-start(bf16[8,4224]{1,0:T(8,128)(2,1)S(1)} %get-tuple-element.62.refs_3_.refs_0_), channel_id=1, source_target_pairs={{0,1},{1,0},{2,3},{3,2},{4,5},{5,4},{6,7},{7,6},{8,9},{9,8},{10,11... | collective-permute-start | bytes 202760 | tf_op jit(solution)/shard_map/ppermute | solution.py:471
  43.2 6.1 %collective-permute-start.13 = (bf16[8,4096]{1,0:T(8,128)(2,1)S(1)}, bf16[8,4096]{1,0:T(8,128)(2,1)S(1)}, u32[]{:S(2)}, u32[]{:S(2)}) collective-permute-start(bf16[8,4096]{1,0:T(8,128)(2,1)S(1)} %get-tuple-element.70), channel_id=1, source_target_pairs={{0,3},{1,2},{2,1},{3,0},{4,7},{5,6},{6,5},{7,4},{8,11},{9,10},{10,... | collective-permute-start | bytes 196616 | tf_op jit(solution)/shard_map/ppermute | solution.py:471
  45.4 5.6 %collective-permute-start.14 = (bf16[8,4096]{1,0:T(8,128)(2,1)S(1)}, bf16[8,4096]{1,0:T(8,128)(2,1)S(1)}, u32[]{:S(2)}, u32[]{:S(2)}) collective-permute-start(bf16[8,4096]{1,0:T(8,128)(2,1)S(1)} %get-tuple-element.71), channel_id=1, source_target_pairs={{0,2},{1,3},{2,0},{3,1},{4,6},{5,7},{6,4},{7,5},{8,10},{9,11},{10,... | collective-permute-start | bytes 196616 | tf_op jit(solution)/shard_map/ppermute | solution.py:471
  45.4 5.6 %collective-permute-start.15 = (bf16[8,4096]{1,0:T(8,128)(2,1)S(1)}, bf16[8,4096]{1,0:T(8,128)(2,1)S(1)}, u32[]{:S(2)}, u32[]{:S(2)}) collective-permute-start(bf16[8,4096]{1,0:T(8,128)(2,1)S(1)} %get-tuple-element.72), channel_id=1, source_target_pairs={{0,1},{1,0},{2,3},{3,2},{4,5},{5,4},{6,7},{7,6},{8,9},{9,8},{10,11... | collective-permute-start | bytes 196616 | tf_op jit(solution)/shard_map/ppermute | solution.py:471
  51.2 6.1 %collective-permute-start.18 = (bf16[8,4096]{1,0:T(8,128)(2,1)S(1)}, bf16[8,4096]{1,0:T(8,128)(2,1)S(1)}, u32[]{:S(2)}, u32[]{:S(2)}) collective-permute-start(bf16[8,4096]{1,0:T(8,128)(2,1)S(1)} %get-tuple-element.74.refs_3_.refs_1_), channel_id=1, source_target_pairs={{0,3},{1,2},{2,1},{3,0},{4,7},{5,6},{6,5},{7,4},{8,11},{9,10},{10,... | collective-permute-start | bytes 196616 | tf_op jit(solution)/shard_map/ppermute | solution.py:471
  53.2 7.0 %collective-permute-start.17 = (bf16[8,4096]{1,0:T(8,128)(2,1)S(1)}, bf16[8,4096]{1,0:T(8,128)(2,1)S(1)}, u32[]{:S(2)}, u32[]{:S(2)}) collective-permute-start(bf16[8,4096]{1,0:T(8,128)(2,1)S(1)} %get-tuple-element.74.refs_3_.refs_1_), channel_id=1, source_target_pairs={{0,2},{1,3},{2,0},{3,1},{4,6},{5,7},{6,4},{7,5},{8,10},{9,11},{10,... | collective-permute-start | bytes 196616 | tf_op jit(solution)/shard_map/ppermute | solution.py:471
  53.9 6.3 %collective-permute-start.16 = (bf16[8,4096]{1,0:T(8,128)(2,1)S(1)}, bf16[8,4096]{1,0:T(8,128)(2,1)S(1)}, u32[]{:S(2)}, u32[]{:S(2)}) collective-permute-start(bf16[8,4096]{1,0:T(8,128)(2,1)S(1)} %get-tuple-element.74.refs_3_.refs_1_), channel_id=1, source_target_pairs={{0,1},{1,0},{2,3},{3,2},{4,5},{5,4},{6,7},{7,6},{8,9},{9,8},{10,11... | collective-permute-start | bytes 196616 | tf_op jit(solution)/shard_map/ppermute | solution.py:471
  68.3 4.6 %collective-permute-start.22 = (f32[8,128]{1,0:T(8,128)S(1)}, f32[8,128]{1,0:T(8,128)S(1)}, u32[]{:S(2)}, u32[]{:S(2)}) collective-permute-start(f32[8,128]{1,0:T(8,128)S(1)} %add_moments.5.first_ref), channel_id=1, source_target_pairs={{0,2},{1,3},{2,0},{3,1},{4,6},{5,7},{6,4},{7,5},{8,10},{9,11},{10,... | collective-permute-start | bytes 12296 | tf_op jit(solution)/shard_map/ppermute | solution.py:471
  70.1 21.8 %collective-permute-start.26 = (f32[8,4096]{1,0:T(8,128)S(1)}, f32[8,4096]{1,0:T(8,128)S(1)}, u32[]{:S(2)}, u32[]{:S(2)}) collective-permute-start(f32[8,4096]{1,0:T(8,128)S(1)} %get-tuple-element.86), channel_id=1, source_target_pairs={{0,3},{1,2},{2,1},{3,0},{4,7},{5,6},{6,5},{7,4},{8,11},{9,10},{10,... | collective-permute-start | bytes 393224 | tf_op jit(solution)/shard_map/ppermute | solution.py:471
  70.9 21.0 %collective-permute-start.27 = (f32[8,4096]{1,0:T(8,128)S(1)}, f32[8,4096]{1,0:T(8,128)S(1)}, u32[]{:S(2)}, u32[]{:S(2)}) collective-permute-start(f32[8,4096]{1,0:T(8,128)S(1)} %get-tuple-element.90), channel_id=1, source_target_pairs={{0,2},{1,3},{2,0},{3,1},{4,6},{5,7},{6,4},{7,5},{8,10},{9,11},{10,... | collective-permute-start | bytes 393224 | tf_op jit(solution)/shard_map/ppermute | solution.py:471
  72.9 19.0 %collective-permute-start.28 = (f32[8,4096]{1,0:T(8,128)S(1)}, f32[8,4096]{1,0:T(8,128)S(1)}, u32[]{:S(2)}, u32[]{:S(2)}) collective-permute-start(f32[8,4096]{1,0:T(8,128)S(1)} %get-tuple-element.93), channel_id=1, source_target_pairs={{0,1},{1,0},{2,3},{3,2},{4,5},{5,4},{6,7},{7,6},{8,9},{9,8},{10,11... | collective-permute-start | bytes 393224 | tf_op jit(solution)/shard_map/ppermute | solution.py:471
  74.6 6.7 %collective-permute-start.23 = (f32[8,128]{1,0:T(8,128)S(1)}, f32[8,128]{1,0:T(8,128)S(1)}, u32[]{:S(2)}, u32[]{:S(2)}) collective-permute-start(f32[8,128]{1,0:T(8,128)S(1)} %add_moments.6.first_ref), channel_id=1, source_target_pairs={{0,4},{4,0},{8,12},{12,8},{16,20},{20,16},{24,28},{28,24},{1,5},{5... | collective-permute-start | bytes 12296 | tf_op jit(solution)/shard_map/ppermute | solution.py:471
  81.4 4.7 %collective-permute-start.24 = (f32[8,128]{1,0:T(8,128)S(1)}, f32[8,128]{1,0:T(8,128)S(1)}, u32[]{:S(2)}, u32[]{:S(2)}) collective-permute-start(f32[8,128]{1,0:T(8,128)S(1)} %add_moments.7.first_ref), channel_id=1, source_target_pairs={{0,8},{4,12},{8,0},{12,4},{16,24},{20,28},{24,16},{28,20},{1,9},{5... | collective-permute-start | bytes 12296 | tf_op jit(solution)/shard_map/ppermute | solution.py:471
  86.1 5.6 %collective-permute-start.25 = (f32[8,128]{1,0:T(8,128)S(1)}, f32[8,128]{1,0:T(8,128)S(1)}, u32[]{:S(2)}, u32[]{:S(2)}) collective-permute-start(f32[8,128]{1,0:T(8,128)S(1)} %add_moments.8.first_ref), channel_id=1, source_target_pairs={{0,16},{4,20},{8,24},{12,28},{16,0},{20,4},{24,8},{28,12},{1,17},{... | collective-permute-start | bytes 12296 | tf_op jit(solution)/shard_map/ppermute | solution.py:471
  (9 other events, 40.3 us)

commit v12 on v11

--- a/solution.py
+++ b/solution.py
@@ -13,6 +13,7 @@
 SHORT_GROUP = 8
 TURN_GROUP = 24
 TURN_PRODUCTS = 6
+QUARTERS = 4
 F32 = jnp.float32
 BF16 = jnp.bfloat16
 VMEM = pl.BlockSpec(memory_space=pltpu.VMEM)
@@ -331,7 +332,10 @@
         ratios_ref, sides_ref, *refs = refs
     if index + 1 == ITERS:
         lost_refs, refs = refs[: sub_count - 1], refs[sub_count - 1 :]
-    part_refs, moments_ref, *kept_refs = refs[:sub_count], *refs[sub_count:]
+    part_refs, kept_refs = refs[:sub_count], refs[sub_count:]
+    if index + 1 < ITERS:
+        moments_ref, *kept_refs = kept_refs
+        moments_ref[...] = moments_in_ref[...]
     block_len = blocks_ref.shape[1]
     sub_index, blocks_dev, own_first, tile_blocks = device_place(block_len, part_refs[0], sub_count)
     is_odd = lax.axis_index("tile") % 2 == 1
@@ -357,9 +361,8 @@
         total[block] = begun_ref[block]
     total[begun_ref.shape[0] - 1] = jnp.zeros(total.shape[1:], F32)
     add_products(lists_ref, blocks_ref, slot_count, ahead, total, FROM_AHEAD, SHORT_GROUP, tile_blocks, 0)
-    moments = moments_in_ref[...]
     if index + 1 == ITERS:
-        weight = lost_weight(moments) * ratios_ref[:, :1]
+        weight = lost_weight(moments_in_ref[...]) * ratios_ref[:, :1]
     for step in range(sub_count):
         first = (sub_index ^ step) * blocks_dev
         for block in range(blocks_dev):
@@ -371,7 +374,6 @@
             part_refs[step][:, span] = rounded
             if step and kept_refs:
                 kept_refs[step - 1][:, span] = value - rounded.astype(F32)
-    moments_ref[...] = moments
 
 
 def join_kernel(index, after_ref, unit_ref, ratios_ref, own_ref, old_ref, moments_in_ref, *refs):
@@ -415,8 +417,8 @@
 
 
 def finish_kernel(sub_count, moments_ref, unit_ref, ratios_ref, *refs):
-    part_refs, basis_refs = refs[:sub_count], refs[sub_count:-2]
-    solution_ref, residual_ref = refs[-2:]
+    part_refs, basis_refs = refs[:sub_count], refs[sub_count:-5]
+    outs, (solution_ref, residual_ref, sems) = refs[-5:-3], refs[-3:]
     moments = [moments_ref[:, order : order + 1] for order in range(2 * ITERS)]
     largest = moments_ref[:, 2 * ITERS : 2 * ITERS + 1]
     unit = unit_ref[:, :1]
@@ -448,8 +450,6 @@
                 for value, old in zip(residual, direction + [zero])
             ]
             norm_now = norm_next
-    fields = [basis_ref[...] for basis_ref in basis_refs]
-    fields.append(sum(part_ref[...].astype(F32) for part_ref in part_refs))
     for order in range(1, ITERS + 1):
         scale = raised(ratio, order)
         if order < ITERS:
@@ -458,8 +458,19 @@
             scale = scale / (raised(ratios_ref[:, :1], ITERS - 1) * unit)
         residual[order] = residual[order] * scale
     answer = [weight / largest for weight in answer]
-    solution_ref[...] = sum(weight * field for weight, field in zip(answer, fields))
-    residual_ref[...] = sum(weight * field for weight, field in zip(residual, fields))
+    size = solution_ref.shape[1] // QUARTERS
+    copies = []
+    for quarter in range(QUARTERS):
+        span = slice(quarter * size, (quarter + 1) * size)
+        fields = [basis_ref[:, span] for basis_ref in basis_refs]
+        fields.append(sum(part_ref[:, span].astype(F32) for part_ref in part_refs))
+        for index, (ref, weights) in enumerate(((solution_ref, answer), (residual_ref, residual))):
+            ref[:, span] = sum(weight * field for weight, field in zip(weights, fields))
+            copy = pltpu.make_async_copy(ref.at[:, span], outs[index].at[:, span], sems.at[index, quarter])
+            copy.start()
+            copies.append(copy)
+    for copy in copies:
+        copy.wait()
 
 
 def shape(rows, columns, kind):
@@ -527,7 +538,6 @@
             pltpu.SemaphoreType.DMA(()),
         ],
     )
-    blocks = pair_blocks
     field, rounded = call(
         order_kernel,
         (full, half),
@@ -541,6 +551,7 @@
             pltpu.SemaphoreType.DMA((2,)),
         ],
     )
+    blocks = pair_blocks
     basis = [field]
     moments = jnp.zeros(scalars.shape, F32)
     ratios = sides = ()
@@ -587,7 +598,7 @@
             functools.partial(part_kernel, index, sub_count, slot_count),
             (full,)
             + (part,) * (sub_count - 1)
-            + (scalars,)
+            + (() if is_last else (scalars,))
             + ((full,) * (sub_count - 1) if index + 2 == ITERS else ())
             + ((shape(rhs_count, 2 * LANES, F32),) if index == 1 else ()),
             (lists, blocks, begun, tile_field, even, odd, moments, *ratios, *sides, *(lost if is_last else ())),
@@ -595,7 +606,9 @@
             1,
             scratch_shapes=[scratch(extended + 1), scratch(blocks_dev)],
         )
-        parts, moments = list(found[:sub_count]), found[sub_count]
+        parts = list(found[:sub_count])
+        if not is_last:
+            moments = found[sub_count]
         if index == 1:
             sides = (found[-1],)
         lost = found[sub_count + 1 : 2 * sub_count]
@@ -641,6 +654,12 @@
         (full, full),
         (moments, unit, *ratios, parts[0], *arrived, *basis),
         "finish",
+        out_specs=(pl.BlockSpec(memory_space=pltpu.HBM),) * 2,
+        scratch_shapes=[
+            pltpu.VMEM(right_side.shape, F32),
+            pltpu.VMEM(right_side.shape, F32),
+            pltpu.SemaphoreType.DMA((2, QUARTERS)),
+        ],
     )
 
 

time: 93.9 us -> 93.2 us (level)
  starting transfers between devices: 45.5 us -> 52.8 us
  Pallas kernels: 25.1 us -> 20.8 us
  waiting for transfers between devices: 21.3 us -> 17.5 us
    ppermute x6, starting transfers between devices: 3 us -> 9.02 us  [swap(): return lax.ppermute(block, axis, route)]
    pallas_call x25, Pallas kernels: 25.1 us -> 20.8 us  [call(): pl.pallas_call(kernel, out_shape=outs, compiler_params=PARAMS, name=name,...]
    ppermute x23, waiting for transfers between devices: 21.3 us -> 17.5 us  [exchange(): return lax.ppermute(block, axis, [(i, i ^ step) for i in range(count)])]
    ppermute x23, starting transfers between devices: 42.5 us -> 43.7 us  [exchange(): return lax.ppermute(block, axis, [(i, i ^ step) for i in range(count)])]
  transfers between devices with their start and end apart: 29 -> 29, of which waited for: 13 -> 13; matrix products, arithmetic and copies ran while one was open for 0% -> 0% of each run, Pallas kernels for 19% -> 16%
where the time goes in v12:
time: 93.2 us; the launch traced here: 92 us
  starting transfers between devices  52.8 us (57%)
  Pallas kernels  20.8 us (22%)
  waiting for transfers between devices  17.5 us (19%)
    ppermute x23, starting transfers between devices, exchange(): return lax.ppermute(block, axis, [(i, i ^ step) for i in range(count)])  43.7 us
    pallas_call x25, Pallas kernels, call(): pl.pallas_call(kernel, out_shape=outs, compiler_params=PARAMS, name=name,...  20.8 us
    ppermute x23, waiting for transfers between devices, exchange(): return lax.ppermute(block, axis, [(i, i ^ step) for i in range(count)])  17.5 us
    ppermute x6, starting transfers between devices, swap(): return lax.ppermute(block, axis, route)  9.02 us
  transfers between devices with their start and end apart: 29, of which 13 were waited for; matrix products, arithmetic and copies ran while one was open for 0% of the time, Pallas kernels for 16%

profile of v12, /device:TPU:0, one launch (start us, length us, event | category | flops | bytes accessed | tf_op | source)
XLA Modules:
  0.0 92.0 jit_solution(4825446332227088814)
XLA Ops:
  0.7 2.3 %curve_order.1 = (f32[8,4096]{1,0:T(8,128)S(1)}, bf16[8,4096]{1,0:T(8,128)(2,1)S(1)}) custom-call(f32[8,4096]{1,0:T(8,128)} %right_in.1, s32[1,4096]{1,0:T(1,128)} %order_in.1), custom_call_target="tpu_custom_call" | custom-call | flops 10000000000 | tf_op jit(solution)/shard_map/curve_order/pallas_call | solution.py:498
  3.0 5.1 %collective-permute-start.2 = (bf16[8,4096]{1,0:T(8,128)(2,1)S(1)}, bf16[8,4096]{1,0:T(8,128)(2,1)S(1)}, u32[]{:S(2)}, u32[]{:S(2)}) collective-permute-start(bf16[8,4096]{1,0:T(8,128)(2,1)S(1)} %get-tuple-element.49.refs_0_.rounded_ref), channel_id=1, source_target_pairs={{0,3},{1,2},{2,1},{3,0},{4,7},{5,6},{6,5},{7,4},{8,11},{9,10},{10,... | collective-permute-start | bytes 196616 | tf_op jit(solution)/shard_map/ppermute | solution.py:482
  11.4 2.3 %collective-permute-done.1.refs_2_ = bf16[8,4096]{1,0:T(8,128)(2,1)S(1)} collective-permute-done((bf16[8,4096]{1,0:T(8,128)(2,1)S(1)}, bf16[8,4096]{1,0:T(8,128)(2,1)S(1)}, u32[]{:S(2)}, u32[]{:S(2)}) %collective-permute-start.1) | collective-permute-done | bytes 65568 | tf_op jit(solution)/shard_map/ppermute | solution.py:482
  15.0 2.2 %late.3.begun_ref = f32[81,8,256]{2,1,0:T(8,128)S(1)} custom-call(s32[1,1280]{1,0:T(1,128)S(4)} %lists.1.lists_ref, bf16[96,256,256]{2,1,0:T(8,128)(2,1)S(1)} %copy-done, f32[81,8,256]{2,1,0:T(8,128)S(1)} %early.3.begun_ref, f32[64,8,256]{2,1,0:T(8,128)S(1)} %get-tuple-element.50.field_ref), custom_call_target="tpu_custom_call" | custom-call | flops 3000000000 | tf_op jit(solution)/shard_map/late/pallas_call | solution.py:498
  17.7 3.4 %collective-permute-start.5 = (bf16[8,4096]{1,0:T(8,128)(2,1)S(1)}, bf16[8,4096]{1,0:T(8,128)(2,1)S(1)}, u32[]{:S(2)}, u32[]{:S(2)}) collective-permute-start(bf16[8,4096]{1,0:T(8,128)(2,1)S(1)} %get-tuple-element.57), channel_id=1, source_target_pairs={{0,3},{1,2},{2,1},{3,0},{4,7},{5,6},{6,5},{7,4},{8,11},{9,10},{10,... | collective-permute-start | bytes 196616 | tf_op jit(solution)/shard_map/ppermute | solution.py:482
  21.1 1.8 %collective-permute-start.6 = (bf16[8,4096]{1,0:T(8,128)(2,1)S(1)}, bf16[8,4096]{1,0:T(8,128)(2,1)S(1)}, u32[]{:S(2)}, u32[]{:S(2)}) collective-permute-start(bf16[8,4096]{1,0:T(8,128)(2,1)S(1)} %get-tuple-element.58), channel_id=1, source_target_pairs={{0,2},{1,3},{2,0},{3,1},{4,6},{5,7},{6,4},{7,5},{8,10},{9,11},{10,... | collective-permute-start | bytes 196616 | tf_op jit(solution)/shard_map/ppermute | solution.py:482
  22.9 3.6 %turn.1.after_ref.blocks_ref = bf16[192,256,256]{2,1,0:T(8,128)(2,1)S(1)} custom-call(bf16[96,256,256]{2,1,0:T(8,128)(2,1)S(1)} %copy-done, f32[8,128]{1,0:T(8,128)S(1)} %get-tuple-element.53.after_ref.moments_in_ref), custom_call_target="tpu_custom_call" | custom-call | flops 4000000000 | tf_op jit(solution)/shard_map/turn/pallas_call | solution.py:498
  28.1 2.6 %collective-permute-start.10 = (bf16[8,4224]{1,0:T(8,128)(2,1)S(1)}, bf16[8,4224]{1,0:T(8,128)(2,1)S(1)}, u32[]{:S(2)}, u32[]{:S(2)}) collective-permute-start(bf16[8,4224]{1,0:T(8,128)(2,1)S(1)} %get-tuple-element.62.refs_3_.refs_0_), channel_id=1, source_target_pairs={{0,3},{1,2},{2,1},{3,0},{4,7},{5,6},{6,5},{7,4},{8,11},{9,10},{10,... | collective-permute-start | bytes 202760 | tf_op jit(solution)/shard_map/ppermute | solution.py:482
  34.3 2.6 %collective-permute-done.9.refs_2_ = bf16[8,4224]{1,0:T(8,128)(2,1)S(1)} collective-permute-done((bf16[8,4224]{1,0:T(8,128)(2,1)S(1)}, bf16[8,4224]{1,0:T(8,128)(2,1)S(1)}, u32[]{:S(2)}, u32[]{:S(2)}) %collective-permute-start.9) | collective-permute-done | bytes 67616 | tf_op jit(solution)/shard_map/ppermute | solution.py:482
  37.2 2.6 %collective-permute-start.11 = (bf16[8,4224]{1,0:T(8,128)(2,1)S(1)}, bf16[8,4224]{1,0:T(8,128)(2,1)S(1)}, u32[]{:S(2)}, u32[]{:S(2)}) collective-permute-start(bf16[8,4224]{1,0:T(8,128)(2,1)S(1)} %get-tuple-element.65), channel_id=1, source_target_pairs={{0,4},{4,0},{8,12},{12,8},{16,20},{20,16},{24,28},{28,24},{1,5},{5... | collective-permute-start | bytes 202760 | tf_op jit(solution)/shard_map/ppermute | solution.py:490
  42.1 2.2 %collective-permute-start.13 = (bf16[8,4096]{1,0:T(8,128)(2,1)S(1)}, bf16[8,4096]{1,0:T(8,128)(2,1)S(1)}, u32[]{:S(2)}, u32[]{:S(2)}) collective-permute-start(bf16[8,4096]{1,0:T(8,128)(2,1)S(1)} %get-tuple-element.70), channel_id=1, source_target_pairs={{0,3},{1,2},{2,1},{3,0},{4,7},{5,6},{6,5},{7,4},{8,11},{9,10},{10,... | collective-permute-start | bytes 196616 | tf_op jit(solution)/shard_map/ppermute | solution.py:482
  44.3 2.3 %collective-permute-start.14 = (bf16[8,4096]{1,0:T(8,128)(2,1)S(1)}, bf16[8,4096]{1,0:T(8,128)(2,1)S(1)}, u32[]{:S(2)}, u32[]{:S(2)}) collective-permute-start(bf16[8,4096]{1,0:T(8,128)(2,1)S(1)} %get-tuple-element.71), channel_id=1, source_target_pairs={{0,2},{1,3},{2,0},{3,1},{4,6},{5,7},{6,4},{7,5},{8,10},{9,11},{10,... | collective-permute-start | bytes 196616 | tf_op jit(solution)/shard_map/ppermute | solution.py:482
  46.6 1.7 %collective-permute-done.13.refs_0_ = bf16[8,4096]{1,0:T(8,128)(2,1)S(1)} collective-permute-done((bf16[8,4096]{1,0:T(8,128)(2,1)S(1)}, bf16[8,4096]{1,0:T(8,128)(2,1)S(1)}, u32[]{:S(2)}, u32[]{:S(2)}) %collective-permute-start.13) | collective-permute-done | bytes 65568 | tf_op jit(solution)/shard_map/ppermute | solution.py:482
  48.3 2.1 %collective-permute-done.14.refs_1_ = bf16[8,4096]{1,0:T(8,128)(2,1)S(1)} collective-permute-done((bf16[8,4096]{1,0:T(8,128)(2,1)S(1)}, bf16[8,4096]{1,0:T(8,128)(2,1)S(1)}, u32[]{:S(2)}, u32[]{:S(2)}) %collective-permute-start.14) | collective-permute-done | bytes 65568 | tf_op jit(solution)/shard_map/ppermute | solution.py:482
  53.1 2.5 %collective-permute-start.16 = (bf16[8,4096]{1,0:T(8,128)(2,1)S(1)}, bf16[8,4096]{1,0:T(8,128)(2,1)S(1)}, u32[]{:S(2)}, u32[]{:S(2)}) collective-permute-start(bf16[8,4096]{1,0:T(8,128)(2,1)S(1)} %get-tuple-element.74.refs_3_.refs_1_), channel_id=1, source_target_pairs={{0,1},{1,0},{2,3},{3,2},{4,5},{5,4},{6,7},{7,6},{8,9},{9,8},{10,11... | collective-permute-start | bytes 196616 | tf_op jit(solution)/shard_map/ppermute | solution.py:482
  58.9 4.2 %collective-permute-start.19 = (bf16[8,4096]{1,0:T(8,128)(2,1)S(1)}, bf16[8,4096]{1,0:T(8,128)(2,1)S(1)}, u32[]{:S(2)}, u32[]{:S(2)}) collective-permute-start(bf16[8,4096]{1,0:T(8,128)(2,1)S(1)} %get-tuple-element.76), channel_id=1, source_target_pairs={{0,4},{4,0},{8,12},{12,8},{16,20},{20,16},{24,28},{28,24},{1,5},{5... | collective-permute-start | bytes 196616 | tf_op jit(solution)/shard_map/ppermute | solution.py:490
  65.3 2.5 %collective-permute-start.21 = (f32[8,128]{1,0:T(8,128)S(1)}, f32[8,128]{1,0:T(8,128)S(1)}, u32[]{:S(2)}, u32[]{:S(2)}) collective-permute-start(f32[8,128]{1,0:T(8,128)S(1)} %curvature.1.first_ref), channel_id=1, source_target_pairs={{0,1},{1,0},{2,3},{3,2},{4,5},{5,4},{6,7},{7,6},{8,9},{9,8},{10,11... | collective-permute-start | bytes 12296 | tf_op jit(solution)/shard_map/ppermute | solution.py:482
  69.4 1.6 %collective-permute-start.22 = (f32[8,128]{1,0:T(8,128)S(1)}, f32[8,128]{1,0:T(8,128)S(1)}, u32[]{:S(2)}, u32[]{:S(2)}) collective-permute-start(f32[8,128]{1,0:T(8,128)S(1)} %add_moments.5.first_ref), channel_id=1, source_target_pairs={{0,2},{1,3},{2,0},{3,1},{4,6},{5,7},{6,4},{7,5},{8,10},{9,11},{10,... | collective-permute-start | bytes 12296 | tf_op jit(solution)/shard_map/ppermute | solution.py:482
  71.0 2.8 %collective-permute-start.26 = (f32[8,4096]{1,0:T(8,128)S(1)}, f32[8,4096]{1,0:T(8,128)S(1)}, u32[]{:S(2)}, u32[]{:S(2)}) collective-permute-start(f32[8,4096]{1,0:T(8,128)S(1)} %get-tuple-element.86), channel_id=1, source_target_pairs={{0,3},{1,2},{2,1},{3,0},{4,7},{5,6},{6,5},{7,4},{8,11},{9,10},{10,... | collective-permute-start | bytes 393224 | tf_op jit(solution)/shard_map/ppermute | solution.py:482
  74.1 2.2 %collective-permute-start.28 = (f32[8,4096]{1,0:T(8,128)S(1)}, f32[8,4096]{1,0:T(8,128)S(1)}, u32[]{:S(2)}, u32[]{:S(2)}) collective-permute-start(f32[8,4096]{1,0:T(8,128)S(1)} %get-tuple-element.93), channel_id=1, source_target_pairs={{0,1},{1,0},{2,3},{3,2},{4,5},{5,4},{6,7},{7,6},{8,9},{9,8},{10,11... | collective-permute-start | bytes 393224 | tf_op jit(solution)/shard_map/ppermute | solution.py:482
  76.3 4.7 %collective-permute-start.23 = (f32[8,128]{1,0:T(8,128)S(1)}, f32[8,128]{1,0:T(8,128)S(1)}, u32[]{:S(2)}, u32[]{:S(2)}) collective-permute-start(f32[8,128]{1,0:T(8,128)S(1)} %add_moments.6.first_ref), channel_id=1, source_target_pairs={{0,4},{4,0},{8,12},{12,8},{16,20},{20,16},{24,28},{28,24},{1,5},{5... | collective-permute-start | bytes 12296 | tf_op jit(solution)/shard_map/ppermute | solution.py:482
  81.9 2.4 %collective-permute-start.24 = (f32[8,128]{1,0:T(8,128)S(1)}, f32[8,128]{1,0:T(8,128)S(1)}, u32[]{:S(2)}, u32[]{:S(2)}) collective-permute-start(f32[8,128]{1,0:T(8,128)S(1)} %add_moments.7.first_ref), channel_id=1, source_target_pairs={{0,8},{4,12},{8,0},{12,4},{16,24},{20,28},{24,16},{28,20},{1,9},{5... | collective-permute-start | bytes 12296 | tf_op jit(solution)/shard_map/ppermute | solution.py:482
  84.3 1.6 %collective-permute-done.24.second_ref = f32[8,128]{1,0:T(8,128)S(1)} collective-permute-done((f32[8,128]{1,0:T(8,128)S(1)}, f32[8,128]{1,0:T(8,128)S(1)}, u32[]{:S(2)}, u32[]{:S(2)}) %collective-permute-start.24) | collective-permute-done | bytes 4128 | tf_op jit(solution)/shard_map/ppermute | solution.py:482
  86.0 3.3 %collective-permute-start.25 = (f32[8,128]{1,0:T(8,128)S(1)}, f32[8,128]{1,0:T(8,128)S(1)}, u32[]{:S(2)}, u32[]{:S(2)}) collective-permute-start(f32[8,128]{1,0:T(8,128)S(1)} %add_moments.8.first_ref), channel_id=1, source_target_pairs={{0,16},{4,20},{8,24},{12,28},{16,0},{20,4},{24,8},{28,12},{1,17},{... | collective-permute-start | bytes 12296 | tf_op jit(solution)/shard_map/ppermute | solution.py:482
  (68 shorter events, 26.5 us)
Async XLA Ops:
  3.0 8.4 %collective-permute-start.2 = (bf16[8,4096]{1,0:T(8,128)(2,1)S(1)}, bf16[8,4096]{1,0:T(8,128)(2,1)S(1)}, u32[]{:S(2)}, u32[]{:S(2)}) collective-permute-start(bf16[8,4096]{1,0:T(8,128)(2,1)S(1)} %get-tuple-element.49.refs_0_.rounded_ref), channel_id=1, source_target_pairs={{0,3},{1,2},{2,1},{3,0},{4,7},{5,6},{6,5},{7,4},{8,11},{9,10},{10,... | collective-permute-start | bytes 196616 | tf_op jit(solution)/shard_map/ppermute | solution.py:482
  8.1 5.6 %collective-permute-start.1 = (bf16[8,4096]{1,0:T(8,128)(2,1)S(1)}, bf16[8,4096]{1,0:T(8,128)(2,1)S(1)}, u32[]{:S(2)}, u32[]{:S(2)}) collective-permute-start(bf16[8,4096]{1,0:T(8,128)(2,1)S(1)} %get-tuple-element.49.refs_0_.rounded_ref), channel_id=1, source_target_pairs={{0,2},{1,3},{2,0},{3,1},{4,6},{5,7},{6,4},{7,5},{8,10},{9,11},{10,... | collective-permute-start | bytes 196616 | tf_op jit(solution)/shard_map/ppermute | solution.py:482
  8.1 5.6 %collective-permute-start = (bf16[8,4096]{1,0:T(8,128)(2,1)S(1)}, bf16[8,4096]{1,0:T(8,128)(2,1)S(1)}, u32[]{:S(2)}, u32[]{:S(2)}) collective-permute-start(bf16[8,4096]{1,0:T(8,128)(2,1)S(1)} %get-tuple-element.49.refs_0_.rounded_ref), channel_id=1, source_target_pairs={{0,1},{1,0},{2,3},{3,2},{4,5},{5,4},{6,7},{7,6},{8,9},{9,8},{10,11... | collective-permute-start | bytes 196616 | tf_op jit(solution)/shard_map/ppermute | solution.py:482
  17.7 10.3 %collective-permute-start.5 = (bf16[8,4096]{1,0:T(8,128)(2,1)S(1)}, bf16[8,4096]{1,0:T(8,128)(2,1)S(1)}, u32[]{:S(2)}, u32[]{:S(2)}) collective-permute-start(bf16[8,4096]{1,0:T(8,128)(2,1)S(1)} %get-tuple-element.57), channel_id=1, source_target_pairs={{0,3},{1,2},{2,1},{3,0},{4,7},{5,6},{6,5},{7,4},{8,11},{9,10},{10,... | collective-permute-start | bytes 196616 | tf_op jit(solution)/shard_map/ppermute | solution.py:482
  21.1 6.8 %collective-permute-start.6 = (bf16[8,4096]{1,0:T(8,128)(2,1)S(1)}, bf16[8,4096]{1,0:T(8,128)(2,1)S(1)}, u32[]{:S(2)}, u32[]{:S(2)}) collective-permute-start(bf16[8,4096]{1,0:T(8,128)(2,1)S(1)} %get-tuple-element.58), channel_id=1, source_target_pairs={{0,2},{1,3},{2,0},{3,1},{4,6},{5,7},{6,4},{7,5},{8,10},{9,11},{10,... | collective-permute-start | bytes 196616 | tf_op jit(solution)/shard_map/ppermute | solution.py:482
  22.9 5.1 %collective-permute-start.7 = (bf16[8,4096]{1,0:T(8,128)(2,1)S(1)}, bf16[8,4096]{1,0:T(8,128)(2,1)S(1)}, u32[]{:S(2)}, u32[]{:S(2)}) collective-permute-start(bf16[8,4096]{1,0:T(8,128)(2,1)S(1)} %get-tuple-element.59), channel_id=1, source_target_pairs={{0,1},{1,0},{2,3},{3,2},{4,5},{5,4},{6,7},{7,6},{8,9},{9,8},{10,11... | collective-permute-start | bytes 196616 | tf_op jit(solution)/shard_map/ppermute | solution.py:482
  28.1 6.2 %collective-permute-start.10 = (bf16[8,4224]{1,0:T(8,128)(2,1)S(1)}, bf16[8,4224]{1,0:T(8,128)(2,1)S(1)}, u32[]{:S(2)}, u32[]{:S(2)}) collective-permute-start(bf16[8,4224]{1,0:T(8,128)(2,1)S(1)} %get-tuple-element.62.refs_3_.refs_0_), channel_id=1, source_target_pairs={{0,3},{1,2},{2,1},{3,0},{4,7},{5,6},{6,5},{7,4},{8,11},{9,10},{10,... | collective-permute-start | bytes 202760 | tf_op jit(solution)/shard_map/ppermute | solution.py:482
  30.7 6.2 %collective-permute-start.9 = (bf16[8,4224]{1,0:T(8,128)(2,1)S(1)}, bf16[8,4224]{1,0:T(8,128)(2,1)S(1)}, u32[]{:S(2)}, u32[]{:S(2)}) collective-permute-start(bf16[8,4224]{1,0:T(8,128)(2,1)S(1)} %get-tuple-element.62.refs_3_.refs_0_), channel_id=1, source_target_pairs={{0,2},{1,3},{2,0},{3,1},{4,6},{5,7},{6,4},{7,5},{8,10},{9,11},{10,... | collective-permute-start | bytes 202760 | tf_op jit(solution)/shard_map/ppermute | solution.py:482
  31.6 5.3 %collective-permute-start.8 = (bf16[8,4224]{1,0:T(8,128)(2,1)S(1)}, bf16[8,4224]{1,0:T(8,128)(2,1)S(1)}, u32[]{:S(2)}, u32[]{:S(2)}) collective-permute-start(bf16[8,4224]{1,0:T(8,128)(2,1)S(1)} %get-tuple-element.62.refs_3_.refs_0_), channel_id=1, source_target_pairs={{0,1},{1,0},{2,3},{3,2},{4,5},{5,4},{6,7},{7,6},{8,9},{9,8},{10,11... | collective-permute-start | bytes 202760 | tf_op jit(solution)/shard_map/ppermute | solution.py:482
  37.2 4.5 %collective-permute-start.11 = (bf16[8,4224]{1,0:T(8,128)(2,1)S(1)}, bf16[8,4224]{1,0:T(8,128)(2,1)S(1)}, u32[]{:S(2)}, u32[]{:S(2)}) collective-permute-start(bf16[8,4224]{1,0:T(8,128)(2,1)S(1)} %get-tuple-element.65), channel_id=1, source_target_pairs={{0,4},{4,0},{8,12},{12,8},{16,20},{20,16},{24,28},{28,24},{1,5},{5... | collective-permute-start | bytes 202760 | tf_op jit(solution)/shard_map/ppermute | solution.py:490
  42.1 6.1 %collective-permute-start.13 = (bf16[8,4096]{1,0:T(8,128)(2,1)S(1)}, bf16[8,4096]{1,0:T(8,128)(2,1)S(1)}, u32[]{:S(2)}, u32[]{:S(2)}) collective-permute-start(bf16[8,4096]{1,0:T(8,128)(2,1)S(1)} %get-tuple-element.70), channel_id=1, source_target_pairs={{0,3},{1,2},{2,1},{3,0},{4,7},{5,6},{6,5},{7,4},{8,11},{9,10},{10,... | collective-permute-start | bytes 196616 | tf_op jit(solution)/shard_map/ppermute | solution.py:482
  44.3 6.1 %collective-permute-start.14 = (bf16[8,4096]{1,0:T(8,128)(2,1)S(1)}, bf16[8,4096]{1,0:T(8,128)(2,1)S(1)}, u32[]{:S(2)}, u32[]{:S(2)}) collective-permute-start(bf16[8,4096]{1,0:T(8,128)(2,1)S(1)} %get-tuple-element.71), channel_id=1, source_target_pairs={{0,2},{1,3},{2,0},{3,1},{4,6},{5,7},{6,4},{7,5},{8,10},{9,11},{10,... | collective-permute-start | bytes 196616 | tf_op jit(solution)/shard_map/ppermute | solution.py:482
  46.5 4.5 %collective-permute-start.15 = (bf16[8,4096]{1,0:T(8,128)(2,1)S(1)}, bf16[8,4096]{1,0:T(8,128)(2,1)S(1)}, u32[]{:S(2)}, u32[]{:S(2)}) collective-permute-start(bf16[8,4096]{1,0:T(8,128)(2,1)S(1)} %get-tuple-element.72), channel_id=1, source_target_pairs={{0,1},{1,0},{2,3},{3,2},{4,5},{5,4},{6,7},{7,6},{8,9},{9,8},{10,11... | collective-permute-start | bytes 196616 | tf_op jit(solution)/shard_map/ppermute | solution.py:482
  51.2 6.2 %collective-permute-start.18 = (bf16[8,4096]{1,0:T(8,128)(2,1)S(1)}, bf16[8,4096]{1,0:T(8,128)(2,1)S(1)}, u32[]{:S(2)}, u32[]{:S(2)}) collective-permute-start(bf16[8,4096]{1,0:T(8,128)(2,1)S(1)} %get-tuple-element.74.refs_3_.refs_1_), channel_id=1, source_target_pairs={{0,3},{1,2},{2,1},{3,0},{4,7},{5,6},{6,5},{7,4},{8,11},{9,10},{10,... | collective-permute-start | bytes 196616 | tf_op jit(solution)/shard_map/ppermute | solution.py:482
  52.0 6.6 %collective-permute-start.17 = (bf16[8,4096]{1,0:T(8,128)(2,1)S(1)}, bf16[8,4096]{1,0:T(8,128)(2,1)S(1)}, u32[]{:S(2)}, u32[]{:S(2)}) collective-permute-start(bf16[8,4096]{1,0:T(8,128)(2,1)S(1)} %get-tuple-element.74.refs_3_.refs_1_), channel_id=1, source_target_pairs={{0,2},{1,3},{2,0},{3,1},{4,6},{5,7},{6,4},{7,5},{8,10},{9,11},{10,... | collective-permute-start | bytes 196616 | tf_op jit(solution)/shard_map/ppermute | solution.py:482
  53.1 5.5 %collective-permute-start.16 = (bf16[8,4096]{1,0:T(8,128)(2,1)S(1)}, bf16[8,4096]{1,0:T(8,128)(2,1)S(1)}, u32[]{:S(2)}, u32[]{:S(2)}) collective-permute-start(bf16[8,4096]{1,0:T(8,128)(2,1)S(1)} %get-tuple-element.74.refs_3_.refs_1_), channel_id=1, source_target_pairs={{0,1},{1,0},{2,3},{3,2},{4,5},{5,4},{6,7},{7,6},{8,9},{9,8},{10,11... | collective-permute-start | bytes 196616 | tf_op jit(solution)/shard_map/ppermute | solution.py:482
  58.9 6.1 %collective-permute-start.19 = (bf16[8,4096]{1,0:T(8,128)(2,1)S(1)}, bf16[8,4096]{1,0:T(8,128)(2,1)S(1)}, u32[]{:S(2)}, u32[]{:S(2)}) collective-permute-start(bf16[8,4096]{1,0:T(8,128)(2,1)S(1)} %get-tuple-element.76), channel_id=1, source_target_pairs={{0,4},{4,0},{8,12},{12,8},{16,20},{20,16},{24,28},{28,24},{1,5},{5... | collective-permute-start | bytes 196616 | tf_op jit(solution)/shard_map/ppermute | solution.py:490
  65.3 4.1 %collective-permute-start.21 = (f32[8,128]{1,0:T(8,128)S(1)}, f32[8,128]{1,0:T(8,128)S(1)}, u32[]{:S(2)}, u32[]{:S(2)}) collective-permute-start(f32[8,128]{1,0:T(8,128)S(1)} %curvature.1.first_ref), channel_id=1, source_target_pairs={{0,1},{1,0},{2,3},{3,2},{4,5},{5,4},{6,7},{7,6},{8,9},{9,8},{10,11... | collective-permute-start | bytes 12296 | tf_op jit(solution)/shard_map/ppermute | solution.py:482
  69.4 4.6 %collective-permute-start.22 = (f32[8,128]{1,0:T(8,128)S(1)}, f32[8,128]{1,0:T(8,128)S(1)}, u32[]{:S(2)}, u32[]{:S(2)}) collective-permute-start(f32[8,128]{1,0:T(8,128)S(1)} %add_moments.5.first_ref), channel_id=1, source_target_pairs={{0,2},{1,3},{2,0},{3,1},{4,6},{5,7},{6,4},{7,5},{8,10},{9,11},{10,... | collective-permute-start | bytes 12296 | tf_op jit(solution)/shard_map/ppermute | solution.py:482
  71.0 19.9 %collective-permute-start.26 = (f32[8,4096]{1,0:T(8,128)S(1)}, f32[8,4096]{1,0:T(8,128)S(1)}, u32[]{:S(2)}, u32[]{:S(2)}) collective-permute-start(f32[8,4096]{1,0:T(8,128)S(1)} %get-tuple-element.86), channel_id=1, source_target_pairs={{0,3},{1,2},{2,1},{3,0},{4,7},{5,6},{6,5},{7,4},{8,11},{9,10},{10,... | collective-permute-start | bytes 393224 | tf_op jit(solution)/shard_map/ppermute | solution.py:482
  73.9 17.1 %collective-permute-start.27 = (f32[8,4096]{1,0:T(8,128)S(1)}, f32[8,4096]{1,0:T(8,128)S(1)}, u32[]{:S(2)}, u32[]{:S(2)}) collective-permute-start(f32[8,4096]{1,0:T(8,128)S(1)} %get-tuple-element.90), channel_id=1, source_target_pairs={{0,2},{1,3},{2,0},{3,1},{4,6},{5,7},{6,4},{7,5},{8,10},{9,11},{10,... | collective-permute-start | bytes 393224 | tf_op jit(solution)/shard_map/ppermute | solution.py:482
  74.1 16.9 %collective-permute-start.28 = (f32[8,4096]{1,0:T(8,128)S(1)}, f32[8,4096]{1,0:T(8,128)S(1)}, u32[]{:S(2)}, u32[]{:S(2)}) collective-permute-start(f32[8,4096]{1,0:T(8,128)S(1)} %get-tuple-element.93), channel_id=1, source_target_pairs={{0,1},{1,0},{2,3},{3,2},{4,5},{5,4},{6,7},{7,6},{8,9},{9,8},{10,11... | collective-permute-start | bytes 393224 | tf_op jit(solution)/shard_map/ppermute | solution.py:482
  76.3 5.6 %collective-permute-start.23 = (f32[8,128]{1,0:T(8,128)S(1)}, f32[8,128]{1,0:T(8,128)S(1)}, u32[]{:S(2)}, u32[]{:S(2)}) collective-permute-start(f32[8,128]{1,0:T(8,128)S(1)} %add_moments.6.first_ref), channel_id=1, source_target_pairs={{0,4},{4,0},{8,12},{12,8},{16,20},{20,16},{24,28},{28,24},{1,5},{5... | collective-permute-start | bytes 12296 | tf_op jit(solution)/shard_map/ppermute | solution.py:482
  86.0 4.9 %collective-permute-start.25 = (f32[8,128]{1,0:T(8,128)S(1)}, f32[8,128]{1,0:T(8,128)S(1)}, u32[]{:S(2)}, u32[]{:S(2)}) collective-permute-start(f32[8,128]{1,0:T(8,128)S(1)} %add_moments.8.first_ref), channel_id=1, source_target_pairs={{0,16},{4,20},{8,24},{12,28},{16,0},{20,4},{24,8},{28,12},{1,17},{... | collective-permute-start | bytes 12296 | tf_op jit(solution)/shard_map/ppermute | solution.py:482
  (9 other events, 38.7 us)

commit v13 on v12

--- a/solution.py
+++ b/solution.py
@@ -9,8 +9,8 @@
 
 ITERS = 3
 LANES = 128
-LONG_GROUP = 16
-SHORT_GROUP = 8
+LONG_GROUP = 24
+SHORT_GROUP = 12
 TURN_GROUP = 24
 TURN_PRODUCTS = 6
 QUARTERS = 4

time: 93.2 us -> 94.6 us (1.015); the launches traced: 92 us -> 94.6 us
  starting transfers between devices: 52.8 us -> 45.7 us
  waiting for transfers between devices: 17.5 us -> 22.4 us
  Pallas kernels: 20.8 us -> 25.6 us
    ppermute x6, starting transfers between devices: 9.02 us -> 2.93 us  [swap(): return lax.ppermute(block, axis, route)]
    ppermute x23, waiting for transfers between devices: 17.5 us -> 22.4 us  [exchange(): return lax.ppermute(block, axis, [(i, i ^ step) for i in range(count)])]
    pallas_call x25, Pallas kernels: 20.8 us -> 25.6 us  [call(): pl.pallas_call(kernel, out_shape=outs, compiler_params=PARAMS, name=name,...]
    ppermute x23, starting transfers between devices: 43.7 us -> 42.8 us  [exchange(): return lax.ppermute(block, axis, [(i, i ^ step) for i in range(count)])]
  transfers between devices with their start and end apart: 29 -> 29, of which waited for: 13 -> 11; matrix products, arithmetic and copies ran while one was open for 0% -> 0% of each run, Pallas kernels for 16% -> 20%
where the time goes in v13:
time: 94.6 us
  starting transfers between devices  45.7 us (48%)
  Pallas kernels  25.6 us (27%)
  waiting for transfers between devices  22.4 us (24%)
    ppermute x23, starting transfers between devices, exchange(): return lax.ppermute(block, axis, [(i, i ^ step) for i in range(count)])  42.8 us
    pallas_call x25, Pallas kernels, call(): pl.pallas_call(kernel, out_shape=outs, compiler_params=PARAMS, name=name,...  25.6 us
    ppermute x23, waiting for transfers between devices, exchange(): return lax.ppermute(block, axis, [(i, i ^ step) for i in range(count)])  22.4 us
    ppermute x6, starting transfers between devices, swap(): return lax.ppermute(block, axis, route)  2.93 us
  transfers between devices with their start and end apart: 29, of which 11 were waited for; matrix products, arithmetic and copies ran while one was open for 0% of the time, Pallas kernels for 20%

profile of v13, /device:TPU:0, one launch (start us, length us, event | category | flops | bytes accessed | tf_op | source)
XLA Modules:
  0.0 94.6 jit_solution(5755636646187739444)
XLA Ops:
  0.7 2.3 %curve_order.1 = (f32[8,4096]{1,0:T(8,128)S(1)}, bf16[8,4096]{1,0:T(8,128)(2,1)S(1)}) custom-call(f32[8,4096]{1,0:T(8,128)} %right_in.1, s32[1,4096]{1,0:T(1,128)} %order_in.1), custom_call_target="tpu_custom_call" | custom-call | flops 10000000000 | tf_op jit(solution)/shard_map/curve_order/pallas_call | solution.py:498
  3.0 5.1 %collective-permute-start.2 = (bf16[8,4096]{1,0:T(8,128)(2,1)S(1)}, bf16[8,4096]{1,0:T(8,128)(2,1)S(1)}, u32[]{:S(2)}, u32[]{:S(2)}) collective-permute-start(bf16[8,4096]{1,0:T(8,128)(2,1)S(1)} %get-tuple-element.49.refs_0_.rounded_ref), channel_id=1, source_target_pairs={{0,3},{1,2},{2,1},{3,0},{4,7},{5,6},{6,5},{7,4},{8,11},{9,10},{10,... | collective-permute-start | bytes 196616 | tf_op jit(solution)/shard_map/ppermute | solution.py:482
  11.8 1.9 %collective-permute-done.1.refs_2_ = bf16[8,4096]{1,0:T(8,128)(2,1)S(1)} collective-permute-done((bf16[8,4096]{1,0:T(8,128)(2,1)S(1)}, bf16[8,4096]{1,0:T(8,128)(2,1)S(1)}, u32[]{:S(2)}, u32[]{:S(2)}) %collective-permute-start.1) | collective-permute-done | bytes 65568 | tf_op jit(solution)/shard_map/ppermute | solution.py:482
  14.9 3.9 %late.3.begun_ref = f32[81,8,256]{2,1,0:T(8,128)S(1)} custom-call(s32[1,1280]{1,0:T(1,128)S(4)} %lists.1.lists_ref, bf16[96,256,256]{2,1,0:T(8,128)(2,1)S(1)} %copy-done, f32[81,8,256]{2,1,0:T(8,128)S(1)} %early.3.begun_ref, f32[64,8,256]{2,1,0:T(8,128)S(1)} %get-tuple-element.50.field_ref), custom_call_target="tpu_custom_call" | custom-call | flops 3000000000 | tf_op jit(solution)/shard_map/late/pallas_call | solution.py:498
  19.5 4.1 %collective-permute-start.5 = (bf16[8,4096]{1,0:T(8,128)(2,1)S(1)}, bf16[8,4096]{1,0:T(8,128)(2,1)S(1)}, u32[]{:S(2)}, u32[]{:S(2)}) collective-permute-start(bf16[8,4096]{1,0:T(8,128)(2,1)S(1)} %get-tuple-element.57), channel_id=1, source_target_pairs={{0,3},{1,2},{2,1},{3,0},{4,7},{5,6},{6,5},{7,4},{8,11},{9,10},{10,... | collective-permute-start | bytes 196616 | tf_op jit(solution)/shard_map/ppermute | solution.py:482
  24.2 3.6 %turn.1.after_ref.blocks_ref = bf16[192,256,256]{2,1,0:T(8,128)(2,1)S(1)} custom-call(bf16[96,256,256]{2,1,0:T(8,128)(2,1)S(1)} %copy-done, f32[8,128]{1,0:T(8,128)S(1)} %get-tuple-element.53.after_ref.moments_in_ref), custom_call_target="tpu_custom_call" | custom-call | flops 4000000000 | tf_op jit(solution)/shard_map/turn/pallas_call | solution.py:498
  29.4 3.7 %collective-permute-start.10 = (bf16[8,4224]{1,0:T(8,128)(2,1)S(1)}, bf16[8,4224]{1,0:T(8,128)(2,1)S(1)}, u32[]{:S(2)}, u32[]{:S(2)}) collective-permute-start(bf16[8,4224]{1,0:T(8,128)(2,1)S(1)} %get-tuple-element.62.refs_3_.refs_0_), channel_id=1, source_target_pairs={{0,3},{1,2},{2,1},{3,0},{4,7},{5,6},{6,5},{7,4},{8,11},{9,10},{10,... | collective-permute-start | bytes 202760 | tf_op jit(solution)/shard_map/ppermute | solution.py:482
  35.8 4.6 %collective-permute-done.9.refs_2_ = bf16[8,4224]{1,0:T(8,128)(2,1)S(1)} collective-permute-done((bf16[8,4224]{1,0:T(8,128)(2,1)S(1)}, bf16[8,4224]{1,0:T(8,128)(2,1)S(1)}, u32[]{:S(2)}, u32[]{:S(2)}) %collective-permute-start.9) | collective-permute-done | bytes 67616 | tf_op jit(solution)/shard_map/ppermute | solution.py:482
  41.8 2.2 %late.4.begun_ref = f32[81,8,256]{2,1,0:T(8,128)S(1)} custom-call(s32[1,1280]{1,0:T(1,128)S(4)} %lists.1.lists_ref, bf16[192,256,256]{2,1,0:T(8,128)(2,1)S(1)} %turn.1.after_ref.blocks_ref, f32[81,8,256]{2,1,0:T(8,128)S(1)} %early.4.begun_ref, f32[64,8,256]{2,1,0:T(8,128)S(1)} %get-tuple-element.64.field_ref, f32[8,640]{1,0:T(8,128)S(1)} %get-tuple-element.63.refs_0_.ratios_ref), custom_call_target="tpu_custom_call" | custom-call | flops 3000000000 | tf_op jit(solution)/shard_map/late/pallas_call | solution.py:498
  44.5 2.7 %collective-permute-start.13 = (bf16[8,4096]{1,0:T(8,128)(2,1)S(1)}, bf16[8,4096]{1,0:T(8,128)(2,1)S(1)}, u32[]{:S(2)}, u32[]{:S(2)}) collective-permute-start(bf16[8,4096]{1,0:T(8,128)(2,1)S(1)} %get-tuple-element.70), channel_id=1, source_target_pairs={{0,3},{1,2},{2,1},{3,0},{4,7},{5,6},{6,5},{7,4},{8,11},{9,10},{10,... | collective-permute-start | bytes 196616 | tf_op jit(solution)/shard_map/ppermute | solution.py:482
  47.1 1.8 %collective-permute-start.15 = (bf16[8,4096]{1,0:T(8,128)(2,1)S(1)}, bf16[8,4096]{1,0:T(8,128)(2,1)S(1)}, u32[]{:S(2)}, u32[]{:S(2)}) collective-permute-start(bf16[8,4096]{1,0:T(8,128)(2,1)S(1)} %get-tuple-element.72), channel_id=1, source_target_pairs={{0,1},{1,0},{2,3},{3,2},{4,5},{5,4},{6,7},{7,6},{8,9},{9,8},{10,11... | collective-permute-start | bytes 196616 | tf_op jit(solution)/shard_map/ppermute | solution.py:482
  48.9 1.7 %collective-permute-done.13.refs_0_ = bf16[8,4096]{1,0:T(8,128)(2,1)S(1)} collective-permute-done((bf16[8,4096]{1,0:T(8,128)(2,1)S(1)}, bf16[8,4096]{1,0:T(8,128)(2,1)S(1)}, u32[]{:S(2)}, u32[]{:S(2)}) %collective-permute-start.13) | collective-permute-done | bytes 65568 | tf_op jit(solution)/shard_map/ppermute | solution.py:482
  50.6 2.4 %collective-permute-done.14.refs_1_ = bf16[8,4096]{1,0:T(8,128)(2,1)S(1)} collective-permute-done((bf16[8,4096]{1,0:T(8,128)(2,1)S(1)}, bf16[8,4096]{1,0:T(8,128)(2,1)S(1)}, u32[]{:S(2)}, u32[]{:S(2)}) %collective-permute-start.14) | collective-permute-done | bytes 65568 | tf_op jit(solution)/shard_map/ppermute | solution.py:482
  53.2 3.5 %collective-permute-start.18 = (bf16[8,4096]{1,0:T(8,128)(2,1)S(1)}, bf16[8,4096]{1,0:T(8,128)(2,1)S(1)}, u32[]{:S(2)}, u32[]{:S(2)}) collective-permute-start(bf16[8,4096]{1,0:T(8,128)(2,1)S(1)} %get-tuple-element.74.refs_3_.refs_1_), channel_id=1, source_target_pairs={{0,3},{1,2},{2,1},{3,0},{4,7},{5,6},{6,5},{7,4},{8,11},{9,10},{10,... | collective-permute-start | bytes 196616 | tf_op jit(solution)/shard_map/ppermute | solution.py:482
  59.4 3.5 %collective-permute-done.17.refs_3_ = bf16[8,4096]{1,0:T(8,128)(2,1)S(1)} collective-permute-done((bf16[8,4096]{1,0:T(8,128)(2,1)S(1)}, bf16[8,4096]{1,0:T(8,128)(2,1)S(1)}, u32[]{:S(2)}, u32[]{:S(2)}) %collective-permute-start.17) | collective-permute-done | bytes 65568 | tf_op jit(solution)/shard_map/ppermute | solution.py:482
  64.4 2.2 %late.5.begun_ref = f32[81,8,256]{2,1,0:T(8,128)S(1)} custom-call(s32[1,1280]{1,0:T(1,128)S(4)} %lists.1.lists_ref, bf16[192,256,256]{2,1,0:T(8,128)(2,1)S(1)} %turn.1.after_ref.blocks_ref, f32[81,8,256]{2,1,0:T(8,128)S(1)} %early.5.begun_ref, f32[64,8,256]{2,1,0:T(8,128)S(1)} %get-tuple-element.75.field_ref, f32[8,640]{1,0:T(8,128)S(1)} %get-tuple-element.63.refs_0_.ratios_ref), custom_call_target="tpu_custom_call" | custom-call | flops 3000000000 | tf_op jit(solution)/shard_map/late/pallas_call | solution.py:498
  68.0 2.4 %collective-permute-done.21.second_ref = f32[8,128]{1,0:T(8,128)S(1)} collective-permute-done((f32[8,128]{1,0:T(8,128)S(1)}, f32[8,128]{1,0:T(8,128)S(1)}, u32[]{:S(2)}, u32[]{:S(2)}) %collective-permute-start.21) | collective-permute-done | bytes 4128 | tf_op jit(solution)/shard_map/ppermute | solution.py:482
  70.5 1.7 %collective-permute-start.22 = (f32[8,128]{1,0:T(8,128)S(1)}, f32[8,128]{1,0:T(8,128)S(1)}, u32[]{:S(2)}, u32[]{:S(2)}) collective-permute-start(f32[8,128]{1,0:T(8,128)S(1)} %add_moments.5.first_ref), channel_id=1, source_target_pairs={{0,2},{1,3},{2,0},{3,1},{4,6},{5,7},{6,4},{7,5},{8,10},{9,11},{10,... | collective-permute-start | bytes 12296 | tf_op jit(solution)/shard_map/ppermute | solution.py:482
  73.8 1.9 %collective-permute-start.27 = (f32[8,4096]{1,0:T(8,128)S(1)}, f32[8,4096]{1,0:T(8,128)S(1)}, u32[]{:S(2)}, u32[]{:S(2)}) collective-permute-start(f32[8,4096]{1,0:T(8,128)S(1)} %get-tuple-element.90), channel_id=1, source_target_pairs={{0,2},{1,3},{2,0},{3,1},{4,6},{5,7},{6,4},{7,5},{8,10},{9,11},{10,... | collective-permute-start | bytes 393224 | tf_op jit(solution)/shard_map/ppermute | solution.py:482
  76.8 4.0 %collective-permute-start.23 = (f32[8,128]{1,0:T(8,128)S(1)}, f32[8,128]{1,0:T(8,128)S(1)}, u32[]{:S(2)}, u32[]{:S(2)}) collective-permute-start(f32[8,128]{1,0:T(8,128)S(1)} %add_moments.6.first_ref), channel_id=1, source_target_pairs={{0,4},{4,0},{8,12},{12,8},{16,20},{20,16},{24,28},{28,24},{1,5},{5... | collective-permute-start | bytes 12296 | tf_op jit(solution)/shard_map/ppermute | solution.py:482
  81.7 2.6 %collective-permute-start.24 = (f32[8,128]{1,0:T(8,128)S(1)}, f32[8,128]{1,0:T(8,128)S(1)}, u32[]{:S(2)}, u32[]{:S(2)}) collective-permute-start(f32[8,128]{1,0:T(8,128)S(1)} %add_moments.7.first_ref), channel_id=1, source_target_pairs={{0,8},{4,12},{8,0},{12,4},{16,24},{20,28},{24,16},{28,20},{1,9},{5... | collective-permute-start | bytes 12296 | tf_op jit(solution)/shard_map/ppermute | solution.py:482
  84.3 1.6 %collective-permute-done.24.second_ref = f32[8,128]{1,0:T(8,128)S(1)} collective-permute-done((f32[8,128]{1,0:T(8,128)S(1)}, f32[8,128]{1,0:T(8,128)S(1)}, u32[]{:S(2)}, u32[]{:S(2)}) %collective-permute-start.24) | collective-permute-done | bytes 4128 | tf_op jit(solution)/shard_map/ppermute | solution.py:482
  86.0 6.0 %collective-permute-start.25 = (f32[8,128]{1,0:T(8,128)S(1)}, f32[8,128]{1,0:T(8,128)S(1)}, u32[]{:S(2)}, u32[]{:S(2)}) collective-permute-start(f32[8,128]{1,0:T(8,128)S(1)} %add_moments.8.first_ref), channel_id=1, source_target_pairs={{0,16},{4,20},{8,24},{12,28},{16,0},{20,4},{24,8},{28,12},{1,17},{... | collective-permute-start | bytes 12296 | tf_op jit(solution)/shard_map/ppermute | solution.py:482
  92.0 1.6 %collective-permute-done.25.second_ref = f32[8,128]{1,0:T(8,128)S(1)} collective-permute-done((f32[8,128]{1,0:T(8,128)S(1)}, f32[8,128]{1,0:T(8,128)S(1)}, u32[]{:S(2)}, u32[]{:S(2)}) %collective-permute-start.25) | collective-permute-done | bytes 4128 | tf_op jit(solution)/shard_map/ppermute | solution.py:482
  (68 shorter events, 22.8 us)
Async XLA Ops:
  3.0 8.8 %collective-permute-start.2 = (bf16[8,4096]{1,0:T(8,128)(2,1)S(1)}, bf16[8,4096]{1,0:T(8,128)(2,1)S(1)}, u32[]{:S(2)}, u32[]{:S(2)}) collective-permute-start(bf16[8,4096]{1,0:T(8,128)(2,1)S(1)} %get-tuple-element.49.refs_0_.rounded_ref), channel_id=1, source_target_pairs={{0,3},{1,2},{2,1},{3,0},{4,7},{5,6},{6,5},{7,4},{8,11},{9,10},{10,... | collective-permute-start | bytes 196616 | tf_op jit(solution)/shard_map/ppermute | solution.py:482
  8.1 5.6 %collective-permute-start.1 = (bf16[8,4096]{1,0:T(8,128)(2,1)S(1)}, bf16[8,4096]{1,0:T(8,128)(2,1)S(1)}, u32[]{:S(2)}, u32[]{:S(2)}) collective-permute-start(bf16[8,4096]{1,0:T(8,128)(2,1)S(1)} %get-tuple-element.49.refs_0_.rounded_ref), channel_id=1, source_target_pairs={{0,2},{1,3},{2,0},{3,1},{4,6},{5,7},{6,4},{7,5},{8,10},{9,11},{10,... | collective-permute-start | bytes 196616 | tf_op jit(solution)/shard_map/ppermute | solution.py:482
  8.1 5.6 %collective-permute-start = (bf16[8,4096]{1,0:T(8,128)(2,1)S(1)}, bf16[8,4096]{1,0:T(8,128)(2,1)S(1)}, u32[]{:S(2)}, u32[]{:S(2)}) collective-permute-start(bf16[8,4096]{1,0:T(8,128)(2,1)S(1)} %get-tuple-element.49.refs_0_.rounded_ref), channel_id=1, source_target_pairs={{0,1},{1,0},{2,3},{3,2},{4,5},{5,4},{6,7},{7,6},{8,9},{9,8},{10,11... | collective-permute-start | bytes 196616 | tf_op jit(solution)/shard_map/ppermute | solution.py:482
  14.1 4.7 %collective-permute-start.3 = (bf16[8,4096]{1,0:T(8,128)(2,1)S(1)}, bf16[8,4096]{1,0:T(8,128)(2,1)S(1)}, u32[]{:S(2)}, u32[]{:S(2)}) collective-permute-start(bf16[8,4096]{1,0:T(8,128)(2,1)S(1)} %get-tuple-element.51), channel_id=1, source_target_pairs={{0,4},{4,0},{8,12},{12,8},{16,20},{20,16},{24,28},{28,24},{1,5},{5... | collective-permute-start | bytes 196616 | tf_op jit(solution)/shard_map/ppermute | solution.py:490
  14.2 4.6 %collective-permute-start.4 = (bf16[8,4096]{1,0:T(8,128)(2,1)S(1)}, bf16[8,4096]{1,0:T(8,128)(2,1)S(1)}, u32[]{:S(2)}, u32[]{:S(2)}) collective-permute-start(bf16[8,4096]{1,0:T(8,128)(2,1)S(1)} %get-tuple-element.52), channel_id=1, source_target_pairs={{4,8},{8,4},{12,16},{16,12},{20,24},{24,20},{5,9},{9,5},{13,17},{1... | collective-permute-start | bytes 196616 | tf_op jit(solution)/shard_map/ppermute | solution.py:490
  19.5 9.8 %collective-permute-start.5 = (bf16[8,4096]{1,0:T(8,128)(2,1)S(1)}, bf16[8,4096]{1,0:T(8,128)(2,1)S(1)}, u32[]{:S(2)}, u32[]{:S(2)}) collective-permute-start(bf16[8,4096]{1,0:T(8,128)(2,1)S(1)} %get-tuple-element.57), channel_id=1, source_target_pairs={{0,3},{1,2},{2,1},{3,0},{4,7},{5,6},{6,5},{7,4},{8,11},{9,10},{10,... | collective-permute-start | bytes 196616 | tf_op jit(solution)/shard_map/ppermute | solution.py:482
  23.6 5.7 %collective-permute-start.6 = (bf16[8,4096]{1,0:T(8,128)(2,1)S(1)}, bf16[8,4096]{1,0:T(8,128)(2,1)S(1)}, u32[]{:S(2)}, u32[]{:S(2)}) collective-permute-start(bf16[8,4096]{1,0:T(8,128)(2,1)S(1)} %get-tuple-element.58), channel_id=1, source_target_pairs={{0,2},{1,3},{2,0},{3,1},{4,6},{5,7},{6,4},{7,5},{8,10},{9,11},{10,... | collective-permute-start | bytes 196616 | tf_op jit(solution)/shard_map/ppermute | solution.py:482
  23.6 5.7 %collective-permute-start.7 = (bf16[8,4096]{1,0:T(8,128)(2,1)S(1)}, bf16[8,4096]{1,0:T(8,128)(2,1)S(1)}, u32[]{:S(2)}, u32[]{:S(2)}) collective-permute-start(bf16[8,4096]{1,0:T(8,128)(2,1)S(1)} %get-tuple-element.59), channel_id=1, source_target_pairs={{0,1},{1,0},{2,3},{3,2},{4,5},{5,4},{6,7},{7,6},{8,9},{9,8},{10,11... | collective-permute-start | bytes 196616 | tf_op jit(solution)/shard_map/ppermute | solution.py:482
  29.4 6.3 %collective-permute-start.10 = (bf16[8,4224]{1,0:T(8,128)(2,1)S(1)}, bf16[8,4224]{1,0:T(8,128)(2,1)S(1)}, u32[]{:S(2)}, u32[]{:S(2)}) collective-permute-start(bf16[8,4224]{1,0:T(8,128)(2,1)S(1)} %get-tuple-element.62.refs_3_.refs_0_), channel_id=1, source_target_pairs={{0,3},{1,2},{2,1},{3,0},{4,7},{5,6},{6,5},{7,4},{8,11},{9,10},{10,... | collective-permute-start | bytes 202760 | tf_op jit(solution)/shard_map/ppermute | solution.py:482
  33.2 7.1 %collective-permute-start.9 = (bf16[8,4224]{1,0:T(8,128)(2,1)S(1)}, bf16[8,4224]{1,0:T(8,128)(2,1)S(1)}, u32[]{:S(2)}, u32[]{:S(2)}) collective-permute-start(bf16[8,4224]{1,0:T(8,128)(2,1)S(1)} %get-tuple-element.62.refs_3_.refs_0_), channel_id=1, source_target_pairs={{0,2},{1,3},{2,0},{3,1},{4,6},{5,7},{6,4},{7,5},{8,10},{9,11},{10,... | collective-permute-start | bytes 202760 | tf_op jit(solution)/shard_map/ppermute | solution.py:482
  33.2 7.1 %collective-permute-start.8 = (bf16[8,4224]{1,0:T(8,128)(2,1)S(1)}, bf16[8,4224]{1,0:T(8,128)(2,1)S(1)}, u32[]{:S(2)}, u32[]{:S(2)}) collective-permute-start(bf16[8,4224]{1,0:T(8,128)(2,1)S(1)} %get-tuple-element.62.refs_3_.refs_0_), channel_id=1, source_target_pairs={{0,1},{1,0},{2,3},{3,2},{4,5},{5,4},{6,7},{7,6},{8,9},{9,8},{10,11... | collective-permute-start | bytes 202760 | tf_op jit(solution)/shard_map/ppermute | solution.py:482
  44.5 6.1 %collective-permute-start.13 = (bf16[8,4096]{1,0:T(8,128)(2,1)S(1)}, bf16[8,4096]{1,0:T(8,128)(2,1)S(1)}, u32[]{:S(2)}, u32[]{:S(2)}) collective-permute-start(bf16[8,4096]{1,0:T(8,128)(2,1)S(1)} %get-tuple-element.70), channel_id=1, source_target_pairs={{0,3},{1,2},{2,1},{3,0},{4,7},{5,6},{6,5},{7,4},{8,11},{9,10},{10,... | collective-permute-start | bytes 196616 | tf_op jit(solution)/shard_map/ppermute | solution.py:482
  47.1 5.9 %collective-permute-start.14 = (bf16[8,4096]{1,0:T(8,128)(2,1)S(1)}, bf16[8,4096]{1,0:T(8,128)(2,1)S(1)}, u32[]{:S(2)}, u32[]{:S(2)}) collective-permute-start(bf16[8,4096]{1,0:T(8,128)(2,1)S(1)} %get-tuple-element.71), channel_id=1, source_target_pairs={{0,2},{1,3},{2,0},{3,1},{4,6},{5,7},{6,4},{7,5},{8,10},{9,11},{10,... | collective-permute-start | bytes 196616 | tf_op jit(solution)/shard_map/ppermute | solution.py:482
  47.1 5.9 %collective-permute-start.15 = (bf16[8,4096]{1,0:T(8,128)(2,1)S(1)}, bf16[8,4096]{1,0:T(8,128)(2,1)S(1)}, u32[]{:S(2)}, u32[]{:S(2)}) collective-permute-start(bf16[8,4096]{1,0:T(8,128)(2,1)S(1)} %get-tuple-element.72), channel_id=1, source_target_pairs={{0,1},{1,0},{2,3},{3,2},{4,5},{5,4},{6,7},{7,6},{8,9},{9,8},{10,11... | collective-permute-start | bytes 196616 | tf_op jit(solution)/shard_map/ppermute | solution.py:482
  53.2 6.3 %collective-permute-start.18 = (bf16[8,4096]{1,0:T(8,128)(2,1)S(1)}, bf16[8,4096]{1,0:T(8,128)(2,1)S(1)}, u32[]{:S(2)}, u32[]{:S(2)}) collective-permute-start(bf16[8,4096]{1,0:T(8,128)(2,1)S(1)} %get-tuple-element.74.refs_3_.refs_1_), channel_id=1, source_target_pairs={{0,3},{1,2},{2,1},{3,0},{4,7},{5,6},{6,5},{7,4},{8,11},{9,10},{10,... | collective-permute-start | bytes 196616 | tf_op jit(solution)/shard_map/ppermute | solution.py:482
  56.7 6.2 %collective-permute-start.17 = (bf16[8,4096]{1,0:T(8,128)(2,1)S(1)}, bf16[8,4096]{1,0:T(8,128)(2,1)S(1)}, u32[]{:S(2)}, u32[]{:S(2)}) collective-permute-start(bf16[8,4096]{1,0:T(8,128)(2,1)S(1)} %get-tuple-element.74.refs_3_.refs_1_), channel_id=1, source_target_pairs={{0,2},{1,3},{2,0},{3,1},{4,6},{5,7},{6,4},{7,5},{8,10},{9,11},{10,... | collective-permute-start | bytes 196616 | tf_op jit(solution)/shard_map/ppermute | solution.py:482
  56.7 6.2 %collective-permute-start.16 = (bf16[8,4096]{1,0:T(8,128)(2,1)S(1)}, bf16[8,4096]{1,0:T(8,128)(2,1)S(1)}, u32[]{:S(2)}, u32[]{:S(2)}) collective-permute-start(bf16[8,4096]{1,0:T(8,128)(2,1)S(1)} %get-tuple-element.74.refs_3_.refs_1_), channel_id=1, source_target_pairs={{0,1},{1,0},{2,3},{3,2},{4,5},{5,4},{6,7},{7,6},{8,9},{9,8},{10,11... | collective-permute-start | bytes 196616 | tf_op jit(solution)/shard_map/ppermute | solution.py:482
  70.5 5.2 %collective-permute-start.22 = (f32[8,128]{1,0:T(8,128)S(1)}, f32[8,128]{1,0:T(8,128)S(1)}, u32[]{:S(2)}, u32[]{:S(2)}) collective-permute-start(f32[8,128]{1,0:T(8,128)S(1)} %add_moments.5.first_ref), channel_id=1, source_target_pairs={{0,2},{1,3},{2,0},{3,1},{4,6},{5,7},{6,4},{7,5},{8,10},{9,11},{10,... | collective-permute-start | bytes 12296 | tf_op jit(solution)/shard_map/ppermute | solution.py:482
  72.2 21.4 %collective-permute-start.26 = (f32[8,4096]{1,0:T(8,128)S(1)}, f32[8,4096]{1,0:T(8,128)S(1)}, u32[]{:S(2)}, u32[]{:S(2)}) collective-permute-start(f32[8,4096]{1,0:T(8,128)S(1)} %get-tuple-element.86), channel_id=1, source_target_pairs={{0,3},{1,2},{2,1},{3,0},{4,7},{5,6},{6,5},{7,4},{8,11},{9,10},{10,... | collective-permute-start | bytes 393224 | tf_op jit(solution)/shard_map/ppermute | solution.py:482
  73.8 19.9 %collective-permute-start.27 = (f32[8,4096]{1,0:T(8,128)S(1)}, f32[8,4096]{1,0:T(8,128)S(1)}, u32[]{:S(2)}, u32[]{:S(2)}) collective-permute-start(f32[8,4096]{1,0:T(8,128)S(1)} %get-tuple-element.90), channel_id=1, source_target_pairs={{0,2},{1,3},{2,0},{3,1},{4,6},{5,7},{6,4},{7,5},{8,10},{9,11},{10,... | collective-permute-start | bytes 393224 | tf_op jit(solution)/shard_map/ppermute | solution.py:482
  75.8 17.8 %collective-permute-start.28 = (f32[8,4096]{1,0:T(8,128)S(1)}, f32[8,4096]{1,0:T(8,128)S(1)}, u32[]{:S(2)}, u32[]{:S(2)}) collective-permute-start(f32[8,4096]{1,0:T(8,128)S(1)} %get-tuple-element.93), channel_id=1, source_target_pairs={{0,1},{1,0},{2,3},{3,2},{4,5},{5,4},{6,7},{7,6},{8,9},{9,8},{10,11... | collective-permute-start | bytes 393224 | tf_op jit(solution)/shard_map/ppermute | solution.py:482
  76.8 4.8 %collective-permute-start.23 = (f32[8,128]{1,0:T(8,128)S(1)}, f32[8,128]{1,0:T(8,128)S(1)}, u32[]{:S(2)}, u32[]{:S(2)}) collective-permute-start(f32[8,128]{1,0:T(8,128)S(1)} %add_moments.6.first_ref), channel_id=1, source_target_pairs={{0,4},{4,0},{8,12},{12,8},{16,20},{20,16},{24,28},{28,24},{1,5},{5... | collective-permute-start | bytes 12296 | tf_op jit(solution)/shard_map/ppermute | solution.py:482
  81.7 4.2 %collective-permute-start.24 = (f32[8,128]{1,0:T(8,128)S(1)}, f32[8,128]{1,0:T(8,128)S(1)}, u32[]{:S(2)}, u32[]{:S(2)}) collective-permute-start(f32[8,128]{1,0:T(8,128)S(1)} %add_moments.7.first_ref), channel_id=1, source_target_pairs={{0,8},{4,12},{8,0},{12,4},{16,24},{20,28},{24,16},{28,20},{1,9},{5... | collective-permute-start | bytes 12296 | tf_op jit(solution)/shard_map/ppermute | solution.py:482
  86.0 7.6 %collective-permute-start.25 = (f32[8,128]{1,0:T(8,128)S(1)}, f32[8,128]{1,0:T(8,128)S(1)}, u32[]{:S(2)}, u32[]{:S(2)}) collective-permute-start(f32[8,128]{1,0:T(8,128)S(1)} %add_moments.8.first_ref), channel_id=1, source_target_pairs={{0,16},{4,20},{8,24},{12,28},{16,0},{20,4},{24,8},{28,12},{1,17},{... | collective-permute-start | bytes 12296 | tf_op jit(solution)/shard_map/ppermute | solution.py:482
  (9 other events, 40.9 us)

commit v14 on v12

--- a/solution.py
+++ b/solution.py
@@ -638,7 +638,7 @@
         basis.append(field)
     moments = curved
     arrived = []
-    for axis, count in (("sub", sub_count), ("tile", tile_count)):
+    for axis, count in (("tile", tile_count), ("sub", sub_count)):
         step = 1
         while step < count:
             moments = call(add_moments_kernel, scalars, (moments, exchange(moments, axis, step)), "add_moments")

time: 93.2 us -> 95.1 us (1.020)
  waiting for transfers between devices: 17.5 us -> 23.6 us
  starting transfers between devices: 52.8 us -> 49.2 us
    ppermute x23, waiting for transfers between devices: 17.5 us -> 23.5 us  [exchange(): return lax.ppermute(block, axis, [(i, i ^ step) for i in range(count)])]
    ppermute x23, starting transfers between devices: 43.7 us -> 41.2 us  [exchange(): return lax.ppermute(block, axis, [(i, i ^ step) for i in range(count)])]
    ppermute x6, starting transfers between devices: 9.02 us -> 8 us  [swap(): return lax.ppermute(block, axis, route)]
  transfers between devices with their start and end apart: 29 -> 29, of which waited for: 13 -> 11; matrix products, arithmetic and copies ran while one was open for 0% -> 0% of each run, Pallas kernels for 16% -> 16%
where the time goes in v14:
time: 95.1 us; the launch traced here: 94.4 us
  starting transfers between devices  49.2 us (52%)
  waiting for transfers between devices  23.6 us (25%)
  Pallas kernels  20.7 us (22%)
    ppermute x23, starting transfers between devices, exchange(): return lax.ppermute(block, axis, [(i, i ^ step) for i in range(count)])  41.2 us
    ppermute x23, waiting for transfers between devices, exchange(): return lax.ppermute(block, axis, [(i, i ^ step) for i in range(count)])  23.5 us
    pallas_call x25, Pallas kernels, call(): pl.pallas_call(kernel, out_shape=outs, compiler_params=PARAMS, name=name,...  20.7 us
    ppermute x6, starting transfers between devices, swap(): return lax.ppermute(block, axis, route)  8 us
  transfers between devices with their start and end apart: 29, of which 11 were waited for; matrix products, arithmetic and copies ran while one was open for 0% of the time, Pallas kernels for 16%

profile of v14, /device:TPU:0, one launch (start us, length us, event | category | flops | bytes accessed | tf_op | source)
XLA Modules:
  0.0 94.4 jit_solution(5589906235938192033)
XLA Ops:
  0.7 2.3 %curve_order.1 = (f32[8,4096]{1,0:T(8,128)S(1)}, bf16[8,4096]{1,0:T(8,128)(2,1)S(1)}) custom-call(f32[8,4096]{1,0:T(8,128)} %right_in.1, s32[1,4096]{1,0:T(1,128)} %order_in.1), custom_call_target="tpu_custom_call" | custom-call | flops 10000000000 | tf_op jit(solution)/shard_map/curve_order/pallas_call | solution.py:498
  3.0 5.1 %collective-permute-start.2 = (bf16[8,4096]{1,0:T(8,128)(2,1)S(1)}, bf16[8,4096]{1,0:T(8,128)(2,1)S(1)}, u32[]{:S(2)}, u32[]{:S(2)}) collective-permute-start(bf16[8,4096]{1,0:T(8,128)(2,1)S(1)} %get-tuple-element.49.refs_0_.rounded_ref), channel_id=1, source_target_pairs={{0,3},{1,2},{2,1},{3,0},{4,7},{5,6},{6,5},{7,4},{8,11},{9,10},{10,... | collective-permute-start | bytes 196616 | tf_op jit(solution)/shard_map/ppermute | solution.py:482
  8.7 1.5 %lists.1.lists_ref = s32[1,1280]{1,0:T(1,128)S(4)} custom-call(s32[2,96]{1,0:T(2,128)S(1)} %bitcast.5), custom_call_target="tpu_custom_call" | custom-call | flops 1000000000 | tf_op jit(solution)/shard_map/lists/pallas_call | solution.py:498
  11.4 2.3 %collective-permute-done.1.refs_2_ = bf16[8,4096]{1,0:T(8,128)(2,1)S(1)} collective-permute-done((bf16[8,4096]{1,0:T(8,128)(2,1)S(1)}, bf16[8,4096]{1,0:T(8,128)(2,1)S(1)}, u32[]{:S(2)}, u32[]{:S(2)}) %collective-permute-start.1) | collective-permute-done | bytes 65568 | tf_op jit(solution)/shard_map/ppermute | solution.py:482
  15.0 2.2 %late.3.begun_ref = f32[81,8,256]{2,1,0:T(8,128)S(1)} custom-call(s32[1,1280]{1,0:T(1,128)S(4)} %lists.1.lists_ref, bf16[96,256,256]{2,1,0:T(8,128)(2,1)S(1)} %copy-done, f32[81,8,256]{2,1,0:T(8,128)S(1)} %early.3.begun_ref, f32[64,8,256]{2,1,0:T(8,128)S(1)} %get-tuple-element.50.field_ref), custom_call_target="tpu_custom_call" | custom-call | flops 3000000000 | tf_op jit(solution)/shard_map/late/pallas_call | solution.py:498
  17.7 3.2 %collective-permute-start.5 = (bf16[8,4096]{1,0:T(8,128)(2,1)S(1)}, bf16[8,4096]{1,0:T(8,128)(2,1)S(1)}, u32[]{:S(2)}, u32[]{:S(2)}) collective-permute-start(bf16[8,4096]{1,0:T(8,128)(2,1)S(1)} %get-tuple-element.57), channel_id=1, source_target_pairs={{0,3},{1,2},{2,1},{3,0},{4,7},{5,6},{6,5},{7,4},{8,11},{9,10},{10,... | collective-permute-start | bytes 196616 | tf_op jit(solution)/shard_map/ppermute | solution.py:482
  20.8 2.1 %collective-permute-start.6 = (bf16[8,4096]{1,0:T(8,128)(2,1)S(1)}, bf16[8,4096]{1,0:T(8,128)(2,1)S(1)}, u32[]{:S(2)}, u32[]{:S(2)}) collective-permute-start(bf16[8,4096]{1,0:T(8,128)(2,1)S(1)} %get-tuple-element.58), channel_id=1, source_target_pairs={{0,2},{1,3},{2,0},{3,1},{4,6},{5,7},{6,4},{7,5},{8,10},{9,11},{10,... | collective-permute-start | bytes 196616 | tf_op jit(solution)/shard_map/ppermute | solution.py:482
  22.9 3.6 %turn.1.after_ref.blocks_ref = bf16[192,256,256]{2,1,0:T(8,128)(2,1)S(1)} custom-call(bf16[96,256,256]{2,1,0:T(8,128)(2,1)S(1)} %copy-done, f32[8,128]{1,0:T(8,128)S(1)} %get-tuple-element.53.after_ref.moments_in_ref), custom_call_target="tpu_custom_call" | custom-call | flops 4000000000 | tf_op jit(solution)/shard_map/turn/pallas_call | solution.py:498
  28.1 2.3 %collective-permute-start.10 = (bf16[8,4224]{1,0:T(8,128)(2,1)S(1)}, bf16[8,4224]{1,0:T(8,128)(2,1)S(1)}, u32[]{:S(2)}, u32[]{:S(2)}) collective-permute-start(bf16[8,4224]{1,0:T(8,128)(2,1)S(1)} %get-tuple-element.62.refs_3_.refs_0_), channel_id=1, source_target_pairs={{0,3},{1,2},{2,1},{3,0},{4,7},{5,6},{6,5},{7,4},{8,11},{9,10},{10,... | collective-permute-start | bytes 202760 | tf_op jit(solution)/shard_map/ppermute | solution.py:482
  34.3 2.4 %collective-permute-done.9.refs_2_ = bf16[8,4224]{1,0:T(8,128)(2,1)S(1)} collective-permute-done((bf16[8,4224]{1,0:T(8,128)(2,1)S(1)}, bf16[8,4224]{1,0:T(8,128)(2,1)S(1)}, u32[]{:S(2)}, u32[]{:S(2)}) %collective-permute-start.9) | collective-permute-done | bytes 67616 | tf_op jit(solution)/shard_map/ppermute | solution.py:482
  37.0 2.7 %collective-permute-start.11 = (bf16[8,4224]{1,0:T(8,128)(2,1)S(1)}, bf16[8,4224]{1,0:T(8,128)(2,1)S(1)}, u32[]{:S(2)}, u32[]{:S(2)}) collective-permute-start(bf16[8,4224]{1,0:T(8,128)(2,1)S(1)} %get-tuple-element.65), channel_id=1, source_target_pairs={{0,4},{4,0},{8,12},{12,8},{16,20},{20,16},{24,28},{28,24},{1,5},{5... | collective-permute-start | bytes 202760 | tf_op jit(solution)/shard_map/ppermute | solution.py:490
  42.0 2.3 %collective-permute-start.13 = (bf16[8,4096]{1,0:T(8,128)(2,1)S(1)}, bf16[8,4096]{1,0:T(8,128)(2,1)S(1)}, u32[]{:S(2)}, u32[]{:S(2)}) collective-permute-start(bf16[8,4096]{1,0:T(8,128)(2,1)S(1)} %get-tuple-element.70), channel_id=1, source_target_pairs={{0,3},{1,2},{2,1},{3,0},{4,7},{5,6},{6,5},{7,4},{8,11},{9,10},{10,... | collective-permute-start | bytes 196616 | tf_op jit(solution)/shard_map/ppermute | solution.py:482
  44.3 2.1 %collective-permute-start.14 = (bf16[8,4096]{1,0:T(8,128)(2,1)S(1)}, bf16[8,4096]{1,0:T(8,128)(2,1)S(1)}, u32[]{:S(2)}, u32[]{:S(2)}) collective-permute-start(bf16[8,4096]{1,0:T(8,128)(2,1)S(1)} %get-tuple-element.71), channel_id=1, source_target_pairs={{0,2},{1,3},{2,0},{3,1},{4,6},{5,7},{6,4},{7,5},{8,10},{9,11},{10,... | collective-permute-start | bytes 196616 | tf_op jit(solution)/shard_map/ppermute | solution.py:482
  46.4 1.7 %collective-permute-done.13.refs_0_ = bf16[8,4096]{1,0:T(8,128)(2,1)S(1)} collective-permute-done((bf16[8,4096]{1,0:T(8,128)(2,1)S(1)}, bf16[8,4096]{1,0:T(8,128)(2,1)S(1)}, u32[]{:S(2)}, u32[]{:S(2)}) %collective-permute-start.13) | collective-permute-done | bytes 65568 | tf_op jit(solution)/shard_map/ppermute | solution.py:482
  48.1 2.1 %collective-permute-done.14.refs_1_ = bf16[8,4096]{1,0:T(8,128)(2,1)S(1)} collective-permute-done((bf16[8,4096]{1,0:T(8,128)(2,1)S(1)}, bf16[8,4096]{1,0:T(8,128)(2,1)S(1)}, u32[]{:S(2)}, u32[]{:S(2)}) %collective-permute-start.14) | collective-permute-done | bytes 65568 | tf_op jit(solution)/shard_map/ppermute | solution.py:482
  52.9 2.6 %collective-permute-start.16 = (bf16[8,4096]{1,0:T(8,128)(2,1)S(1)}, bf16[8,4096]{1,0:T(8,128)(2,1)S(1)}, u32[]{:S(2)}, u32[]{:S(2)}) collective-permute-start(bf16[8,4096]{1,0:T(8,128)(2,1)S(1)} %get-tuple-element.74.refs_3_.refs_1_), channel_id=1, source_target_pairs={{0,1},{1,0},{2,3},{3,2},{4,5},{5,4},{6,7},{7,6},{8,9},{9,8},{10,11... | collective-permute-start | bytes 196616 | tf_op jit(solution)/shard_map/ppermute | solution.py:482
  58.9 3.1 %collective-permute-start.19 = (bf16[8,4096]{1,0:T(8,128)(2,1)S(1)}, bf16[8,4096]{1,0:T(8,128)(2,1)S(1)}, u32[]{:S(2)}, u32[]{:S(2)}) collective-permute-start(bf16[8,4096]{1,0:T(8,128)(2,1)S(1)} %get-tuple-element.76), channel_id=1, source_target_pairs={{0,4},{4,0},{8,12},{12,8},{16,20},{20,16},{24,28},{28,24},{1,5},{5... | collective-permute-start | bytes 196616 | tf_op jit(solution)/shard_map/ppermute | solution.py:490
  64.1 9.3 %collective-permute-start.21 = (f32[8,128]{1,0:T(8,128)S(1)}, f32[8,128]{1,0:T(8,128)S(1)}, u32[]{:S(2)}, u32[]{:S(2)}) collective-permute-start(f32[8,128]{1,0:T(8,128)S(1)} %curvature.1.first_ref), channel_id=1, source_target_pairs={{0,4},{4,0},{8,12},{12,8},{16,20},{20,16},{24,28},{28,24},{1,5},{5... | collective-permute-start | bytes 12296 | tf_op jit(solution)/shard_map/ppermute | solution.py:482
  74.3 2.0 %collective-permute-start.22 = (f32[8,128]{1,0:T(8,128)S(1)}, f32[8,128]{1,0:T(8,128)S(1)}, u32[]{:S(2)}, u32[]{:S(2)}) collective-permute-start(f32[8,128]{1,0:T(8,128)S(1)} %add_moments.5.first_ref), channel_id=1, source_target_pairs={{0,8},{4,12},{8,0},{12,4},{16,24},{20,28},{24,16},{28,20},{1,9},{5... | collective-permute-start | bytes 12296 | tf_op jit(solution)/shard_map/ppermute | solution.py:482
  76.3 2.1 %collective-permute-start.26 = (f32[8,4096]{1,0:T(8,128)S(1)}, f32[8,4096]{1,0:T(8,128)S(1)}, u32[]{:S(2)}, u32[]{:S(2)}) collective-permute-start(f32[8,4096]{1,0:T(8,128)S(1)} %get-tuple-element.86), channel_id=1, source_target_pairs={{0,3},{1,2},{2,1},{3,0},{4,7},{5,6},{6,5},{7,4},{8,11},{9,10},{10,... | collective-permute-start | bytes 393224 | tf_op jit(solution)/shard_map/ppermute | solution.py:482
  78.5 2.3 %collective-permute-start.28 = (f32[8,4096]{1,0:T(8,128)S(1)}, f32[8,4096]{1,0:T(8,128)S(1)}, u32[]{:S(2)}, u32[]{:S(2)}) collective-permute-start(f32[8,4096]{1,0:T(8,128)S(1)} %get-tuple-element.93), channel_id=1, source_target_pairs={{0,1},{1,0},{2,3},{3,2},{4,5},{5,4},{6,7},{7,6},{8,9},{9,8},{10,11... | collective-permute-start | bytes 393224 | tf_op jit(solution)/shard_map/ppermute | solution.py:482
  80.9 3.6 %collective-permute-done.23.second_ref = f32[8,128]{1,0:T(8,128)S(1)} collective-permute-done((f32[8,128]{1,0:T(8,128)S(1)}, f32[8,128]{1,0:T(8,128)S(1)}, u32[]{:S(2)}, u32[]{:S(2)}) %collective-permute-start.23) | collective-permute-done | bytes 4128 | tf_op jit(solution)/shard_map/ppermute | solution.py:482
  84.7 3.9 %collective-permute-done.24.second_ref = f32[8,128]{1,0:T(8,128)S(1)} collective-permute-done((f32[8,128]{1,0:T(8,128)S(1)}, f32[8,128]{1,0:T(8,128)S(1)}, u32[]{:S(2)}, u32[]{:S(2)}) %collective-permute-start.24) | collective-permute-done | bytes 4128 | tf_op jit(solution)/shard_map/ppermute | solution.py:482
  89.8 3.5 %collective-permute-done.25.second_ref = f32[8,128]{1,0:T(8,128)S(1)} collective-permute-done((f32[8,128]{1,0:T(8,128)S(1)}, f32[8,128]{1,0:T(8,128)S(1)}, u32[]{:S(2)}, u32[]{:S(2)}) %collective-permute-start.25) | collective-permute-done | bytes 4128 | tf_op jit(solution)/shard_map/ppermute | solution.py:482
  (68 shorter events, 23.2 us)
Async XLA Ops:
  3.0 8.4 %collective-permute-start.2 = (bf16[8,4096]{1,0:T(8,128)(2,1)S(1)}, bf16[8,4096]{1,0:T(8,128)(2,1)S(1)}, u32[]{:S(2)}, u32[]{:S(2)}) collective-permute-start(bf16[8,4096]{1,0:T(8,128)(2,1)S(1)} %get-tuple-element.49.refs_0_.rounded_ref), channel_id=1, source_target_pairs={{0,3},{1,2},{2,1},{3,0},{4,7},{5,6},{6,5},{7,4},{8,11},{9,10},{10,... | collective-permute-start | bytes 196616 | tf_op jit(solution)/shard_map/ppermute | solution.py:482
  8.1 5.6 %collective-permute-start.1 = (bf16[8,4096]{1,0:T(8,128)(2,1)S(1)}, bf16[8,4096]{1,0:T(8,128)(2,1)S(1)}, u32[]{:S(2)}, u32[]{:S(2)}) collective-permute-start(bf16[8,4096]{1,0:T(8,128)(2,1)S(1)} %get-tuple-element.49.refs_0_.rounded_ref), channel_id=1, source_target_pairs={{0,2},{1,3},{2,0},{3,1},{4,6},{5,7},{6,4},{7,5},{8,10},{9,11},{10,... | collective-permute-start | bytes 196616 | tf_op jit(solution)/shard_map/ppermute | solution.py:482
  8.1 5.6 %collective-permute-start = (bf16[8,4096]{1,0:T(8,128)(2,1)S(1)}, bf16[8,4096]{1,0:T(8,128)(2,1)S(1)}, u32[]{:S(2)}, u32[]{:S(2)}) collective-permute-start(bf16[8,4096]{1,0:T(8,128)(2,1)S(1)} %get-tuple-element.49.refs_0_.rounded_ref), channel_id=1, source_target_pairs={{0,1},{1,0},{2,3},{3,2},{4,5},{5,4},{6,7},{7,6},{8,9},{9,8},{10,11... | collective-permute-start | bytes 196616 | tf_op jit(solution)/shard_map/ppermute | solution.py:482
  17.7 10.3 %collective-permute-start.5 = (bf16[8,4096]{1,0:T(8,128)(2,1)S(1)}, bf16[8,4096]{1,0:T(8,128)(2,1)S(1)}, u32[]{:S(2)}, u32[]{:S(2)}) collective-permute-start(bf16[8,4096]{1,0:T(8,128)(2,1)S(1)} %get-tuple-element.57), channel_id=1, source_target_pairs={{0,3},{1,2},{2,1},{3,0},{4,7},{5,6},{6,5},{7,4},{8,11},{9,10},{10,... | collective-permute-start | bytes 196616 | tf_op jit(solution)/shard_map/ppermute | solution.py:482
  20.8 7.1 %collective-permute-start.6 = (bf16[8,4096]{1,0:T(8,128)(2,1)S(1)}, bf16[8,4096]{1,0:T(8,128)(2,1)S(1)}, u32[]{:S(2)}, u32[]{:S(2)}) collective-permute-start(bf16[8,4096]{1,0:T(8,128)(2,1)S(1)} %get-tuple-element.58), channel_id=1, source_target_pairs={{0,2},{1,3},{2,0},{3,1},{4,6},{5,7},{6,4},{7,5},{8,10},{9,11},{10,... | collective-permute-start | bytes 196616 | tf_op jit(solution)/shard_map/ppermute | solution.py:482
  22.9 5.1 %collective-permute-start.7 = (bf16[8,4096]{1,0:T(8,128)(2,1)S(1)}, bf16[8,4096]{1,0:T(8,128)(2,1)S(1)}, u32[]{:S(2)}, u32[]{:S(2)}) collective-permute-start(bf16[8,4096]{1,0:T(8,128)(2,1)S(1)} %get-tuple-element.59), channel_id=1, source_target_pairs={{0,1},{1,0},{2,3},{3,2},{4,5},{5,4},{6,7},{7,6},{8,9},{9,8},{10,11... | collective-permute-start | bytes 196616 | tf_op jit(solution)/shard_map/ppermute | solution.py:482
  28.1 6.2 %collective-permute-start.10 = (bf16[8,4224]{1,0:T(8,128)(2,1)S(1)}, bf16[8,4224]{1,0:T(8,128)(2,1)S(1)}, u32[]{:S(2)}, u32[]{:S(2)}) collective-permute-start(bf16[8,4224]{1,0:T(8,128)(2,1)S(1)} %get-tuple-element.62.refs_3_.refs_0_), channel_id=1, source_target_pairs={{0,3},{1,2},{2,1},{3,0},{4,7},{5,6},{6,5},{7,4},{8,11},{9,10},{10,... | collective-permute-start | bytes 202760 | tf_op jit(solution)/shard_map/ppermute | solution.py:482
  30.4 6.2 %collective-permute-start.9 = (bf16[8,4224]{1,0:T(8,128)(2,1)S(1)}, bf16[8,4224]{1,0:T(8,128)(2,1)S(1)}, u32[]{:S(2)}, u32[]{:S(2)}) collective-permute-start(bf16[8,4224]{1,0:T(8,128)(2,1)S(1)} %get-tuple-element.62.refs_3_.refs_0_), channel_id=1, source_target_pairs={{0,2},{1,3},{2,0},{3,1},{4,6},{5,7},{6,4},{7,5},{8,10},{9,11},{10,... | collective-permute-start | bytes 202760 | tf_op jit(solution)/shard_map/ppermute | solution.py:482
  31.6 5.1 %collective-permute-start.8 = (bf16[8,4224]{1,0:T(8,128)(2,1)S(1)}, bf16[8,4224]{1,0:T(8,128)(2,1)S(1)}, u32[]{:S(2)}, u32[]{:S(2)}) collective-permute-start(bf16[8,4224]{1,0:T(8,128)(2,1)S(1)} %get-tuple-element.62.refs_3_.refs_0_), channel_id=1, source_target_pairs={{0,1},{1,0},{2,3},{3,2},{4,5},{5,4},{6,7},{7,6},{8,9},{9,8},{10,11... | collective-permute-start | bytes 202760 | tf_op jit(solution)/shard_map/ppermute | solution.py:482
  37.0 4.6 %collective-permute-start.11 = (bf16[8,4224]{1,0:T(8,128)(2,1)S(1)}, bf16[8,4224]{1,0:T(8,128)(2,1)S(1)}, u32[]{:S(2)}, u32[]{:S(2)}) collective-permute-start(bf16[8,4224]{1,0:T(8,128)(2,1)S(1)} %get-tuple-element.65), channel_id=1, source_target_pairs={{0,4},{4,0},{8,12},{12,8},{16,20},{20,16},{24,28},{28,24},{1,5},{5... | collective-permute-start | bytes 202760 | tf_op jit(solution)/shard_map/ppermute | solution.py:490
  42.0 6.2 %collective-permute-start.13 = (bf16[8,4096]{1,0:T(8,128)(2,1)S(1)}, bf16[8,4096]{1,0:T(8,128)(2,1)S(1)}, u32[]{:S(2)}, u32[]{:S(2)}) collective-permute-start(bf16[8,4096]{1,0:T(8,128)(2,1)S(1)} %get-tuple-element.70), channel_id=1, source_target_pairs={{0,3},{1,2},{2,1},{3,0},{4,7},{5,6},{6,5},{7,4},{8,11},{9,10},{10,... | collective-permute-start | bytes 196616 | tf_op jit(solution)/shard_map/ppermute | solution.py:482
  44.3 6.0 %collective-permute-start.14 = (bf16[8,4096]{1,0:T(8,128)(2,1)S(1)}, bf16[8,4096]{1,0:T(8,128)(2,1)S(1)}, u32[]{:S(2)}, u32[]{:S(2)}) collective-permute-start(bf16[8,4096]{1,0:T(8,128)(2,1)S(1)} %get-tuple-element.71), channel_id=1, source_target_pairs={{0,2},{1,3},{2,0},{3,1},{4,6},{5,7},{6,4},{7,5},{8,10},{9,11},{10,... | collective-permute-start | bytes 196616 | tf_op jit(solution)/shard_map/ppermute | solution.py:482
  46.3 4.6 %collective-permute-start.15 = (bf16[8,4096]{1,0:T(8,128)(2,1)S(1)}, bf16[8,4096]{1,0:T(8,128)(2,1)S(1)}, u32[]{:S(2)}, u32[]{:S(2)}) collective-permute-start(bf16[8,4096]{1,0:T(8,128)(2,1)S(1)} %get-tuple-element.72), channel_id=1, source_target_pairs={{0,1},{1,0},{2,3},{3,2},{4,5},{5,4},{6,7},{7,6},{8,9},{9,8},{10,11... | collective-permute-start | bytes 196616 | tf_op jit(solution)/shard_map/ppermute | solution.py:482
  51.1 6.2 %collective-permute-start.18 = (bf16[8,4096]{1,0:T(8,128)(2,1)S(1)}, bf16[8,4096]{1,0:T(8,128)(2,1)S(1)}, u32[]{:S(2)}, u32[]{:S(2)}) collective-permute-start(bf16[8,4096]{1,0:T(8,128)(2,1)S(1)} %get-tuple-element.74.refs_3_.refs_1_), channel_id=1, source_target_pairs={{0,3},{1,2},{2,1},{3,0},{4,7},{5,6},{6,5},{7,4},{8,11},{9,10},{10,... | collective-permute-start | bytes 196616 | tf_op jit(solution)/shard_map/ppermute | solution.py:482
  51.9 6.6 %collective-permute-start.17 = (bf16[8,4096]{1,0:T(8,128)(2,1)S(1)}, bf16[8,4096]{1,0:T(8,128)(2,1)S(1)}, u32[]{:S(2)}, u32[]{:S(2)}) collective-permute-start(bf16[8,4096]{1,0:T(8,128)(2,1)S(1)} %get-tuple-element.74.refs_3_.refs_1_), channel_id=1, source_target_pairs={{0,2},{1,3},{2,0},{3,1},{4,6},{5,7},{6,4},{7,5},{8,10},{9,11},{10,... | collective-permute-start | bytes 196616 | tf_op jit(solution)/shard_map/ppermute | solution.py:482
  52.9 5.6 %collective-permute-start.16 = (bf16[8,4096]{1,0:T(8,128)(2,1)S(1)}, bf16[8,4096]{1,0:T(8,128)(2,1)S(1)}, u32[]{:S(2)}, u32[]{:S(2)}) collective-permute-start(bf16[8,4096]{1,0:T(8,128)(2,1)S(1)} %get-tuple-element.74.refs_3_.refs_1_), channel_id=1, source_target_pairs={{0,1},{1,0},{2,3},{3,2},{4,5},{5,4},{6,7},{7,6},{8,9},{9,8},{10,11... | collective-permute-start | bytes 196616 | tf_op jit(solution)/shard_map/ppermute | solution.py:482
  58.9 5.0 %collective-permute-start.19 = (bf16[8,4096]{1,0:T(8,128)(2,1)S(1)}, bf16[8,4096]{1,0:T(8,128)(2,1)S(1)}, u32[]{:S(2)}, u32[]{:S(2)}) collective-permute-start(bf16[8,4096]{1,0:T(8,128)(2,1)S(1)} %get-tuple-element.76), channel_id=1, source_target_pairs={{0,4},{4,0},{8,12},{12,8},{16,20},{20,16},{24,28},{28,24},{1,5},{5... | collective-permute-start | bytes 196616 | tf_op jit(solution)/shard_map/ppermute | solution.py:490
  64.1 10.1 %collective-permute-start.21 = (f32[8,128]{1,0:T(8,128)S(1)}, f32[8,128]{1,0:T(8,128)S(1)}, u32[]{:S(2)}, u32[]{:S(2)}) collective-permute-start(f32[8,128]{1,0:T(8,128)S(1)} %curvature.1.first_ref), channel_id=1, source_target_pairs={{0,4},{4,0},{8,12},{12,8},{16,20},{20,16},{24,28},{28,24},{1,5},{5... | collective-permute-start | bytes 12296 | tf_op jit(solution)/shard_map/ppermute | solution.py:482
  74.3 4.2 %collective-permute-start.22 = (f32[8,128]{1,0:T(8,128)S(1)}, f32[8,128]{1,0:T(8,128)S(1)}, u32[]{:S(2)}, u32[]{:S(2)}) collective-permute-start(f32[8,128]{1,0:T(8,128)S(1)} %add_moments.5.first_ref), channel_id=1, source_target_pairs={{0,8},{4,12},{8,0},{12,4},{16,24},{20,28},{24,16},{28,20},{1,9},{5... | collective-permute-start | bytes 12296 | tf_op jit(solution)/shard_map/ppermute | solution.py:482
  76.3 17.1 %collective-permute-start.26 = (f32[8,4096]{1,0:T(8,128)S(1)}, f32[8,4096]{1,0:T(8,128)S(1)}, u32[]{:S(2)}, u32[]{:S(2)}) collective-permute-start(f32[8,4096]{1,0:T(8,128)S(1)} %get-tuple-element.86), channel_id=1, source_target_pairs={{0,3},{1,2},{2,1},{3,0},{4,7},{5,6},{6,5},{7,4},{8,11},{9,10},{10,... | collective-permute-start | bytes 393224 | tf_op jit(solution)/shard_map/ppermute | solution.py:482
  78.4 15.0 %collective-permute-start.27 = (f32[8,4096]{1,0:T(8,128)S(1)}, f32[8,4096]{1,0:T(8,128)S(1)}, u32[]{:S(2)}, u32[]{:S(2)}) collective-permute-start(f32[8,4096]{1,0:T(8,128)S(1)} %get-tuple-element.90), channel_id=1, source_target_pairs={{0,2},{1,3},{2,0},{3,1},{4,6},{5,7},{6,4},{7,5},{8,10},{9,11},{10,... | collective-permute-start | bytes 393224 | tf_op jit(solution)/shard_map/ppermute | solution.py:482
  78.5 14.9 %collective-permute-start.28 = (f32[8,4096]{1,0:T(8,128)S(1)}, f32[8,4096]{1,0:T(8,128)S(1)}, u32[]{:S(2)}, u32[]{:S(2)}) collective-permute-start(f32[8,4096]{1,0:T(8,128)S(1)} %get-tuple-element.93), channel_id=1, source_target_pairs={{0,1},{1,0},{2,3},{3,2},{4,5},{5,4},{6,7},{7,6},{8,9},{9,8},{10,11... | collective-permute-start | bytes 393224 | tf_op jit(solution)/shard_map/ppermute | solution.py:482
  84.6 4.1 %collective-permute-start.24 = (f32[8,128]{1,0:T(8,128)S(1)}, f32[8,128]{1,0:T(8,128)S(1)}, u32[]{:S(2)}, u32[]{:S(2)}) collective-permute-start(f32[8,128]{1,0:T(8,128)S(1)} %add_moments.7.first_ref), channel_id=1, source_target_pairs={{0,1},{1,0},{2,3},{3,2},{4,5},{5,4},{6,7},{7,6},{8,9},{9,8},{10,11... | collective-permute-start | bytes 12296 | tf_op jit(solution)/shard_map/ppermute | solution.py:482
  88.7 4.6 %collective-permute-start.25 = (f32[8,128]{1,0:T(8,128)S(1)}, f32[8,128]{1,0:T(8,128)S(1)}, u32[]{:S(2)}, u32[]{:S(2)}) collective-permute-start(f32[8,128]{1,0:T(8,128)S(1)} %add_moments.8.first_ref), channel_id=1, source_target_pairs={{0,2},{1,3},{2,0},{3,1},{4,6},{5,7},{6,4},{7,5},{8,10},{9,11},{10,... | collective-permute-start | bytes 12296 | tf_op jit(solution)/shard_map/ppermute | solution.py:482
  (9 other events, 38.4 us)

commit v15 on v12

--- a/solution.py
+++ b/solution.py
@@ -11,8 +11,8 @@
 LANES = 128
 LONG_GROUP = 16
 SHORT_GROUP = 8
-TURN_GROUP = 24
-TURN_PRODUCTS = 6
+TURN_GROUP = 32
+TURN_PRODUCTS = 10
 QUARTERS = 4
 F32 = jnp.float32
 BF16 = jnp.bfloat16

time: 93.2 us -> 93.6 us (level)
  starting transfers between devices: 52.8 us -> 42.9 us
  waiting for transfers between devices: 17.5 us -> 22.9 us
  Pallas kernels: 20.8 us -> 25.5 us
    ppermute x6, starting transfers between devices: 9.02 us -> 2.77 us  [swap(): return lax.ppermute(block, axis, route)]
    ppermute x23, waiting for transfers between devices: 17.5 us -> 22.9 us  [exchange(): return lax.ppermute(block, axis, [(i, i ^ step) for i in range(count)])]
    pallas_call x25, Pallas kernels: 20.8 us -> 25.5 us  [call(): pl.pallas_call(kernel, out_shape=outs, compiler_params=PARAMS, name=name,...]
    ppermute x23, starting transfers between devices: 43.7 us -> 40.1 us  [exchange(): return lax.ppermute(block, axis, [(i, i ^ step) for i in range(count)])]
  transfers between devices with their start and end apart: 29 -> 29, of which waited for: 13 -> 14; matrix products, arithmetic and copies ran while one was open for 0% -> 0% of each run, Pallas kernels for 16% -> 20%
where the time goes in v15:
time: 93.6 us; the launch traced here: 92.2 us
  starting transfers between devices  42.9 us (46%)
  Pallas kernels  25.5 us (27%)
  waiting for transfers between devices  22.9 us (24%)
    ppermute x23, starting transfers between devices, exchange(): return lax.ppermute(block, axis, [(i, i ^ step) for i in range(count)])  40.1 us
    pallas_call x25, Pallas kernels, call(): pl.pallas_call(kernel, out_shape=outs, compiler_params=PARAMS, name=name,...  25.5 us
    ppermute x23, waiting for transfers between devices, exchange(): return lax.ppermute(block, axis, [(i, i ^ step) for i in range(count)])  22.9 us
    ppermute x6, starting transfers between devices, swap(): return lax.ppermute(block, axis, route)  2.77 us
  transfers between devices with their start and end apart: 29, of which 14 were waited for; matrix products, arithmetic and copies ran while one was open for 0% of the time, Pallas kernels for 20%

profile of v15, /device:TPU:0, one launch (start us, length us, event | category | flops | bytes accessed | tf_op | source)
XLA Modules:
  0.0 92.2 jit_solution(6942702369276744580)
XLA Ops:
  0.7 2.3 %curve_order.1 = (f32[8,4096]{1,0:T(8,128)S(1)}, bf16[8,4096]{1,0:T(8,128)(2,1)S(1)}) custom-call(f32[8,4096]{1,0:T(8,128)} %right_in.1, s32[1,4096]{1,0:T(1,128)} %order_in.1), custom_call_target="tpu_custom_call" | custom-call | flops 10000000000 | tf_op jit(solution)/shard_map/curve_order/pallas_call | solution.py:498
  3.0 5.1 %collective-permute-start.2 = (bf16[8,4096]{1,0:T(8,128)(2,1)S(1)}, bf16[8,4096]{1,0:T(8,128)(2,1)S(1)}, u32[]{:S(2)}, u32[]{:S(2)}) collective-permute-start(bf16[8,4096]{1,0:T(8,128)(2,1)S(1)} %get-tuple-element.49.refs_0_.rounded_ref), channel_id=1, source_target_pairs={{0,3},{1,2},{2,1},{3,0},{4,7},{5,6},{6,5},{7,4},{8,11},{9,10},{10,... | collective-permute-start | bytes 196616 | tf_op jit(solution)/shard_map/ppermute | solution.py:482
  11.4 2.3 %collective-permute-done.1.refs_2_ = bf16[8,4096]{1,0:T(8,128)(2,1)S(1)} collective-permute-done((bf16[8,4096]{1,0:T(8,128)(2,1)S(1)}, bf16[8,4096]{1,0:T(8,128)(2,1)S(1)}, u32[]{:S(2)}, u32[]{:S(2)}) %collective-permute-start.1) | collective-permute-done | bytes 65568 | tf_op jit(solution)/shard_map/ppermute | solution.py:482
  15.1 3.2 %late.3.begun_ref = f32[81,8,256]{2,1,0:T(8,128)S(1)} custom-call(s32[1,1280]{1,0:T(1,128)S(4)} %lists.1.lists_ref, bf16[96,256,256]{2,1,0:T(8,128)(2,1)S(1)} %copy-done, f32[81,8,256]{2,1,0:T(8,128)S(1)} %early.3.begun_ref, f32[64,8,256]{2,1,0:T(8,128)S(1)} %get-tuple-element.50.field_ref), custom_call_target="tpu_custom_call" | custom-call | flops 3000000000 | tf_op jit(solution)/shard_map/late/pallas_call | solution.py:498
  19.2 4.1 %collective-permute-start.5 = (bf16[8,4096]{1,0:T(8,128)(2,1)S(1)}, bf16[8,4096]{1,0:T(8,128)(2,1)S(1)}, u32[]{:S(2)}, u32[]{:S(2)}) collective-permute-start(bf16[8,4096]{1,0:T(8,128)(2,1)S(1)} %get-tuple-element.57), channel_id=1, source_target_pairs={{0,3},{1,2},{2,1},{3,0},{4,7},{5,6},{6,5},{7,4},{8,11},{9,10},{10,... | collective-permute-start | bytes 196616 | tf_op jit(solution)/shard_map/ppermute | solution.py:482
  24.0 3.3 %turn.1.after_ref.blocks_ref = bf16[192,256,256]{2,1,0:T(8,128)(2,1)S(1)} custom-call(bf16[96,256,256]{2,1,0:T(8,128)(2,1)S(1)} %copy-done, f32[8,128]{1,0:T(8,128)S(1)} %get-tuple-element.53.after_ref.moments_in_ref), custom_call_target="tpu_custom_call" | custom-call | flops 4000000000 | tf_op jit(solution)/shard_map/turn/pallas_call | solution.py:498
  29.1 3.6 %collective-permute-start.10 = (bf16[8,4224]{1,0:T(8,128)(2,1)S(1)}, bf16[8,4224]{1,0:T(8,128)(2,1)S(1)}, u32[]{:S(2)}, u32[]{:S(2)}) collective-permute-start(bf16[8,4224]{1,0:T(8,128)(2,1)S(1)} %get-tuple-element.62.refs_3_.refs_0_), channel_id=1, source_target_pairs={{0,3},{1,2},{2,1},{3,0},{4,7},{5,6},{6,5},{7,4},{8,11},{9,10},{10,... | collective-permute-start | bytes 202760 | tf_op jit(solution)/shard_map/ppermute | solution.py:482
  35.2 4.6 %collective-permute-done.9.refs_2_ = bf16[8,4224]{1,0:T(8,128)(2,1)S(1)} collective-permute-done((bf16[8,4224]{1,0:T(8,128)(2,1)S(1)}, bf16[8,4224]{1,0:T(8,128)(2,1)S(1)}, u32[]{:S(2)}, u32[]{:S(2)}) %collective-permute-start.9) | collective-permute-done | bytes 67616 | tf_op jit(solution)/shard_map/ppermute | solution.py:482
  41.4 2.0 %late.4.begun_ref = f32[81,8,256]{2,1,0:T(8,128)S(1)} custom-call(s32[1,1280]{1,0:T(1,128)S(4)} %lists.1.lists_ref, bf16[192,256,256]{2,1,0:T(8,128)(2,1)S(1)} %turn.1.after_ref.blocks_ref, f32[81,8,256]{2,1,0:T(8,128)S(1)} %early.4.begun_ref, f32[64,8,256]{2,1,0:T(8,128)S(1)} %get-tuple-element.64.field_ref, f32[8,640]{1,0:T(8,128)S(1)} %get-tuple-element.63.refs_0_.ratios_ref), custom_call_target="tpu_custom_call" | custom-call | flops 3000000000 | tf_op jit(solution)/shard_map/late/pallas_call | solution.py:498
  44.1 2.6 %collective-permute-start.13 = (bf16[8,4096]{1,0:T(8,128)(2,1)S(1)}, bf16[8,4096]{1,0:T(8,128)(2,1)S(1)}, u32[]{:S(2)}, u32[]{:S(2)}) collective-permute-start(bf16[8,4096]{1,0:T(8,128)(2,1)S(1)} %get-tuple-element.70), channel_id=1, source_target_pairs={{0,3},{1,2},{2,1},{3,0},{4,7},{5,6},{6,5},{7,4},{8,11},{9,10},{10,... | collective-permute-start | bytes 196616 | tf_op jit(solution)/shard_map/ppermute | solution.py:482
  46.7 1.9 %collective-permute-start.15 = (bf16[8,4096]{1,0:T(8,128)(2,1)S(1)}, bf16[8,4096]{1,0:T(8,128)(2,1)S(1)}, u32[]{:S(2)}, u32[]{:S(2)}) collective-permute-start(bf16[8,4096]{1,0:T(8,128)(2,1)S(1)} %get-tuple-element.72), channel_id=1, source_target_pairs={{0,1},{1,0},{2,3},{3,2},{4,5},{5,4},{6,7},{7,6},{8,9},{9,8},{10,11... | collective-permute-start | bytes 196616 | tf_op jit(solution)/shard_map/ppermute | solution.py:482
  48.5 1.7 %collective-permute-done.13.refs_0_ = bf16[8,4096]{1,0:T(8,128)(2,1)S(1)} collective-permute-done((bf16[8,4096]{1,0:T(8,128)(2,1)S(1)}, bf16[8,4096]{1,0:T(8,128)(2,1)S(1)}, u32[]{:S(2)}, u32[]{:S(2)}) %collective-permute-start.13) | collective-permute-done | bytes 65568 | tf_op jit(solution)/shard_map/ppermute | solution.py:482
  50.2 2.1 %collective-permute-done.14.refs_1_ = bf16[8,4096]{1,0:T(8,128)(2,1)S(1)} collective-permute-done((bf16[8,4096]{1,0:T(8,128)(2,1)S(1)}, bf16[8,4096]{1,0:T(8,128)(2,1)S(1)}, u32[]{:S(2)}, u32[]{:S(2)}) %collective-permute-start.14) | collective-permute-done | bytes 65568 | tf_op jit(solution)/shard_map/ppermute | solution.py:482
  52.5 3.9 %collective-permute-start.18 = (bf16[8,4096]{1,0:T(8,128)(2,1)S(1)}, bf16[8,4096]{1,0:T(8,128)(2,1)S(1)}, u32[]{:S(2)}, u32[]{:S(2)}) collective-permute-start(bf16[8,4096]{1,0:T(8,128)(2,1)S(1)} %get-tuple-element.74.refs_3_.refs_1_), channel_id=1, source_target_pairs={{0,3},{1,2},{2,1},{3,0},{4,7},{5,6},{6,5},{7,4},{8,11},{9,10},{10,... | collective-permute-start | bytes 196616 | tf_op jit(solution)/shard_map/ppermute | solution.py:482
  58.9 3.5 %collective-permute-done.17.refs_3_ = bf16[8,4096]{1,0:T(8,128)(2,1)S(1)} collective-permute-done((bf16[8,4096]{1,0:T(8,128)(2,1)S(1)}, bf16[8,4096]{1,0:T(8,128)(2,1)S(1)}, u32[]{:S(2)}, u32[]{:S(2)}) %collective-permute-start.17) | collective-permute-done | bytes 65568 | tf_op jit(solution)/shard_map/ppermute | solution.py:482
  64.7 2.0 %late.5.begun_ref = f32[81,8,256]{2,1,0:T(8,128)S(1)} custom-call(s32[1,1280]{1,0:T(1,128)S(4)} %lists.1.lists_ref, bf16[192,256,256]{2,1,0:T(8,128)(2,1)S(1)} %turn.1.after_ref.blocks_ref, f32[81,8,256]{2,1,0:T(8,128)S(1)} %early.5.begun_ref, f32[64,8,256]{2,1,0:T(8,128)S(1)} %get-tuple-element.75.field_ref, f32[8,640]{1,0:T(8,128)S(1)} %get-tuple-element.63.refs_0_.ratios_ref), custom_call_target="tpu_custom_call" | custom-call | flops 3000000000 | tf_op jit(solution)/shard_map/late/pallas_call | solution.py:498
  68.1 2.4 %collective-permute-done.21.second_ref = f32[8,128]{1,0:T(8,128)S(1)} collective-permute-done((f32[8,128]{1,0:T(8,128)S(1)}, f32[8,128]{1,0:T(8,128)S(1)}, u32[]{:S(2)}, u32[]{:S(2)}) %collective-permute-start.21) | collective-permute-done | bytes 4128 | tf_op jit(solution)/shard_map/ppermute | solution.py:482
  71.5 1.7 %collective-permute-start.26 = (f32[8,4096]{1,0:T(8,128)S(1)}, f32[8,4096]{1,0:T(8,128)S(1)}, u32[]{:S(2)}, u32[]{:S(2)}) collective-permute-start(f32[8,4096]{1,0:T(8,128)S(1)} %get-tuple-element.86), channel_id=1, source_target_pairs={{0,3},{1,2},{2,1},{3,0},{4,7},{5,6},{6,5},{7,4},{8,11},{9,10},{10,... | collective-permute-start | bytes 393224 | tf_op jit(solution)/shard_map/ppermute | solution.py:482
  73.2 1.8 %collective-permute-start.27 = (f32[8,4096]{1,0:T(8,128)S(1)}, f32[8,4096]{1,0:T(8,128)S(1)}, u32[]{:S(2)}, u32[]{:S(2)}) collective-permute-start(f32[8,4096]{1,0:T(8,128)S(1)} %get-tuple-element.90), channel_id=1, source_target_pairs={{0,2},{1,3},{2,0},{3,1},{4,6},{5,7},{6,4},{7,5},{8,10},{9,11},{10,... | collective-permute-start | bytes 393224 | tf_op jit(solution)/shard_map/ppermute | solution.py:482
  76.0 4.4 %collective-permute-start.23 = (f32[8,128]{1,0:T(8,128)S(1)}, f32[8,128]{1,0:T(8,128)S(1)}, u32[]{:S(2)}, u32[]{:S(2)}) collective-permute-start(f32[8,128]{1,0:T(8,128)S(1)} %add_moments.6.first_ref), channel_id=1, source_target_pairs={{0,4},{4,0},{8,12},{12,8},{16,20},{20,16},{24,28},{28,24},{1,5},{5... | collective-permute-start | bytes 12296 | tf_op jit(solution)/shard_map/ppermute | solution.py:482
  81.4 3.0 %collective-permute-start.24 = (f32[8,128]{1,0:T(8,128)S(1)}, f32[8,128]{1,0:T(8,128)S(1)}, u32[]{:S(2)}, u32[]{:S(2)}) collective-permute-start(f32[8,128]{1,0:T(8,128)S(1)} %add_moments.7.first_ref), channel_id=1, source_target_pairs={{0,8},{4,12},{8,0},{12,4},{16,24},{20,28},{24,16},{28,20},{1,9},{5... | collective-permute-start | bytes 12296 | tf_op jit(solution)/shard_map/ppermute | solution.py:482
  84.4 1.6 %collective-permute-done.24.second_ref = f32[8,128]{1,0:T(8,128)S(1)} collective-permute-done((f32[8,128]{1,0:T(8,128)S(1)}, f32[8,128]{1,0:T(8,128)S(1)}, u32[]{:S(2)}, u32[]{:S(2)}) %collective-permute-start.24) | collective-permute-done | bytes 4128 | tf_op jit(solution)/shard_map/ppermute | solution.py:482
  86.1 3.4 %collective-permute-start.25 = (f32[8,128]{1,0:T(8,128)S(1)}, f32[8,128]{1,0:T(8,128)S(1)}, u32[]{:S(2)}, u32[]{:S(2)}) collective-permute-start(f32[8,128]{1,0:T(8,128)S(1)} %add_moments.8.first_ref), channel_id=1, source_target_pairs={{0,16},{4,20},{8,24},{12,28},{16,0},{20,4},{24,8},{28,12},{1,17},{... | collective-permute-start | bytes 12296 | tf_op jit(solution)/shard_map/ppermute | solution.py:482
  89.5 1.6 %collective-permute-done.25.second_ref = f32[8,128]{1,0:T(8,128)S(1)} collective-permute-done((f32[8,128]{1,0:T(8,128)S(1)}, f32[8,128]{1,0:T(8,128)S(1)}, u32[]{:S(2)}, u32[]{:S(2)}) %collective-permute-start.25) | collective-permute-done | bytes 4128 | tf_op jit(solution)/shard_map/ppermute | solution.py:482
  (68 shorter events, 23.1 us)
Async XLA Ops:
  3.0 8.4 %collective-permute-start.2 = (bf16[8,4096]{1,0:T(8,128)(2,1)S(1)}, bf16[8,4096]{1,0:T(8,128)(2,1)S(1)}, u32[]{:S(2)}, u32[]{:S(2)}) collective-permute-start(bf16[8,4096]{1,0:T(8,128)(2,1)S(1)} %get-tuple-element.49.refs_0_.rounded_ref), channel_id=1, source_target_pairs={{0,3},{1,2},{2,1},{3,0},{4,7},{5,6},{6,5},{7,4},{8,11},{9,10},{10,... | collective-permute-start | bytes 196616 | tf_op jit(solution)/shard_map/ppermute | solution.py:482
  8.1 5.6 %collective-permute-start.1 = (bf16[8,4096]{1,0:T(8,128)(2,1)S(1)}, bf16[8,4096]{1,0:T(8,128)(2,1)S(1)}, u32[]{:S(2)}, u32[]{:S(2)}) collective-permute-start(bf16[8,4096]{1,0:T(8,128)(2,1)S(1)} %get-tuple-element.49.refs_0_.rounded_ref), channel_id=1, source_target_pairs={{0,2},{1,3},{2,0},{3,1},{4,6},{5,7},{6,4},{7,5},{8,10},{9,11},{10,... | collective-permute-start | bytes 196616 | tf_op jit(solution)/shard_map/ppermute | solution.py:482
  8.1 5.6 %collective-permute-start = (bf16[8,4096]{1,0:T(8,128)(2,1)S(1)}, bf16[8,4096]{1,0:T(8,128)(2,1)S(1)}, u32[]{:S(2)}, u32[]{:S(2)}) collective-permute-start(bf16[8,4096]{1,0:T(8,128)(2,1)S(1)} %get-tuple-element.49.refs_0_.rounded_ref), channel_id=1, source_target_pairs={{0,1},{1,0},{2,3},{3,2},{4,5},{5,4},{6,7},{7,6},{8,9},{9,8},{10,11... | collective-permute-start | bytes 196616 | tf_op jit(solution)/shard_map/ppermute | solution.py:482
  14.3 4.0 %collective-permute-start.3 = (bf16[8,4096]{1,0:T(8,128)(2,1)S(1)}, bf16[8,4096]{1,0:T(8,128)(2,1)S(1)}, u32[]{:S(2)}, u32[]{:S(2)}) collective-permute-start(bf16[8,4096]{1,0:T(8,128)(2,1)S(1)} %get-tuple-element.51), channel_id=1, source_target_pairs={{0,4},{4,0},{8,12},{12,8},{16,20},{20,16},{24,28},{28,24},{1,5},{5... | collective-permute-start | bytes 196616 | tf_op jit(solution)/shard_map/ppermute | solution.py:490
  14.4 3.9 %collective-permute-start.4 = (bf16[8,4096]{1,0:T(8,128)(2,1)S(1)}, bf16[8,4096]{1,0:T(8,128)(2,1)S(1)}, u32[]{:S(2)}, u32[]{:S(2)}) collective-permute-start(bf16[8,4096]{1,0:T(8,128)(2,1)S(1)} %get-tuple-element.52), channel_id=1, source_target_pairs={{4,8},{8,4},{12,16},{16,12},{20,24},{24,20},{5,9},{9,5},{13,17},{1... | collective-permute-start | bytes 196616 | tf_op jit(solution)/shard_map/ppermute | solution.py:490
  19.2 9.5 %collective-permute-start.5 = (bf16[8,4096]{1,0:T(8,128)(2,1)S(1)}, bf16[8,4096]{1,0:T(8,128)(2,1)S(1)}, u32[]{:S(2)}, u32[]{:S(2)}) collective-permute-start(bf16[8,4096]{1,0:T(8,128)(2,1)S(1)} %get-tuple-element.57), channel_id=1, source_target_pairs={{0,3},{1,2},{2,1},{3,0},{4,7},{5,6},{6,5},{7,4},{8,11},{9,10},{10,... | collective-permute-start | bytes 196616 | tf_op jit(solution)/shard_map/ppermute | solution.py:482
  23.3 5.6 %collective-permute-start.6 = (bf16[8,4096]{1,0:T(8,128)(2,1)S(1)}, bf16[8,4096]{1,0:T(8,128)(2,1)S(1)}, u32[]{:S(2)}, u32[]{:S(2)}) collective-permute-start(bf16[8,4096]{1,0:T(8,128)(2,1)S(1)} %get-tuple-element.58), channel_id=1, source_target_pairs={{0,2},{1,3},{2,0},{3,1},{4,6},{5,7},{6,4},{7,5},{8,10},{9,11},{10,... | collective-permute-start | bytes 196616 | tf_op jit(solution)/shard_map/ppermute | solution.py:482
  23.3 5.6 %collective-permute-start.7 = (bf16[8,4096]{1,0:T(8,128)(2,1)S(1)}, bf16[8,4096]{1,0:T(8,128)(2,1)S(1)}, u32[]{:S(2)}, u32[]{:S(2)}) collective-permute-start(bf16[8,4096]{1,0:T(8,128)(2,1)S(1)} %get-tuple-element.59), channel_id=1, source_target_pairs={{0,1},{1,0},{2,3},{3,2},{4,5},{5,4},{6,7},{7,6},{8,9},{9,8},{10,11... | collective-permute-start | bytes 196616 | tf_op jit(solution)/shard_map/ppermute | solution.py:482
  29.1 6.1 %collective-permute-start.10 = (bf16[8,4224]{1,0:T(8,128)(2,1)S(1)}, bf16[8,4224]{1,0:T(8,128)(2,1)S(1)}, u32[]{:S(2)}, u32[]{:S(2)}) collective-permute-start(bf16[8,4224]{1,0:T(8,128)(2,1)S(1)} %get-tuple-element.62.refs_3_.refs_0_), channel_id=1, source_target_pairs={{0,3},{1,2},{2,1},{3,0},{4,7},{5,6},{6,5},{7,4},{8,11},{9,10},{10,... | collective-permute-start | bytes 202760 | tf_op jit(solution)/shard_map/ppermute | solution.py:482
  32.7 7.1 %collective-permute-start.9 = (bf16[8,4224]{1,0:T(8,128)(2,1)S(1)}, bf16[8,4224]{1,0:T(8,128)(2,1)S(1)}, u32[]{:S(2)}, u32[]{:S(2)}) collective-permute-start(bf16[8,4224]{1,0:T(8,128)(2,1)S(1)} %get-tuple-element.62.refs_3_.refs_0_), channel_id=1, source_target_pairs={{0,2},{1,3},{2,0},{3,1},{4,6},{5,7},{6,4},{7,5},{8,10},{9,11},{10,... | collective-permute-start | bytes 202760 | tf_op jit(solution)/shard_map/ppermute | solution.py:482
  32.7 7.1 %collective-permute-start.8 = (bf16[8,4224]{1,0:T(8,128)(2,1)S(1)}, bf16[8,4224]{1,0:T(8,128)(2,1)S(1)}, u32[]{:S(2)}, u32[]{:S(2)}) collective-permute-start(bf16[8,4224]{1,0:T(8,128)(2,1)S(1)} %get-tuple-element.62.refs_3_.refs_0_), channel_id=1, source_target_pairs={{0,1},{1,0},{2,3},{3,2},{4,5},{5,4},{6,7},{7,6},{8,9},{9,8},{10,11... | collective-permute-start | bytes 202760 | tf_op jit(solution)/shard_map/ppermute | solution.py:482
  44.1 6.1 %collective-permute-start.13 = (bf16[8,4096]{1,0:T(8,128)(2,1)S(1)}, bf16[8,4096]{1,0:T(8,128)(2,1)S(1)}, u32[]{:S(2)}, u32[]{:S(2)}) collective-permute-start(bf16[8,4096]{1,0:T(8,128)(2,1)S(1)} %get-tuple-element.70), channel_id=1, source_target_pairs={{0,3},{1,2},{2,1},{3,0},{4,7},{5,6},{6,5},{7,4},{8,11},{9,10},{10,... | collective-permute-start | bytes 196616 | tf_op jit(solution)/shard_map/ppermute | solution.py:482
  46.7 5.6 %collective-permute-start.14 = (bf16[8,4096]{1,0:T(8,128)(2,1)S(1)}, bf16[8,4096]{1,0:T(8,128)(2,1)S(1)}, u32[]{:S(2)}, u32[]{:S(2)}) collective-permute-start(bf16[8,4096]{1,0:T(8,128)(2,1)S(1)} %get-tuple-element.71), channel_id=1, source_target_pairs={{0,2},{1,3},{2,0},{3,1},{4,6},{5,7},{6,4},{7,5},{8,10},{9,11},{10,... | collective-permute-start | bytes 196616 | tf_op jit(solution)/shard_map/ppermute | solution.py:482
  46.7 5.6 %collective-permute-start.15 = (bf16[8,4096]{1,0:T(8,128)(2,1)S(1)}, bf16[8,4096]{1,0:T(8,128)(2,1)S(1)}, u32[]{:S(2)}, u32[]{:S(2)}) collective-permute-start(bf16[8,4096]{1,0:T(8,128)(2,1)S(1)} %get-tuple-element.72), channel_id=1, source_target_pairs={{0,1},{1,0},{2,3},{3,2},{4,5},{5,4},{6,7},{7,6},{8,9},{9,8},{10,11... | collective-permute-start | bytes 196616 | tf_op jit(solution)/shard_map/ppermute | solution.py:482
  52.5 6.4 %collective-permute-start.18 = (bf16[8,4096]{1,0:T(8,128)(2,1)S(1)}, bf16[8,4096]{1,0:T(8,128)(2,1)S(1)}, u32[]{:S(2)}, u32[]{:S(2)}) collective-permute-start(bf16[8,4096]{1,0:T(8,128)(2,1)S(1)} %get-tuple-element.74.refs_3_.refs_1_), channel_id=1, source_target_pairs={{0,3},{1,2},{2,1},{3,0},{4,7},{5,6},{6,5},{7,4},{8,11},{9,10},{10,... | collective-permute-start | bytes 196616 | tf_op jit(solution)/shard_map/ppermute | solution.py:482
  56.4 6.0 %collective-permute-start.17 = (bf16[8,4096]{1,0:T(8,128)(2,1)S(1)}, bf16[8,4096]{1,0:T(8,128)(2,1)S(1)}, u32[]{:S(2)}, u32[]{:S(2)}) collective-permute-start(bf16[8,4096]{1,0:T(8,128)(2,1)S(1)} %get-tuple-element.74.refs_3_.refs_1_), channel_id=1, source_target_pairs={{0,2},{1,3},{2,0},{3,1},{4,6},{5,7},{6,4},{7,5},{8,10},{9,11},{10,... | collective-permute-start | bytes 196616 | tf_op jit(solution)/shard_map/ppermute | solution.py:482
  56.4 6.6 %collective-permute-start.16 = (bf16[8,4096]{1,0:T(8,128)(2,1)S(1)}, bf16[8,4096]{1,0:T(8,128)(2,1)S(1)}, u32[]{:S(2)}, u32[]{:S(2)}) collective-permute-start(bf16[8,4096]{1,0:T(8,128)(2,1)S(1)} %get-tuple-element.74.refs_3_.refs_1_), channel_id=1, source_target_pairs={{0,1},{1,0},{2,3},{3,2},{4,5},{5,4},{6,7},{7,6},{8,9},{9,8},{10,11... | collective-permute-start | bytes 196616 | tf_op jit(solution)/shard_map/ppermute | solution.py:482
  70.6 4.6 %collective-permute-start.22 = (f32[8,128]{1,0:T(8,128)S(1)}, f32[8,128]{1,0:T(8,128)S(1)}, u32[]{:S(2)}, u32[]{:S(2)}) collective-permute-start(f32[8,128]{1,0:T(8,128)S(1)} %add_moments.5.first_ref), channel_id=1, source_target_pairs={{0,2},{1,3},{2,0},{3,1},{4,6},{5,7},{6,4},{7,5},{8,10},{9,11},{10,... | collective-permute-start | bytes 12296 | tf_op jit(solution)/shard_map/ppermute | solution.py:482
  71.5 19.7 %collective-permute-start.26 = (f32[8,4096]{1,0:T(8,128)S(1)}, f32[8,4096]{1,0:T(8,128)S(1)}, u32[]{:S(2)}, u32[]{:S(2)}) collective-permute-start(f32[8,4096]{1,0:T(8,128)S(1)} %get-tuple-element.86), channel_id=1, source_target_pairs={{0,3},{1,2},{2,1},{3,0},{4,7},{5,6},{6,5},{7,4},{8,11},{9,10},{10,... | collective-permute-start | bytes 393224 | tf_op jit(solution)/shard_map/ppermute | solution.py:482
  73.2 18.0 %collective-permute-start.27 = (f32[8,4096]{1,0:T(8,128)S(1)}, f32[8,4096]{1,0:T(8,128)S(1)}, u32[]{:S(2)}, u32[]{:S(2)}) collective-permute-start(f32[8,4096]{1,0:T(8,128)S(1)} %get-tuple-element.90), channel_id=1, source_target_pairs={{0,2},{1,3},{2,0},{3,1},{4,6},{5,7},{6,4},{7,5},{8,10},{9,11},{10,... | collective-permute-start | bytes 393224 | tf_op jit(solution)/shard_map/ppermute | solution.py:482
  75.2 16.0 %collective-permute-start.28 = (f32[8,4096]{1,0:T(8,128)S(1)}, f32[8,4096]{1,0:T(8,128)S(1)}, u32[]{:S(2)}, u32[]{:S(2)}) collective-permute-start(f32[8,4096]{1,0:T(8,128)S(1)} %get-tuple-element.93), channel_id=1, source_target_pairs={{0,1},{1,0},{2,3},{3,2},{4,5},{5,4},{6,7},{7,6},{8,9},{9,8},{10,11... | collective-permute-start | bytes 393224 | tf_op jit(solution)/shard_map/ppermute | solution.py:482
  76.0 5.3 %collective-permute-start.23 = (f32[8,128]{1,0:T(8,128)S(1)}, f32[8,128]{1,0:T(8,128)S(1)}, u32[]{:S(2)}, u32[]{:S(2)}) collective-permute-start(f32[8,128]{1,0:T(8,128)S(1)} %add_moments.6.first_ref), channel_id=1, source_target_pairs={{0,4},{4,0},{8,12},{12,8},{16,20},{20,16},{24,28},{28,24},{1,5},{5... | collective-permute-start | bytes 12296 | tf_op jit(solution)/shard_map/ppermute | solution.py:482
  81.4 4.6 %collective-permute-start.24 = (f32[8,128]{1,0:T(8,128)S(1)}, f32[8,128]{1,0:T(8,128)S(1)}, u32[]{:S(2)}, u32[]{:S(2)}) collective-permute-start(f32[8,128]{1,0:T(8,128)S(1)} %add_moments.7.first_ref), channel_id=1, source_target_pairs={{0,8},{4,12},{8,0},{12,4},{16,24},{20,28},{24,16},{28,20},{1,9},{5... | collective-permute-start | bytes 12296 | tf_op jit(solution)/shard_map/ppermute | solution.py:482
  86.1 5.0 %collective-permute-start.25 = (f32[8,128]{1,0:T(8,128)S(1)}, f32[8,128]{1,0:T(8,128)S(1)}, u32[]{:S(2)}, u32[]{:S(2)}) collective-permute-start(f32[8,128]{1,0:T(8,128)S(1)} %add_moments.8.first_ref), channel_id=1, source_target_pairs={{0,16},{4,20},{8,24},{12,28},{16,0},{20,4},{24,8},{28,12},{1,17},{... | collective-permute-start | bytes 12296 | tf_op jit(solution)/shard_map/ppermute | solution.py:482
  (9 other events, 39.5 us)
